TPU v7x, 32 devices: a whole 2x2x4 slice. The times are simulated.
32 devices in a mesh: expert: 8 (over z, core), replica: 4 (over y, x).
Axes of the slice: x: 2, y: 2, z: 4, core: 2. Of those that a mesh axis runs over, the one named last changes fastest.
Arguments:
- weights: bfloat16 [8, 3, 2048, 512], P('expert', None, 'replica'), may hold values from -0.125 to 0.125
- first_moment: float32 [8, 3, 2048, 512], P('expert', None, 'replica'), may hold values from -128 to 128
- second_moment: float32 [8, 3, 2048, 512], P('expert', None, 'replica'), may hold values from 100 to 100000
- out_grads: bfloat16 [4, 1024, 2048], P('replica', 'expert'), may hold values from -8 to 8
- routes: int32 [4, 1024, 1], P('replica', 'expert'), may hold values from 0 to 7; in each aligned block of 128 rows (0 to 127, 128 to 255, ..., all dimensions but the last counted through in order) at most 32 rows name the same one
- task_ids: int32 [4, 8], P('replica', 'expert'), may hold values from 0 to 7
- task_weights: float32 [8], replicated, may hold values from 0.25 to 4
- saved_inputs: bfloat16 [4, 8, 256, 2048], P('replica', 'expert'), may hold values from -8 to 8
Outputs:
- input_grads: bfloat16 [4, 1024, 2048], P('replica', 'expert')
- adam_step: float32 [8, 3, 2048, 512], P('expert', None, 'replica')
Inputs may be any that keep to these rules, and one draw needn't show every extreme that they name: `routes`: at most 32 of the rows of one device go to one expert, and in every draw some device sends exactly 32 rows to some expert.
All inputs are finite; a program needn't handle non-finite values.
Results may differ from a plain program's by a relative error of at most 0.0057.
Values may be sent and summed in bfloat16 or wider, within the bound.
No kernel may reach another device: no remote copies, remote signals or barrier semaphores. Data moves between devices by JAX's collectives and lax.ppermute only.
A program may use at most 128 MiB of HBM per device.

v0:
```python
import jax
import jax.numpy as jnp
from jax import lax
from jax.sharding import PartitionSpec as P

beta_first = 0.9
beta_second = 0.95
adam_eps = 1e-08
norm_eps = 1e-06
first_fix = 1.0 - (0.9**50) ** 2
second_fix = 1.0 - (0.95**50) ** 2


def from_partner(array, axis, bit):
    return lax.ppermute(array, axis, [(i, i ^ 1 << bit) for i in range(lax.axis_size(axis))])


def contract_rows(left, right):
    return lax.dot_general(
        left, right, (((0,), (0,)), ((), ())), preferred_element_type=jnp.float32
    )


def contract_last(left, right):
    return lax.dot_general(
        left, right, (((1,), (1,)), ((), ())), preferred_element_type=jnp.float32
    )


def group_total(partials, level_now):
    totals = partials
    for bit_pos in range(level_now + 1):
        totals = totals + from_partner(totals, "replica", bit_pos)
    return totals


def merge_level(kept_part, got_part, bit_now, level_now):
    own_square = jnp.sum(kept_part * kept_part)
    got_square = jnp.sum(got_part * got_part)
    cross_sum = jnp.sum(kept_part * got_part)
    low_side = bit_now == 0
    norm_first = jnp.where(low_side, own_square, got_square)
    norm_second = jnp.where(low_side, got_square, own_square)
    totals = group_total(jnp.stack([cross_sum, norm_first, norm_second]), level_now)
    coef_first = 1.0 - totals[0] / (2.0 * (totals[1] + norm_eps))
    coef_second = 1.0 - totals[0] / (2.0 * (totals[2] + norm_eps))
    kept_coef = jnp.where(low_side, coef_first, coef_second)
    got_coef = jnp.where(low_side, coef_second, coef_first)
    return kept_coef * kept_part + got_coef * got_part


def split_level(pieces, level_now, rep_index):
    bit_now = rep_index >> level_now & 1
    paired = pieces.reshape(
        pieces.shape[0], pieces.shape[1] // 2, 2, pieces.shape[2], pieces.shape[3]
    )
    kept_part = lax.dynamic_index_in_dim(paired, bit_now, axis=2, keepdims=False)
    give_part = lax.dynamic_index_in_dim(paired, 1 - bit_now, axis=2, keepdims=False)
    got_part = from_partner(give_part.astype(jnp.bfloat16), "replica", level_now).astype(
        jnp.float32
    )
    return merge_level(kept_part, got_part, bit_now, level_now)


def shards(
    weights, first_moment, second_moment, out_grads, routes, task_ids, task_weights, saved_inputs
):
    expert_count = lax.axis_size("expert")
    rep_count = lax.axis_size("replica")
    rep_index = lax.axis_index("replica")
    row_count = out_grads.shape[1]
    model_width = out_grads.shape[2]
    hidden_width = weights.shape[3]
    slot_count = saved_inputs.shape[2]
    capacity = slot_count // expert_count
    block_count = task_ids.shape[1]
    block_rows = row_count // block_count
    task_count = task_weights.shape[0]
    seg_rows = model_width // rep_count
    levels = rep_count.bit_length() - 1
    chosen_task = (task_ids[0][:, None] == jnp.arange(task_count, dtype=jnp.int32)[None, :]).astype(
        jnp.float32
    )
    block_weight = jnp.sum(chosen_task * task_weights[None, :], axis=1)
    scaled = (
        (out_grads[0].reshape(block_count, block_rows, model_width) * block_weight[:, None, None])
        .reshape(row_count, model_width)
        .astype(jnp.bfloat16)
    )
    expert_of = routes[0, :, 0]
    chosen = (expert_of[:, None] == jnp.arange(expert_count, dtype=jnp.int32)[None, :]).astype(
        jnp.int32
    )
    slot_rank = jnp.sum((jnp.cumsum(chosen, axis=0) - chosen) * chosen, axis=1)
    slot_index = expert_of * capacity + slot_rank
    placing = (slot_index[:, None] == jnp.arange(slot_count, dtype=jnp.int32)[None, :]).astype(
        jnp.bfloat16
    )
    outgoing = (
        contract_rows(placing, scaled)
        .astype(jnp.bfloat16)
        .reshape(expert_count, capacity, model_width)
    )
    incoming = lax.all_to_all(outgoing, "expert", split_axis=0, concat_axis=0, tiled=True).reshape(
        slot_count, model_width
    )
    gathered = lax.all_gather(weights, "replica", axis=2, tiled=True)[0]
    inputs = saved_inputs[0, 0]
    gate_pre = jnp.dot(inputs, gathered[0], preferred_element_type=jnp.float32)
    up_pre = jnp.dot(inputs, gathered[1], preferred_element_type=jnp.float32)
    gate_act = jax.nn.silu(gate_pre)
    hidden = (gate_act * up_pre).astype(jnp.bfloat16)
    hidden_grad = jnp.dot(incoming, gathered[2], preferred_element_type=jnp.float32)
    sigmoid_gate = jax.nn.sigmoid(gate_pre)
    gate_grad = (
        hidden_grad * up_pre * sigmoid_gate * (1.0 + gate_pre * (1.0 - sigmoid_gate))
    ).astype(jnp.bfloat16)
    up_grad = (hidden_grad * gate_act).astype(jnp.bfloat16)
    slot_grads = (
        contract_last(gate_grad, gathered[0]) + contract_last(up_grad, gathered[1])
    ).astype(jnp.bfloat16)
    returned = lax.all_to_all(
        slot_grads.reshape(expert_count, capacity, model_width),
        "expert",
        split_axis=0,
        concat_axis=0,
        tiled=True,
    ).reshape(slot_count, model_width)
    input_grads = jnp.dot(placing, returned, preferred_element_type=jnp.float32).astype(
        jnp.bfloat16
    )[None]
    bit_first = rep_index & 1
    half_width = model_width // 2

    def kept_columns(matrix, pick_side):
        shaped = matrix.reshape(slot_count, rep_count // 2, 2, seg_rows)
        return lax.dynamic_index_in_dim(shaped, pick_side, axis=2, keepdims=False).reshape(
            slot_count, half_width
        )

    mine_inputs = kept_columns(inputs, bit_first)
    mine_incoming = kept_columns(incoming, bit_first)
    sending = jnp.concatenate(
        [
            kept_columns(inputs, 1 - bit_first),
            kept_columns(incoming, 1 - bit_first),
            gate_grad,
            up_grad,
            hidden,
        ],
        axis=1,
    )
    partner = from_partner(sending, "replica", 0)
    partner_inputs = partner[:, :half_width]
    partner_incoming = partner[:, half_width:model_width]
    partner_gate = partner[:, model_width : model_width + hidden_width]
    partner_up = partner[:, model_width + hidden_width : model_width + 2 * hidden_width]
    partner_hidden = partner[:, model_width + 2 * hidden_width :]
    kept_part = jnp.stack(
        [
            contract_rows(mine_inputs, gate_grad),
            contract_rows(mine_inputs, up_grad),
            contract_rows(mine_incoming, hidden),
        ]
    )
    partner_grads = jnp.stack(
        [
            contract_rows(partner_inputs, partner_gate),
            contract_rows(partner_inputs, partner_up),
            contract_rows(partner_incoming, partner_hidden),
        ]
    )
    narrow = lax.optimization_barrier(partner_grads.astype(jnp.bfloat16))
    got_part = narrow.astype(jnp.float32)
    kept_part = kept_part.reshape(3, rep_count // 2, seg_rows, hidden_width)
    got_part = got_part.reshape(3, rep_count // 2, seg_rows, hidden_width)
    pieces = merge_level(kept_part, got_part, bit_first, 0)
    start_level = 1
    for level_now in range(start_level, levels):
        pieces = split_level(pieces, level_now, rep_index)
    merged = pieces.reshape(3, seg_rows, hidden_width)
    first_new = beta_first * first_moment[0] + (1.0 - beta_first) * merged
    second_new = beta_second * second_moment[0] + (1.0 - beta_second) * merged * merged
    adam_step = (first_new / first_fix / (jnp.sqrt(second_new / second_fix) + adam_eps))[None]
    return (input_grads, adam_step)


def solution(mesh):
    return jax.shard_map(
        shards,
        mesh=mesh,
        in_specs=(
            P("expert", None, "replica", None),
            P("expert", None, "replica", None),
            P("expert", None, "replica", None),
            P("replica", "expert", None),
            P("replica", "expert", None),
            P("replica", "expert"),
            P(),
            P("replica", "expert", None, None),
        ),
        out_specs=(P("replica", "expert", None), P("expert", None, "replica", None)),
        check_vma=False,
    )
```

profile of v0, /device:TPU:0, one launch (start us, length us, event | category | flops | bytes accessed | tf_op | source)
XLA Modules:
  0.0 227.7 jit_solution(13185863820624870168)
XLA Ops:
  7.2 0.7 all-gather.2.cloned.1.call-update
  8.6 0.7 fusion.34
  9.3 0.2 reduce_window_sum.11
  9.5 1.3 fusion.35
  10.7 0.8 select_reduce_fusion
  11.6 0.7 multiply_add_fusion
  12.2 3.2 %convolution_convert_fusion = bf16[256,2048]{1,0:T(8,128)(2,1)} fusion(bf16[1,128,2048]{2,1,0:T(8,128)(2,1)} %param.11, f32[]{:T(128)} %fusion.35, s32[128]{0:T(128)S(1)} %multiply_add_fusion), kind=kOutput, calls=%fused_computation.26 | convolution fusion | flops 135561216 | bytes 1573380 | tf_op jit(solution)/shard_map/dot_general | solution.py:19
  15.4 6.3 %all-to-all-start = ((bf16[8,32,2048]{2,1,0:T(8,128)(2,1)}), bf16[8,32,2048]{2,1,0:T(8,128)(2,1)S(1)}, u32[]{:S(2)}, u32[]{:S(2)}) async-start(bf16[8,32,2048]{2,1,0:T(8,128)(2,1)} %bitcast.3), calls=%async_computation | async-start | bytes 2097152 | tf_op jit(solution)/shard_map/all_to_all | solution.py:104
  21.8 0.5 copy.21
  22.4 0.8 constant_dynamic-update-slice_fusion.4
  23.2 25.1 %all-to-all-done = bf16[8,32,2048]{2,1,0:T(8,128)(2,1)S(1)} async-done(((bf16[8,32,2048]{2,1,0:T(8,128)(2,1)}), bf16[8,32,2048]{2,1,0:T(8,128)(2,1)S(1)}, u32[]{:S(2)}, u32[]{:S(2)}) %all-to-all-start) | async-done | bytes 1048608 | tf_op jit(solution)/shard_map/all_to_all | solution.py:104
  48.4 1.0 copy-done.6
  49.3 0.8 reshape_reshape.4
  50.1 3.2 %constant_dynamic-slice_fusion.2 = (bf16[256,2,1,512]{3,2,1,0:T(2,128)(2,1)S(1)}, bf16[256,2,1,512]{3,2,1,0:T(2,128)(2,1)}) fusion(bf16[256,2,2,512]{3,2,1,0:T(2,128)(2,1)S(1)} %reshape_reshape.4, s32[]{:T(128)S(6)} %select_n.41, s32[]{:T(128)S(6)} %select_n.42), kind=kLoop, calls=%fused_computation.72 | loop fusion | bytes 2097160 | tf_op jit(solution)/shard_map/jit(dynamic_index_in_dim)/dynamic_slice | solution.py:137
  53.3 2.3 %copy.23 = bf16[256,2,1,512]{0,3,1,2:T(8,128)(2,1)S(1)} copy(bf16[256,2,1,512]{3,2,1,0:T(2,128)(2,1)} %get-tuple-element.10) | data formatting | bytes 1048576 | tf_op jit(solution)/shard_map/jit(dynamic_index_in_dim)/dynamic_slice | solution.py:137
  55.6 2.0 copy.22
  57.6 0.8 constant_dynamic-update-slice_fusion.3
  58.4 24.3 %all-gather.2.cloned.1.call-done = bf16[1,3,2048,512]{3,2,1,0:T(8,128)(2,1)} async-done(((bf16[1,3,512,512]{3,2,1,0:T(8,128)(2,1)}), bf16[1,3,2048,512]{3,2,1,0:T(8,128)(2,1)}) %all-gather.2.cloned.1.call-update) | async-done | bytes 6291472 | tf_op jit(solution)/shard_map/all_gather | solution.py:107
  82.7 2.6 %fusion.16 = f32[256,512]{1,0:T(8,128)S(1)} fusion(bf16[1,3,2048,512]{3,2,1,0:T(8,128)(2,1)} %all-gather.2.cloned.1.call-done, bf16[1,1,256,2048]{3,2,1,0:T(8,128)(2,1)} %param.15), kind=kOutput, calls=%fused_computation.35 | convolution fusion | flops 536870912 | bytes 3670016 | tf_op jit(solution)/shard_map/dot_general | solution.py:109
  85.4 2.4 %fusion.13 = f32[256,512]{1,0:T(8,128)S(1)} fusion(bf16[256,2048]{1,0:T(8,128)(2,1)S(1)} %bitcast.93, bf16[1,3,2048,512]{3,2,1,0:T(8,128)(2,1)} %all-gather.2.cloned.1.call-done), kind=kOutput, calls=%fused_computation.32 | convolution fusion | flops 536870912 | bytes 3670016 | tf_op jit(solution)/shard_map/dot_general | solution.py:113
  87.8 2.5 %multiply_convert_fusion.1 = (bf16[256,512]{1,0:T(8,128)(2,1)S(1)}, bf16[256,512]{1,0:T(8,128)(2,1)S(1)}, bf16[256,512]{1,0:T(8,128)(2,1)S(1)}) fusion(f32[256,512]{1,0:T(8,128)S(1)} %fusion.16, f32[256,512]{1,0:T(8,128)S(1)} %fusion.13, bf16[1,3,2048,512]{3,2,1,0:T(8,128)(2,1)} %all-gather.2.cloned.1.call-done, bf16[1,1,256,2048]{3,2,1,0:T(8,128)(2,1)S(1)} %copy-done.10), kind=kOutput, calls=%fused_computation.47 | convolution fusion | flops 538836992 | bytes 4980736 | tf_op jit(solution)/shard_map/dot_general | solution.py:110
  90.2 0.1 copy.24
  90.4 0.1 copy.25
  90.7 0.7 constant_dynamic-update-slice_fusion.2
  91.4 0.7 constant_dynamic-update-slice_fusion.1
  92.1 0.7 constant_dynamic-update-slice_fusion
  92.8 1.5 collective-permute-start
  94.3 2.3 %fusion.15 = f32[256,2048]{1,0:T(8,128)S(1)} fusion(bf16[256,512]{1,0:T(8,128)(2,1)S(1)} %get-tuple-element.12, bf16[1,3,2048,512]{3,2,1,0:T(8,128)(2,1)} %all-gather.2.cloned.1.call-done), kind=kOutput, calls=%fused_computation.34 | convolution fusion | flops 536870912 | bytes 4456448 | tf_op jit(solution)/shard_map/dot_general | solution.py:25
  96.6 3.3 %fusion.11 = bf16[256,2048]{1,0:T(8,128)(2,1)} fusion(f32[256,2048]{1,0:T(8,128)S(1)} %fusion.15, bf16[256,512]{1,0:T(8,128)(2,1)S(1)} %get-tuple-element.13, bf16[1,3,2048,512]{3,2,1,0:T(8,128)(2,1)} %all-gather.2.cloned.1.call-done), kind=kOutput, calls=%fused_computation.25 | convolution fusion | flops 537919488 | bytes 5505024 | tf_op jit(solution)/shard_map/dot_general | solution.py:25
  99.9 4.6 %all-to-all-start.1 = ((bf16[8,32,2048]{2,1,0:T(8,128)(2,1)}), bf16[8,32,2048]{2,1,0:T(8,128)(2,1)}, u32[]{:S(2)}, u32[]{:S(2)}) async-start(bf16[8,32,2048]{2,1,0:T(8,128)(2,1)} %bitcast.9), calls=%async_computation.1 | async-start | bytes 2097152 | tf_op jit(solution)/shard_map/all_to_all | solution.py:122
  104.5 0.4 fusion.39
  105.0 0.4 fusion.38
  105.4 0.2 copy-done.8
  105.6 0.4 fusion.40
  106.0 2.2 multiply_reduce_fusion
  108.3 26.6 %collective-permute-done = bf16[256,3584]{0,1:T(8,128)(2,1)} collective-permute-done((bf16[256,3584]{0,1:T(8,128)(2,1)}, bf16[256,3584]{0,1:T(8,128)(2,1)}, u32[]{:S(2)}, u32[]{:S(2)}) %collective-permute-start) | collective-permute-done | bytes 1835040 | tf_op jit(solution)/shard_map/ppermute | solution.py:15
  134.9 1.6 fusion.19
  136.5 1.6 fusion.18
  138.1 1.6 fusion.17
  139.6 0.3 pad_maximum_fusion.1
  140.0 2.3 %fusion = (f32[]{:T(128)}, f32[]{:T(128)}) fusion(bf16[3,1024,512]{2,1,0:T(8,128)(2,1)S(1)} %pad_maximum_fusion.1, f32[1,1024,512]{2,1,0:T(8,128)S(1)} %bitcast.88, f32[1,1024,512]{2,1,0:T(8,128)S(1)} %bitcast.82, f32[1,1024,512]{2,1,0:T(8,128)S(1)} %bitcast.85), kind=kLoop, calls=%fused_computation.3 | loop fusion | flops 11010046 | bytes 9437192 | tf_op jit(solution)/shard_map/reduce_sum | solution.py:40
  144.9 0.7 pad_maximum_fusion.2
  145.6 1.5 collective-permute-start.1
  147.1 2.1 collective-permute-done.1
  149.1 0.7 fusion.52
  149.9 0.7 fusion.37
  153.2 2.9 %convert_multiply_fusion = f32[3,1024,512]{2,1,0:T(8,128)S(1)} fusion(bf16[3,1024,512]{2,1,0:T(8,128)(2,1)} %copy-done.5, f32[]{:T(128)S(6)} %select_n.46), kind=kLoop, calls=%fused_computation | loop fusion | flops 3145728 | bytes 9437188 | tf_op jit(solution)/shard_map/mul | solution.py:49
  156.1 0.2 copy-done.3
  156.3 1.5 copy_add_fusion
  157.9 2.6 %copy-done.4 = f32[3,2,512,512]{3,2,0,1:T(8,128)} copy-done((f32[3,2,512,512]{3,2,0,1:T(8,128)}, f32[3,2,512,512]{3,2,0,1:T(8,128)S(1)}, u32[]{:S(2)}) %copy-start.4) | copy-done | bytes 6291480
  160.5 0.2 dynamic-slice_convert_fusion
  160.7 1.5 collective-permute-start.2
  162.2 2.4 %fusion.12 = bf16[1,128,2048]{2,1,0:T(8,128)(2,1)} fusion(bf16[256,2048]{1,0:T(8,128)(2,1)} %bitcast.10, s32[128]{0:T(128)S(1)} %multiply_add_fusion), kind=kOutput, calls=%fused_computation.28 | convolution fusion | flops 134512640 | bytes 1573376 | tf_op jit(solution)/shard_map/dot_general | solution.py:129
  164.6 30.3 %collective-permute-done.2 = bf16[3,1,512,512]{3,2,0,1:T(8,128)(2,1)S(1)} collective-permute-done((bf16[3,1,512,512]{3,2,0,1:T(8,128)(2,1)S(1)}, bf16[3,1,512,512]{3,2,0,1:T(8,128)(2,1)S(1)}, u32[]{:S(2)}, u32[]{:S(2)}) %collective-permute-start.2) | collective-permute-done | bytes 1572896 | tf_op jit(solution)/shard_map/ppermute | solution.py:15
  194.9 3.3 %fusion.2 = (f32[]{:T(128)}, f32[]{:T(128)}, f32[]{:T(128)}) fusion(bf16[3,1,512,512]{3,2,0,1:T(8,128)(2,1)S(1)} %collective-permute-done.2, f32[3,2,512,512]{3,2,0,1:T(8,128)} %copy-done.4, s32[]{:T(128)S(6)} %select_n.47), kind=kLoop, calls=%fused_computation.12 | loop fusion | flops 5505021 | bytes 4718608 | tf_op jit(solution)/shard_map/reduce_sum | solution.py:40
  200.7 0.7 pad_maximum_fusion.3
  201.4 1.5 collective-permute-start.3
  202.9 2.1 collective-permute-done.3
  204.9 0.7 fusion.51
  205.7 1.5 collective-permute-start.4
  207.1 2.1 collective-permute-done.4
  209.2 0.7 fusion.53
  209.9 0.6 fusion.36
  213.1 7.8 %fusion.10 = f32[1,3,512,512]{3,2,1,0:T(8,128)} fusion(f32[1,3,512,512]{3,2,1,0:T(8,128)} %param.10, bf16[3,1,512,512]{3,2,0,1:T(8,128)(2,1)S(1)} %collective-permute-done.2, f32[1,3,512,512]{3,2,1,0:T(8,128)} %param.9, f32[3,2,512,512]{3,2,0,1:T(8,128)} %copy-done.4, s32[]{:T(128)S(6)} %select_n.47, f32[]{:T(128)S(6)} %select_n.52, f32[]{:T(128)S(6)} %select_n.51), kind=kLoop, calls=%fused_computation.20 | loop fusion | flops 11796480 | bytes 14155788 | tf_op jit(solution)/shard_map/div | solution.py:184
  (22 shorter events, 0.3 us)
Async XLA Ops:
  7.2 14.6 %copy-start.9 = (bf16[1,1,256,2048]{3,2,1,0:T(8,128)(2,1)S(1)}, bf16[1,1,256,2048]{3,2,1,0:T(8,128)(2,1)}, u32[]{:S(2)}) copy-start(bf16[1,1,256,2048]{3,2,1,0:T(8,128)(2,1)} %param.15) | copy-start | bytes 3145732
  7.2 75.6 %all-gather.2.cloned.1.call-start = ((), (), s32[]{:S(2)}) async-start(), calls=%async_computation.2 | async-start | bytes 7864320 | tf_op jit(solution)/shard_map/all_gather | solution.py:107
  15.4 32.9 %all-to-all-start = ((bf16[8,32,2048]{2,1,0:T(8,128)(2,1)}), bf16[8,32,2048]{2,1,0:T(8,128)(2,1)S(1)}, u32[]{:S(2)}, u32[]{:S(2)}) async-start(bf16[8,32,2048]{2,1,0:T(8,128)(2,1)} %bitcast.3), calls=%async_computation | async-start | bytes 2097152 | tf_op jit(solution)/shard_map/all_to_all | solution.py:104
  48.4 1.0 copy-start.6
  57.6 27.8 %copy-start.7 = (bf16[8,32,2048]{2,1,0:T(8,128)(2,1)S(1)}, bf16[8,32,2048]{2,1,0:T(8,128)(2,1)}, u32[]{:S(2)}) copy-start(bf16[8,32,2048]{2,1,0:T(8,128)(2,1)} %copy-done.6) | copy-start | bytes 3145732
  85.4 2.4 %copy-start.10 = (bf16[1,1,256,2048]{3,2,1,0:T(8,128)(2,1)S(1)}, bf16[1,1,256,2048]{3,2,1,0:T(8,128)(2,1)}, u32[]{:S(2)}) copy-start(bf16[1,1,256,2048]{3,2,1,0:T(8,128)(2,1)} %param.15) | copy-start | bytes 3145732
  92.8 42.1 %collective-permute-start = (bf16[256,3584]{0,1:T(8,128)(2,1)}, bf16[256,3584]{0,1:T(8,128)(2,1)}, u32[]{:S(2)}, u32[]{:S(2)}) collective-permute-start(bf16[256,3584]{0,1:T(8,128)(2,1)} %constant_dynamic-update-slice_fusion), channel_id=1, source_target_pairs={{0,1},{1,0},{2,3},{3,2},{4,5},{5,4},{6,7},{7,6},{8,9},{9,8},{10,11... | collective-permute-start | bytes 5505032 | tf_op jit(solution)/shard_map/ppermute | solution.py:15
  99.9 62.3 %all-to-all-start.1 = ((bf16[8,32,2048]{2,1,0:T(8,128)(2,1)}), bf16[8,32,2048]{2,1,0:T(8,128)(2,1)}, u32[]{:S(2)}, u32[]{:S(2)}) async-start(bf16[8,32,2048]{2,1,0:T(8,128)(2,1)} %bitcast.9), calls=%async_computation.1 | async-start | bytes 2097152 | tf_op jit(solution)/shard_map/all_to_all | solution.py:122
  104.5 1.0 copy-start.8
  105.4 34.6 %copy-start = (f32[1024,512]{1,0:T(8,128)}, f32[1024,512]{1,0:T(8,128)S(1)}, u32[]{:S(2)}) copy-start(f32[1024,512]{1,0:T(8,128)S(1)} %fusion.38) | copy-start | bytes 6291460
  106.0 34.0 %copy-start.2 = (f32[1024,512]{1,0:T(8,128)}, f32[1024,512]{1,0:T(8,128)S(1)}, u32[]{:S(2)}) copy-start(f32[1024,512]{1,0:T(8,128)S(1)} %fusion.40) | copy-start | bytes 6291460
  140.0 2.4 %copy-start.5 = (bf16[3,1024,512]{2,1,0:T(8,128)(2,1)}, bf16[3,1024,512]{2,1,0:T(8,128)(2,1)S(1)}, u32[]{:S(2)}) copy-start(bf16[3,1024,512]{2,1,0:T(8,128)(2,1)S(1)} %pad_maximum_fusion.1) | copy-start | bytes 9437188
  145.6 3.5 %collective-permute-start.1 = (f32[3]{0:T(128)S(1)}, f32[3]{0:T(128)S(1)}, u32[]{:S(2)}, u32[]{:S(2)}) collective-permute-start(f32[3]{0:T(128)S(1)} %pad_maximum_fusion.2), channel_id=1, source_target_pairs={{0,1},{1,0},{2,3},{3,2},{4,5},{5,4},{6,7},{7,6},{8,9},{9,8},{10,11... | collective-permute-start | bytes 44 | tf_op jit(solution)/shard_map/ppermute | solution.py:15
  153.2 3.0 %copy-start.1 = (f32[1024,512]{1,0:T(8,128)S(1)}, f32[1024,512]{1,0:T(8,128)}, u32[]{:S(2)}) copy-start(f32[1024,512]{1,0:T(8,128)} %copy-done) | copy-start | bytes 6291460
  153.2 3.2 %copy-start.3 = (f32[1024,512]{1,0:T(8,128)S(1)}, f32[1024,512]{1,0:T(8,128)}, u32[]{:S(2)}) copy-start(f32[1024,512]{1,0:T(8,128)} %copy-done.2) | copy-start | bytes 6291460
  157.9 2.6 %copy-start.4 = (f32[3,2,512,512]{3,2,0,1:T(8,128)}, f32[3,2,512,512]{3,2,0,1:T(8,128)S(1)}, u32[]{:S(2)}) copy-start(f32[3,2,512,512]{3,2,0,1:T(8,128)S(1)} %copy_add_fusion) | copy-start | bytes 18874372
  160.7 34.2 %collective-permute-start.2 = (bf16[3,1,512,512]{3,2,0,1:T(8,128)(2,1)S(1)}, bf16[3,1,512,512]{3,2,0,1:T(8,128)(2,1)S(1)}, u32[]{:S(2)}, u32[]{:S(2)}) collective-permute-start(bf16[3,1,512,512]{3,2,0,1:T(8,128)(2,1)S(1)} %dynamic-slice_convert_fusion), channel_id=1, source_target_pairs={{0,2},{1,3},{2,0},{3,1},{4,6},{5,7},{6,4},{7,5},{8,10},{9,11},{10,... | collective-permute-start | bytes 4718600 | tf_op jit(solution)/shard_map/ppermute | solution.py:15
  201.4 3.5 %collective-permute-start.3 = (f32[3]{0:T(128)S(1)}, f32[3]{0:T(128)S(1)}, u32[]{:S(2)}, u32[]{:S(2)}) collective-permute-start(f32[3]{0:T(128)S(1)} %pad_maximum_fusion.3), channel_id=1, source_target_pairs={{0,1},{1,0},{2,3},{3,2},{4,5},{5,4},{6,7},{7,6},{8,9},{9,8},{10,11... | collective-permute-start | bytes 44 | tf_op jit(solution)/shard_map/ppermute | solution.py:15
  205.7 3.5 %collective-permute-start.4 = (f32[3]{0:T(128)S(1)}, f32[3]{0:T(128)S(1)}, u32[]{:S(2)}, u32[]{:S(2)}) collective-permute-start(f32[3]{0:T(128)S(1)} %fusion.51), channel_id=1, source_target_pairs={{0,2},{1,3},{2,0},{3,1},{4,6},{5,7},{6,4},{7,5},{8,10},{9,11},{10,... | collective-permute-start | bytes 44 | tf_op jit(solution)/shard_map/ppermute | solution.py:15
Sparse Core Ops, SparseCore 0:
  9.9 72.8 all-gather.1
where the time goes:
time: 229 us; the launch traced here: 228 us
  waiting for transfers between devices  113 us (49%)
  other arithmetic  27.8 us (12%)
  between operations  25.1 us (11%)
  matrix products  24.7 us (11%)
  local copies, waits for them, and re-layouts  18.5 us (8%)
  starting transfers between devices  18.4 us (8%)
    ppermute x5, waiting for transfers between devices, from_partner(): lax.ppermute(array, axis, [(i, i ^ 1 << bit) for i in range(lax.axis_size...  63.2 us
    all_to_all x1, waiting for transfers between devices, shards(): lax.all_to_all(outgoing, 'expert', split_axis=0, concat_axis=0, tiled=True)  25.1 us
    all_gather x1, waiting for transfers between devices, shards(): gathered = lax.all_gather(weights, 'replica', axis=2, tiled=True)[0]  24.3 us
    dot_general x7, matrix products, contract_rows(): lax.dot_general(left, right, (((0,), (0,)), ((), ())), preferred_element_...  9.21 us
    div x1, other arithmetic, shards(): first_new / first_fix / (jnp.sqrt(second_new / second_fix) + adam_eps)  7.77 us
    unnamed x27, local copies, waits for them, and re-layouts  7.59 us
    dynamic_slice x4, local copies, waits for them, and re-layouts, kept_columns(): lax.dynamic_index_in_dim(shaped, pick_side, axis=2, keepdims=False)  7.56 us
    ppermute x5, starting transfers between devices, from_partner(): lax.ppermute(array, axis, [(i, i ^ 1 << bit) for i in range(lax.axis_size...  7.39 us
  transfers between devices with their start and end apart: 8, of which 7 were waited for; matrix products, arithmetic and copies ran while one was open for 19% of the time, Pallas kernels for 0%

commit v1 on v0

v1 whole, which is shorter than its diff:
```python
import functools

import jax
import jax.numpy as jnp
from jax import lax
from jax.experimental import pallas as pl
from jax.experimental.pallas import tpu as pltpu
from jax.sharding import PartitionSpec as P

beta_first = 0.9
beta_second = 0.95
adam_eps = 1e-08
norm_eps = 1e-06
first_fix = 1.0 - (0.9**50) ** 2
second_fix = 1.0 - (0.95**50) ** 2
VMEM_BYTES = 56 * 1024 * 1024


def contract_first(left, right):
    return lax.dot_general(
        left, right, (((0,), (0,)), ((), ())), preferred_element_type=jnp.float32
    )


def contract_last(left, right):
    return lax.dot_general(
        left, right, (((1,), (1,)), ((), ())), preferred_element_type=jnp.float32
    )


def swap(blocks, axis):
    return lax.all_to_all(blocks, axis, split_axis=0, concat_axis=0, tiled=True)


def pair_list(count):
    return [(i, j) for i in range(count) for j in range(i, count)]


def gram_kernel(inputs_ref, incoming_ref, factors_ref, gram_ref, grads_ref):
    count = inputs_ref.shape[0]

    @pl.when(pl.program_id(0) == 0)
    def _():
        gram_ref[...] = jnp.zeros_like(gram_ref)

    for matrix in range(3):
        rows_ref = incoming_ref if matrix == 2 else inputs_ref
        for rep in range(count):
            grads_ref[rep] = contract_first(rows_ref[rep], factors_ref[rep, matrix])
        for place, (i, j) in enumerate(pair_list(count)):
            column_sum = jnp.sum(grads_ref[i] * grads_ref[j], axis=0, keepdims=True)
            gram_ref[pl.ds(place, 1), :] += column_sum


def merge_coefs(gram, count):
    vectors = [{rep: None} for rep in range(count)]

    def term(coef, value):
        return value if coef is None else coef * value

    def inner(left, right):
        total = None
        for i, left_coef in left.items():
            for j, right_coef in right.items():
                value = term(left_coef, term(right_coef, gram[min(i, j), max(i, j)]))
                total = value if total is None else total + value
        return total

    while len(vectors) > 1:
        merged = []
        for first, second in zip(vectors[0::2], vectors[1::2]):
            norm_first = jnp.maximum(inner(first, first), 0.0)
            norm_second = jnp.maximum(inner(second, second), 0.0)
            bound = jnp.sqrt(norm_first) * jnp.sqrt(norm_second)
            cross = jnp.minimum(jnp.maximum(inner(first, second), -bound), bound)
            coef_first = 1.0 - cross / (2.0 * (norm_first + norm_eps))
            coef_second = 1.0 - cross / (2.0 * (norm_second + norm_eps))
            joined = {rep: term(coef, coef_first) for rep, coef in first.items()}
            joined.update({rep: term(coef, coef_second) for rep, coef in second.items()})
            merged.append(joined)
        vectors = merged
    return [vectors[0][rep] for rep in range(count)]


def adam_kernel(
    gram_ref, inputs_ref, incoming_ref, factors_ref, first_ref, second_ref, step_ref, coef_ref
):
    count = inputs_ref.shape[0]

    @pl.when(pl.program_id(0) == 0)
    def _():
        sums = jnp.sum(jnp.sum(gram_ref[...], axis=0), axis=1, keepdims=True)
        gram = {pair: sums[place : place + 1] for place, pair in enumerate(pair_list(count))}
        for rep, coef in enumerate(merge_coefs(gram, count)):
            coef_ref[pl.ds(rep, 1), :] = jnp.broadcast_to(coef, (1, coef_ref.shape[1]))

    for matrix in range(3):
        rows_ref = incoming_ref if matrix == 2 else inputs_ref
        merged = None
        for rep in range(count):
            part = contract_first(rows_ref[rep], factors_ref[rep, matrix])
            part = part * coef_ref[pl.ds(rep, 1), :]
            merged = part if merged is None else merged + part
        first_new = beta_first * first_ref[0, matrix] + (1.0 - beta_first) * merged
        second_new = beta_second * second_ref[0, matrix] + (1.0 - beta_second) * merged * merged
        step_ref[0, matrix] = (first_new / first_fix) / (
            jnp.sqrt(second_new / second_fix) + adam_eps
        )


def adasum_adam(inputs, incoming, factors, first_moment, second_moment):
    count, slot_count, seg_rows = inputs.shape
    hidden_width = factors.shape[3]
    tile = min(seg_rows, 128)
    grid = (seg_rows // tile,)
    pairs = len(pair_list(count))
    rows_spec = pl.BlockSpec((count, slot_count, tile), lambda d: (0, 0, d))
    factors_spec = pl.BlockSpec(factors.shape, lambda d: (0, 0, 0, 0))
    moment_spec = pl.BlockSpec((1, 3, tile, hidden_width), lambda d: (0, 0, d, 0))
    params = pltpu.CompilerParams(
        dimension_semantics=("arbitrary",), vmem_limit_bytes=VMEM_BYTES
    )
    flops = 6 * count * slot_count * seg_rows * hidden_width
    row_bytes = 2 * (inputs.size + incoming.size + factors.size)
    partial = pl.pallas_call(
        gram_kernel,
        grid=grid,
        in_specs=[rows_spec, rows_spec, factors_spec],
        out_specs=pl.BlockSpec((pairs, hidden_width), lambda d: (0, 0)),
        out_shape=jax.ShapeDtypeStruct((pairs, hidden_width), jnp.float32),
        scratch_shapes=[pltpu.VMEM((count, tile, hidden_width), jnp.float32)],
        compiler_params=params,
        cost_estimate=pl.CostEstimate(
            flops=flops, bytes_accessed=row_bytes, transcendentals=0
        ),
        name="gram",
    )(inputs, incoming, factors)
    shared = jnp.sum(partial.reshape(pairs, hidden_width // 128, 128), axis=1)
    gathered = swap(jnp.broadcast_to(shared[None], (count, pairs, 128)), "replica")
    return pl.pallas_call(
        adam_kernel,
        grid=grid,
        in_specs=[
            pl.BlockSpec(gathered.shape, lambda d: (0, 0, 0)),
            rows_spec,
            rows_spec,
            factors_spec,
            moment_spec,
            moment_spec,
        ],
        out_specs=moment_spec,
        out_shape=jax.ShapeDtypeStruct(first_moment.shape, jnp.float32),
        scratch_shapes=[pltpu.VMEM((count, hidden_width), jnp.float32)],
        compiler_params=params,
        cost_estimate=pl.CostEstimate(
            flops=flops,
            bytes_accessed=row_bytes + 12 * first_moment.size,
            transcendentals=first_moment.size,
        ),
        name="adam",
    )(gathered, inputs, incoming, factors, first_moment, second_moment)


def shards(
    weights, first_moment, second_moment, out_grads, routes, task_ids, task_weights, saved_inputs
):
    expert_count = lax.axis_size("expert")
    rep_count = lax.axis_size("replica")
    row_count = out_grads.shape[1]
    model_width = out_grads.shape[2]
    hidden_width = weights.shape[3]
    slot_count = saved_inputs.shape[2]
    capacity = slot_count // expert_count
    block_count = task_ids.shape[1]
    block_rows = row_count // block_count
    task_count = task_weights.shape[0]
    seg_rows = model_width // rep_count

    def by_segment(matrix):
        return matrix.reshape(matrix.shape[0], rep_count, seg_rows).swapaxes(0, 1)

    chosen_task = (task_ids[0][:, None] == jnp.arange(task_count, dtype=jnp.int32)[None, :]).astype(
        jnp.float32
    )
    block_weight = jnp.sum(chosen_task * task_weights[None, :], axis=1)
    scaled = (
        (out_grads[0].reshape(block_count, block_rows, model_width) * block_weight[:, None, None])
        .reshape(row_count, model_width)
        .astype(jnp.bfloat16)
    )
    expert_of = routes[0, :, 0]
    chosen = (expert_of[:, None] == jnp.arange(expert_count, dtype=jnp.int32)[None, :]).astype(
        jnp.int32
    )
    slot_rank = jnp.sum((jnp.cumsum(chosen, axis=0) - chosen) * chosen, axis=1)
    label_rows = -(-row_count // seg_rows)

    def as_rows(labels):
        padded = jnp.pad(labels, (0, label_rows * seg_rows - row_count))
        return padded.reshape(label_rows, seg_rows).astype(jnp.bfloat16)

    labels = jnp.concatenate([as_rows(expert_of), as_rows(slot_rank)], axis=0)
    labels = jnp.pad(labels, ((0, -labels.shape[0] % 16), (0, 0)))
    labels = jnp.broadcast_to(labels[None], (rep_count,) + labels.shape)
    routed = swap(jnp.concatenate([by_segment(scaled), labels], axis=1), "replica")
    inputs = swap(by_segment(saved_inputs[0, 0]), "replica")

    def read_labels(first_row):
        rows = routed[:, row_count + first_row : row_count + first_row + label_rows]
        return rows.reshape(rep_count, label_rows * seg_rows)[:, :row_count].astype(jnp.int32)

    slot_index = read_labels(0) * capacity + read_labels(label_rows)
    placing = (
        slot_index[:, None, :] == jnp.arange(slot_count, dtype=jnp.int32)[None, :, None]
    ).astype(jnp.bfloat16)
    outgoing = jnp.einsum(
        "rqt,rtd->rqd", placing, routed[:, :row_count], preferred_element_type=jnp.float32
    ).astype(jnp.bfloat16)
    outgoing = outgoing.reshape(rep_count, expert_count, capacity, seg_rows).swapaxes(0, 1)
    incoming = swap(outgoing, "expert").swapaxes(0, 1).reshape(rep_count, slot_count, seg_rows)

    def product(rows, matrix):
        flat = rows.reshape(rep_count * slot_count, seg_rows)
        total = jnp.dot(flat, matrix, preferred_element_type=jnp.float32)
        return total.astype(jnp.bfloat16).reshape(rep_count, 1, slot_count, hidden_width)

    own_weights = weights[0]
    forward = jnp.concatenate(
        [product(inputs, own_weights[0]), product(inputs, own_weights[1])], axis=1
    )
    forward = jnp.sum(swap(forward, "replica").astype(jnp.float32), axis=0)
    backward = product(incoming, own_weights[2])
    hidden_grad = jnp.sum(swap(backward, "replica").astype(jnp.float32), axis=0)[0]
    gate_pre, up_pre = forward[0], forward[1]
    gate_act = jax.nn.silu(gate_pre)
    hidden = (gate_act * up_pre).astype(jnp.bfloat16)
    sigmoid_gate = jax.nn.sigmoid(gate_pre)
    gate_grad = (
        hidden_grad * up_pre * sigmoid_gate * (1.0 + gate_pre * (1.0 - sigmoid_gate))
    ).astype(jnp.bfloat16)
    up_grad = (hidden_grad * gate_act).astype(jnp.bfloat16)
    factors = jnp.stack([gate_grad, up_grad, hidden])
    factors = swap(jnp.broadcast_to(factors[None], (rep_count,) + factors.shape), "replica")

    slot_grads = (
        contract_last(factors[:, 0].reshape(-1, hidden_width), own_weights[0])
        + contract_last(factors[:, 1].reshape(-1, hidden_width), own_weights[1])
    ).astype(jnp.bfloat16)
    slot_grads = slot_grads.reshape(rep_count, expert_count, capacity, seg_rows).swapaxes(0, 1)
    returned = swap(slot_grads, "expert").swapaxes(0, 1).reshape(rep_count, slot_count, seg_rows)
    row_grads = jnp.einsum(
        "rqt,rqd->rtd", placing, returned, preferred_element_type=jnp.float32
    ).astype(jnp.bfloat16)
    input_grads = swap(row_grads, "replica").swapaxes(0, 1).reshape(1, row_count, model_width)

    adam_step = adasum_adam(inputs, incoming, factors, first_moment, second_moment)
    return (input_grads, adam_step)


def solution(mesh):
    return jax.shard_map(
        shards,
        mesh=mesh,
        in_specs=(
            P("expert", None, "replica", None),
            P("expert", None, "replica", None),
            P("expert", None, "replica", None),
            P("replica", "expert", None),
            P("replica", "expert", None),
            P("replica", "expert"),
            P(),
            P("replica", "expert", None, None),
        ),
        out_specs=(P("replica", "expert", None), P("expert", None, "replica", None)),
        check_vma=False,
    )
```

time: 229 us -> 216 us (0.943)
  blocking collectives: 0 us -> 38.6 us
  between operations: 25.1 us -> 1.56 us
  other arithmetic: 27.8 us -> 9.08 us
  waiting for transfers between devices: 113 us -> 95.5 us
  Pallas kernels: 0 us -> 15.5 us
  matrix products: 24.7 us -> 9.87 us
  starting transfers between devices: 18.4 us -> 31.7 us
  local copies, waits for them, and re-layouts: 18.5 us -> 13.4 us
    all_to_all x2 -> x8, waiting for transfers between devices: 25.1 us -> 95.5 us  [swap(): return lax.all_to_all(blocks, axis, split_axis=0, concat_axis=0, tiled=True)]
    ppermute x5 -> x0, waiting for transfers between devices: 63.2 us -> none  [from_partner(): lax.ppermute(array, axis, [(i, i ^ 1 << bit) for i in range(lax.axis_size...]
    all_to_all x0 -> x1, blocking collectives: none -> 38.6 us  [swap(): return lax.all_to_all(blocks, axis, split_axis=0, concat_axis=0, tiled=True)]
    all_gather x1 -> x0, waiting for transfers between devices: 24.3 us -> none  [shards(): gathered = lax.all_gather(weights, 'replica', axis=2, tiled=True)[0]]
    all_to_all x2 -> x8, starting transfers between devices: 10.9 us -> 31.7 us  [swap(): return lax.all_to_all(blocks, axis, split_axis=0, concat_axis=0, tiled=True)]
    pallas_call x0 -> x2, Pallas kernels: none -> 15.5 us  [the longest x1 9.05 us: adasum_adam(): pl.pallas_call(adam_kernel, grid=grid, in_specs=[pl.BlockSpec(gathered.sh...]
    dot_general x11 -> x5, matrix products: 19 us -> 8.4 us  [the longest x3 6.64 us: product(): total = jnp.dot(flat, matrix, preferred_element_type=jnp.float32)]
    div x1 -> x0, other arithmetic: 7.77 us -> none  [shards(): first_new / first_fix / (jnp.sqrt(second_new / second_fix) + adam_eps)]
  transfers between devices with their start and end apart: 8 -> 8, of which waited for: 7 -> 7; matrix products, arithmetic and copies ran while one was open for 19% -> 7% of each run, Pallas kernels for 0% -> 7%
where the time goes in v1:
time: 216 us; the launch traced here: 215 us
  waiting for transfers between devices  95.5 us (44%)
  blocking collectives  38.6 us (18%)
  starting transfers between devices  31.7 us (15%)
  Pallas kernels  15.5 us (7%)
  local copies, waits for them, and re-layouts  13.4 us (6%)
  matrix products  9.87 us (5%)
  other arithmetic  9.08 us (4%)
    all_to_all x8, waiting for transfers between devices, swap(): return lax.all_to_all(blocks, axis, split_axis=0, concat_axis=0, tiled=True)  95.5 us
    all_to_all x1, blocking collectives, swap(): return lax.all_to_all(blocks, axis, split_axis=0, concat_axis=0, tiled=True)  38.6 us
    all_to_all x8, starting transfers between devices, swap(): return lax.all_to_all(blocks, axis, split_axis=0, concat_axis=0, tiled=True)  31.7 us
    pallas_call x1, Pallas kernels, adasum_adam(): pl.pallas_call(adam_kernel, grid=grid, in_specs=[pl.BlockSpec(gathered.sh...  9.05 us
    dot_general x3, matrix products, product(): total = jnp.dot(flat, matrix, preferred_element_type=jnp.float32)  6.64 us
    pallas_call x1, Pallas kernels, adasum_adam(): pl.pallas_call(gram_kernel, grid=grid, in_specs=[rows_spec, rows_spec, fa...  6.5 us
    unnamed x18, local copies, waits for them, and re-layouts  6.23 us
  transfers between devices with their start and end apart: 8, of which 7 were waited for; matrix products, arithmetic and copies ran while one was open for 7% of the time, Pallas kernels for 7%

profile of v1, /device:TPU:0, one launch (start us, length us, event | category | flops | bytes accessed | tf_op | source)
XLA Modules:
  0.0 215.2 jit_solution(10684190814963355206)
XLA Ops:
  1.3 0.7 bitcast_convert_fusion
  2.0 0.7 fusion.19
  2.7 0.2 reduce_window_sum.11
  2.9 0.8 select_reduce_fusion
  3.7 1.3 copy.40
  5.1 1.3 fusion.23
  6.3 0.0 copy-start.4
  6.3 0.8 multiply_convert_fusion
  7.2 0.2 copy.41
  7.4 0.9 pad_maximum_fusion.2
  8.3 5.2 %all-to-all-start = ((bf16[4,144,512]{2,1,0:T(8,128)(2,1)}), bf16[4,144,512]{2,1,0:T(8,128)(2,1)S(1)}, u32[]{:S(2)}, u32[]{:S(2)}) async-start(bf16[4,144,512]{2,1,0:T(8,128)(2,1)} %pad_maximum_fusion.2), calls=%async_computation | async-start | bytes 1179648 | tf_op jit(solution)/shard_map/all_to_all | solution.py:32
  13.5 0.0 copy-done.4
  13.5 0.5 copy.46
  14.0 1.3 copy.47
  15.3 6.9 %all-to-all-done = bf16[4,144,512]{2,1,0:T(8,128)(2,1)S(1)} async-done(((bf16[4,144,512]{2,1,0:T(8,128)(2,1)}), bf16[4,144,512]{2,1,0:T(8,128)(2,1)S(1)}, u32[]{:S(2)}, u32[]{:S(2)}) %all-to-all-start) | async-done | bytes 589856 | tf_op jit(solution)/shard_map/all_to_all | solution.py:32
  22.2 3.5 %all-to-all-start.3 = ((bf16[4,256,512]{2,1,0:T(8,128)(2,1)}), bf16[4,256,512]{2,1,0:T(8,128)(2,1)S(1)}, u32[]{:S(2)}, u32[]{:S(2)}) async-start(bf16[4,256,512]{2,1,0:T(8,128)(2,1)} %bitcast.13), calls=%async_computation.3 | async-start | bytes 2097152 | tf_op jit(solution)/shard_map/all_to_all | solution.py:32
  25.7 0.6 convolution_convert_fusion
  26.4 1.0 copy.62
  27.4 11.1 %all-to-all-done.3.inputs_ref = bf16[4,256,512]{2,1,0:T(8,128)(2,1)S(1)} async-done(((bf16[4,256,512]{2,1,0:T(8,128)(2,1)}), bf16[4,256,512]{2,1,0:T(8,128)(2,1)S(1)}, u32[]{:S(2)}, u32[]{:S(2)}) %all-to-all-start.3) | async-done | bytes 1048608 | tf_op jit(solution)/shard_map/all_to_all | solution.py:32
  38.5 0.0 copy-start.1
  38.5 4.9 %all-to-all-start.1 = ((bf16[8,4,32,512]{3,2,1,0:T(8,128)(2,1)}), bf16[8,4,32,512]{3,2,1,0:T(8,128)(2,1)S(1)}, u32[]{:S(2)}, u32[]{:S(2)}) async-start(bf16[8,4,32,512]{3,2,1,0:T(8,128)(2,1)} %bitcast.69), calls=%async_computation.1 | async-start | bytes 2097152 | tf_op jit(solution)/shard_map/all_to_all | solution.py:32
  43.4 1.7 convolution_convert_fusion.1
  45.1 0.0 copy-done.1
  45.1 1.7 convolution_convert_fusion.2
  46.9 1.5 pad_maximum_fusion
  48.4 21.6 %all-to-all-done.1 = bf16[8,4,32,512]{3,2,1,0:T(8,128)(2,1)S(1)} async-done(((bf16[8,4,32,512]{3,2,1,0:T(8,128)(2,1)}), bf16[8,4,32,512]{3,2,1,0:T(8,128)(2,1)S(1)}, u32[]{:S(2)}, u32[]{:S(2)}) %all-to-all-start.1) | async-done | bytes 1048608 | tf_op jit(solution)/shard_map/all_to_all | solution.py:32
  70.0 0.0 copy-start.3
  70.0 1.0 copy-done.3
  71.0 3.6 %all-to-all-start.4 = ((bf16[4,2,256,512]{3,2,1,0:T(8,128)(2,1)}), bf16[4,2,256,512]{3,2,1,0:T(8,128)(2,1)S(1)}, u32[]{:S(2)}, u32[]{:S(2)}) async-start(bf16[4,2,256,512]{3,2,1,0:T(8,128)(2,1)} %pad_maximum_fusion), calls=%async_computation.4 | async-start | bytes 4194304 | tf_op jit(solution)/shard_map/all_to_all | solution.py:32
  74.6 1.3 copy.44
  75.9 0.0 copy-start.2
  75.9 3.2 %convolution_convert_fusion.3 = bf16[1024,512]{1,0:T(8,128)(2,1)} fusion(bf16[1024,512]{1,0:T(8,128)(2,1)S(1)} %bitcast.73, bf16[1,3,512,512]{3,2,1,0:T(8,128)(2,1)} %param.8), kind=kOutput, calls=%fused_computation.7 | convolution fusion | flops 537395200 | bytes 2621440 | tf_op jit(solution)/shard_map/dot_general | solution.py:224
  79.0 20.5 %all-to-all-done.4 = bf16[4,2,256,512]{3,2,1,0:T(8,128)(2,1)S(1)} async-done(((bf16[4,2,256,512]{3,2,1,0:T(8,128)(2,1)}), bf16[4,2,256,512]{3,2,1,0:T(8,128)(2,1)S(1)}, u32[]{:S(2)}, u32[]{:S(2)}) %all-to-all-start.4) | async-done | bytes 2097184 | tf_op jit(solution)/shard_map/all_to_all | solution.py:32
  99.5 0.0 copy-done.2
  99.5 4.2 %all-to-all-start.2 = ((bf16[4,1,256,512]{3,2,1,0:T(8,128)(2,1)}), bf16[4,1,256,512]{3,2,1,0:T(8,128)(2,1)}, u32[]{:S(2)}, u32[]{:S(2)}) async-start(bf16[4,1,256,512]{3,2,1,0:T(8,128)(2,1)} %bitcast.87), calls=%async_computation.2 | async-start | bytes 2097152 | tf_op jit(solution)/shard_map/all_to_all | solution.py:32
  103.7 0.3 convert_reduce_fusion
  104.1 12.8 %all-to-all-done.2 = bf16[4,1,256,512]{3,2,1,0:T(8,128)(2,1)} async-done(((bf16[4,1,256,512]{3,2,1,0:T(8,128)(2,1)}), bf16[4,1,256,512]{3,2,1,0:T(8,128)(2,1)}, u32[]{:S(2)}, u32[]{:S(2)}) %all-to-all-start.2) | async-done | bytes 1048608 | tf_op jit(solution)/shard_map/all_to_all | solution.py:32
  116.9 1.4 convert_reduce_fusion.1
  118.3 0.3 fusion.8
  118.7 0.1 pad_maximum_fusion.1
  118.8 0.3 broadcast_in_dim.7
  119.1 38.6 %all_to_all.45.factors_ref = bf16[4,3,256,512]{3,2,1,0:T(8,128)(2,1)S(1)} all-to-all(bf16[4,3,256,512]{3,2,1,0:T(8,128)(2,1)S(1)} %broadcast_in_dim.7), channel_id=1, replica_groups=mesh['expert'=8,'replica'=4] {'replica'}, dimensions={0} | all-to-all | bytes 6291456 | tf_op jit(solution)/shard_map/all_to_all | solution.py:32
  157.6 0.0 copy-start
  157.6 0.1 fusion.24
  157.8 1.5 copy-done
  159.3 0.9 copy-done.5
  160.2 0.7 fusion.3
  160.9 0.7 add_convert_fusion
  161.7 1.0 copy.61
  162.7 3.6 %all-to-all-start.6 = ((bf16[8,4,32,512]{3,2,1,0:T(8,128)(2,1)}), bf16[8,4,32,512]{3,2,1,0:T(8,128)(2,1)S(1)}, u32[]{:S(2)}, u32[]{:S(2)}) async-start(bf16[8,4,32,512]{3,2,1,0:T(8,128)(2,1)} %bitcast.68), calls=%async_computation.6 | async-start | bytes 2097152 | tf_op jit(solution)/shard_map/all_to_all | solution.py:32
  166.3 6.5 %gram.1 = f32[10,512]{1,0:T(8,128)} custom-call(bf16[4,256,512]{2,1,0:T(8,128)(2,1)} %copy-done.1, bf16[4,256,512]{2,1,0:T(8,128)(2,1)} %bitcast.74, bf16[4,3,256,512]{3,2,1,0:T(8,128)(2,1)} %copy-done), custom_call_target="tpu_custom_call" | custom-call | flops 1610612736 | bytes 5242880 | tf_op jit(solution)/shard_map/gram/pallas_call | solution.py:125
  172.8 0.8 reshape.82
  173.6 19.2 %all-to-all-done.6 = bf16[8,4,32,512]{3,2,1,0:T(8,128)(2,1)S(1)} async-done(((bf16[8,4,32,512]{3,2,1,0:T(8,128)(2,1)}), bf16[8,4,32,512]{3,2,1,0:T(8,128)(2,1)S(1)}, u32[]{:S(2)}, u32[]{:S(2)}) %all-to-all-start.6) | async-done | bytes 1048608 | tf_op jit(solution)/shard_map/all_to_all | solution.py:32
  192.8 0.6 broadcast_in_dim.8
  193.4 3.3 %all-to-all-start.8 = ((f32[4,10,128]{2,1,0:T(8,128)}), f32[4,10,128]{2,1,0:T(8,128)S(1)}, u32[]{:S(2)}, u32[]{:S(2)}) async-start(f32[4,10,128]{2,1,0:T(8,128)} %broadcast_in_dim.8), calls=%async_computation.8 | async-start | bytes 65536 | tf_op jit(solution)/shard_map/all_to_all | solution.py:32
  196.7 0.1 copy.51
  196.8 1.2 convolution_convert_fusion.4
  197.9 3.5 %all-to-all-done.8.gram_ref = f32[4,10,128]{2,1,0:T(8,128)S(1)} async-done(((f32[4,10,128]{2,1,0:T(8,128)}), f32[4,10,128]{2,1,0:T(8,128)S(1)}, u32[]{:S(2)}, u32[]{:S(2)}) %all-to-all-start.8) | async-done | bytes 20512 | tf_op jit(solution)/shard_map/all_to_all | solution.py:32
  201.4 3.5 %all-to-all-start.7 = ((bf16[4,128,512]{2,1,0:T(8,128)(2,1)}), bf16[4,128,512]{2,1,0:T(8,128)(2,1)S(1)}, u32[]{:S(2)}, u32[]{:S(2)}) async-start(bf16[4,128,512]{2,1,0:T(8,128)(2,1)} %convolution_convert_fusion.4), calls=%async_computation.7 | async-start | bytes 1048576 | tf_op jit(solution)/shard_map/all_to_all | solution.py:32
  204.9 0.0 copy-done.6
  204.9 9.0 %adam.1 = f32[1,3,512,512]{3,2,1,0:T(8,128)} custom-call(f32[4,10,128]{2,1,0:T(8,128)} %copy-done.6, bf16[4,256,512]{2,1,0:T(8,128)(2,1)} %copy-done.1, bf16[4,256,512]{2,1,0:T(8,128)(2,1)} %bitcast.75, bf16[4,3,256,512]{3,2,1,0:T(8,128)(2,1)} %copy-done, f32[1,3,512,512]{3,2,1,0:T(8,128)} %first_ref.1, f32[1,3,512,512]{3,2,1,0:T(8,128)} %second_ref.1), custom_call_target="tpu_custom_call" | custom-call | flops 1610612736 | bytes 14680064 | tf_op jit(solution)/shard_map/adam/pallas_call | solution.py:140
  213.9 0.0 all-to-all-done.7
  213.9 0.3 copy.52
  214.2 1.0 copy.53
  (13 shorter events, 0.1 us)
Async XLA Ops:
  6.3 7.1 %copy-start.4 = (bf16[1,1,256,2048]{3,2,1,0:T(8,128)(2,1)S(1)}, bf16[1,1,256,2048]{3,2,1,0:T(8,128)(2,1)}, u32[]{:S(2)}) copy-start(bf16[1,1,256,2048]{3,2,1,0:T(8,128)(2,1)} %param.15) | copy-start | bytes 3145732
  8.3 13.9 %all-to-all-start = ((bf16[4,144,512]{2,1,0:T(8,128)(2,1)}), bf16[4,144,512]{2,1,0:T(8,128)(2,1)S(1)}, u32[]{:S(2)}, u32[]{:S(2)}) async-start(bf16[4,144,512]{2,1,0:T(8,128)(2,1)} %pad_maximum_fusion.2), calls=%async_computation | async-start | bytes 1179648 | tf_op jit(solution)/shard_map/all_to_all | solution.py:32
  22.2 16.3 %all-to-all-start.3 = ((bf16[4,256,512]{2,1,0:T(8,128)(2,1)}), bf16[4,256,512]{2,1,0:T(8,128)(2,1)S(1)}, u32[]{:S(2)}, u32[]{:S(2)}) async-start(bf16[4,256,512]{2,1,0:T(8,128)(2,1)} %bitcast.13), calls=%async_computation.3 | async-start | bytes 2097152 | tf_op jit(solution)/shard_map/all_to_all | solution.py:32
  38.5 6.6 %copy-start.1 = (bf16[4,256,512]{2,1,0:T(8,128)(2,1)}, bf16[4,256,512]{2,1,0:T(8,128)(2,1)S(1)}, u32[]{:S(2)}) copy-start(bf16[4,256,512]{2,1,0:T(8,128)(2,1)S(1)} %all-to-all-done.3.inputs_ref) | copy-start | bytes 3145732
  38.5 31.5 %all-to-all-start.1 = ((bf16[8,4,32,512]{3,2,1,0:T(8,128)(2,1)}), bf16[8,4,32,512]{3,2,1,0:T(8,128)(2,1)S(1)}, u32[]{:S(2)}, u32[]{:S(2)}) async-start(bf16[8,4,32,512]{3,2,1,0:T(8,128)(2,1)} %bitcast.69), calls=%async_computation.1 | async-start | bytes 2097152 | tf_op jit(solution)/shard_map/all_to_all | solution.py:32
  70.0 1.0 copy-start.3
  71.0 28.5 %all-to-all-start.4 = ((bf16[4,2,256,512]{3,2,1,0:T(8,128)(2,1)}), bf16[4,2,256,512]{3,2,1,0:T(8,128)(2,1)S(1)}, u32[]{:S(2)}, u32[]{:S(2)}) async-start(bf16[4,2,256,512]{3,2,1,0:T(8,128)(2,1)} %pad_maximum_fusion), calls=%async_computation.4 | async-start | bytes 4194304 | tf_op jit(solution)/shard_map/all_to_all | solution.py:32
  75.9 23.6 %copy-start.2 = (bf16[8,4,32,512]{3,2,0,1:T(8,128)(2,1)}, bf16[8,4,32,512]{3,2,0,1:T(8,128)(2,1)S(1)}, u32[]{:S(2)}) copy-start(bf16[8,4,32,512]{3,2,0,1:T(8,128)(2,1)S(1)} %copy.44) | copy-start | bytes 3145732
  99.5 17.4 %all-to-all-start.2 = ((bf16[4,1,256,512]{3,2,1,0:T(8,128)(2,1)}), bf16[4,1,256,512]{3,2,1,0:T(8,128)(2,1)}, u32[]{:S(2)}, u32[]{:S(2)}) async-start(bf16[4,1,256,512]{3,2,1,0:T(8,128)(2,1)} %bitcast.87), calls=%async_computation.2 | async-start | bytes 2097152 | tf_op jit(solution)/shard_map/all_to_all | solution.py:32
  157.6 1.6 copy-start
  157.6 2.5 %copy-start.5 = (bf16[1,3,512,512]{3,2,1,0:T(8,128)(2,1)S(1)}, bf16[1,3,512,512]{3,2,1,0:T(8,128)(2,1)}, u32[]{:S(2)}) copy-start(bf16[1,3,512,512]{3,2,1,0:T(8,128)(2,1)} %param.8) | copy-start | bytes 4718596
  162.7 30.1 %all-to-all-start.6 = ((bf16[8,4,32,512]{3,2,1,0:T(8,128)(2,1)}), bf16[8,4,32,512]{3,2,1,0:T(8,128)(2,1)S(1)}, u32[]{:S(2)}, u32[]{:S(2)}) async-start(bf16[8,4,32,512]{3,2,1,0:T(8,128)(2,1)} %bitcast.68), calls=%async_computation.6 | async-start | bytes 2097152 | tf_op jit(solution)/shard_map/all_to_all | solution.py:32
  193.4 8.0 %all-to-all-start.8 = ((f32[4,10,128]{2,1,0:T(8,128)}), f32[4,10,128]{2,1,0:T(8,128)S(1)}, u32[]{:S(2)}, u32[]{:S(2)}) async-start(f32[4,10,128]{2,1,0:T(8,128)} %broadcast_in_dim.8), calls=%async_computation.8 | async-start | bytes 65536 | tf_op jit(solution)/shard_map/all_to_all | solution.py:32
  201.4 3.5 %copy-start.6 = (f32[4,10,128]{2,1,0:T(8,128)}, f32[4,10,128]{2,1,0:T(8,128)S(1)}, u32[]{:S(2)}) copy-start(f32[4,10,128]{2,1,0:T(8,128)S(1)} %all-to-all-done.8.gram_ref) | copy-start | bytes 61444
  201.4 12.5 %all-to-all-start.7 = ((bf16[4,128,512]{2,1,0:T(8,128)(2,1)}), bf16[4,128,512]{2,1,0:T(8,128)(2,1)S(1)}, u32[]{:S(2)}, u32[]{:S(2)}) async-start(bf16[4,128,512]{2,1,0:T(8,128)(2,1)} %convolution_convert_fusion.4), calls=%async_computation.7 | async-start | bytes 1048576 | tf_op jit(solution)/shard_map/all_to_all | solution.py:32

commit v2 on v1

v2 whole, which is shorter than its diff:
```python
import functools

import jax
import jax.numpy as jnp
from jax import lax
from jax.experimental import pallas as pl
from jax.experimental.pallas import tpu as pltpu
from jax.sharding import PartitionSpec as P

beta_first = 0.9
beta_second = 0.95
adam_eps = 1e-08
norm_eps = 1e-06
first_fix = 1.0 - (0.9**50) ** 2
second_fix = 1.0 - (0.95**50) ** 2
VMEM_BYTES = 56 * 1024 * 1024
LABEL_ROWS = 16


def contract_first(left, right):
    return lax.dot_general(
        left, right, (((0,), (0,)), ((), ())), preferred_element_type=jnp.float32
    )


def contract_last(left, right):
    return lax.dot_general(
        left, right, (((1,), (1,)), ((), ())), preferred_element_type=jnp.float32
    )


def multiply(left, right):
    return jnp.dot(left, right, preferred_element_type=jnp.float32)


def from_peer(array, offset):
    count = lax.axis_size("replica")
    return lax.ppermute(array, "replica", [(i, i ^ offset) for i in range(count)])


def exchange(parts):
    return [parts[0]] + [from_peer(part, k) for k, part in enumerate(parts) if k]


def gather_pair(first, second):
    count = lax.axis_size("replica")
    if count != 4:
        return list(zip(exchange([first] * count), exchange([second] * count)))
    first_two = from_peer(first, 2)
    second_one = from_peer(second, 1)
    first_one = from_peer(first, 1)
    second_two = from_peer(second, 2)
    first_three = from_peer(first_two, 1)
    second_three = from_peer(second_one, 2)
    return [
        (first, second),
        (first_one, second_one),
        (first_two, second_two),
        (first_three, second_three),
    ]


def pair_list(count):
    return [(i, j) for i in range(count) for j in range(i, count)]


def whole(array):
    return pl.BlockSpec(array.shape, lambda *_: (0,) * array.ndim)


SMEM = pl.BlockSpec(memory_space=pltpu.SMEM)


def call(kernel, name, operands, specs, outs, out_specs=None, grid=(1,), scratch=(), flops=0):
    size = sum(x.size * x.dtype.itemsize for x in list(operands) + list(outs))
    return pl.pallas_call(
        kernel,
        grid=grid,
        in_specs=specs,
        out_specs=out_specs if out_specs is not None else [whole(out) for out in outs],
        out_shape=outs,
        scratch_shapes=list(scratch),
        compiler_params=pltpu.CompilerParams(
            dimension_semantics=("arbitrary",) * len(grid), vmem_limit_bytes=VMEM_BYTES
        ),
        cost_estimate=pl.CostEstimate(flops=flops, bytes_accessed=size, transcendentals=0),
        name=name,
    )(*operands)


def segment(rep_ref, offset, width):
    return pl.ds(pl.multiple_of((rep_ref[0] ^ offset) * width, width), width)


def rows_kernel(rep_ref, ids_ref, task_ref, column_ref, row_ref, grads_ref, *out_refs):
    row_count = grads_ref.shape[0]
    seg_rows = out_refs[0].shape[1]
    block_count = ids_ref.shape[1]
    block_rows = row_count // block_count
    square = (row_count, row_count)
    earlier = lax.broadcasted_iota(jnp.int32, square, 0) < lax.broadcasted_iota(
        jnp.int32, square, 1
    )
    counted = jnp.where(column_ref[...] == row_ref[...], 1.0, 0.0)
    rank = jnp.sum(jnp.where(earlier, counted, 0.0), axis=0, keepdims=True)
    line = lax.broadcasted_iota(jnp.int32, (LABEL_ROWS, row_count), 0)
    labels = jnp.where(line == 0, row_ref[...].astype(jnp.float32), 0.0)
    labels = jnp.where(line == 1, rank, labels).astype(jnp.bfloat16)
    for offset, out_ref in enumerate(out_refs):
        columns = segment(rep_ref, offset, seg_rows)
        for block in range(block_count):
            rows = pl.ds(block * block_rows, block_rows)
            weight = task_ref[ids_ref[0, block]]
            out_ref[rows, :] = (grads_ref[rows, columns].astype(jnp.float32) * weight).astype(
                jnp.bfloat16
            )
        if row_count < seg_rows:
            out_ref[pl.ds(row_count, LABEL_ROWS), :] = jnp.zeros(
                (LABEL_ROWS, seg_rows), jnp.bfloat16
            )
        out_ref[pl.ds(row_count, LABEL_ROWS), pl.ds(0, row_count)] = labels


def split_kernel(rep_ref, matrix_ref, *out_refs):
    for offset, out_ref in enumerate(out_refs):
        out_ref[...] = matrix_ref[:, segment(rep_ref, offset, out_ref.shape[1])]


def one_hot(block_ref, row_count, slot_count, capacity):
    labels = block_ref[pl.ds(row_count, LABEL_ROWS), pl.ds(0, row_count)].astype(jnp.float32)
    slot = (labels[0:1] * capacity + labels[1:2]).astype(jnp.int32)
    places = lax.broadcasted_iota(jnp.int32, (slot_count, row_count), 0)
    return jnp.where(places == slot, 1.0, 0.0).astype(jnp.bfloat16)


def place_kernel(row_count, *refs):
    block_refs, out_ref = refs[:-1], refs[-1]
    expert_count, _, capacity, seg_rows = out_ref.shape
    slot_count = expert_count * capacity
    for offset, block_ref in enumerate(block_refs):
        placing = one_hot(block_ref, row_count, slot_count, capacity)
        placed = multiply(placing, block_ref[pl.ds(0, row_count), :])
        placed = placed.reshape(expert_count, capacity, seg_rows)
        out_ref[:, offset] = placed.astype(jnp.bfloat16)


def unplace_kernel(block_ref, returned_ref, out_ref):
    expert_count, capacity, model_width = returned_ref.shape
    slot_count = expert_count * capacity
    row_count = out_ref.shape[1]
    placing = one_hot(block_ref, row_count, slot_count, capacity)
    returned = flat_rows(returned_ref[...])
    out_ref[0] = contract_first(placing, returned).astype(jnp.bfloat16)


def flat_rows(blocks):
    rows = blocks.shape[0] * blocks.shape[1]
    if blocks.shape[1] % 16:
        wide = blocks.astype(jnp.float32).reshape(rows, blocks.shape[2])
        return wide.astype(jnp.bfloat16)
    return blocks.reshape(rows, blocks.shape[2])


def back_kernel(incoming_ref, weight_ref, *out_refs):
    for offset, out_ref in enumerate(out_refs):
        rows = flat_rows(incoming_ref[:, offset])
        out_ref[...] = multiply(rows, weight_ref[0, 0]).astype(out_ref.dtype)


def forward_kernel(offsets, has_start, rep_ref, inputs_ref, *refs):
    out_ref = refs[-1]
    weight_refs = refs[:-1]
    gate = up = None
    if has_start:
        gate, up = weight_refs[0][0], weight_refs[0][1]
        weight_refs = weight_refs[1:]
    for place, offset in enumerate(offsets):
        gate_ref, up_ref = weight_refs[2 * place : 2 * place + 2]
        rows = inputs_ref[:, segment(rep_ref, offset, gate_ref.shape[0])]
        gate_part, up_part = multiply(rows, gate_ref[...]), multiply(rows, up_ref[...])
        gate = gate_part if gate is None else gate + gate_part
        up = up_part if up is None else up + up_part
    out_ref[0] = gate
    out_ref[1] = up


def factor_kernel(forward_ref, *refs):
    back_refs, (first_ref, second_ref) = refs[:-2], refs[-2:]
    slot_count = forward_ref.shape[1]
    half = slot_count // 2
    hidden_grad = back_refs[0][...]
    for back_ref in back_refs[1:]:
        hidden_grad = hidden_grad + back_ref[...].astype(jnp.float32)
    gate_pre, up_pre = forward_ref[0], forward_ref[1]
    sigmoid_gate = jax.nn.sigmoid(gate_pre)
    gate_act = gate_pre * sigmoid_gate
    hidden = (gate_act * up_pre).astype(jnp.bfloat16)
    first_ref[pl.ds(0, slot_count), :] = (
        hidden_grad * up_pre * sigmoid_gate * (1.0 + gate_pre * (1.0 - sigmoid_gate))
    ).astype(jnp.bfloat16)
    second_ref[pl.ds(0, slot_count), :] = (hidden_grad * gate_act).astype(jnp.bfloat16)
    first_ref[pl.ds(slot_count, half), :] = hidden[:half]
    second_ref[pl.ds(slot_count, half), :] = hidden[half:]


def slot_kernel(rep_ref, first_ref, second_ref, *refs):
    weight_refs, out_ref = refs[:-1], refs[-1]
    expert_count, capacity, _ = out_ref.shape
    slot_count = expert_count * capacity
    gate_grad = first_ref[pl.ds(0, slot_count), :]
    up_grad = second_ref[pl.ds(0, slot_count), :]
    for offset in range(len(weight_refs) // 2):
        gate_ref, up_ref = weight_refs[2 * offset : 2 * offset + 2]
        total = contract_last(gate_grad, gate_ref[...]) + contract_last(up_grad, up_ref[...])
        total = total.reshape(expert_count, capacity, total.shape[1]).astype(jnp.bfloat16)
        out_ref[:, :, segment(rep_ref, offset, total.shape[2])] = total


def weight_grad(matrix, offset, inputs_refs, incoming_ref, factor_refs):
    first_ref, second_ref = factor_refs[2 * offset : 2 * offset + 2]
    slot_count = inputs_refs[offset].shape[0]
    if matrix < 2:
        factor_ref = second_ref if matrix else first_ref
        return contract_first(inputs_refs[offset][...], factor_ref[pl.ds(0, slot_count), :])
    half = slot_count // 2
    middle = incoming_ref.shape[0] // 2
    return contract_first(
        flat_rows(incoming_ref[:middle, offset]), first_ref[pl.ds(slot_count, half), :]
    ) + contract_first(
        flat_rows(incoming_ref[middle:, offset]), second_ref[pl.ds(slot_count, half), :]
    )


def gram_kernel(count, rep_ref, *refs):
    inputs_refs, incoming_ref = refs[:count], refs[count]
    factor_refs = refs[count + 1 : 3 * count + 1]
    gram_ref, grads_ref, sums_ref = refs[3 * count + 1 :]

    @pl.when(pl.program_id(0) == 0)
    def _():
        sums_ref[...] = jnp.zeros_like(sums_ref)

    for matrix in range(3):
        for offset in range(count):
            grads_ref[rep_ref[0] ^ offset] = weight_grad(
                matrix, offset, inputs_refs, incoming_ref, factor_refs
            )
        for place, (i, j) in enumerate(pair_list(count)):
            sums_ref[pl.ds(place, 1), :] += jnp.sum(
                grads_ref[i] * grads_ref[j], axis=0, keepdims=True
            )

    @pl.when(pl.program_id(0) == pl.num_programs(0) - 1)
    def _():
        total = sums_ref[:, pl.ds(0, 128)]
        for lane in range(128, sums_ref.shape[1], 128):
            total = total + sums_ref[:, pl.ds(lane, 128)]
        gram_ref[...] = total


def merge_coefs(gram, count):
    vectors = [{rep: None} for rep in range(count)]

    def term(coef, value):
        return value if coef is None else coef * value

    def inner(left, right):
        total = None
        for i, left_coef in left.items():
            for j, right_coef in right.items():
                value = term(left_coef, term(right_coef, gram[min(i, j), max(i, j)]))
                total = value if total is None else total + value
        return total

    while len(vectors) > 1:
        merged = []
        for first, second in zip(vectors[0::2], vectors[1::2]):
            norm_first = jnp.maximum(inner(first, first), 0.0)
            norm_second = jnp.maximum(inner(second, second), 0.0)
            bound = jnp.sqrt(norm_first) * jnp.sqrt(norm_second)
            cross = jnp.minimum(jnp.maximum(inner(first, second), -bound), bound)
            coef_first = 1.0 - cross / (2.0 * (norm_first + norm_eps))
            coef_second = 1.0 - cross / (2.0 * (norm_second + norm_eps))
            joined = {rep: term(coef, coef_first) for rep, coef in first.items()}
            joined.update({rep: term(coef, coef_second) for rep, coef in second.items()})
            merged.append(joined)
        vectors = merged
    return [vectors[0][rep] for rep in range(count)]


def adam_kernel(count, rep_ref, *refs):
    gram_refs, refs = refs[:count], refs[count:]
    inputs_refs, incoming_ref = refs[:count], refs[count]
    factor_refs = refs[count + 1 : 3 * count + 1]
    first_ref, second_ref, step_ref, coef_ref = refs[3 * count + 1 :]

    @pl.when(pl.program_id(0) == 0)
    def _():
        sums = gram_refs[0][...]
        for gram_ref in gram_refs[1:]:
            sums = sums + gram_ref[...]
        sums = jnp.sum(sums, axis=1, keepdims=True)
        gram = {pair: sums[place : place + 1] for place, pair in enumerate(pair_list(count))}
        for rep, coef in enumerate(merge_coefs(gram, count)):
            coef_ref[rep] = jnp.broadcast_to(coef, coef_ref.shape[1:])

    for matrix in range(3):
        merged = None
        for offset in range(count):
            part = weight_grad(matrix, offset, inputs_refs, incoming_ref, factor_refs)
            part = part * coef_ref[rep_ref[0] ^ offset]
            merged = part if merged is None else merged + part
        first_new = beta_first * first_ref[0, matrix] + (1.0 - beta_first) * merged
        second_new = beta_second * second_ref[0, matrix] + (1.0 - beta_second) * merged * merged
        step_ref[0, matrix] = (first_new / first_fix) / (
            jnp.sqrt(second_new / second_fix) + adam_eps
        )


def adasum_adam_many(rep, inputs, incoming, factors, first_moment, second_moment):
    count = len(inputs)
    half = inputs[0].shape[0] // 2
    grads = []
    for offset, (first, second) in enumerate(factors):
        received = incoming[:, offset].reshape(2 * half, incoming.shape[3])
        hidden = jnp.concatenate([first[2 * half :], second[2 * half :]])
        grads.append(
            jnp.stack(
                [
                    contract_first(inputs[offset], first[: 2 * half]),
                    contract_first(inputs[offset], second[: 2 * half]),
                    contract_first(received, hidden),
                ]
            )
        )
    grads = jnp.stack(grads)[rep[0] ^ jnp.arange(count)]
    flat = grads.reshape(count, -1)
    gram = lax.psum(jnp.matmul(flat, flat.T, precision=lax.Precision.HIGHEST), "replica")
    coefs = jnp.eye(count, dtype=jnp.float32)
    while coefs.shape[0] > 1:
        inner = jnp.matmul(
            jnp.matmul(coefs, gram, precision=lax.Precision.HIGHEST),
            coefs.T,
            precision=lax.Precision.HIGHEST,
        )
        norms = jnp.maximum(jnp.diagonal(inner), 0.0)
        norm_first, norm_second = norms[0::2], norms[1::2]
        bound = jnp.sqrt(norm_first) * jnp.sqrt(norm_second)
        cross = jnp.clip(jnp.diagonal(inner, offset=1)[0::2], -bound, bound)
        coef_first = 1.0 - cross / (2.0 * (norm_first + norm_eps))
        coef_second = 1.0 - cross / (2.0 * (norm_second + norm_eps))
        coefs = coef_first[:, None] * coefs[0::2] + coef_second[:, None] * coefs[1::2]
    merged = jnp.sum(coefs[0][:, None, None, None] * grads, axis=0)
    first_new = beta_first * first_moment[0] + (1.0 - beta_first) * merged
    second_new = beta_second * second_moment[0] + (1.0 - beta_second) * merged * merged
    return ((first_new / first_fix) / (jnp.sqrt(second_new / second_fix) + adam_eps))[None]


def adasum_adam(rep, inputs, incoming, factors, first_moment, second_moment):
    count = len(inputs)
    if count > 4:
        return adasum_adam_many(rep, inputs, incoming, factors, first_moment, second_moment)
    slot_count, seg_rows = inputs[0].shape
    hidden_width = first_moment.shape[3]
    expert_count, _, capacity, _ = incoming.shape
    tile = min(seg_rows, 128)
    grid = (seg_rows // tile,)
    pairs = -(-len(pair_list(count)) // 8) * 8
    flat = [array for pair in factors for array in pair]
    operands = [*inputs, incoming, *flat]
    specs = [
        *[pl.BlockSpec((slot_count, tile), lambda d: (0, d)) for _ in inputs],
        pl.BlockSpec((expert_count, count, capacity, tile), lambda d: (0, 0, 0, d)),
        *[whole(array) for array in flat],
    ]
    flops = 6 * count * slot_count * seg_rows * hidden_width
    (partial,) = call(
        functools.partial(gram_kernel, count),
        "gram",
        [rep, *operands],
        [SMEM, *specs],
        [jax.ShapeDtypeStruct((pairs, 128), jnp.float32)],
        grid=grid,
        scratch=[
            pltpu.VMEM((count, tile, hidden_width), jnp.float32),
            pltpu.VMEM((pairs, hidden_width), jnp.float32),
        ],
        flops=flops,
    )
    grams = exchange([partial] * count)
    moment_spec = pl.BlockSpec((1, 3, tile, hidden_width), lambda d: (0, 0, d, 0))
    (adam_step,) = call(
        functools.partial(adam_kernel, count),
        "adam",
        [rep, *grams, *operands, first_moment, second_moment],
        [SMEM, *[whole(gram) for gram in grams], *specs, moment_spec, moment_spec],
        [jax.ShapeDtypeStruct(first_moment.shape, jnp.float32)],
        out_specs=[moment_spec],
        grid=grid,
        scratch=[pltpu.VMEM((count, 1, hidden_width), jnp.float32)],
        flops=flops,
    )
    return adam_step


def shards(
    weights, first_moment, second_moment, out_grads, routes, task_ids, task_weights, saved_inputs
):
    expert_count = lax.axis_size("expert")
    rep_count = lax.axis_size("replica")
    row_count = out_grads.shape[1]
    model_width = out_grads.shape[2]
    hidden_width = weights.shape[3]
    slot_count = saved_inputs.shape[2]
    capacity = slot_count // expert_count
    seg_rows = model_width // rep_count
    half = slot_count // 2
    offsets = range(rep_count)
    rep = lax.axis_index("replica").astype(jnp.int32).reshape(1)
    shape = jax.ShapeDtypeStruct

    block = shape((row_count + LABEL_ROWS, seg_rows), jnp.bfloat16)
    row_blocks = call(
        rows_kernel,
        "rows",
        [
            rep,
            task_ids,
            task_weights,
            routes[0],
            routes[0].reshape(1, row_count),
            out_grads[0],
        ],
        [SMEM, SMEM, SMEM]
        + [whole(x) for x in (routes[0], routes[0].reshape(1, row_count), out_grads[0])],
        [block for _ in offsets],
    )
    routed = exchange(row_blocks)

    own_weights = [weights[0, 0], weights[0, 1]]
    projections = gather_pair(*own_weights)

    inputs_home = saved_inputs[0, 0]
    inputs = exchange(
        call(
            split_kernel,
            "split",
            [rep, inputs_home],
            [SMEM, whole(inputs_home)],
            [shape((slot_count, seg_rows), jnp.bfloat16) for _ in offsets],
        )
    )

    (outgoing,) = call(
        functools.partial(place_kernel, row_count),
        "place",
        routed,
        [whole(x) for x in routed],
        [shape((expert_count, rep_count, capacity, seg_rows), jnp.bfloat16)],
        flops=2 * rep_count * slot_count * row_count * seg_rows,
    )
    incoming = lax.all_to_all(outgoing, "expert", split_axis=0, concat_axis=0, tiled=True)

    forward = None
    late = [3] if rep_count == 4 else []
    for name, group in (("forward", [k for k in offsets if k not in late]), ("rest", late)):
        if not group:
            continue
        operands = [rep, inputs_home] + ([] if forward is None else [forward])
        operands += [array for k in group for array in projections[k]]
        (forward,) = call(
            functools.partial(forward_kernel, group, forward is not None),
            name,
            operands,
            [SMEM] + [whole(x) for x in operands[1:]],
            [shape((2, slot_count, hidden_width), jnp.float32)],
            flops=4 * len(group) * slot_count * seg_rows * hidden_width,
        )

    back_shape = (slot_count, hidden_width)
    back = exchange(
        call(
            back_kernel,
            "back",
            [incoming, weights],
            [
                whole(incoming),
                pl.BlockSpec((1, 1, seg_rows, hidden_width), lambda i: (0, 2, 0, 0)),
            ],
            [shape(back_shape, jnp.bfloat16 if k else jnp.float32) for k in offsets],
            flops=2 * rep_count * slot_count * seg_rows * hidden_width,
        )
    )
    first, second = call(
        factor_kernel,
        "factors",
        [forward, *back],
        [whole(x) for x in (forward, *back)],
        [shape((slot_count + half, hidden_width), jnp.bfloat16)] * 2,
    )
    factors = gather_pair(first, second)

    operands = [rep, first, second] + [array for pair in projections for array in pair]
    (slot_grads,) = call(
        slot_kernel,
        "slots",
        operands,
        [SMEM] + [whole(x) for x in operands[1:]],
        [shape((expert_count, capacity, model_width), jnp.bfloat16)],
        flops=4 * slot_count * model_width * hidden_width,
    )
    returned = lax.all_to_all(slot_grads, "expert", split_axis=0, concat_axis=0, tiled=True)
    (input_grads,) = call(
        unplace_kernel,
        "unplace",
        [routed[0], returned],
        [whole(routed[0]), whole(returned)],
        [shape((1, row_count, model_width), jnp.bfloat16)],
        flops=2 * slot_count * row_count * model_width,
    )

    adam_step = adasum_adam(rep, inputs, incoming, factors, first_moment, second_moment)
    return (input_grads, adam_step)


def solution(mesh):
    return jax.shard_map(
        shards,
        mesh=mesh,
        in_specs=(
            P("expert", None, "replica", None),
            P("expert", None, "replica", None),
            P("expert", None, "replica", None),
            P("replica", "expert", None),
            P("replica", "expert", None),
            P("replica", "expert"),
            P(),
            P("replica", "expert", None, None),
        ),
        out_specs=(P("replica", "expert", None), P("expert", None, "replica", None)),
        check_vma=False,
    )
```

time: 216 us -> 161 us (0.75)
  blocking collectives: 38.6 us -> 0 us
  Pallas kernels: 15.5 us -> 44.9 us
  waiting for transfers between devices: 95.5 us -> 68.5 us
  matrix products: 9.87 us -> 0 us
  other arithmetic: 9.08 us -> 0 us
  starting transfers between devices: 31.7 us -> 36.2 us
  local copies, waits for them, and re-layouts: 13.4 us -> 9.1 us
    all_to_all x8 -> x2, waiting for transfers between devices: 95.5 us -> 8.35 us  [the longest x1 8.35 us: shards(): lax.all_to_all(outgoing, 'expert', split_axis=0, concat_axis=0, tiled=True)]
    ppermute x0 -> x24, waiting for transfers between devices: none -> 60.1 us  [from_peer(): lax.ppermute(array, 'replica', [(i, i ^ offset) for i in range(count)])]
    all_to_all x1 -> x0, blocking collectives: 38.6 us -> none  [swap(): return lax.all_to_all(blocks, axis, split_axis=0, concat_axis=0, tiled=True)]
    pallas_call x2 -> x11, Pallas kernels: 15.5 us -> 44.9 us  [call(): pl.pallas_call(kernel, grid=grid, in_specs=specs, out_specs=out_specs if...]
    ppermute x0 -> x24, starting transfers between devices: none -> 26.5 us  [from_peer(): lax.ppermute(array, 'replica', [(i, i ^ offset) for i in range(count)])]
    all_to_all x8 -> x2, starting transfers between devices: 31.7 us -> 9.62 us  [the longest x1 4.88 us: shards(): lax.all_to_all(outgoing, 'expert', split_axis=0, concat_axis=0, tiled=True)]
    dot_general x7 -> x0, matrix products: 9.87 us -> none  [the longest x3 6.64 us: product(): total = jnp.dot(flat, matrix, preferred_element_type=jnp.float32)]
    reduce_sum x5 -> x0, other arithmetic: 3.85 us -> none  [the longest x1 1.42 us: shards(): jnp.sum(swap(backward, 'replica').astype(jnp.float32), axis=0)[0]]
  transfers between devices with their start and end apart: 8 -> 26, of which waited for: 7 -> 14; matrix products, arithmetic and copies ran while one was open for 7% -> 1% of each run, Pallas kernels for 7% -> 19%
where the time goes in v2:
time: 161 us; the launch traced here: 160 us
  waiting for transfers between devices  68.5 us (43%)
  Pallas kernels  44.9 us (28%)
  starting transfers between devices  36.2 us (22%)
  local copies, waits for them, and re-layouts  9.1 us (6%)
    ppermute x24, waiting for transfers between devices, from_peer(): lax.ppermute(array, 'replica', [(i, i ^ offset) for i in range(count)])  60.1 us
    pallas_call x11, Pallas kernels, call(): pl.pallas_call(kernel, grid=grid, in_specs=specs, out_specs=out_specs if...  44.9 us
    ppermute x24, starting transfers between devices, from_peer(): lax.ppermute(array, 'replica', [(i, i ^ offset) for i in range(count)])  26.5 us
    all_to_all x1, waiting for transfers between devices, shards(): lax.all_to_all(outgoing, 'expert', split_axis=0, concat_axis=0, tiled=True)  8.35 us
    unnamed x52, local copies, waits for them, and re-layouts  6.46 us
    all_to_all x1, starting transfers between devices, shards(): lax.all_to_all(outgoing, 'expert', split_axis=0, concat_axis=0, tiled=True)  4.88 us
    all_to_all x1, starting transfers between devices, shards(): lax.all_to_all(slot_grads, 'expert', split_axis=0, concat_axis=0, tiled=T...  4.74 us
  transfers between devices with their start and end apart: 26, of which 14 were waited for; matrix products, arithmetic and copies ran while one was open for 1% of the time, Pallas kernels for 19%

profile of v2, /device:TPU:0, one launch (start us, length us, event | category | flops | bytes accessed | tf_op | source)
XLA Modules:
  0.0 160.1 jit_solution(5749708316285418307)
XLA Ops:
  1.3 1.4 copy.10.column_ref
  2.7 2.0 %rows.1 = (bf16[144,512]{1,0:T(8,128)(2,1)}, bf16[144,512]{1,0:T(8,128)(2,1)}, bf16[144,512]{1,0:T(8,128)(2,1)}, bf16[144,512]{1,0:T(8,128)(2,1)}) custom-call(s32[1]{0:T(128)} %bitcast.rep_ref, s32[1,1]{1,0:T(1,128)S(6)} %copy.11.ids_ref, f32[8]{0:T(128)} %task_ref.1, s32[128,1]{1,0:T(8,128)} %copy.10.column_ref, s32[1,128]{1,0:T(1,128)} %bitcast.14, ...), custom_call_target="tpu_custom_call" | custom-call | bytes 1115176 | tf_op jit(solution)/shard_map/rows/pallas_call | solution.py:76
  4.7 2.9 %collective-permute-start.6 = (bf16[144,512]{1,0:T(8,128)(2,1)}, bf16[144,512]{1,0:T(8,128)(2,1)S(1)}, u32[]{:S(2)}, u32[]{:S(2)}) collective-permute-start(bf16[144,512]{1,0:T(8,128)(2,1)} %get-tuple-element.17), channel_id=1, source_target_pairs={{0,1},{1,0},{2,3},{3,2},{4,5},{5,4},{6,7},{7,6},{8,9},{9,8},{10,11... | collective-permute-start | bytes 442376 | tf_op jit(solution)/shard_map/ppermute | solution.py:38
  7.6 1.5 collective-permute-start.7
  9.1 0.0 collective-permute-start.8
  9.1 3.0 %collective-permute-done.6.refs_1_ = bf16[144,512]{1,0:T(8,128)(2,1)S(1)} collective-permute-done((bf16[144,512]{1,0:T(8,128)(2,1)}, bf16[144,512]{1,0:T(8,128)(2,1)S(1)}, u32[]{:S(2)}, u32[]{:S(2)}) %collective-permute-start.6) | collective-permute-done | bytes 147488 | tf_op jit(solution)/shard_map/ppermute | solution.py:38
  12.2 4.1 %collective-permute-done.7.refs_2_ = bf16[144,512]{1,0:T(8,128)(2,1)S(1)} collective-permute-done((bf16[144,512]{1,0:T(8,128)(2,1)}, bf16[144,512]{1,0:T(8,128)(2,1)S(1)}, u32[]{:S(2)}, u32[]{:S(2)}) %collective-permute-start.7) | collective-permute-done | bytes 147488 | tf_op jit(solution)/shard_map/ppermute | solution.py:38
  16.3 0.6 copy-done.21
  17.0 0.1 copy-done.22
  17.0 2.5 %place.1 = bf16[8,4,32,512]{3,2,1,0:T(8,128)(2,1)} custom-call(bf16[144,512]{1,0:T(8,128)(2,1)} %get-tuple-element.16.refs_0_.block_ref, bf16[144,512]{1,0:T(8,128)(2,1)} %copy-done.20, bf16[144,512]{1,0:T(8,128)(2,1)} %copy-done.21, bf16[144,512]{1,0:T(8,128)(2,1)} %copy-done.22), custom_call_target="tpu_custom_call" | custom-call | flops 134217728 | bytes 1638400 | tf_op jit(solution)/shard_map/place/pallas_call | solution.py:76
  19.5 4.9 %all-to-all-start = ((bf16[8,4,32,512]{3,2,1,0:T(8,128)(2,1)}), bf16[8,4,32,512]{3,2,1,0:T(8,128)(2,1)S(1)}, u32[]{:S(2)}, u32[]{:S(2)}) async-start(bf16[8,4,32,512]{3,2,1,0:T(8,128)(2,1)} %place.1), calls=%async_computation | async-start | bytes 2097152 | tf_op jit(solution)/shard_map/all_to_all | solution.py:462
  24.4 1.3 slice_bitcast_fusion
  25.7 0.0 copy-start.2
  25.7 1.6 collective-permute-start.2
  27.3 0.5 collective-permute-start.1
  27.8 1.5 collective-permute-start
  29.3 0.5 collective-permute-start.3
  29.8 10.8 %collective-permute-done.2.refs_4_ = bf16[512,512]{1,0:T(8,128)(2,1)} collective-permute-done((bf16[512,512]{1,0:T(8,128)(2,1)S(1)}, bf16[512,512]{1,0:T(8,128)(2,1)}, u32[]{:S(2)}, u32[]{:S(2)}) %collective-permute-start.2) | collective-permute-done | bytes 524320 | tf_op jit(solution)/shard_map/ppermute | solution.py:38
  40.6 1.2 collective-permute-start.4
  41.8 0.4 collective-permute-done.1.refs_3_
  42.1 0.5 collective-permute-start.5
  42.7 8.3 %all-to-all-done.incoming_ref.refs_4_.refs_8_ = bf16[8,4,32,512]{3,2,1,0:T(8,128)(2,1)S(1)} async-done(((bf16[8,4,32,512]{3,2,1,0:T(8,128)(2,1)}), bf16[8,4,32,512]{3,2,1,0:T(8,128)(2,1)S(1)}, u32[]{:S(2)}, u32[]{:S(2)}) %all-to-all-start) | async-done | bytes 1048608 | tf_op jit(solution)/shard_map/all_to_all | solution.py:462
  51.0 1.0 copy-done
  52.0 2.8 %back.1 = (f32[256,512]{1,0:T(8,128)}, bf16[256,512]{1,0:T(8,128)(2,1)}, bf16[256,512]{1,0:T(8,128)(2,1)}, bf16[256,512]{1,0:T(8,128)(2,1)}) custom-call(bf16[8,4,32,512]{3,2,1,0:T(8,128)(2,1)} %copy-done, bf16[1,3,512,512]{3,2,1,0:T(8,128)(2,1)} %weight_ref.1), custom_call_target="tpu_custom_call" | custom-call | flops 536870912 | bytes 3932160 | tf_op jit(solution)/shard_map/back/pallas_call | solution.py:76
  54.8 1.2 collective-permute-start.9
  56.0 0.0 collective-permute-done.refs_2_
  56.0 0.9 collective-permute-start.10
  56.9 1.4 collective-permute-start.11
  58.3 4.1 %forward.1.refs_0_ = f32[2,256,512]{2,1,0:T(8,128)} custom-call(s32[1]{0:T(128)} %bitcast.rep_ref, bf16[256,2048]{1,0:T(8,128)(2,1)} %bitcast.9, bf16[512,512]{1,0:T(8,128)(2,1)} %copy-done.2, bf16[512,512]{1,0:T(8,128)(2,1)} %copy-done.1, bf16[512,512]{1,0:T(8,128)(2,1)} %collective-permute-done.refs_2_, bf16[512,512]{1,0:T(8,128)(2,1)} %collective-permute-done.1.refs_3_, ...), custom_call_target="tpu_custom_call" | custom-call | flops 805306368 | bytes 5242884 | tf_op jit(solution)/shard_map/forward/pallas_call | solution.py:76
  62.4 2.1 %collective-permute-done.4.refs_1_.refs_6_ = bf16[512,512]{1,0:T(8,128)(2,1)S(1)} collective-permute-done((bf16[512,512]{1,0:T(8,128)(2,1)}, bf16[512,512]{1,0:T(8,128)(2,1)S(1)}, u32[]{:S(2)}, u32[]{:S(2)}) %collective-permute-start.4) | collective-permute-done | bytes 524320 | tf_op jit(solution)/shard_map/ppermute | solution.py:38
  64.5 0.8 copy-done.4
  65.3 0.8 copy-done.5
  66.1 3.2 %rest.1.forward_ref = f32[2,256,512]{2,1,0:T(8,128)} custom-call(s32[1]{0:T(128)} %bitcast.rep_ref, bf16[256,2048]{1,0:T(8,128)(2,1)} %bitcast.10, f32[2,256,512]{2,1,0:T(8,128)} %forward.1.refs_0_, bf16[512,512]{1,0:T(8,128)(2,1)} %copy-done.4, bf16[512,512]{1,0:T(8,128)(2,1)} %copy-done.5), custom_call_target="tpu_custom_call" | custom-call | flops 268435456 | bytes 4194308 | tf_op jit(solution)/shard_map/rest/pallas_call | solution.py:76
  69.4 0.8 collective-permute-done.9.refs_1_
  70.1 4.9 %collective-permute-done.11.refs_3_ = bf16[256,512]{1,0:T(8,128)(2,1)S(1)} collective-permute-done((bf16[256,512]{1,0:T(8,128)(2,1)}, bf16[256,512]{1,0:T(8,128)(2,1)S(1)}, u32[]{:S(2)}, u32[]{:S(2)}) %collective-permute-start.11) | collective-permute-done | bytes 262176 | tf_op jit(solution)/shard_map/ppermute | solution.py:38
  75.0 0.7 copy-done.19
  75.7 2.8 %factors.1 = (bf16[384,512]{1,0:T(8,128)(2,1)}, bf16[384,512]{1,0:T(8,128)(2,1)}) custom-call(f32[2,256,512]{2,1,0:T(8,128)} %rest.1.forward_ref, f32[256,512]{1,0:T(8,128)} %get-tuple-element.20.refs_0_, bf16[256,512]{1,0:T(8,128)(2,1)} %copy-done.17, bf16[256,512]{1,0:T(8,128)(2,1)} %copy-done.18, bf16[256,512]{1,0:T(8,128)(2,1)} %copy-done.19), custom_call_target="tpu_custom_call" | custom-call | bytes 3145728 | tf_op jit(solution)/shard_map/factors/pallas_call | solution.py:76
  78.6 4.7 %slots.1 = bf16[8,32,2048]{2,1,0:T(8,128)(2,1)} custom-call(s32[1]{0:T(128)} %bitcast.rep_ref, bf16[384,512]{1,0:T(8,128)(2,1)} %get-tuple-element.24.first_ref.refs_5_.refs_9_, bf16[384,512]{1,0:T(8,128)(2,1)} %get-tuple-element.25.second_ref.refs_6_.refs_10_, bf16[512,512]{1,0:T(8,128)(2,1)} %copy-done.2, bf16[512,512]{1,0:T(8,128)(2,1)} %copy-done.1, ...), custom_call_target="tpu_custom_call" | custom-call | flops 1073741824 | bytes 6029316 | tf_op jit(solution)/shard_map/slots/pallas_call | solution.py:76
  83.3 4.7 %all-to-all-start.1 = ((bf16[8,32,2048]{2,1,0:T(8,128)(2,1)}), bf16[8,32,2048]{2,1,0:T(8,128)(2,1)S(1)}, u32[]{:S(2)}, u32[]{:S(2)}) async-start(bf16[8,32,2048]{2,1,0:T(8,128)(2,1)} %slots.1), calls=%async_computation.1 | async-start | bytes 2097152 | tf_op jit(solution)/shard_map/all_to_all | solution.py:512
  88.0 1.6 collective-permute-start.17
  89.6 0.5 collective-permute-start.16
  90.1 2.3 %split.1 = (bf16[256,512]{1,0:T(8,128)(2,1)}, bf16[256,512]{1,0:T(8,128)(2,1)}, bf16[256,512]{1,0:T(8,128)(2,1)}, bf16[256,512]{1,0:T(8,128)(2,1)}) custom-call(s32[1]{0:T(128)} %bitcast.rep_ref, bf16[256,2048]{1,0:T(8,128)(2,1)} %bitcast.11), custom_call_target="tpu_custom_call" | custom-call | bytes 2097156 | tf_op jit(solution)/shard_map/split/pallas_call | solution.py:76
  92.4 1.5 collective-permute-start.12
  93.9 0.5 collective-permute-start.13
  94.4 1.2 collective-permute-start.15
  95.6 11.6 %collective-permute-done.12.refs_1_.refs_5_ = bf16[256,512]{1,0:T(8,128)(2,1)S(1)} collective-permute-done((bf16[256,512]{1,0:T(8,128)(2,1)}, bf16[256,512]{1,0:T(8,128)(2,1)S(1)}, u32[]{:S(2)}, u32[]{:S(2)}) %collective-permute-start.12) | collective-permute-done | bytes 262176 | tf_op jit(solution)/shard_map/ppermute | solution.py:38
  107.2 0.5 collective-permute-start.18
  107.7 1.2 collective-permute-start.19
  108.9 0.9 collective-permute-start.20
  109.8 1.4 collective-permute-start.14
  111.2 17.7 %collective-permute-done.14.refs_3_.refs_7_ = bf16[256,512]{1,0:T(8,128)(2,1)S(1)} collective-permute-done((bf16[256,512]{1,0:T(8,128)(2,1)}, bf16[256,512]{1,0:T(8,128)(2,1)S(1)}, u32[]{:S(2)}, u32[]{:S(2)}) %collective-permute-start.14) | collective-permute-done | bytes 262176 | tf_op jit(solution)/shard_map/ppermute | solution.py:38
  129.0 1.8 %collective-permute-done.20.refs_12_.refs_16_ = bf16[384,512]{1,0:T(8,128)(2,1)S(1)} collective-permute-done((bf16[384,512]{1,0:T(8,128)(2,1)S(1)}, bf16[384,512]{1,0:T(8,128)(2,1)S(1)}, u32[]{:S(2)}, u32[]{:S(2)}) %collective-permute-start.20) | collective-permute-done | bytes 393248 | tf_op jit(solution)/shard_map/ppermute | solution.py:38
  130.8 0.7 copy-done.13
  131.5 8.6 %gram.1.refs_0_ = f32[16,128]{1,0:T(8,128)} custom-call(s32[1]{0:T(128)} %bitcast.rep_ref, bf16[256,512]{1,0:T(8,128)(2,1)} %get-tuple-element.26.refs_0_.refs_4_, bf16[256,512]{1,0:T(8,128)(2,1)} %copy-done.14, bf16[256,512]{1,0:T(8,128)(2,1)} %copy-done.15, bf16[256,512]{1,0:T(8,128)(2,1)} %copy-done.16, bf16[8,4,32,512]{3,2,1,0:T(8,128)(2,1)} %copy-done, ...), custom_call_target="tpu_custom_call" | custom-call | flops 1610612736 | bytes 5251076 | tf_op jit(solution)/shard_map/gram/pallas_call | solution.py:76
  140.1 0.5 collective-permute-start.21
  140.7 1.1 collective-permute-start.22
  141.8 1.8 %collective-permute-start.23 = (f32[16,128]{1,0:T(8,128)}, f32[16,128]{1,0:T(8,128)S(1)}, u32[]{:S(2)}, u32[]{:S(2)}) collective-permute-start(f32[16,128]{1,0:T(8,128)} %gram.1.refs_0_), channel_id=1, source_target_pairs={{0,3},{1,2},{2,1},{3,0},{4,7},{5,6},{6,5},{7,4},{8,11},{9,10},{10,... | collective-permute-start | bytes 24584 | tf_op jit(solution)/shard_map/ppermute | solution.py:38
  143.6 0.4 collective-permute-done.21.refs_1_
  144.0 0.5 collective-permute-done.22.refs_2_
  144.5 2.0 %collective-permute-done.23.refs_3_ = f32[16,128]{1,0:T(8,128)S(1)} collective-permute-done((f32[16,128]{1,0:T(8,128)}, f32[16,128]{1,0:T(8,128)S(1)}, u32[]{:S(2)}, u32[]{:S(2)}) %collective-permute-start.23) | collective-permute-done | bytes 8224 | tf_op jit(solution)/shard_map/ppermute | solution.py:38
  146.6 0.6 copy-done.25
  147.2 9.4 %adam.1 = f32[1,3,512,512]{3,2,1,0:T(8,128)} custom-call(s32[1]{0:T(128)} %bitcast.rep_ref, f32[16,128]{1,0:T(8,128)} %gram.1.refs_0_, f32[16,128]{1,0:T(8,128)} %copy-done.23, f32[16,128]{1,0:T(8,128)} %copy-done.24, f32[16,128]{1,0:T(8,128)} %copy-done.25, bf16[256,512]{1,0:T(8,128)(2,1)} %get-tuple-element.26.refs_0_.refs_4_, ...), custom_call_target="tpu_custom_call" | custom-call | flops 1610612736 | bytes 14712836 | tf_op jit(solution)/shard_map/adam/pallas_call | solution.py:76
  156.6 1.0 copy-done.3
  157.6 2.4 %unplace.1 = bf16[1,128,2048]{2,1,0:T(8,128)(2,1)} custom-call(bf16[144,512]{1,0:T(8,128)(2,1)} %get-tuple-element.16.refs_0_.block_ref, bf16[8,32,2048]{2,1,0:T(8,128)(2,1)} %copy-done.3), custom_call_target="tpu_custom_call" | custom-call | flops 134217728 | bytes 1720320 | tf_op jit(solution)/shard_map/unplace/pallas_call | solution.py:76
  (53 shorter events, 0.1 us)
Async XLA Ops:
  4.7 7.5 %collective-permute-start.6 = (bf16[144,512]{1,0:T(8,128)(2,1)}, bf16[144,512]{1,0:T(8,128)(2,1)S(1)}, u32[]{:S(2)}, u32[]{:S(2)}) collective-permute-start(bf16[144,512]{1,0:T(8,128)(2,1)} %get-tuple-element.17), channel_id=1, source_target_pairs={{0,1},{1,0},{2,3},{3,2},{4,5},{5,4},{6,7},{7,6},{8,9},{9,8},{10,11... | collective-permute-start | bytes 442376 | tf_op jit(solution)/shard_map/ppermute | solution.py:38
  7.6 8.7 %collective-permute-start.7 = (bf16[144,512]{1,0:T(8,128)(2,1)}, bf16[144,512]{1,0:T(8,128)(2,1)S(1)}, u32[]{:S(2)}, u32[]{:S(2)}) collective-permute-start(bf16[144,512]{1,0:T(8,128)(2,1)} %get-tuple-element.18), channel_id=1, source_target_pairs={{0,2},{1,3},{2,0},{3,1},{4,6},{5,7},{6,4},{7,5},{8,10},{9,11},{10,... | collective-permute-start | bytes 442376 | tf_op jit(solution)/shard_map/ppermute | solution.py:38
  9.1 7.2 %collective-permute-start.8 = (bf16[144,512]{1,0:T(8,128)(2,1)}, bf16[144,512]{1,0:T(8,128)(2,1)S(1)}, u32[]{:S(2)}, u32[]{:S(2)}) collective-permute-start(bf16[144,512]{1,0:T(8,128)(2,1)} %get-tuple-element.19), channel_id=1, source_target_pairs={{0,3},{1,2},{2,1},{3,0},{4,7},{5,6},{6,5},{7,4},{8,11},{9,10},{10,... | collective-permute-start | bytes 442376 | tf_op jit(solution)/shard_map/ppermute | solution.py:38
  12.2 4.1 %copy-start.20 = (bf16[144,512]{1,0:T(8,128)(2,1)}, bf16[144,512]{1,0:T(8,128)(2,1)S(1)}, u32[]{:S(2)}) copy-start(bf16[144,512]{1,0:T(8,128)(2,1)S(1)} %collective-permute-done.6.refs_1_) | copy-start | bytes 442372
  16.3 0.7 copy-start.21
  16.3 0.7 copy-start.22
  19.5 31.5 %all-to-all-start = ((bf16[8,4,32,512]{3,2,1,0:T(8,128)(2,1)}), bf16[8,4,32,512]{3,2,1,0:T(8,128)(2,1)S(1)}, u32[]{:S(2)}, u32[]{:S(2)}) async-start(bf16[8,4,32,512]{3,2,1,0:T(8,128)(2,1)} %place.1), calls=%async_computation | async-start | bytes 2097152 | tf_op jit(solution)/shard_map/all_to_all | solution.py:462
  25.7 32.6 %copy-start.1 = (bf16[512,512]{1,0:T(8,128)(2,1)}, bf16[512,512]{1,0:T(8,128)(2,1)S(1)}, u32[]{:S(2)}) copy-start(bf16[512,512]{1,0:T(8,128)(2,1)S(1)} %get-tuple-element.30.refs_1_) | copy-start | bytes 1572868
  25.7 32.6 %copy-start.2 = (bf16[512,512]{1,0:T(8,128)(2,1)}, bf16[512,512]{1,0:T(8,128)(2,1)S(1)}, u32[]{:S(2)}) copy-start(bf16[512,512]{1,0:T(8,128)(2,1)S(1)} %get-tuple-element.31.refs_0_) | copy-start | bytes 1572868
  25.7 14.9 %collective-permute-start.2 = (bf16[512,512]{1,0:T(8,128)(2,1)S(1)}, bf16[512,512]{1,0:T(8,128)(2,1)}, u32[]{:S(2)}, u32[]{:S(2)}) collective-permute-start(bf16[512,512]{1,0:T(8,128)(2,1)S(1)} %get-tuple-element.31.refs_0_), channel_id=1, source_target_pairs={{0,2},{1,3},{2,0},{3,1},{4,6},{5,7},{6,4},{7,5},{8,10},{9,11},{10,... | collective-permute-start | bytes 1572872 | tf_op jit(solution)/shard_map/ppermute | solution.py:38
  27.3 14.9 %collective-permute-start.1 = (bf16[512,512]{1,0:T(8,128)(2,1)S(1)}, bf16[512,512]{1,0:T(8,128)(2,1)}, u32[]{:S(2)}, u32[]{:S(2)}) collective-permute-start(bf16[512,512]{1,0:T(8,128)(2,1)S(1)} %get-tuple-element.30.refs_1_), channel_id=1, source_target_pairs={{0,1},{1,0},{2,3},{3,2},{4,5},{5,4},{6,7},{7,6},{8,9},{9,8},{10,11... | collective-permute-start | bytes 1572872 | tf_op jit(solution)/shard_map/ppermute | solution.py:38
  27.8 28.2 %collective-permute-start = (bf16[512,512]{1,0:T(8,128)(2,1)S(1)}, bf16[512,512]{1,0:T(8,128)(2,1)}, u32[]{:S(2)}, u32[]{:S(2)}) collective-permute-start(bf16[512,512]{1,0:T(8,128)(2,1)S(1)} %get-tuple-element.31.refs_0_), channel_id=1, source_target_pairs={{0,1},{1,0},{2,3},{3,2},{4,5},{5,4},{6,7},{7,6},{8,9},{9,8},{10,11... | collective-permute-start | bytes 1572872 | tf_op jit(solution)/shard_map/ppermute | solution.py:38
  29.3 27.6 %collective-permute-start.3 = (bf16[512,512]{1,0:T(8,128)(2,1)S(1)}, bf16[512,512]{1,0:T(8,128)(2,1)}, u32[]{:S(2)}, u32[]{:S(2)}) collective-permute-start(bf16[512,512]{1,0:T(8,128)(2,1)S(1)} %get-tuple-element.30.refs_1_), channel_id=1, source_target_pairs={{0,2},{1,3},{2,0},{3,1},{4,6},{5,7},{6,4},{7,5},{8,10},{9,11},{10,... | collective-permute-start | bytes 1572872 | tf_op jit(solution)/shard_map/ppermute | solution.py:38
  40.6 23.9 %collective-permute-start.4 = (bf16[512,512]{1,0:T(8,128)(2,1)}, bf16[512,512]{1,0:T(8,128)(2,1)S(1)}, u32[]{:S(2)}, u32[]{:S(2)}) collective-permute-start(bf16[512,512]{1,0:T(8,128)(2,1)} %collective-permute-done.2.refs_4_), channel_id=1, source_target_pairs={{0,1},{1,0},{2,3},{3,2},{4,5},{5,4},{6,7},{7,6},{8,9},{9,8},{10,11... | collective-permute-start | bytes 1572872 | tf_op jit(solution)/shard_map/ppermute | solution.py:38
  42.1 22.4 %collective-permute-start.5 = (bf16[512,512]{1,0:T(8,128)(2,1)}, bf16[512,512]{1,0:T(8,128)(2,1)S(1)}, u32[]{:S(2)}, u32[]{:S(2)}) collective-permute-start(bf16[512,512]{1,0:T(8,128)(2,1)} %collective-permute-done.1.refs_3_), channel_id=1, source_target_pairs={{0,2},{1,3},{2,0},{3,1},{4,6},{5,7},{6,4},{7,5},{8,10},{9,11},{10,... | collective-permute-start | bytes 1572872 | tf_op jit(solution)/shard_map/ppermute | solution.py:38
  51.0 1.0 copy-start
  54.8 15.3 %collective-permute-start.9 = (bf16[256,512]{1,0:T(8,128)(2,1)}, bf16[256,512]{1,0:T(8,128)(2,1)S(1)}, u32[]{:S(2)}, u32[]{:S(2)}) collective-permute-start(bf16[256,512]{1,0:T(8,128)(2,1)} %get-tuple-element.21), channel_id=1, source_target_pairs={{0,1},{1,0},{2,3},{3,2},{4,5},{5,4},{6,7},{7,6},{8,9},{9,8},{10,11... | collective-permute-start | bytes 786440 | tf_op jit(solution)/shard_map/ppermute | solution.py:38
  56.0 14.1 %collective-permute-start.10 = (bf16[256,512]{1,0:T(8,128)(2,1)}, bf16[256,512]{1,0:T(8,128)(2,1)S(1)}, u32[]{:S(2)}, u32[]{:S(2)}) collective-permute-start(bf16[256,512]{1,0:T(8,128)(2,1)} %get-tuple-element.22), channel_id=1, source_target_pairs={{0,2},{1,3},{2,0},{3,1},{4,6},{5,7},{6,4},{7,5},{8,10},{9,11},{10,... | collective-permute-start | bytes 786440 | tf_op jit(solution)/shard_map/ppermute | solution.py:38
  56.9 18.1 %collective-permute-start.11 = (bf16[256,512]{1,0:T(8,128)(2,1)}, bf16[256,512]{1,0:T(8,128)(2,1)S(1)}, u32[]{:S(2)}, u32[]{:S(2)}) collective-permute-start(bf16[256,512]{1,0:T(8,128)(2,1)} %get-tuple-element.23), channel_id=1, source_target_pairs={{0,3},{1,2},{2,1},{3,0},{4,7},{5,6},{6,5},{7,4},{8,11},{9,10},{10,... | collective-permute-start | bytes 786440 | tf_op jit(solution)/shard_map/ppermute | solution.py:38
  64.5 0.8 copy-start.4
  65.3 0.8 copy-start.5
  70.1 4.9 %copy-start.17 = (bf16[256,512]{1,0:T(8,128)(2,1)}, bf16[256,512]{1,0:T(8,128)(2,1)S(1)}, u32[]{:S(2)}) copy-start(bf16[256,512]{1,0:T(8,128)(2,1)S(1)} %collective-permute-done.9.refs_1_) | copy-start | bytes 786436
  70.1 4.9 %copy-start.18 = (bf16[256,512]{1,0:T(8,128)(2,1)}, bf16[256,512]{1,0:T(8,128)(2,1)S(1)}, u32[]{:S(2)}) copy-start(bf16[256,512]{1,0:T(8,128)(2,1)S(1)} %collective-permute-done.10.refs_2_) | copy-start | bytes 786436
  75.0 0.7 copy-start.19
  78.5 9.5 %copy-start.6 = (bf16[384,512]{1,0:T(8,128)(2,1)S(1)}, bf16[384,512]{1,0:T(8,128)(2,1)}, u32[]{:S(2)}) copy-start(bf16[384,512]{1,0:T(8,128)(2,1)} %get-tuple-element.24.first_ref.refs_5_.refs_9_) | copy-start | bytes 1179652
  78.6 11.0 %copy-start.7 = (bf16[384,512]{1,0:T(8,128)(2,1)S(1)}, bf16[384,512]{1,0:T(8,128)(2,1)}, u32[]{:S(2)}) copy-start(bf16[384,512]{1,0:T(8,128)(2,1)} %get-tuple-element.25.second_ref.refs_6_.refs_10_) | copy-start | bytes 1179652
  83.3 73.3 %all-to-all-start.1 = ((bf16[8,32,2048]{2,1,0:T(8,128)(2,1)}), bf16[8,32,2048]{2,1,0:T(8,128)(2,1)S(1)}, u32[]{:S(2)}, u32[]{:S(2)}) async-start(bf16[8,32,2048]{2,1,0:T(8,128)(2,1)} %slots.1), calls=%async_computation.1 | async-start | bytes 2097152 | tf_op jit(solution)/shard_map/all_to_all | solution.py:512
  88.0 19.7 %collective-permute-start.17 = (bf16[384,512]{1,0:T(8,128)(2,1)S(1)}, bf16[384,512]{1,0:T(8,128)(2,1)S(1)}, u32[]{:S(2)}, u32[]{:S(2)}) collective-permute-start(bf16[384,512]{1,0:T(8,128)(2,1)S(1)} %copy-done.6), channel_id=1, source_target_pairs={{0,2},{1,3},{2,0},{3,1},{4,6},{5,7},{6,4},{7,5},{8,10},{9,11},{10,... | collective-permute-start | bytes 1179656 | tf_op jit(solution)/shard_map/ppermute | solution.py:38
  89.6 19.3 %collective-permute-start.16 = (bf16[384,512]{1,0:T(8,128)(2,1)S(1)}, bf16[384,512]{1,0:T(8,128)(2,1)S(1)}, u32[]{:S(2)}, u32[]{:S(2)}) collective-permute-start(bf16[384,512]{1,0:T(8,128)(2,1)S(1)} %copy-done.7), channel_id=1, source_target_pairs={{0,1},{1,0},{2,3},{3,2},{4,5},{5,4},{6,7},{7,6},{8,9},{9,8},{10,11... | collective-permute-start | bytes 1179656 | tf_op jit(solution)/shard_map/ppermute | solution.py:38
  92.4 14.8 %collective-permute-start.12 = (bf16[256,512]{1,0:T(8,128)(2,1)}, bf16[256,512]{1,0:T(8,128)(2,1)S(1)}, u32[]{:S(2)}, u32[]{:S(2)}) collective-permute-start(bf16[256,512]{1,0:T(8,128)(2,1)} %get-tuple-element.27), channel_id=1, source_target_pairs={{0,1},{1,0},{2,3},{3,2},{4,5},{5,4},{6,7},{7,6},{8,9},{9,8},{10,11... | collective-permute-start | bytes 786440 | tf_op jit(solution)/shard_map/ppermute | solution.py:38
  93.9 15.9 %collective-permute-start.13 = (bf16[256,512]{1,0:T(8,128)(2,1)}, bf16[256,512]{1,0:T(8,128)(2,1)S(1)}, u32[]{:S(2)}, u32[]{:S(2)}) collective-permute-start(bf16[256,512]{1,0:T(8,128)(2,1)} %get-tuple-element.28), channel_id=1, source_target_pairs={{0,2},{1,3},{2,0},{3,1},{4,6},{5,7},{6,4},{7,5},{8,10},{9,11},{10,... | collective-permute-start | bytes 786440 | tf_op jit(solution)/shard_map/ppermute | solution.py:38
  94.4 34.5 %collective-permute-start.15 = (bf16[384,512]{1,0:T(8,128)(2,1)S(1)}, bf16[384,512]{1,0:T(8,128)(2,1)S(1)}, u32[]{:S(2)}, u32[]{:S(2)}) collective-permute-start(bf16[384,512]{1,0:T(8,128)(2,1)S(1)} %copy-done.6), channel_id=1, source_target_pairs={{0,1},{1,0},{2,3},{3,2},{4,5},{5,4},{6,7},{7,6},{8,9},{9,8},{10,11... | collective-permute-start | bytes 1179656 | tf_op jit(solution)/shard_map/ppermute | solution.py:38
  107.2 23.6 %copy-start.14 = (bf16[256,512]{1,0:T(8,128)(2,1)}, bf16[256,512]{1,0:T(8,128)(2,1)S(1)}, u32[]{:S(2)}) copy-start(bf16[256,512]{1,0:T(8,128)(2,1)S(1)} %collective-permute-done.12.refs_1_.refs_5_) | copy-start | bytes 786436
  107.2 21.7 %collective-permute-start.18 = (bf16[384,512]{1,0:T(8,128)(2,1)S(1)}, bf16[384,512]{1,0:T(8,128)(2,1)S(1)}, u32[]{:S(2)}, u32[]{:S(2)}) collective-permute-start(bf16[384,512]{1,0:T(8,128)(2,1)S(1)} %copy-done.7), channel_id=1, source_target_pairs={{0,2},{1,3},{2,0},{3,1},{4,6},{5,7},{6,4},{7,5},{8,10},{9,11},{10,... | collective-permute-start | bytes 1179656 | tf_op jit(solution)/shard_map/ppermute | solution.py:38
  107.7 23.1 %copy-start.8 = (bf16[384,512]{1,0:T(8,128)(2,1)}, bf16[384,512]{1,0:T(8,128)(2,1)S(1)}, u32[]{:S(2)}) copy-start(bf16[384,512]{1,0:T(8,128)(2,1)S(1)} %collective-permute-done.17.refs_9_.refs_13_) | copy-start | bytes 1179652
  107.7 21.2 %collective-permute-start.19 = (bf16[384,512]{1,0:T(8,128)(2,1)S(1)}, bf16[384,512]{1,0:T(8,128)(2,1)S(1)}, u32[]{:S(2)}, u32[]{:S(2)}) collective-permute-start(bf16[384,512]{1,0:T(8,128)(2,1)S(1)} %collective-permute-done.17.refs_9_.refs_13_), channel_id=1, source_target_pairs={{0,1},{1,0},{2,3},{3,2},{4,5},{5,4},{6,7},{7,6},{8,9},{9,8},{10,11... | collective-permute-start | bytes 1179656 | tf_op jit(solution)/shard_map/ppermute | solution.py:38
  108.9 21.9 %copy-start.9 = (bf16[384,512]{1,0:T(8,128)(2,1)}, bf16[384,512]{1,0:T(8,128)(2,1)S(1)}, u32[]{:S(2)}) copy-start(bf16[384,512]{1,0:T(8,128)(2,1)S(1)} %collective-permute-done.16.refs_8_.refs_12_) | copy-start | bytes 1179652
  108.9 21.9 %collective-permute-start.20 = (bf16[384,512]{1,0:T(8,128)(2,1)S(1)}, bf16[384,512]{1,0:T(8,128)(2,1)S(1)}, u32[]{:S(2)}, u32[]{:S(2)}) collective-permute-start(bf16[384,512]{1,0:T(8,128)(2,1)S(1)} %collective-permute-done.16.refs_8_.refs_12_), channel_id=1, source_target_pairs={{0,2},{1,3},{2,0},{3,1},{4,6},{5,7},{6,4},{7,5},{8,10},{9,11},{10,... | collective-permute-start | bytes 1179656 | tf_op jit(solution)/shard_map/ppermute | solution.py:38
  109.8 21.0 %copy-start.15 = (bf16[256,512]{1,0:T(8,128)(2,1)}, bf16[256,512]{1,0:T(8,128)(2,1)S(1)}, u32[]{:S(2)}) copy-start(bf16[256,512]{1,0:T(8,128)(2,1)S(1)} %collective-permute-done.13.refs_2_.refs_6_) | copy-start | bytes 786436
  109.8 19.2 %collective-permute-start.14 = (bf16[256,512]{1,0:T(8,128)(2,1)}, bf16[256,512]{1,0:T(8,128)(2,1)S(1)}, u32[]{:S(2)}, u32[]{:S(2)}) collective-permute-start(bf16[256,512]{1,0:T(8,128)(2,1)} %get-tuple-element.29), channel_id=1, source_target_pairs={{0,3},{1,2},{2,1},{3,0},{4,7},{5,6},{6,5},{7,4},{8,11},{9,10},{10,... | collective-permute-start | bytes 786440 | tf_op jit(solution)/shard_map/ppermute | solution.py:38
  128.9 1.9 %copy-start.16 = (bf16[256,512]{1,0:T(8,128)(2,1)}, bf16[256,512]{1,0:T(8,128)(2,1)S(1)}, u32[]{:S(2)}) copy-start(bf16[256,512]{1,0:T(8,128)(2,1)S(1)} %collective-permute-done.14.refs_3_.refs_7_) | copy-start | bytes 786436
  128.9 1.9 %copy-start.10 = (bf16[384,512]{1,0:T(8,128)(2,1)}, bf16[384,512]{1,0:T(8,128)(2,1)S(1)}, u32[]{:S(2)}) copy-start(bf16[384,512]{1,0:T(8,128)(2,1)S(1)} %collective-permute-done.15.refs_7_.refs_11_) | copy-start | bytes 1179652
  128.9 1.9 %copy-start.11 = (bf16[384,512]{1,0:T(8,128)(2,1)}, bf16[384,512]{1,0:T(8,128)(2,1)S(1)}, u32[]{:S(2)}) copy-start(bf16[384,512]{1,0:T(8,128)(2,1)S(1)} %collective-permute-done.18.refs_10_.refs_14_) | copy-start | bytes 1179652
  128.9 1.9 %copy-start.12 = (bf16[384,512]{1,0:T(8,128)(2,1)}, bf16[384,512]{1,0:T(8,128)(2,1)S(1)}, u32[]{:S(2)}) copy-start(bf16[384,512]{1,0:T(8,128)(2,1)S(1)} %collective-permute-done.19.refs_11_.refs_15_) | copy-start | bytes 1179652
  130.8 0.8 copy-start.13
  140.1 3.9 %collective-permute-start.21 = (f32[16,128]{1,0:T(8,128)}, f32[16,128]{1,0:T(8,128)S(1)}, u32[]{:S(2)}, u32[]{:S(2)}) collective-permute-start(f32[16,128]{1,0:T(8,128)} %gram.1.refs_0_), channel_id=1, source_target_pairs={{0,1},{1,0},{2,3},{3,2},{4,5},{5,4},{6,7},{7,6},{8,9},{9,8},{10,11... | collective-permute-start | bytes 24584 | tf_op jit(solution)/shard_map/ppermute | solution.py:38
  140.7 3.9 %collective-permute-start.22 = (f32[16,128]{1,0:T(8,128)}, f32[16,128]{1,0:T(8,128)S(1)}, u32[]{:S(2)}, u32[]{:S(2)}) collective-permute-start(f32[16,128]{1,0:T(8,128)} %gram.1.refs_0_), channel_id=1, source_target_pairs={{0,2},{1,3},{2,0},{3,1},{4,6},{5,7},{6,4},{7,5},{8,10},{9,11},{10,... | collective-permute-start | bytes 24584 | tf_op jit(solution)/shard_map/ppermute | solution.py:38
  141.8 4.8 %collective-permute-start.23 = (f32[16,128]{1,0:T(8,128)}, f32[16,128]{1,0:T(8,128)S(1)}, u32[]{:S(2)}, u32[]{:S(2)}) collective-permute-start(f32[16,128]{1,0:T(8,128)} %gram.1.refs_0_), channel_id=1, source_target_pairs={{0,3},{1,2},{2,1},{3,0},{4,7},{5,6},{6,5},{7,4},{8,11},{9,10},{10,... | collective-permute-start | bytes 24584 | tf_op jit(solution)/shard_map/ppermute | solution.py:38
  144.0 2.6 %copy-start.23 = (f32[16,128]{1,0:T(8,128)}, f32[16,128]{1,0:T(8,128)S(1)}, u32[]{:S(2)}) copy-start(f32[16,128]{1,0:T(8,128)S(1)} %collective-permute-done.21.refs_1_) | copy-start | bytes 24580
  144.5 2.0 %copy-start.24 = (f32[16,128]{1,0:T(8,128)}, f32[16,128]{1,0:T(8,128)S(1)}, u32[]{:S(2)}) copy-start(f32[16,128]{1,0:T(8,128)S(1)} %collective-permute-done.22.refs_2_) | copy-start | bytes 24580
  146.6 0.6 copy-start.25
  156.6 1.0 copy-start.3

commit v3 on v2

--- a/solution.py
+++ b/solution.py
@@ -13,7 +13,7 @@
 norm_eps = 1e-06
 first_fix = 1.0 - (0.9**50) ** 2
 second_fix = 1.0 - (0.95**50) ** 2
-VMEM_BYTES = 56 * 1024 * 1024
+MIB = 1024 * 1024
 LABEL_ROWS = 16
 
 
@@ -64,26 +64,24 @@
     return [(i, j) for i in range(count) for j in range(i, count)]
 
 
-def whole(array):
-    return pl.BlockSpec(array.shape, lambda *_: (0,) * array.ndim)
-
-
 SMEM = pl.BlockSpec(memory_space=pltpu.SMEM)
-
-
-def call(kernel, name, operands, specs, outs, out_specs=None, grid=(1,), scratch=(), flops=0):
+VMEM = pl.BlockSpec(memory_space=pltpu.VMEM)
+
+
+def call(kernel, name, operands, specs, outs, out_specs=None, grid=(), scratch=(), extra=8):
     size = sum(x.size * x.dtype.itemsize for x in list(operands) + list(outs))
     return pl.pallas_call(
         kernel,
         grid=grid,
         in_specs=specs,
-        out_specs=out_specs if out_specs is not None else [whole(out) for out in outs],
+        out_specs=out_specs if out_specs is not None else [VMEM for _ in outs],
         out_shape=outs,
         scratch_shapes=list(scratch),
         compiler_params=pltpu.CompilerParams(
-            dimension_semantics=("arbitrary",) * len(grid), vmem_limit_bytes=VMEM_BYTES
+            dimension_semantics=("arbitrary",) * len(grid),
+            vmem_limit_bytes=min(56 * MIB, size + extra * MIB),
         ),
-        cost_estimate=pl.CostEstimate(flops=flops, bytes_accessed=size, transcendentals=0),
+        cost_estimate=pl.CostEstimate(flops=0, bytes_accessed=0, transcendentals=0),
         name=name,
     )(*operands)
 
@@ -92,7 +90,7 @@
     return pl.ds(pl.multiple_of((rep_ref[0] ^ offset) * width, width), width)
 
 
-def rows_kernel(rep_ref, ids_ref, task_ref, column_ref, row_ref, grads_ref, *out_refs):
+def rows_kernel(expert_count, rep_ref, ids_ref, task_ref, row_ref, grads_ref, *out_refs):
     row_count = grads_ref.shape[0]
     seg_rows = out_refs[0].shape[1]
     block_count = ids_ref.shape[1]
@@ -101,8 +99,12 @@
     earlier = lax.broadcasted_iota(jnp.int32, square, 0) < lax.broadcasted_iota(
         jnp.int32, square, 1
     )
-    counted = jnp.where(column_ref[...] == row_ref[...], 1.0, 0.0)
-    rank = jnp.sum(jnp.where(earlier, counted, 0.0), axis=0, keepdims=True)
+    experts = lax.broadcasted_iota(jnp.int32, (expert_count, row_count), 0)
+    chosen = jnp.where(experts == row_ref[...], 1.0, 0.0)
+    before = multiply(
+        chosen.astype(jnp.bfloat16), jnp.where(earlier, 1.0, 0.0).astype(jnp.bfloat16)
+    )
+    rank = jnp.sum(chosen * before, axis=0, keepdims=True)
     line = lax.broadcasted_iota(jnp.int32, (LABEL_ROWS, row_count), 0)
     labels = jnp.where(line == 0, row_ref[...].astype(jnp.float32), 0.0)
     labels = jnp.where(line == 1, rank, labels).astype(jnp.bfloat16)
@@ -164,7 +166,7 @@
 def back_kernel(incoming_ref, weight_ref, *out_refs):
     for offset, out_ref in enumerate(out_refs):
         rows = flat_rows(incoming_ref[:, offset])
-        out_ref[...] = multiply(rows, weight_ref[0, 0]).astype(out_ref.dtype)
+        out_ref[...] = multiply(rows, weight_ref[...]).astype(out_ref.dtype)
 
 
 def forward_kernel(offsets, has_start, rep_ref, inputs_ref, *refs):
@@ -184,31 +186,33 @@
     out_ref[1] = up
 
 
+def hidden_kernel(forward_ref, first_ref, second_ref):
+    half = forward_ref.shape[1] // 2
+    for part, out_ref in enumerate((first_ref, second_ref)):
+        rows = pl.ds(part * half, half)
+        gate_pre = forward_ref[0, rows]
+        gate_act = gate_pre * jax.nn.sigmoid(gate_pre)
+        out_ref[...] = (gate_act * forward_ref[1, rows]).astype(jnp.bfloat16)
+
+
 def factor_kernel(forward_ref, *refs):
-    back_refs, (first_ref, second_ref) = refs[:-2], refs[-2:]
-    slot_count = forward_ref.shape[1]
-    half = slot_count // 2
+    back_refs, (gate_ref, up_ref) = refs[:-2], refs[-2:]
     hidden_grad = back_refs[0][...]
     for back_ref in back_refs[1:]:
         hidden_grad = hidden_grad + back_ref[...].astype(jnp.float32)
     gate_pre, up_pre = forward_ref[0], forward_ref[1]
     sigmoid_gate = jax.nn.sigmoid(gate_pre)
     gate_act = gate_pre * sigmoid_gate
-    hidden = (gate_act * up_pre).astype(jnp.bfloat16)
-    first_ref[pl.ds(0, slot_count), :] = (
+    gate_ref[...] = (
         hidden_grad * up_pre * sigmoid_gate * (1.0 + gate_pre * (1.0 - sigmoid_gate))
     ).astype(jnp.bfloat16)
-    second_ref[pl.ds(0, slot_count), :] = (hidden_grad * gate_act).astype(jnp.bfloat16)
-    first_ref[pl.ds(slot_count, half), :] = hidden[:half]
-    second_ref[pl.ds(slot_count, half), :] = hidden[half:]
+    up_ref[...] = (hidden_grad * gate_act).astype(jnp.bfloat16)
 
 
 def slot_kernel(rep_ref, first_ref, second_ref, *refs):
     weight_refs, out_ref = refs[:-1], refs[-1]
     expert_count, capacity, _ = out_ref.shape
-    slot_count = expert_count * capacity
-    gate_grad = first_ref[pl.ds(0, slot_count), :]
-    up_grad = second_ref[pl.ds(0, slot_count), :]
+    gate_grad, up_grad = first_ref[...], second_ref[...]
     for offset in range(len(weight_refs) // 2):
         gate_ref, up_ref = weight_refs[2 * offset : 2 * offset + 2]
         total = contract_last(gate_grad, gate_ref[...]) + contract_last(up_grad, up_ref[...])
@@ -216,46 +220,41 @@
         out_ref[:, :, segment(rep_ref, offset, total.shape[2])] = total
 
 
-def weight_grad(matrix, offset, inputs_refs, incoming_ref, factor_refs):
-    first_ref, second_ref = factor_refs[2 * offset : 2 * offset + 2]
-    slot_count = inputs_refs[offset].shape[0]
-    if matrix < 2:
-        factor_ref = second_ref if matrix else first_ref
-        return contract_first(inputs_refs[offset][...], factor_ref[pl.ds(0, slot_count), :])
-    half = slot_count // 2
+def gram_kernel(count, offsets, place, rep_ref, *refs):
+    if place:
+        before_ref, earlier_ref, refs = refs[0], refs[1], refs[2:]
+    incoming_ref, operand_refs, grads_ref, gram_ref = refs[0], refs[1:-2], refs[-2], refs[-1]
     middle = incoming_ref.shape[0] // 2
-    return contract_first(
-        flat_rows(incoming_ref[:middle, offset]), first_ref[pl.ds(slot_count, half), :]
-    ) + contract_first(
-        flat_rows(incoming_ref[middle:, offset]), second_ref[pl.ds(slot_count, half), :]
-    )
-
-
-def gram_kernel(count, rep_ref, *refs):
-    inputs_refs, incoming_ref = refs[:count], refs[count]
-    factor_refs = refs[count + 1 : 3 * count + 1]
-    gram_ref, grads_ref, sums_ref = refs[3 * count + 1 :]
-
-    @pl.when(pl.program_id(0) == 0)
-    def _():
-        sums_ref[...] = jnp.zeros_like(sums_ref)
-
-    for matrix in range(3):
-        for offset in range(count):
-            grads_ref[rep_ref[0] ^ offset] = weight_grad(
-                matrix, offset, inputs_refs, incoming_ref, factor_refs
-            )
-        for place, (i, j) in enumerate(pair_list(count)):
-            sums_ref[pl.ds(place, 1), :] += jnp.sum(
-                grads_ref[i] * grads_ref[j], axis=0, keepdims=True
-            )
-
-    @pl.when(pl.program_id(0) == pl.num_programs(0) - 1)
-    def _():
-        total = sums_ref[:, pl.ds(0, 128)]
-        for lane in range(128, sums_ref.shape[1], 128):
-            total = total + sums_ref[:, pl.ds(lane, 128)]
-        gram_ref[...] = total
+    seg_rows, hidden_width = grads_ref.shape[2:]
+    for at, offset in enumerate(offsets):
+        inputs_ref, gate_ref, up_ref, first_ref, second_ref = operand_refs[5 * at : 5 * at + 5]
+        grads_ref[at, 0] = contract_first(inputs_ref[...], gate_ref[...])
+        grads_ref[at, 1] = contract_first(inputs_ref[...], up_ref[...])
+        grads_ref[at, 2] = contract_first(
+            flat_rows(incoming_ref[:middle, offset]), first_ref[...]
+        ) + contract_first(flat_rows(incoming_ref[middle:, offset]), second_ref[...])
+    gram_ref[...] = before_ref[...] if place else jnp.zeros_like(gram_ref)
+    known = list(range(place)) + list(offsets)
+    pairs = [(i, j) for i, j in pair_list(len(known)) if j >= place]
+    lines = 8
+
+    def add(step, sums):
+        rows = pl.ds(pl.multiple_of(lax.rem(step, seg_rows // lines) * lines, lines), lines)
+        matrix = lax.div(step, seg_rows // lines)
+        blocks = [earlier_ref[at, matrix, rows] for at in range(place)]
+        blocks += [grads_ref[at, matrix, rows] for at in range(len(offsets))]
+        return tuple(total + blocks[i] * blocks[j] for total, (i, j) in zip(sums, pairs))
+
+    zero = jnp.zeros((lines, hidden_width), jnp.float32)
+    sums = lax.fori_loop(0, 3 * (seg_rows // lines), add, tuple(zero for _ in pairs))
+    for total, (i, j) in zip(sums, pairs):
+        total = jnp.sum(total, axis=0, keepdims=True)
+        part = total[:, :128]
+        for lane in range(128, hidden_width, 128):
+            part = part + total[:, lane : lane + 128]
+        first, second = rep_ref[0] ^ known[i], rep_ref[0] ^ known[j]
+        row = jnp.minimum(first, second) * count + jnp.maximum(first, second)
+        gram_ref[pl.ds(row, 1), :] = part
 
 
 def merge_coefs(gram, count):
@@ -288,11 +287,10 @@
     return [vectors[0][rep] for rep in range(count)]
 
 
-def adam_kernel(count, rep_ref, *refs):
-    gram_refs, refs = refs[:count], refs[count:]
-    inputs_refs, incoming_ref = refs[:count], refs[count]
-    factor_refs = refs[count + 1 : 3 * count + 1]
-    first_ref, second_ref, step_ref, coef_ref = refs[3 * count + 1 :]
+def adam_kernel(count, places, rep_ref, *refs):
+    gram_refs, grads_refs = refs[:count], refs[count : count + len(places)]
+    first_ref, second_ref, step_ref, coef_ref = refs[count + len(places) :]
+    hidden_width = step_ref.shape[3]
 
     @pl.when(pl.program_id(0) == 0)
     def _():
@@ -300,35 +298,44 @@
         for gram_ref in gram_refs[1:]:
             sums = sums + gram_ref[...]
         sums = jnp.sum(sums, axis=1, keepdims=True)
-        gram = {pair: sums[place : place + 1] for place, pair in enumerate(pair_list(count))}
+        gram = {(i, j): sums[i * count + j : i * count + j + 1] for i, j in pair_list(count)}
         for rep, coef in enumerate(merge_coefs(gram, count)):
             coef_ref[rep] = jnp.broadcast_to(coef, coef_ref.shape[1:])
 
-    for matrix in range(3):
+    matrix = pl.program_id(0)
+    lines = 16
+
+    def step(index, _):
+        rows = pl.ds(pl.multiple_of(index * lines, lines), lines)
         merged = None
-        for offset in range(count):
-            part = weight_grad(matrix, offset, inputs_refs, incoming_ref, factor_refs)
-            part = part * coef_ref[rep_ref[0] ^ offset]
-            merged = part if merged is None else merged + part
-        first_new = beta_first * first_ref[0, matrix] + (1.0 - beta_first) * merged
-        second_new = beta_second * second_ref[0, matrix] + (1.0 - beta_second) * merged * merged
-        step_ref[0, matrix] = (first_new / first_fix) / (
-            jnp.sqrt(second_new / second_fix) + adam_eps
-        )
+        for grads_ref, offsets in zip(grads_refs, places):
+            for at, offset in enumerate(offsets):
+                part = grads_ref[at, matrix, rows] * coef_ref[rep_ref[0] ^ offset]
+                merged = part if merged is None else merged + part
+        first_new = (beta_first / first_fix) * first_ref[0, 0, rows] + (
+            (1.0 - beta_first) / first_fix
+        ) * merged
+        second_new = (beta_second / second_fix) * second_ref[0, 0, rows] + (
+            (1.0 - beta_second) / second_fix
+        ) * (merged * merged)
+        step_ref[0, 0, rows] = first_new / (jnp.sqrt(second_new) + adam_eps)
+        return 0
+
+    lax.fori_loop(0, step_ref.shape[2] // lines, step, 0)
 
 
 def adasum_adam_many(rep, inputs, incoming, factors, first_moment, second_moment):
     count = len(inputs)
     half = inputs[0].shape[0] // 2
     grads = []
-    for offset, (first, second) in enumerate(factors):
+    for offset, (gate_grad, up_grad, *halves) in enumerate(factors):
         received = incoming[:, offset].reshape(2 * half, incoming.shape[3])
-        hidden = jnp.concatenate([first[2 * half :], second[2 * half :]])
+        hidden = jnp.concatenate(halves)
         grads.append(
             jnp.stack(
                 [
-                    contract_first(inputs[offset], first[: 2 * half]),
-                    contract_first(inputs[offset], second[: 2 * half]),
+                    contract_first(inputs[offset], gate_grad),
+                    contract_first(inputs[offset], up_grad),
                     contract_first(received, hidden),
                 ]
             )
@@ -360,45 +367,37 @@
     count = len(inputs)
     if count > 4:
         return adasum_adam_many(rep, inputs, incoming, factors, first_moment, second_moment)
-    slot_count, seg_rows = inputs[0].shape
-    hidden_width = first_moment.shape[3]
-    expert_count, _, capacity, _ = incoming.shape
-    tile = min(seg_rows, 128)
-    grid = (seg_rows // tile,)
-    pairs = -(-len(pair_list(count)) // 8) * 8
-    flat = [array for pair in factors for array in pair]
-    operands = [*inputs, incoming, *flat]
-    specs = [
-        *[pl.BlockSpec((slot_count, tile), lambda d: (0, d)) for _ in inputs],
-        pl.BlockSpec((expert_count, count, capacity, tile), lambda d: (0, 0, 0, d)),
-        *[whole(array) for array in flat],
-    ]
-    flops = 6 * count * slot_count * seg_rows * hidden_width
-    (partial,) = call(
-        functools.partial(gram_kernel, count),
-        "gram",
-        [rep, *operands],
-        [SMEM, *specs],
-        [jax.ShapeDtypeStruct((pairs, 128), jnp.float32)],
-        grid=grid,
-        scratch=[
-            pltpu.VMEM((count, tile, hidden_width), jnp.float32),
-            pltpu.VMEM((pairs, hidden_width), jnp.float32),
-        ],
-        flops=flops,
-    )
-    grams = exchange([partial] * count)
-    moment_spec = pl.BlockSpec((1, 3, tile, hidden_width), lambda d: (0, 0, d, 0))
+    seg_rows, hidden_width = first_moment.shape[2:]
+    shape = jax.ShapeDtypeStruct
+    groups = [[k for k in range(count) if k < 3], [k for k in range(count) if k == 3]]
+    groups = [group for group in groups if group]
+    grads, gram, place = [], None, 0
+    for group in groups:
+        operands = [rep] if gram is None else [rep, gram, grads[0]]
+        operands += [incoming] + [x for k in group for x in (inputs[k], *factors[k])]
+        more, gram = call(
+            functools.partial(gram_kernel, count, group, place),
+            "gram_late" if place else "gram",
+            operands,
+            [SMEM] + [VMEM] * (len(operands) - 1),
+            [
+                shape((len(group), 3, seg_rows, hidden_width), jnp.float32),
+                shape((max(8, count * count), 128), jnp.float32),
+            ],
+        )
+        grads.append(more)
+        place += len(group)
+    grams = exchange([gram] * count)
+    moment_spec = pl.BlockSpec((1, 1, seg_rows, hidden_width), lambda m: (0, m, 0, 0))
     (adam_step,) = call(
-        functools.partial(adam_kernel, count),
+        functools.partial(adam_kernel, count, groups),
         "adam",
-        [rep, *grams, *operands, first_moment, second_moment],
-        [SMEM, *[whole(gram) for gram in grams], *specs, moment_spec, moment_spec],
-        [jax.ShapeDtypeStruct(first_moment.shape, jnp.float32)],
+        [rep, *grams, *grads, first_moment, second_moment],
+        [SMEM] + [VMEM] * (len(grams) + len(grads)) + [moment_spec, moment_spec],
+        [shape(first_moment.shape, jnp.float32)],
         out_specs=[moment_spec],
-        grid=grid,
+        grid=(3,),
         scratch=[pltpu.VMEM((count, 1, hidden_width), jnp.float32)],
-        flops=flops,
     )
     return adam_step
 
@@ -421,18 +420,10 @@
 
     block = shape((row_count + LABEL_ROWS, seg_rows), jnp.bfloat16)
     row_blocks = call(
-        rows_kernel,
+        functools.partial(rows_kernel, expert_count),
         "rows",
-        [
-            rep,
-            task_ids,
-            task_weights,
-            routes[0],
-            routes[0].reshape(1, row_count),
-            out_grads[0],
-        ],
-        [SMEM, SMEM, SMEM]
-        + [whole(x) for x in (routes[0], routes[0].reshape(1, row_count), out_grads[0])],
+        [rep, task_ids, task_weights, routes[0].reshape(1, row_count), out_grads[0]],
+        [SMEM, SMEM, SMEM, VMEM, VMEM],
         [block for _ in offsets],
     )
     routed = exchange(row_blocks)
@@ -446,7 +437,7 @@
             split_kernel,
             "split",
             [rep, inputs_home],
-            [SMEM, whole(inputs_home)],
+            [SMEM, VMEM],
             [shape((slot_count, seg_rows), jnp.bfloat16) for _ in offsets],
         )
     )
@@ -455,9 +446,8 @@
         functools.partial(place_kernel, row_count),
         "place",
         routed,
-        [whole(x) for x in routed],
+        [VMEM] * len(routed),
         [shape((expert_count, rep_count, capacity, seg_rows), jnp.bfloat16)],
-        flops=2 * rep_count * slot_count * row_count * seg_rows,
     )
     incoming = lax.all_to_all(outgoing, "expert", split_axis=0, concat_axis=0, tiled=True)
 
@@ -472,9 +462,8 @@
             functools.partial(forward_kernel, group, forward is not None),
             name,
             operands,
-            [SMEM] + [whole(x) for x in operands[1:]],
+            [SMEM] + [VMEM] * (len(operands) - 1),
             [shape((2, slot_count, hidden_width), jnp.float32)],
-            flops=4 * len(group) * slot_count * seg_rows * hidden_width,
         )
 
     back_shape = (slot_count, hidden_width)
@@ -482,41 +471,41 @@
         call(
             back_kernel,
             "back",
-            [incoming, weights],
-            [
-                whole(incoming),
-                pl.BlockSpec((1, 1, seg_rows, hidden_width), lambda i: (0, 2, 0, 0)),
-            ],
+            [incoming, weights[0, 2]],
+            [VMEM, VMEM],
             [shape(back_shape, jnp.bfloat16 if k else jnp.float32) for k in offsets],
-            flops=2 * rep_count * slot_count * seg_rows * hidden_width,
         )
     )
-    first, second = call(
+    half_shape = shape((half, hidden_width), jnp.bfloat16)
+    hidden = gather_pair(
+        *call(hidden_kernel, "hidden", [forward], [VMEM], [half_shape, half_shape])
+    )
+    forward, inputs = lax.optimization_barrier((forward, inputs))
+    full_shape = shape((slot_count, hidden_width), jnp.bfloat16)
+    gate_grad, up_grad = call(
         factor_kernel,
         "factors",
         [forward, *back],
-        [whole(x) for x in (forward, *back)],
-        [shape((slot_count + half, hidden_width), jnp.bfloat16)] * 2,
-    )
-    factors = gather_pair(first, second)
-
-    operands = [rep, first, second] + [array for pair in projections for array in pair]
+        [VMEM] * (1 + len(back)),
+        [full_shape, full_shape],
+    )
+    factors = [a + b for a, b in zip(gather_pair(gate_grad, up_grad), hidden)]
+
+    operands = [rep, gate_grad, up_grad] + [array for pair in projections for array in pair]
     (slot_grads,) = call(
         slot_kernel,
         "slots",
         operands,
-        [SMEM] + [whole(x) for x in operands[1:]],
+        [SMEM] + [VMEM] * (len(operands) - 1),
         [shape((expert_count, capacity, model_width), jnp.bfloat16)],
-        flops=4 * slot_count * model_width * hidden_width,
     )
     returned = lax.all_to_all(slot_grads, "expert", split_axis=0, concat_axis=0, tiled=True)
     (input_grads,) = call(
         unplace_kernel,
         "unplace",
         [routed[0], returned],
-        [whole(routed[0]), whole(returned)],
+        [VMEM, VMEM],
         [shape((1, row_count, model_width), jnp.bfloat16)],
-        flops=2 * slot_count * row_count * model_width,
     )
 
     adam_step = adasum_adam(rep, inputs, incoming, factors, first_moment, second_moment)

time: 161 us -> 154 us (0.957)
  Pallas kernels: 44.9 us -> 27.2 us
  local copies, waits for them, and re-layouts: 9.1 us -> 14 us
  starting transfers between devices: 36.2 us -> 41 us
    pallas_call x11 -> x13, Pallas kernels: 44.9 us -> 27.2 us  [call(): pl.pallas_call(kernel, grid=grid, in_specs=specs, out_specs=out_specs if...]
    ppermute x24 -> x30, waiting for transfers between devices: 60.1 us -> 66.5 us  [from_peer(): lax.ppermute(array, 'replica', [(i, i ^ offset) for i in range(count)])]
    all_to_all x1, waiting for transfers between devices: 8.35 us -> 3.02 us  [shards(): lax.all_to_all(outgoing, 'expert', split_axis=0, concat_axis=0, tiled=True)]
    unnamed x52 -> x48, local copies, waits for them, and re-layouts: 6.46 us -> 11.8 us
    ppermute x24 -> x30, starting transfers between devices: 26.5 us -> 31.8 us  [from_peer(): lax.ppermute(array, 'replica', [(i, i ^ offset) for i in range(count)])]
  transfers between devices with their start and end apart: 26 -> 32, of which waited for: 14 -> 14; matrix products, arithmetic and copies ran while one was open for 1% -> 1% of each run, Pallas kernels for 19% -> 13%
where the time goes in v3:
time: 154 us; the launch traced here: 153 us
  waiting for transfers between devices  69.5 us (45%)
  starting transfers between devices  41 us (27%)
  Pallas kernels  27.2 us (18%)
  local copies, waits for them, and re-layouts  14 us (9%)
    ppermute x30, waiting for transfers between devices, from_peer(): lax.ppermute(array, 'replica', [(i, i ^ offset) for i in range(count)])  66.5 us
    ppermute x30, starting transfers between devices, from_peer(): lax.ppermute(array, 'replica', [(i, i ^ offset) for i in range(count)])  31.8 us
    pallas_call x13, Pallas kernels, call(): pl.pallas_call(kernel, grid=grid, in_specs=specs, out_specs=out_specs if...  27.2 us
    unnamed x48, local copies, waits for them, and re-layouts  11.8 us
    all_to_all x1, starting transfers between devices, shards(): lax.all_to_all(outgoing, 'expert', split_axis=0, concat_axis=0, tiled=True)  4.87 us
    all_to_all x1, starting transfers between devices, shards(): lax.all_to_all(slot_grads, 'expert', split_axis=0, concat_axis=0, tiled=T...  4.33 us
  transfers between devices with their start and end apart: 32, of which 14 were waited for; matrix products, arithmetic and copies ran while one was open for 1% of the time, Pallas kernels for 13%

profile of v3, /device:TPU:0, one launch (start us, length us, event | category | flops | bytes accessed | tf_op | source)
XLA Modules:
  0.0 153.2 jit_solution(1406121091813638399)
XLA Ops:
  1.3 1.0 copy-done.11
  2.3 0.7 copy-done.20
  3.0 0.7 copy-done.21
  3.6 0.7 rows.1
  4.3 3.0 %collective-permute-start.9 = (bf16[144,512]{1,0:T(8,128)(2,1)S(1)}, bf16[144,512]{1,0:T(8,128)(2,1)S(1)}, u32[]{:S(2)}, u32[]{:S(2)}) collective-permute-start(bf16[144,512]{1,0:T(8,128)(2,1)S(1)} %get-tuple-element.33), channel_id=1, source_target_pairs={{0,1},{1,0},{2,3},{3,2},{4,5},{5,4},{6,7},{7,6},{8,9},{9,8},{10,11... | collective-permute-start | bytes 442376 | tf_op jit(solution)/shard_map/ppermute | solution.py:38
  7.3 1.5 collective-permute-start.10
  8.9 2.8 %collective-permute-done.9.refs_1_ = bf16[144,512]{1,0:T(8,128)(2,1)S(1)} collective-permute-done((bf16[144,512]{1,0:T(8,128)(2,1)S(1)}, bf16[144,512]{1,0:T(8,128)(2,1)S(1)}, u32[]{:S(2)}, u32[]{:S(2)}) %collective-permute-start.9) | collective-permute-done | bytes 147488 | tf_op jit(solution)/shard_map/ppermute | solution.py:38
  11.6 4.2 %collective-permute-done.10.refs_2_ = bf16[144,512]{1,0:T(8,128)(2,1)S(1)} collective-permute-done((bf16[144,512]{1,0:T(8,128)(2,1)S(1)}, bf16[144,512]{1,0:T(8,128)(2,1)S(1)}, u32[]{:S(2)}, u32[]{:S(2)}) %collective-permute-start.10) | collective-permute-done | bytes 147488 | tf_op jit(solution)/shard_map/ppermute | solution.py:38
  15.8 1.4 place.1
  17.2 4.9 %all-to-all-start = ((bf16[8,4,32,512]{3,2,1,0:T(8,128)(2,1)}), bf16[8,4,32,512]{3,2,1,0:T(8,128)(2,1)S(1)}, u32[]{:S(2)}, u32[]{:S(2)}) async-start(bf16[8,4,32,512]{3,2,1,0:T(8,128)(2,1)} %place.1), calls=%async_computation | async-start | bytes 2097152 | tf_op jit(solution)/shard_map/all_to_all | solution.py:452
  22.1 2.3 %slice_bitcast_fusion = (bf16[512,512]{1,0:T(8,128)(2,1)}, bf16[512,512]{1,0:T(8,128)(2,1)S(1)}, bf16[512,512]{1,0:T(8,128)(2,1)S(1)}) fusion(bf16[1,3,512,512]{3,2,1,0:T(8,128)(2,1)} %param.8), kind=kLoop, calls=%fused_computation | loop fusion | bytes 3145728 | tf_op jit(solution)/shard_map/squeeze | solution.py:474
  24.3 1.5 collective-permute-start.2
  25.9 0.5 collective-permute-start.1
  26.4 1.5 collective-permute-start
  28.4 10.8 %collective-permute-done.2.refs_4_ = bf16[512,512]{1,0:T(8,128)(2,1)} collective-permute-done((bf16[512,512]{1,0:T(8,128)(2,1)S(1)}, bf16[512,512]{1,0:T(8,128)(2,1)}, u32[]{:S(2)}, u32[]{:S(2)}) %collective-permute-start.2) | collective-permute-done | bytes 524320 | tf_op jit(solution)/shard_map/ppermute | solution.py:38
  39.2 1.2 collective-permute-start.4
  41.2 0.8 split.1
  42.0 0.7 copy-done.14
  42.7 0.7 copy-done.22
  43.5 0.7 copy-done.23
  44.2 1.5 collective-permute-start.6
  45.7 3.0 %all-to-all-done.incoming_ref.refs_0_.refs_2_ = bf16[8,4,32,512]{3,2,1,0:T(8,128)(2,1)S(1)} async-done(((bf16[8,4,32,512]{3,2,1,0:T(8,128)(2,1)}), bf16[8,4,32,512]{3,2,1,0:T(8,128)(2,1)S(1)}, u32[]{:S(2)}, u32[]{:S(2)}) %all-to-all-start) | async-done | bytes 1048608 | tf_op jit(solution)/shard_map/all_to_all | solution.py:452
  48.7 1.0 copy-done.8
  49.7 0.7 back.1
  50.4 17.6 %collective-permute-done.6.refs_6_ = bf16[256,512]{1,0:T(8,128)(2,1)S(1)} collective-permute-done((bf16[256,512]{1,0:T(8,128)(2,1)}, bf16[256,512]{1,0:T(8,128)(2,1)S(1)}, u32[]{:S(2)}, u32[]{:S(2)}) %collective-permute-start.6) | collective-permute-done | bytes 262176 | tf_op jit(solution)/shard_map/ppermute | solution.py:38
  68.0 0.7 copy-done.16
  68.7 0.5 collective-permute-start.7
  69.2 1.5 collective-permute-start.8
  70.7 1.5 collective-permute-start.12
  72.2 0.5 collective-permute-start.13
  72.7 1.5 collective-permute-start.14
  74.2 2.5 %forward.1.refs_0_ = f32[2,256,512]{2,1,0:T(8,128)S(1)} custom-call(s32[1]{0:T(128)} %bitcast.rep_ref, bf16[256,2048]{1,0:T(8,128)(2,1)S(1)} %bitcast.11, bf16[512,512]{1,0:T(8,128)(2,1)S(1)} %get-tuple-element.53.refs_0_, bf16[512,512]{1,0:T(8,128)(2,1)S(1)} %get-tuple-element.54.refs_1_, bf16[512,512]{1,0:T(8,128)(2,1)} %collective-permute-done.refs_2_, ...), custom_call_target="tpu_custom_call" | custom-call | tf_op jit(solution)/shard_map/forward/pallas_call | solution.py:73
  76.7 1.7 %rest.1.forward_ref = f32[2,256,512]{2,1,0:T(8,128)S(1)} custom-call(s32[1]{0:T(128)} %bitcast.rep_ref, bf16[256,2048]{1,0:T(8,128)(2,1)S(1)} %bitcast.12, f32[2,256,512]{2,1,0:T(8,128)S(1)} %forward.1.refs_0_, bf16[512,512]{1,0:T(8,128)(2,1)} %collective-permute-done.4.refs_1_.refs_6_, bf16[512,512]{1,0:T(8,128)(2,1)} %collective-permute-done.5.refs_2_.refs_7_), custom_call_target="tpu_custom_call" | custom-call | tf_op jit(solution)/shard_map/rest/pallas_call | solution.py:73
  78.5 10.6 %collective-permute-done.7.refs_11_ = bf16[256,512]{1,0:T(8,128)(2,1)S(1)} collective-permute-done((bf16[256,512]{1,0:T(8,128)(2,1)}, bf16[256,512]{1,0:T(8,128)(2,1)S(1)}, u32[]{:S(2)}, u32[]{:S(2)}) %collective-permute-start.7) | collective-permute-done | bytes 262176 | tf_op jit(solution)/shard_map/ppermute | solution.py:38
  89.1 4.3 %collective-permute-done.13.refs_2_ = bf16[256,512]{1,0:T(8,128)(2,1)S(1)} collective-permute-done((bf16[256,512]{1,0:T(8,128)(2,1)S(1)}, bf16[256,512]{1,0:T(8,128)(2,1)S(1)}, u32[]{:S(2)}, u32[]{:S(2)}) %collective-permute-start.13) | collective-permute-done | bytes 262176 | tf_op jit(solution)/shard_map/ppermute | solution.py:38
  93.8 3.1 %slots.1 = bf16[8,32,2048]{2,1,0:T(8,128)(2,1)S(1)} custom-call(s32[1]{0:T(128)} %bitcast.rep_ref, bf16[256,512]{1,0:T(8,128)(2,1)S(1)} %get-tuple-element.40.first_ref.refs_2_, bf16[256,512]{1,0:T(8,128)(2,1)S(1)} %get-tuple-element.41.second_ref.refs_3_, bf16[512,512]{1,0:T(8,128)(2,1)S(1)} %copy-done.2, bf16[512,512]{1,0:T(8,128)(2,1)S(1)} %copy-done.4, ...), custom_call_target="tpu_custom_call" | custom-call | tf_op jit(solution)/shard_map/slots/pallas_call | solution.py:73
  96.9 1.0 copy-done.5
  98.0 0.7 copy-done.9
  98.7 4.3 %all-to-all-start.1 = ((bf16[8,32,2048]{2,1,0:T(8,128)(2,1)}), bf16[8,32,2048]{2,1,0:T(8,128)(2,1)S(1)}, u32[]{:S(2)}, u32[]{:S(2)}) async-start(bf16[8,32,2048]{2,1,0:T(8,128)(2,1)} %copy-done.5), calls=%async_computation.1 | async-start | bytes 2097152 | tf_op jit(solution)/shard_map/all_to_all | solution.py:502
  103.1 0.6 collective-permute-start.21
  103.7 1.5 collective-permute-start.19
  105.2 0.5 collective-permute-start.16
  105.7 1.5 collective-permute-start.17
  107.7 1.7 %collective-permute-done.21.refs_14_ = bf16[128,512]{1,0:T(8,128)(2,1)S(1)} collective-permute-done((bf16[128,512]{1,0:T(8,128)(2,1)S(1)}, bf16[128,512]{1,0:T(8,128)(2,1)S(1)}, u32[]{:S(2)}, u32[]{:S(2)}) %collective-permute-start.21) | collective-permute-done | bytes 131104 | tf_op jit(solution)/shard_map/ppermute | solution.py:38
  109.5 0.5 collective-permute-start.15
  110.0 7.4 %collective-permute-done.17.refs_9_ = bf16[128,512]{1,0:T(8,128)(2,1)S(1)} collective-permute-done((bf16[128,512]{1,0:T(8,128)(2,1)S(1)}, bf16[128,512]{1,0:T(8,128)(2,1)S(1)}, u32[]{:S(2)}, u32[]{:S(2)}) %collective-permute-start.17) | collective-permute-done | bytes 131104 | tf_op jit(solution)/shard_map/ppermute | solution.py:38
  117.9 1.2 collective-permute-start.18
  119.1 0.8 collective-permute-start.23
  119.9 1.5 collective-permute-start.24
  121.5 4.4 %collective-permute-done.18.refs_10_ = bf16[128,512]{1,0:T(8,128)(2,1)S(1)} collective-permute-done((bf16[128,512]{1,0:T(8,128)(2,1)S(1)}, bf16[128,512]{1,0:T(8,128)(2,1)S(1)}, u32[]{:S(2)}, u32[]{:S(2)}) %collective-permute-start.18) | collective-permute-done | bytes 131104 | tf_op jit(solution)/shard_map/ppermute | solution.py:38
  125.8 0.5 collective-permute-start.25
  126.4 1.2 collective-permute-start.26
  127.5 0.9 copy-done.10
  128.5 0.9 copy-done.15
  129.4 0.9 copy-done.17
  130.4 0.9 copy-done.19
  131.3 5.7 %gram.1 = (f32[3,3,512,512]{3,2,1,0:T(8,128)S(1)}, f32[16,128]{1,0:T(8,128)S(1)}) custom-call(s32[1]{0:T(128)} %bitcast.rep_ref, bf16[8,4,32,512]{3,2,1,0:T(8,128)(2,1)S(1)} %all-to-all-done.incoming_ref.refs_0_.refs_2_, bf16[256,512]{1,0:T(8,128)(2,1)S(1)} %copy-done.15, bf16[256,512]{1,0:T(8,128)(2,1)S(1)} %get-tuple-element.40.first_ref.refs_2_, ...), custom_call_target="tpu_custom_call" | custom-call | tf_op jit(solution)/shard_map/gram/pallas_call | solution.py:73
  137.1 3.8 %gram_late.1 = (f32[1,3,512,512]{3,2,1,0:T(8,128)S(1)}, f32[16,128]{1,0:T(8,128)S(1)}) custom-call(s32[1]{0:T(128)} %bitcast.rep_ref, f32[16,128]{1,0:T(8,128)S(1)} %get-tuple-element.47.refs_0_, f32[3,3,512,512]{3,2,1,0:T(8,128)S(1)} %get-tuple-element.48.refs_1_.refs_4_, bf16[8,4,32,512]{3,2,1,0:T(8,128)(2,1)S(1)} %all-to-all-done.incoming_ref.refs_0_.refs_2_, ...), custom_call_target="tpu_custom_call" | custom-call | tf_op jit(solution)/shard_map/gram_late/pallas_call | solution.py:73
  140.9 1.8 %collective-permute-start.29 = (f32[16,128]{1,0:T(8,128)S(1)}, f32[16,128]{1,0:T(8,128)S(1)}, u32[]{:S(2)}, u32[]{:S(2)}) collective-permute-start(f32[16,128]{1,0:T(8,128)S(1)} %get-tuple-element.50.refs_0_), channel_id=1, source_target_pairs={{0,3},{1,2},{2,1},{3,0},{4,7},{5,6},{6,5},{7,4},{8,11},{9,10},{10,... | collective-permute-start | bytes 24584 | tf_op jit(solution)/shard_map/ppermute | solution.py:38
  143.3 1.2 collective-permute-start.27
  144.5 1.1 collective-permute-done.29.refs_3_
  145.5 0.9 collective-permute-done.28.refs_2_
  146.9 5.2 %adam.1 = f32[1,3,512,512]{3,2,1,0:T(8,128)} custom-call(s32[1]{0:T(128)} %bitcast.rep_ref, f32[16,128]{1,0:T(8,128)S(1)} %get-tuple-element.50.refs_0_, f32[16,128]{1,0:T(8,128)S(1)} %collective-permute-done.27.refs_1_, f32[16,128]{1,0:T(8,128)S(1)} %collective-permute-done.28.refs_2_, f32[16,128]{1,0:T(8,128)S(1)} %collective-permute-done.29.refs_3_, ...), custom_call_target="tpu_custom_call" | custom-call | tf_op jit(solution)/shard_map/adam/pallas_call | solution.py:73
  152.1 1.1 unplace.1
  (62 shorter events, 3.9 us)
Async XLA Ops:
  1.3 1.0 copy-start.11
  2.3 0.7 copy-start.20
  3.0 0.7 copy-start.21
  4.3 7.3 %collective-permute-start.9 = (bf16[144,512]{1,0:T(8,128)(2,1)S(1)}, bf16[144,512]{1,0:T(8,128)(2,1)S(1)}, u32[]{:S(2)}, u32[]{:S(2)}) collective-permute-start(bf16[144,512]{1,0:T(8,128)(2,1)S(1)} %get-tuple-element.33), channel_id=1, source_target_pairs={{0,1},{1,0},{2,3},{3,2},{4,5},{5,4},{6,7},{7,6},{8,9},{9,8},{10,11... | collective-permute-start | bytes 442376 | tf_op jit(solution)/shard_map/ppermute | solution.py:38
  7.3 8.5 %collective-permute-start.10 = (bf16[144,512]{1,0:T(8,128)(2,1)S(1)}, bf16[144,512]{1,0:T(8,128)(2,1)S(1)}, u32[]{:S(2)}, u32[]{:S(2)}) collective-permute-start(bf16[144,512]{1,0:T(8,128)(2,1)S(1)} %get-tuple-element.34), channel_id=1, source_target_pairs={{0,2},{1,3},{2,0},{3,1},{4,6},{5,7},{6,4},{7,5},{8,10},{9,11},{10,... | collective-permute-start | bytes 442376 | tf_op jit(solution)/shard_map/ppermute | solution.py:38
  8.9 7.0 %collective-permute-start.11 = (bf16[144,512]{1,0:T(8,128)(2,1)S(1)}, bf16[144,512]{1,0:T(8,128)(2,1)S(1)}, u32[]{:S(2)}, u32[]{:S(2)}) collective-permute-start(bf16[144,512]{1,0:T(8,128)(2,1)S(1)} %get-tuple-element.35), channel_id=1, source_target_pairs={{0,3},{1,2},{2,1},{3,0},{4,7},{5,6},{6,5},{7,4},{8,11},{9,10},{10,... | collective-permute-start | bytes 442376 | tf_op jit(solution)/shard_map/ppermute | solution.py:38
  15.8 25.4 %copy-start = (bf16[1,1,256,2048]{3,2,1,0:T(8,128)(2,1)S(1)}, bf16[1,1,256,2048]{3,2,1,0:T(8,128)(2,1)}, u32[]{:S(2)}) copy-start(bf16[1,1,256,2048]{3,2,1,0:T(8,128)(2,1)} %param.15) | copy-start | bytes 3145732
  17.2 31.5 %all-to-all-start = ((bf16[8,4,32,512]{3,2,1,0:T(8,128)(2,1)}), bf16[8,4,32,512]{3,2,1,0:T(8,128)(2,1)S(1)}, u32[]{:S(2)}, u32[]{:S(2)}) async-start(bf16[8,4,32,512]{3,2,1,0:T(8,128)(2,1)} %place.1), calls=%async_computation | async-start | bytes 2097152 | tf_op jit(solution)/shard_map/all_to_all | solution.py:452
  24.3 49.9 %copy-start.1 = (bf16[512,512]{1,0:T(8,128)(2,1)}, bf16[512,512]{1,0:T(8,128)(2,1)S(1)}, u32[]{:S(2)}) copy-start(bf16[512,512]{1,0:T(8,128)(2,1)S(1)} %get-tuple-element.53.refs_0_) | copy-start | bytes 1572868
  24.3 49.9 %copy-start.3 = (bf16[512,512]{1,0:T(8,128)(2,1)}, bf16[512,512]{1,0:T(8,128)(2,1)S(1)}, u32[]{:S(2)}) copy-start(bf16[512,512]{1,0:T(8,128)(2,1)S(1)} %get-tuple-element.54.refs_1_) | copy-start | bytes 1572868
  24.3 14.8 %collective-permute-start.2 = (bf16[512,512]{1,0:T(8,128)(2,1)S(1)}, bf16[512,512]{1,0:T(8,128)(2,1)}, u32[]{:S(2)}, u32[]{:S(2)}) collective-permute-start(bf16[512,512]{1,0:T(8,128)(2,1)S(1)} %get-tuple-element.53.refs_0_), channel_id=1, source_target_pairs={{0,2},{1,3},{2,0},{3,1},{4,6},{5,7},{6,4},{7,5},{8,10},{9,11},{10,... | collective-permute-start | bytes 1572872 | tf_op jit(solution)/shard_map/ppermute | solution.py:38
  25.9 14.9 %collective-permute-start.1 = (bf16[512,512]{1,0:T(8,128)(2,1)S(1)}, bf16[512,512]{1,0:T(8,128)(2,1)}, u32[]{:S(2)}, u32[]{:S(2)}) collective-permute-start(bf16[512,512]{1,0:T(8,128)(2,1)S(1)} %get-tuple-element.54.refs_1_), channel_id=1, source_target_pairs={{0,1},{1,0},{2,3},{3,2},{4,5},{5,4},{6,7},{7,6},{8,9},{9,8},{10,11... | collective-permute-start | bytes 1572872 | tf_op jit(solution)/shard_map/ppermute | solution.py:38
  26.4 42.8 %collective-permute-start = (bf16[512,512]{1,0:T(8,128)(2,1)S(1)}, bf16[512,512]{1,0:T(8,128)(2,1)}, u32[]{:S(2)}, u32[]{:S(2)}) collective-permute-start(bf16[512,512]{1,0:T(8,128)(2,1)S(1)} %get-tuple-element.53.refs_0_), channel_id=1, source_target_pairs={{0,1},{1,0},{2,3},{3,2},{4,5},{5,4},{6,7},{7,6},{8,9},{9,8},{10,11... | collective-permute-start | bytes 1572872 | tf_op jit(solution)/shard_map/ppermute | solution.py:38
  27.9 42.8 %collective-permute-start.3 = (bf16[512,512]{1,0:T(8,128)(2,1)S(1)}, bf16[512,512]{1,0:T(8,128)(2,1)}, u32[]{:S(2)}, u32[]{:S(2)}) collective-permute-start(bf16[512,512]{1,0:T(8,128)(2,1)S(1)} %get-tuple-element.54.refs_1_), channel_id=1, source_target_pairs={{0,2},{1,3},{2,0},{3,1},{4,6},{5,7},{6,4},{7,5},{8,10},{9,11},{10,... | collective-permute-start | bytes 1572872 | tf_op jit(solution)/shard_map/ppermute | solution.py:38
  39.2 33.0 %collective-permute-start.4 = (bf16[512,512]{1,0:T(8,128)(2,1)}, bf16[512,512]{1,0:T(8,128)(2,1)}, u32[]{:S(2)}, u32[]{:S(2)}) collective-permute-start(bf16[512,512]{1,0:T(8,128)(2,1)} %collective-permute-done.2.refs_4_), channel_id=1, source_target_pairs={{0,1},{1,0},{2,3},{3,2},{4,5},{5,4},{6,7},{7,6},{8,9},{9,8},{10,11... | collective-permute-start | bytes 1572872 | tf_op jit(solution)/shard_map/ppermute | solution.py:38
  40.7 32.0 %collective-permute-start.5 = (bf16[512,512]{1,0:T(8,128)(2,1)}, bf16[512,512]{1,0:T(8,128)(2,1)}, u32[]{:S(2)}, u32[]{:S(2)}) collective-permute-start(bf16[512,512]{1,0:T(8,128)(2,1)} %collective-permute-done.1.refs_3_), channel_id=1, source_target_pairs={{0,2},{1,3},{2,0},{3,1},{4,6},{5,7},{6,4},{7,5},{8,10},{9,11},{10,... | collective-permute-start | bytes 1572872 | tf_op jit(solution)/shard_map/ppermute | solution.py:38
  42.0 0.7 copy-start.14
  42.7 0.7 copy-start.22
  43.5 0.7 copy-start.23
  44.2 23.8 %collective-permute-start.6 = (bf16[256,512]{1,0:T(8,128)(2,1)}, bf16[256,512]{1,0:T(8,128)(2,1)S(1)}, u32[]{:S(2)}, u32[]{:S(2)}) collective-permute-start(bf16[256,512]{1,0:T(8,128)(2,1)} %get-tuple-element.29), channel_id=1, source_target_pairs={{0,1},{1,0},{2,3},{3,2},{4,5},{5,4},{6,7},{7,6},{8,9},{9,8},{10,11... | collective-permute-start | bytes 786440 | tf_op jit(solution)/shard_map/ppermute | solution.py:38
  48.7 1.0 copy-start.8
  68.0 0.7 copy-start.16
  68.7 20.3 %collective-permute-start.7 = (bf16[256,512]{1,0:T(8,128)(2,1)}, bf16[256,512]{1,0:T(8,128)(2,1)S(1)}, u32[]{:S(2)}, u32[]{:S(2)}) collective-permute-start(bf16[256,512]{1,0:T(8,128)(2,1)} %copy-done.23), channel_id=1, source_target_pairs={{0,2},{1,3},{2,0},{3,1},{4,6},{5,7},{6,4},{7,5},{8,10},{9,11},{10,... | collective-permute-start | bytes 786440 | tf_op jit(solution)/shard_map/ppermute | solution.py:38
  69.2 19.8 %collective-permute-start.8 = (bf16[256,512]{1,0:T(8,128)(2,1)}, bf16[256,512]{1,0:T(8,128)(2,1)S(1)}, u32[]{:S(2)}, u32[]{:S(2)}) collective-permute-start(bf16[256,512]{1,0:T(8,128)(2,1)} %copy-done.22), channel_id=1, source_target_pairs={{0,3},{1,2},{2,1},{3,0},{4,7},{5,6},{6,5},{7,4},{8,11},{9,10},{10,... | collective-permute-start | bytes 786440 | tf_op jit(solution)/shard_map/ppermute | solution.py:38
  70.7 18.4 %collective-permute-start.12 = (bf16[256,512]{1,0:T(8,128)(2,1)S(1)}, bf16[256,512]{1,0:T(8,128)(2,1)S(1)}, u32[]{:S(2)}, u32[]{:S(2)}) collective-permute-start(bf16[256,512]{1,0:T(8,128)(2,1)S(1)} %get-tuple-element.37), channel_id=1, source_target_pairs={{0,1},{1,0},{2,3},{3,2},{4,5},{5,4},{6,7},{7,6},{8,9},{9,8},{10,11... | collective-permute-start | bytes 786440 | tf_op jit(solution)/shard_map/ppermute | solution.py:38
  72.2 21.2 %collective-permute-start.13 = (bf16[256,512]{1,0:T(8,128)(2,1)S(1)}, bf16[256,512]{1,0:T(8,128)(2,1)S(1)}, u32[]{:S(2)}, u32[]{:S(2)}) collective-permute-start(bf16[256,512]{1,0:T(8,128)(2,1)S(1)} %get-tuple-element.38), channel_id=1, source_target_pairs={{0,2},{1,3},{2,0},{3,1},{4,6},{5,7},{6,4},{7,5},{8,10},{9,11},{10,... | collective-permute-start | bytes 786440 | tf_op jit(solution)/shard_map/ppermute | solution.py:38
  72.7 20.7 %collective-permute-start.14 = (bf16[256,512]{1,0:T(8,128)(2,1)S(1)}, bf16[256,512]{1,0:T(8,128)(2,1)S(1)}, u32[]{:S(2)}, u32[]{:S(2)}) collective-permute-start(bf16[256,512]{1,0:T(8,128)(2,1)S(1)} %get-tuple-element.39), channel_id=1, source_target_pairs={{0,3},{1,2},{2,1},{3,0},{4,7},{5,6},{6,5},{7,4},{8,11},{9,10},{10,... | collective-permute-start | bytes 786440 | tf_op jit(solution)/shard_map/ppermute | solution.py:38
  76.7 17.1 %copy-start.2 = (bf16[512,512]{1,0:T(8,128)(2,1)S(1)}, bf16[512,512]{1,0:T(8,128)(2,1)}, u32[]{:S(2)}) copy-start(bf16[512,512]{1,0:T(8,128)(2,1)} %copy-done.1) | copy-start | bytes 1572868
  76.7 17.1 %copy-start.4 = (bf16[512,512]{1,0:T(8,128)(2,1)S(1)}, bf16[512,512]{1,0:T(8,128)(2,1)}, u32[]{:S(2)}) copy-start(bf16[512,512]{1,0:T(8,128)(2,1)} %copy-done.3) | copy-start | bytes 1572868
  89.1 4.7 %copy-start.18 = (bf16[256,512]{1,0:T(8,128)(2,1)}, bf16[256,512]{1,0:T(8,128)(2,1)S(1)}, u32[]{:S(2)}) copy-start(bf16[256,512]{1,0:T(8,128)(2,1)S(1)} %collective-permute-done.7.refs_11_) | copy-start | bytes 786436
  89.1 4.7 %copy-start.12 = (bf16[256,512]{1,0:T(8,128)(2,1)}, bf16[256,512]{1,0:T(8,128)(2,1)S(1)}, u32[]{:S(2)}) copy-start(bf16[256,512]{1,0:T(8,128)(2,1)S(1)} %collective-permute-done.8.refs_3_) | copy-start | bytes 786436
  96.9 1.0 copy-start.5
  98.0 0.7 copy-start.9
  98.7 53.4 %all-to-all-start.1 = ((bf16[8,32,2048]{2,1,0:T(8,128)(2,1)}), bf16[8,32,2048]{2,1,0:T(8,128)(2,1)S(1)}, u32[]{:S(2)}, u32[]{:S(2)}) async-start(bf16[8,32,2048]{2,1,0:T(8,128)(2,1)} %copy-done.5), calls=%async_computation.1 | async-start | bytes 2097152 | tf_op jit(solution)/shard_map/all_to_all | solution.py:502
  103.0 34.1 %copy-start.13 = (bf16[256,512]{1,0:T(8,128)(2,1)S(1)}, bf16[256,512]{1,0:T(8,128)(2,1)}, u32[]{:S(2)}) copy-start(bf16[256,512]{1,0:T(8,128)(2,1)} %copy-done.12) | copy-start | bytes 786436
  103.1 6.4 %collective-permute-start.21 = (bf16[128,512]{1,0:T(8,128)(2,1)S(1)}, bf16[128,512]{1,0:T(8,128)(2,1)S(1)}, u32[]{:S(2)}, u32[]{:S(2)}) collective-permute-start(bf16[128,512]{1,0:T(8,128)(2,1)S(1)} %get-tuple-element.43.refs_4_), channel_id=1, source_target_pairs={{0,2},{1,3},{2,0},{3,1},{4,6},{5,7},{6,4},{7,5},{8,10},{9,11},{10,... | collective-permute-start | bytes 393224 | tf_op jit(solution)/shard_map/ppermute | solution.py:38
  103.7 15.4 %collective-permute-start.19 = (bf16[256,512]{1,0:T(8,128)(2,1)S(1)}, bf16[256,512]{1,0:T(8,128)(2,1)S(1)}, u32[]{:S(2)}, u32[]{:S(2)}) collective-permute-start(bf16[256,512]{1,0:T(8,128)(2,1)S(1)} %get-tuple-element.40.first_ref.refs_2_), channel_id=1, source_target_pairs={{0,2},{1,3},{2,0},{3,1},{4,6},{5,7},{6,4},{7,5},{8,10},{9,11},{10,... | collective-permute-start | bytes 786440 | tf_op jit(solution)/shard_map/ppermute | solution.py:38
  105.2 14.7 %collective-permute-start.16 = (bf16[256,512]{1,0:T(8,128)(2,1)}, bf16[256,512]{1,0:T(8,128)(2,1)S(1)}, u32[]{:S(2)}, u32[]{:S(2)}) collective-permute-start(bf16[256,512]{1,0:T(8,128)(2,1)} %copy-done.9), channel_id=1, source_target_pairs={{0,1},{1,0},{2,3},{3,2},{4,5},{5,4},{6,7},{7,6},{8,9},{9,8},{10,11... | collective-permute-start | bytes 786440 | tf_op jit(solution)/shard_map/ppermute | solution.py:38
  105.7 11.7 %collective-permute-start.17 = (bf16[128,512]{1,0:T(8,128)(2,1)S(1)}, bf16[128,512]{1,0:T(8,128)(2,1)S(1)}, u32[]{:S(2)}, u32[]{:S(2)}) collective-permute-start(bf16[128,512]{1,0:T(8,128)(2,1)S(1)} %get-tuple-element.43.refs_4_), channel_id=1, source_target_pairs={{0,1},{1,0},{2,3},{3,2},{4,5},{5,4},{6,7},{7,6},{8,9},{9,8},{10,11... | collective-permute-start | bytes 393224 | tf_op jit(solution)/shard_map/ppermute | solution.py:38
  107.2 10.7 %collective-permute-start.22 = (bf16[128,512]{1,0:T(8,128)(2,1)S(1)}, bf16[128,512]{1,0:T(8,128)(2,1)S(1)}, u32[]{:S(2)}, u32[]{:S(2)}) collective-permute-start(bf16[128,512]{1,0:T(8,128)(2,1)S(1)} %get-tuple-element.44.refs_5_), channel_id=1, source_target_pairs={{0,2},{1,3},{2,0},{3,1},{4,6},{5,7},{6,4},{7,5},{8,10},{9,11},{10,... | collective-permute-start | bytes 393224 | tf_op jit(solution)/shard_map/ppermute | solution.py:38
  109.5 16.9 %collective-permute-start.15 = (bf16[256,512]{1,0:T(8,128)(2,1)S(1)}, bf16[256,512]{1,0:T(8,128)(2,1)S(1)}, u32[]{:S(2)}, u32[]{:S(2)}) collective-permute-start(bf16[256,512]{1,0:T(8,128)(2,1)S(1)} %get-tuple-element.40.first_ref.refs_2_), channel_id=1, source_target_pairs={{0,1},{1,0},{2,3},{3,2},{4,5},{5,4},{6,7},{7,6},{8,9},{9,8},{10,11... | collective-permute-start | bytes 786440 | tf_op jit(solution)/shard_map/ppermute | solution.py:38
  117.4 10.1 %collective-permute-start.20 = (bf16[256,512]{1,0:T(8,128)(2,1)}, bf16[256,512]{1,0:T(8,128)(2,1)S(1)}, u32[]{:S(2)}, u32[]{:S(2)}) collective-permute-start(bf16[256,512]{1,0:T(8,128)(2,1)} %copy-done.9), channel_id=1, source_target_pairs={{0,2},{1,3},{2,0},{3,1},{4,6},{5,7},{6,4},{7,5},{8,10},{9,11},{10,... | collective-permute-start | bytes 786440 | tf_op jit(solution)/shard_map/ppermute | solution.py:38
  117.9 7.9 %collective-permute-start.18 = (bf16[128,512]{1,0:T(8,128)(2,1)S(1)}, bf16[128,512]{1,0:T(8,128)(2,1)S(1)}, u32[]{:S(2)}, u32[]{:S(2)}) collective-permute-start(bf16[128,512]{1,0:T(8,128)(2,1)S(1)} %get-tuple-element.44.refs_5_), channel_id=1, source_target_pairs={{0,1},{1,0},{2,3},{3,2},{4,5},{5,4},{6,7},{7,6},{8,9},{9,8},{10,11... | collective-permute-start | bytes 393224 | tf_op jit(solution)/shard_map/ppermute | solution.py:38
  119.1 18.0 %collective-permute-start.23 = (bf16[256,512]{1,0:T(8,128)(2,1)S(1)}, bf16[256,512]{1,0:T(8,128)(2,1)S(1)}, u32[]{:S(2)}, u32[]{:S(2)}) collective-permute-start(bf16[256,512]{1,0:T(8,128)(2,1)S(1)} %collective-permute-done.19.refs_12_), channel_id=1, source_target_pairs={{0,1},{1,0},{2,3},{3,2},{4,5},{5,4},{6,7},{7,6},{8,9},{9,8},{10,11... | collective-permute-start | bytes 786440 | tf_op jit(solution)/shard_map/ppermute | solution.py:38
  119.9 17.1 %collective-permute-start.24 = (bf16[256,512]{1,0:T(8,128)(2,1)S(1)}, bf16[256,512]{1,0:T(8,128)(2,1)S(1)}, u32[]{:S(2)}, u32[]{:S(2)}) collective-permute-start(bf16[256,512]{1,0:T(8,128)(2,1)S(1)} %collective-permute-done.16.refs_8_), channel_id=1, source_target_pairs={{0,2},{1,3},{2,0},{3,1},{4,6},{5,7},{6,4},{7,5},{8,10},{9,11},{10,... | collective-permute-start | bytes 786440 | tf_op jit(solution)/shard_map/ppermute | solution.py:38
  125.8 11.2 %collective-permute-start.25 = (bf16[128,512]{1,0:T(8,128)(2,1)S(1)}, bf16[128,512]{1,0:T(8,128)(2,1)S(1)}, u32[]{:S(2)}, u32[]{:S(2)}) collective-permute-start(bf16[128,512]{1,0:T(8,128)(2,1)S(1)} %collective-permute-done.21.refs_14_), channel_id=1, source_target_pairs={{0,1},{1,0},{2,3},{3,2},{4,5},{5,4},{6,7},{7,6},{8,9},{9,8},{10,11... | collective-permute-start | bytes 393224 | tf_op jit(solution)/shard_map/ppermute | solution.py:38
  126.4 10.7 %collective-permute-start.26 = (bf16[128,512]{1,0:T(8,128)(2,1)S(1)}, bf16[128,512]{1,0:T(8,128)(2,1)S(1)}, u32[]{:S(2)}, u32[]{:S(2)}) collective-permute-start(bf16[128,512]{1,0:T(8,128)(2,1)S(1)} %collective-permute-done.18.refs_10_), channel_id=1, source_target_pairs={{0,2},{1,3},{2,0},{3,1},{4,6},{5,7},{6,4},{7,5},{8,10},{9,11},{10,... | collective-permute-start | bytes 393224 | tf_op jit(solution)/shard_map/ppermute | solution.py:38
  127.5 1.0 copy-start.10
  128.5 0.9 copy-start.15
  129.4 0.9 copy-start.17
  130.4 0.9 copy-start.19
  137.1 9.8 %copy-start.6 = (f32[1,3,512,512]{3,2,1,0:T(8,128)S(1)}, f32[1,3,512,512]{3,2,1,0:T(8,128)}, u32[]{:S(2)}) copy-start(f32[1,3,512,512]{3,2,1,0:T(8,128)} %refs_6_.1) | copy-start | bytes 9437188
  137.1 9.8 %copy-start.7 = (f32[1,3,512,512]{3,2,1,0:T(8,128)S(1)}, f32[1,3,512,512]{3,2,1,0:T(8,128)}, u32[]{:S(2)}) copy-start(f32[1,3,512,512]{3,2,1,0:T(8,128)} %refs_7_.1) | copy-start | bytes 9437188
  140.9 4.6 %collective-permute-start.29 = (f32[16,128]{1,0:T(8,128)S(1)}, f32[16,128]{1,0:T(8,128)S(1)}, u32[]{:S(2)}, u32[]{:S(2)}) collective-permute-start(f32[16,128]{1,0:T(8,128)S(1)} %get-tuple-element.50.refs_0_), channel_id=1, source_target_pairs={{0,3},{1,2},{2,1},{3,0},{4,7},{5,6},{6,5},{7,4},{8,11},{9,10},{10,... | collective-permute-start | bytes 24584 | tf_op jit(solution)/shard_map/ppermute | solution.py:38
  142.8 3.7 %collective-permute-start.28 = (f32[16,128]{1,0:T(8,128)S(1)}, f32[16,128]{1,0:T(8,128)S(1)}, u32[]{:S(2)}, u32[]{:S(2)}) collective-permute-start(f32[16,128]{1,0:T(8,128)S(1)} %get-tuple-element.50.refs_0_), channel_id=1, source_target_pairs={{0,2},{1,3},{2,0},{3,1},{4,6},{5,7},{6,4},{7,5},{8,10},{9,11},{10,... | collective-permute-start | bytes 24584 | tf_op jit(solution)/shard_map/ppermute | solution.py:38
  143.3 3.7 %collective-permute-start.27 = (f32[16,128]{1,0:T(8,128)S(1)}, f32[16,128]{1,0:T(8,128)S(1)}, u32[]{:S(2)}, u32[]{:S(2)}) collective-permute-start(f32[16,128]{1,0:T(8,128)S(1)} %get-tuple-element.50.refs_0_), channel_id=1, source_target_pairs={{0,1},{1,0},{2,3},{3,2},{4,5},{5,4},{6,7},{7,6},{8,9},{9,8},{10,11... | collective-permute-start | bytes 24584 | tf_op jit(solution)/shard_map/ppermute | solution.py:38

commit v4 on v3

--- a/solution.py
+++ b/solution.py
@@ -38,26 +38,86 @@
     return lax.ppermute(array, "replica", [(i, i ^ offset) for i in range(count)])
 
 
+def across_chips(parts):
+    count = lax.axis_size("expert")
+    return [parts[0]] + [
+        lax.ppermute(part, "expert", [(i, i ^ 2 * k) for i in range(count)])
+        for k, part in enumerate(parts)
+        if k
+    ]
+
+
+def pick_kernel(chips, *refs):
+    block_refs = [ref.at[k] for ref in refs[chips:] for k in range(ref.shape[0])]
+    for part_ref, block_ref in zip(refs[:chips], block_refs):
+        block_ref[...] = part_ref[1]
+
+
+def finish_spread(came, after=(), pieces=1):
+    count = lax.axis_size("expert")
+    chips = len(came)
+    block = jax.ShapeDtypeStruct((chips // pieces,) + came[0].shape[1:], came[0].dtype)
+    others = call(
+        functools.partial(pick_kernel, chips),
+        "pick",
+        came,
+        [VMEM] * chips,
+        [block] * pieces,
+        after=after,
+    )
+    swapped = [lax.ppermute(x, "expert", [(i, i ^ 1) for i in range(count)]) for x in others]
+    return [*came, *swapped]
+
+
+def spread_block(chips, refs, offset):
+    if offset % 2 == 0:
+        return refs[offset // 2].at[0]
+    blocks = [ref.at[k] for ref in refs[chips:] for k in range(ref.shape[0])]
+    return blocks[offset // 2]
+
+
 def exchange(parts):
     return [parts[0]] + [from_peer(part, k) for k, part in enumerate(parts) if k]
 
 
-def gather_pair(first, second):
+def cut_kernel(from_two_ref, from_one_ref, first_ref, second_ref):
+    first_ref[...] = from_two_ref[0]
+    second_ref[...] = from_one_ref[1]
+
+
+def gather_near(payload):
     count = lax.axis_size("replica")
     if count != 4:
-        return list(zip(exchange([first] * count), exchange([second] * count)))
-    first_two = from_peer(first, 2)
-    second_one = from_peer(second, 1)
-    first_one = from_peer(first, 1)
-    second_two = from_peer(second, 2)
-    first_three = from_peer(first_two, 1)
-    second_three = from_peer(second_one, 2)
-    return [
-        (first, second),
-        (first_one, second_one),
-        (first_two, second_two),
-        (first_three, second_three),
-    ]
+        return exchange([payload] * count)
+    from_two = from_peer(payload, 2)
+    return [payload, from_peer(payload, 1), from_two]
+
+
+def gather_rest(near, after):
+    whole = [(part,) for part in near]
+    if lax.axis_size("replica") != 4:
+        return whole
+    half = jax.ShapeDtypeStruct(near[0].shape[1:], near[0].dtype)
+    first, second = call(
+        cut_kernel, "cut", [near[2], near[1]], [VMEM, VMEM], [half, half], after=after
+    )
+    return whole + [(from_peer(first, 1), from_peer(second, 2))]
+
+
+def halves(refs):
+    return refs if len(refs) == 2 else (refs[0].at[0], refs[0].at[1])
+
+
+def regroup(refs, lengths):
+    groups, at = [], 0
+    for length in lengths:
+        groups.append(refs[at : at + length])
+        at += length
+    return groups
+
+
+def flatten(groups):
+    return [array for group in groups for array in group]
 
 
 def pair_list(count):
@@ -68,29 +128,36 @@
 VMEM = pl.BlockSpec(memory_space=pltpu.VMEM)
 
 
-def call(kernel, name, operands, specs, outs, out_specs=None, grid=(), scratch=(), extra=8):
+def call(
+    kernel, name, operands, specs, outs, out_specs=None, grid=(), scratch=(), after=(), cost=0
+):
     size = sum(x.size * x.dtype.itemsize for x in list(operands) + list(outs))
+    taken = len(operands)
+
+    def body(*refs):
+        kernel(*refs[:taken], *refs[taken + len(after) :])
+
     return pl.pallas_call(
-        kernel,
+        body,
         grid=grid,
-        in_specs=specs,
+        in_specs=list(specs) + [pl.BlockSpec(memory_space=pl.ANY)] * len(after),
         out_specs=out_specs if out_specs is not None else [VMEM for _ in outs],
         out_shape=outs,
         scratch_shapes=list(scratch),
         compiler_params=pltpu.CompilerParams(
             dimension_semantics=("arbitrary",) * len(grid),
-            vmem_limit_bytes=min(56 * MIB, size + extra * MIB),
+            vmem_limit_bytes=min(56 * MIB, size + 8 * MIB),
         ),
-        cost_estimate=pl.CostEstimate(flops=0, bytes_accessed=0, transcendentals=0),
+        cost_estimate=pl.CostEstimate(flops=0, bytes_accessed=cost, transcendentals=0),
         name=name,
-    )(*operands)
-
-
-def segment(rep_ref, offset, width):
-    return pl.ds(pl.multiple_of((rep_ref[0] ^ offset) * width, width), width)
-
-
-def rows_kernel(expert_count, rep_ref, ids_ref, task_ref, row_ref, grads_ref, *out_refs):
+    )(*operands, *after)
+
+
+def segment(pos_ref, offset, width):
+    return pl.ds(pl.multiple_of((pos_ref[0] ^ offset) * width, width), width)
+
+
+def rows_kernel(expert_count, pos_ref, ids_ref, task_ref, row_ref, grads_ref, *out_refs):
     row_count = grads_ref.shape[0]
     seg_rows = out_refs[0].shape[1]
     block_count = ids_ref.shape[1]
@@ -109,7 +176,7 @@
     labels = jnp.where(line == 0, row_ref[...].astype(jnp.float32), 0.0)
     labels = jnp.where(line == 1, rank, labels).astype(jnp.bfloat16)
     for offset, out_ref in enumerate(out_refs):
-        columns = segment(rep_ref, offset, seg_rows)
+        columns = segment(pos_ref, offset, seg_rows)
         for block in range(block_count):
             rows = pl.ds(block * block_rows, block_rows)
             weight = task_ref[ids_ref[0, block]]
@@ -123,9 +190,9 @@
         out_ref[pl.ds(row_count, LABEL_ROWS), pl.ds(0, row_count)] = labels
 
 
-def split_kernel(rep_ref, matrix_ref, *out_refs):
+def split_kernel(pos_ref, matrix_ref, *out_refs):
     for offset, out_ref in enumerate(out_refs):
-        out_ref[...] = matrix_ref[:, segment(rep_ref, offset, out_ref.shape[1])]
+        out_ref[...] = matrix_ref[:, segment(pos_ref, offset, out_ref.shape[1])]
 
 
 def one_hot(block_ref, row_count, slot_count, capacity):
@@ -135,24 +202,30 @@
     return jnp.where(places == slot, 1.0, 0.0).astype(jnp.bfloat16)
 
 
-def place_kernel(row_count, *refs):
-    block_refs, out_ref = refs[:-1], refs[-1]
-    expert_count, _, capacity, seg_rows = out_ref.shape
+def place_kernel(count, pos_ref, *refs):
+    block_refs, out_refs, placed_ref = refs[:count], refs[count:-1], refs[-1]
+    _, expert_count, capacity, seg_rows = placed_ref.shape
     slot_count = expert_count * capacity
+    row_count = block_refs[0].shape[0] - LABEL_ROWS
     for offset, block_ref in enumerate(block_refs):
         placing = one_hot(block_ref, row_count, slot_count, capacity)
         placed = multiply(placing, block_ref[pl.ds(0, row_count), :])
         placed = placed.reshape(expert_count, capacity, seg_rows)
-        out_ref[:, offset] = placed.astype(jnp.bfloat16)
-
-
-def unplace_kernel(block_ref, returned_ref, out_ref):
-    expert_count, capacity, model_width = returned_ref.shape
+        placed_ref[offset] = placed.astype(jnp.bfloat16)
+        for expert in range(expert_count):
+            out_refs[expert // 2][expert % 2, offset] = placed_ref[offset, pos_ref[1] ^ expert]
+
+
+def unplace_kernel(pos_ref, block_ref, *refs):
+    returned_refs, out_ref, slots_ref = refs[:-2], refs[-2], refs[-1]
+    expert_count, capacity, _ = slots_ref.shape
     slot_count = expert_count * capacity
     row_count = out_ref.shape[1]
     placing = one_hot(block_ref, row_count, slot_count, capacity)
-    returned = flat_rows(returned_ref[...])
-    out_ref[0] = contract_first(placing, returned).astype(jnp.bfloat16)
+    for expert in range(expert_count):
+        block_ref = spread_block(expert_count // 2, returned_refs, expert)
+        slots_ref[pos_ref[1] ^ expert] = block_ref[...]
+    out_ref[0] = contract_first(placing, flat_rows(slots_ref[...])).astype(jnp.bfloat16)
 
 
 def flat_rows(blocks):
@@ -163,22 +236,26 @@
     return blocks.reshape(rows, blocks.shape[2])
 
 
-def back_kernel(incoming_ref, weight_ref, *out_refs):
+def back_kernel(chips, arrays, pos_ref, weight_ref, *refs):
+    came_refs, incoming_ref, out_refs = refs[:arrays], refs[arrays], refs[arrays + 1 :]
     for offset, out_ref in enumerate(out_refs):
-        rows = flat_rows(incoming_ref[:, offset])
+        for expert in range(2 * chips):
+            block_ref = spread_block(chips, came_refs, expert)
+            incoming_ref[offset, pos_ref[1] ^ expert] = block_ref[offset]
+        rows = flat_rows(incoming_ref[offset])
         out_ref[...] = multiply(rows, weight_ref[...]).astype(out_ref.dtype)
 
 
-def forward_kernel(offsets, has_start, rep_ref, inputs_ref, *refs):
+def forward_kernel(offsets, lengths, has_start, pos_ref, inputs_ref, *refs):
     out_ref = refs[-1]
     weight_refs = refs[:-1]
     gate = up = None
     if has_start:
         gate, up = weight_refs[0][0], weight_refs[0][1]
         weight_refs = weight_refs[1:]
-    for place, offset in enumerate(offsets):
-        gate_ref, up_ref = weight_refs[2 * place : 2 * place + 2]
-        rows = inputs_ref[:, segment(rep_ref, offset, gate_ref.shape[0])]
+    for offset, group in zip(offsets, regroup(weight_refs, lengths)):
+        gate_ref, up_ref = halves(group)
+        rows = inputs_ref[:, segment(pos_ref, offset, gate_ref.shape[0])]
         gate_part, up_part = multiply(rows, gate_ref[...]), multiply(rows, up_ref[...])
         gate = gate_part if gate is None else gate + gate_part
         up = up_part if up is None else up + up_part
@@ -186,53 +263,59 @@
     out_ref[1] = up
 
 
-def hidden_kernel(forward_ref, first_ref, second_ref):
-    half = forward_ref.shape[1] // 2
-    for part, out_ref in enumerate((first_ref, second_ref)):
-        rows = pl.ds(part * half, half)
-        gate_pre = forward_ref[0, rows]
-        gate_act = gate_pre * jax.nn.sigmoid(gate_pre)
-        out_ref[...] = (gate_act * forward_ref[1, rows]).astype(jnp.bfloat16)
-
-
 def factor_kernel(forward_ref, *refs):
-    back_refs, (gate_ref, up_ref) = refs[:-2], refs[-2:]
+    back_refs, out_ref = refs[:-1], refs[-1]
+    slot_count = forward_ref.shape[1]
+    half = slot_count // 2
     hidden_grad = back_refs[0][...]
     for back_ref in back_refs[1:]:
         hidden_grad = hidden_grad + back_ref[...].astype(jnp.float32)
     gate_pre, up_pre = forward_ref[0], forward_ref[1]
     sigmoid_gate = jax.nn.sigmoid(gate_pre)
     gate_act = gate_pre * sigmoid_gate
-    gate_ref[...] = (
-        hidden_grad * up_pre * sigmoid_gate * (1.0 + gate_pre * (1.0 - sigmoid_gate))
-    ).astype(jnp.bfloat16)
-    up_ref[...] = (hidden_grad * gate_act).astype(jnp.bfloat16)
-
-
-def slot_kernel(rep_ref, first_ref, second_ref, *refs):
-    weight_refs, out_ref = refs[:-1], refs[-1]
-    expert_count, capacity, _ = out_ref.shape
-    gate_grad, up_grad = first_ref[...], second_ref[...]
-    for offset in range(len(weight_refs) // 2):
-        gate_ref, up_ref = weight_refs[2 * offset : 2 * offset + 2]
+    hidden = (gate_act * up_pre).astype(jnp.bfloat16)
+    gate_grad = hidden_grad * up_pre * sigmoid_gate * (1.0 + gate_pre * (1.0 - sigmoid_gate))
+    out_ref[0, pl.ds(0, slot_count)] = gate_grad.astype(jnp.bfloat16)
+    out_ref[1, pl.ds(0, slot_count)] = (hidden_grad * gate_act).astype(jnp.bfloat16)
+    for part in range(2):
+        out_ref[part, pl.ds(slot_count, half)] = hidden[part * half : (part + 1) * half]
+
+
+def slot_kernel(lengths, pos_ref, factor_ref, *refs):
+    chips = refs[-1].shape[1] // 2
+    weight_refs, out_refs, slots_ref = refs[: -chips - 1], refs[-chips - 1 : -1], refs[-1]
+    _, expert_count, capacity, seg_rows = slots_ref.shape
+    rows = pl.ds(0, expert_count * capacity)
+    gate_grad, up_grad = factor_ref[0, rows], factor_ref[1, rows]
+    for offset, group in enumerate(regroup(weight_refs, lengths)):
+        gate_ref, up_ref = halves(group)
         total = contract_last(gate_grad, gate_ref[...]) + contract_last(up_grad, up_ref[...])
-        total = total.reshape(expert_count, capacity, total.shape[1]).astype(jnp.bfloat16)
-        out_ref[:, :, segment(rep_ref, offset, total.shape[2])] = total
-
-
-def gram_kernel(count, offsets, place, rep_ref, *refs):
+        total = total.reshape(expert_count, capacity, seg_rows)
+        slots_ref[offset] = total.astype(jnp.bfloat16)
+        columns = segment(pos_ref, offset, seg_rows)
+        for expert in range(expert_count):
+            out_ref = out_refs[expert // 2]
+            out_ref[expert % 2, :, columns] = slots_ref[offset, pos_ref[1] ^ expert]
+
+
+def gram_kernel(count, offsets, lengths, place, pos_ref, *refs):
     if place:
         before_ref, earlier_ref, refs = refs[0], refs[1], refs[2:]
     incoming_ref, operand_refs, grads_ref, gram_ref = refs[0], refs[1:-2], refs[-2], refs[-1]
-    middle = incoming_ref.shape[0] // 2
+    middle = incoming_ref.shape[1] // 2
     seg_rows, hidden_width = grads_ref.shape[2:]
+    groups = regroup(operand_refs, lengths)
     for at, offset in enumerate(offsets):
-        inputs_ref, gate_ref, up_ref, first_ref, second_ref = operand_refs[5 * at : 5 * at + 5]
+        (inputs_ref,), factor_refs = groups[2 * at : 2 * at + 2]
+        slot_count = inputs_ref.shape[0]
+        rest = pl.ds(slot_count, slot_count // 2)
+        gate_ref, up_ref = (ref.at[pl.ds(0, slot_count)] for ref in halves(factor_refs))
+        first_ref, second_ref = (ref.at[rest] for ref in halves(factor_refs))
         grads_ref[at, 0] = contract_first(inputs_ref[...], gate_ref[...])
         grads_ref[at, 1] = contract_first(inputs_ref[...], up_ref[...])
         grads_ref[at, 2] = contract_first(
-            flat_rows(incoming_ref[:middle, offset]), first_ref[...]
-        ) + contract_first(flat_rows(incoming_ref[middle:, offset]), second_ref[...])
+            flat_rows(incoming_ref[offset, :middle]), first_ref[...]
+        ) + contract_first(flat_rows(incoming_ref[offset, middle:]), second_ref[...])
     gram_ref[...] = before_ref[...] if place else jnp.zeros_like(gram_ref)
     known = list(range(place)) + list(offsets)
     pairs = [(i, j) for i, j in pair_list(len(known)) if j >= place]
@@ -246,13 +329,13 @@
         return tuple(total + blocks[i] * blocks[j] for total, (i, j) in zip(sums, pairs))
 
     zero = jnp.zeros((lines, hidden_width), jnp.float32)
-    sums = lax.fori_loop(0, 3 * (seg_rows // lines), add, tuple(zero for _ in pairs))
+    sums = lax.fori_loop(0, 3 * (seg_rows // lines), add, tuple(zero for _ in pairs), unroll=4)
     for total, (i, j) in zip(sums, pairs):
         total = jnp.sum(total, axis=0, keepdims=True)
         part = total[:, :128]
         for lane in range(128, hidden_width, 128):
             part = part + total[:, lane : lane + 128]
-        first, second = rep_ref[0] ^ known[i], rep_ref[0] ^ known[j]
+        first, second = pos_ref[0] ^ known[i], pos_ref[0] ^ known[j]
         row = jnp.minimum(first, second) * count + jnp.maximum(first, second)
         gram_ref[pl.ds(row, 1), :] = part
 
@@ -287,7 +370,7 @@
     return [vectors[0][rep] for rep in range(count)]
 
 
-def adam_kernel(count, places, rep_ref, *refs):
+def adam_kernel(count, places, pos_ref, *refs):
     gram_refs, grads_refs = refs[:count], refs[count : count + len(places)]
     first_ref, second_ref, step_ref, coef_ref = refs[count + len(places) :]
     hidden_width = step_ref.shape[3]
@@ -310,7 +393,7 @@
         merged = None
         for grads_ref, offsets in zip(grads_refs, places):
             for at, offset in enumerate(offsets):
-                part = grads_ref[at, matrix, rows] * coef_ref[rep_ref[0] ^ offset]
+                part = grads_ref[at, matrix, rows] * coef_ref[pos_ref[0] ^ offset]
                 merged = part if merged is None else merged + part
         first_new = (beta_first / first_fix) * first_ref[0, 0, rows] + (
             (1.0 - beta_first) / first_fix
@@ -321,16 +404,18 @@
         step_ref[0, 0, rows] = first_new / (jnp.sqrt(second_new) + adam_eps)
         return 0
 
-    lax.fori_loop(0, step_ref.shape[2] // lines, step, 0)
+    lax.fori_loop(0, step_ref.shape[2] // lines, step, 0, unroll=4)
 
 
 def adasum_adam_many(rep, inputs, incoming, factors, first_moment, second_moment):
     count = len(inputs)
     half = inputs[0].shape[0] // 2
     grads = []
-    for offset, (gate_grad, up_grad, *halves) in enumerate(factors):
-        received = incoming[:, offset].reshape(2 * half, incoming.shape[3])
-        hidden = jnp.concatenate(halves)
+    for offset in range(count):
+        (payload,) = factors[offset]
+        gate_grad, up_grad = payload[:, : 2 * half]
+        hidden = payload[:, 2 * half :].reshape(2 * half, -1)
+        received = incoming[offset].reshape(2 * half, incoming.shape[3])
         grads.append(
             jnp.stack(
                 [
@@ -363,20 +448,19 @@
     return ((first_new / first_fix) / (jnp.sqrt(second_new / second_fix) + adam_eps))[None]
 
 
-def adasum_adam(rep, inputs, incoming, factors, first_moment, second_moment):
+def adasum(rep, inputs, incoming, factors):
     count = len(inputs)
-    if count > 4:
-        return adasum_adam_many(rep, inputs, incoming, factors, first_moment, second_moment)
-    seg_rows, hidden_width = first_moment.shape[2:]
+    seg_rows, hidden_width = inputs[0].shape[1], factors[0][0].shape[2]
     shape = jax.ShapeDtypeStruct
     groups = [[k for k in range(count) if k < 3], [k for k in range(count) if k == 3]]
     groups = [group for group in groups if group]
-    grads, gram, place = [], None, 0
+    grads, gram, first_gram, place = [], None, None, 0
     for group in groups:
         operands = [rep] if gram is None else [rep, gram, grads[0]]
-        operands += [incoming] + [x for k in group for x in (inputs[k], *factors[k])]
+        parts = [x for k in group for x in ((inputs[k],), factors[k])]
+        operands += [incoming] + flatten(parts)
         more, gram = call(
-            functools.partial(gram_kernel, count, group, place),
+            functools.partial(gram_kernel, count, group, [len(x) for x in parts], place),
             "gram_late" if place else "gram",
             operands,
             [SMEM] + [VMEM] * (len(operands) - 1),
@@ -384,9 +468,17 @@
                 shape((len(group), 3, seg_rows, hidden_width), jnp.float32),
                 shape((max(8, count * count), 128), jnp.float32),
             ],
-        )
+            cost=0 if place else 0,
+        )
+        first_gram = gram if first_gram is None else first_gram
         grads.append(more)
         place += len(group)
+    return groups, grads, gram, first_gram
+
+
+def adam(rep, groups, grads, gram, first_moment, second_moment, after):
+    count = sum(len(group) for group in groups)
+    seg_rows, hidden_width = first_moment.shape[2:]
     grams = exchange([gram] * count)
     moment_spec = pl.BlockSpec((1, 1, seg_rows, hidden_width), lambda m: (0, m, 0, 0))
     (adam_step,) = call(
@@ -394,10 +486,11 @@
         "adam",
         [rep, *grams, *grads, first_moment, second_moment],
         [SMEM] + [VMEM] * (len(grams) + len(grads)) + [moment_spec, moment_spec],
-        [shape(first_moment.shape, jnp.float32)],
+        [jax.ShapeDtypeStruct(first_moment.shape, jnp.float32)],
         out_specs=[moment_spec],
         grid=(3,),
         scratch=[pltpu.VMEM((count, 1, hidden_width), jnp.float32)],
+        after=after,
     )
     return adam_step
 
@@ -415,7 +508,8 @@
     seg_rows = model_width // rep_count
     half = slot_count // 2
     offsets = range(rep_count)
-    rep = lax.axis_index("replica").astype(jnp.int32).reshape(1)
+    chips = expert_count // 2
+    rep = jnp.stack([lax.axis_index("replica"), lax.axis_index("expert")]).astype(jnp.int32)
     shape = jax.ShapeDtypeStruct
 
     block = shape((row_count + LABEL_ROWS, seg_rows), jnp.bfloat16)
@@ -428,8 +522,7 @@
     )
     routed = exchange(row_blocks)
 
-    own_weights = [weights[0, 0], weights[0, 1]]
-    projections = gather_pair(*own_weights)
+    near_projections = gather_near(weights[0, :2])
 
     inputs_home = saved_inputs[0, 0]
     inputs = exchange(
@@ -442,14 +535,22 @@
         )
     )
 
-    (outgoing,) = call(
-        functools.partial(place_kernel, row_count),
-        "place",
-        routed,
-        [VMEM] * len(routed),
-        [shape((expert_count, rep_count, capacity, seg_rows), jnp.bfloat16)],
-    )
-    incoming = lax.all_to_all(outgoing, "expert", split_axis=0, concat_axis=0, tiled=True)
+    part = shape((2, rep_count, capacity, seg_rows), jnp.bfloat16)
+    placed = (
+        call(
+            functools.partial(place_kernel, rep_count),
+            "place",
+            [rep, *routed],
+            [SMEM] + [VMEM] * len(routed),
+            [part] * chips,
+            scratch=[
+                pltpu.VMEM((rep_count, expert_count, capacity, seg_rows), jnp.bfloat16)
+            ],
+        )
+    )
+
+    came = across_chips(placed)
+    projections = gather_rest(near_projections, after=placed[:1])
 
     forward = None
     late = [3] if rep_count == 4 else []
@@ -457,58 +558,75 @@
         if not group:
             continue
         operands = [rep, inputs_home] + ([] if forward is None else [forward])
-        operands += [array for k in group for array in projections[k]]
+        operands += flatten(projections[k] for k in group)
+        lengths = [len(projections[k]) for k in group]
         (forward,) = call(
-            functools.partial(forward_kernel, group, forward is not None),
+            functools.partial(forward_kernel, group, lengths, forward is not None),
             name,
             operands,
             [SMEM] + [VMEM] * (len(operands) - 1),
             [shape((2, slot_count, hidden_width), jnp.float32)],
-        )
+            cost=0 if name == "rest" else 0,
+        )
+
+    came = finish_spread(came)
 
     back_shape = (slot_count, hidden_width)
-    back = exchange(
-        call(
-            back_kernel,
-            "back",
-            [incoming, weights[0, 2]],
-            [VMEM, VMEM],
-            [shape(back_shape, jnp.bfloat16 if k else jnp.float32) for k in offsets],
-        )
-    )
-    half_shape = shape((half, hidden_width), jnp.bfloat16)
-    hidden = gather_pair(
-        *call(hidden_kernel, "hidden", [forward], [VMEM], [half_shape, half_shape])
-    )
-    forward, inputs = lax.optimization_barrier((forward, inputs))
-    full_shape = shape((slot_count, hidden_width), jnp.bfloat16)
-    gate_grad, up_grad = call(
+    incoming, *back = call(
+        functools.partial(back_kernel, chips, len(came)),
+        "back",
+        [rep, weights[0, 2], *came],
+        [SMEM] + [VMEM] * (1 + len(came)),
+        [shape((rep_count, expert_count, capacity, seg_rows), jnp.bfloat16)]
+        + [shape(back_shape, jnp.bfloat16 if k else jnp.float32) for k in offsets],
+        after=[forward],
+    )
+    back = exchange(back)
+    (own_factors,) = call(
         factor_kernel,
         "factors",
         [forward, *back],
         [VMEM] * (1 + len(back)),
-        [full_shape, full_shape],
-    )
-    factors = [a + b for a, b in zip(gather_pair(gate_grad, up_grad), hidden)]
-
-    operands = [rep, gate_grad, up_grad] + [array for pair in projections for array in pair]
-    (slot_grads,) = call(
-        slot_kernel,
-        "slots",
-        operands,
-        [SMEM] + [VMEM] * (len(operands) - 1),
-        [shape((expert_count, capacity, model_width), jnp.bfloat16)],
-    )
-    returned = lax.all_to_all(slot_grads, "expert", split_axis=0, concat_axis=0, tiled=True)
+        [shape((2, slot_count + half, hidden_width), jnp.bfloat16)],
+        after=inputs[1:],
+    )
+    near_factors = gather_near(own_factors)
+
+    operands = [rep, own_factors] + flatten(projections)
+    returning = across_chips(
+        call(
+            functools.partial(slot_kernel, [len(group) for group in projections]),
+            "slots",
+            operands,
+            [SMEM] + [VMEM] * (len(operands) - 1),
+            [shape((2, capacity, model_width), jnp.bfloat16)] * chips,
+            scratch=[
+                pltpu.VMEM((rep_count, expert_count, capacity, seg_rows), jnp.bfloat16)
+            ],
+        )
+    )
+    factors = gather_rest(near_factors, after=returning[:1])
+    if rep_count <= 4:
+        *merging, first_gram = adasum(rep, inputs, incoming, factors)
+        returned = finish_spread(returning, [first_gram], pieces=2)
+        unplace_after = merging[2:]
+    else:
+        returned, unplace_after = finish_spread(returning), ()
     (input_grads,) = call(
         unplace_kernel,
         "unplace",
-        [routed[0], returned],
-        [VMEM, VMEM],
+        [rep, routed[0], *returned],
+        [SMEM] + [VMEM] * (1 + len(returned)),
         [shape((1, row_count, model_width), jnp.bfloat16)],
-    )
-
-    adam_step = adasum_adam(rep, inputs, incoming, factors, first_moment, second_moment)
+        scratch=[pltpu.VMEM((expert_count, capacity, model_width), jnp.bfloat16)],
+        after=unplace_after,
+    )
+    if rep_count <= 4:
+        adam_step = adam(rep, *merging, first_moment, second_moment, [input_grads])
+    else:
+        adam_step = adasum_adam_many(
+            rep, inputs, incoming, factors, first_moment, second_moment
+        )
     return (input_grads, adam_step)
 
 

time: 154 us -> 135 us (0.88)
  local copies, waits for them, and re-layouts: 14 us -> 5.86 us
  starting transfers between devices: 41 us -> 36.3 us
  waiting for transfers between devices: 69.5 us -> 65.3 us
  Pallas kernels: 27.2 us -> 24.7 us
    ppermute x30 -> x20, waiting for transfers between devices: 66.5 us -> 46.8 us  [from_peer(): lax.ppermute(array, 'replica', [(i, i ^ offset) for i in range(count)])]
    ppermute x0 -> x9, waiting for transfers between devices: none -> 18.5 us  [the longest x6 18.5 us: across_chips(): lax.ppermute(part, 'expert', [(i, i ^ 2 * k) for i in range(count)])]
    ppermute x0 -> x9, starting transfers between devices: none -> 11.5 us  [the longest x6 10.9 us: across_chips(): lax.ppermute(part, 'expert', [(i, i ^ 2 * k) for i in range(count)])]
    all_to_all x2 -> x0, starting transfers between devices: 9.21 us -> none  [the longest x1 4.87 us: shards(): lax.all_to_all(outgoing, 'expert', split_axis=0, concat_axis=0, tiled=True)]
    unnamed x48 -> x14, local copies, waits for them, and re-layouts: 11.8 us -> 3.41 us
    ppermute x30 -> x20, starting transfers between devices: 31.8 us -> 24.8 us  [from_peer(): lax.ppermute(array, 'replica', [(i, i ^ offset) for i in range(count)])]
    all_to_all x2 -> x0, waiting for transfers between devices: 3.02 us -> none  [the longest x1 3.02 us: shards(): lax.all_to_all(outgoing, 'expert', split_axis=0, concat_axis=0, tiled=True)]
    pallas_call x13 -> x16, Pallas kernels: 27.2 us -> 24.7 us  [call(): pl.pallas_call(body, grid=grid, in_specs=list(specs) + [pl.BlockSpec(memo...]
  transfers between devices with their start and end apart: 32 -> 29, of which waited for: 14 -> 11; matrix products, arithmetic and copies ran while one was open for 1% -> 1% of each run, Pallas kernels for 13% -> 14%
where the time goes in v4:
time: 135 us; the launch traced here: 134 us
  waiting for transfers between devices  65.3 us (48%)
  starting transfers between devices  36.3 us (27%)
  Pallas kernels  24.7 us (18%)
  local copies, waits for them, and re-layouts  5.86 us (4%)
  between operations  1.45 us (1%)
    ppermute x20, waiting for transfers between devices, from_peer(): lax.ppermute(array, 'replica', [(i, i ^ offset) for i in range(count)])  46.8 us
    ppermute x20, starting transfers between devices, from_peer(): lax.ppermute(array, 'replica', [(i, i ^ offset) for i in range(count)])  24.8 us
    pallas_call x16, Pallas kernels, call(): pl.pallas_call(body, grid=grid, in_specs=list(specs) + [pl.BlockSpec(memo...  24.7 us
    ppermute x6, waiting for transfers between devices, across_chips(): lax.ppermute(part, 'expert', [(i, i ^ 2 * k) for i in range(count)])  18.5 us
    ppermute x6, starting transfers between devices, across_chips(): lax.ppermute(part, 'expert', [(i, i ^ 2 * k) for i in range(count)])  10.9 us
    unnamed x14, local copies, waits for them, and re-layouts  3.41 us
  transfers between devices with their start and end apart: 29, of which 11 were waited for; matrix products, arithmetic and copies ran while one was open for 1% of the time, Pallas kernels for 14%

profile of v4, /device:TPU:0, one launch (start us, length us, event | category | flops | bytes accessed | tf_op | source)
XLA Modules:
  0.0 133.7 jit_solution(3547098149523924626)
XLA Ops:
  0.6 1.4 %slice_bitcast_fusion.refs_2_ = bf16[2,512,512]{2,1,0:T(8,128)(2,1)S(1)} fusion(bf16[1,3,512,512]{3,2,1,0:T(8,128)(2,1)} %param.8), kind=kLoop, calls=%fused_computation | loop fusion | bytes 2097152 | tf_op jit(solution)/shard_map/squeeze | solution.py:525
  2.0 3.0 %collective-permute-start = (bf16[2,512,512]{2,1,0:T(8,128)(2,1)S(1)}, bf16[2,512,512]{2,1,0:T(8,128)(2,1)S(1)}, u32[]{:S(2)}, u32[]{:S(2)}) collective-permute-start(bf16[2,512,512]{2,1,0:T(8,128)(2,1)S(1)} %slice_bitcast_fusion.refs_2_), channel_id=1, source_target_pairs={{0,1},{1,0},{2,3},{3,2},{4,5},{5,4},{6,7},{7,6},{8,9},{9,8},{10,11... | collective-permute-start | bytes 3145736 | tf_op jit(solution)/shard_map/ppermute | solution.py:38
  5.0 1.5 %collective-permute-start.1 = (bf16[2,512,512]{2,1,0:T(8,128)(2,1)S(1)}, bf16[2,512,512]{2,1,0:T(8,128)(2,1)}, u32[]{:S(2)}, u32[]{:S(2)}) collective-permute-start(bf16[2,512,512]{2,1,0:T(8,128)(2,1)S(1)} %slice_bitcast_fusion.refs_2_), channel_id=1, source_target_pairs={{0,2},{1,3},{2,0},{3,1},{4,6},{5,7},{6,4},{7,5},{8,10},{9,11},{10,... | collective-permute-start | bytes 3145736 | tf_op jit(solution)/shard_map/ppermute | solution.py:38
  7.2 0.1 pad_add_fusion.refs_0_
  7.3 1.0 copy-done.4
  8.3 0.7 copy-done.5
  9.0 0.7 copy-done.6
  9.6 0.7 rows.1
  10.3 0.6 collective-permute-start.2
  10.9 0.1 collective-permute-start.3
  11.0 2.9 %collective-permute-start.4 = (bf16[144,512]{1,0:T(8,128)(2,1)S(1)}, bf16[144,512]{1,0:T(8,128)(2,1)S(1)}, u32[]{:S(2)}, u32[]{:S(2)}) collective-permute-start(bf16[144,512]{1,0:T(8,128)(2,1)S(1)} %get-tuple-element.36), channel_id=1, source_target_pairs={{0,3},{1,2},{2,1},{3,0},{4,7},{5,6},{6,5},{7,4},{8,11},{9,10},{10,... | collective-permute-start | bytes 442376 | tf_op jit(solution)/shard_map/ppermute | solution.py:38
  13.9 18.3 %collective-permute-done.2.refs_2_ = bf16[144,512]{1,0:T(8,128)(2,1)S(1)} collective-permute-done((bf16[144,512]{1,0:T(8,128)(2,1)S(1)}, bf16[144,512]{1,0:T(8,128)(2,1)S(1)}, u32[]{:S(2)}, u32[]{:S(2)}) %collective-permute-start.2) | collective-permute-done | bytes 147488 | tf_op jit(solution)/shard_map/ppermute | solution.py:38
  32.2 3.8 %collective-permute-done.3.refs_3_ = bf16[144,512]{1,0:T(8,128)(2,1)S(1)} collective-permute-done((bf16[144,512]{1,0:T(8,128)(2,1)S(1)}, bf16[144,512]{1,0:T(8,128)(2,1)S(1)}, u32[]{:S(2)}, u32[]{:S(2)}) %collective-permute-start.3) | collective-permute-done | bytes 147488 | tf_op jit(solution)/shard_map/ppermute | solution.py:38
  36.0 1.0 place.1
  37.0 1.6 %collective-permute-start.7 = (bf16[2,4,32,512]{3,2,1,0:T(8,128)(2,1)S(1)}, bf16[2,4,32,512]{3,2,1,0:T(8,128)(2,1)S(1)}, u32[]{:S(2)}, u32[]{:S(2)}) collective-permute-start(bf16[2,4,32,512]{3,2,1,0:T(8,128)(2,1)S(1)} %get-tuple-element.40), channel_id=1, source_target_pairs={{0,8},{4,12},{8,0},{12,4},{16,24},{20,28},{24,16},{28,20},{1,9},{5... | collective-permute-start | bytes 786440 | tf_op jit(solution)/shard_map/ppermute | solution.py:44
  38.6 2.6 %collective-permute-start.8 = (bf16[2,4,32,512]{3,2,1,0:T(8,128)(2,1)S(1)}, bf16[2,4,32,512]{3,2,1,0:T(8,128)(2,1)S(1)}, u32[]{:S(2)}, u32[]{:S(2)}) collective-permute-start(bf16[2,4,32,512]{3,2,1,0:T(8,128)(2,1)S(1)} %get-tuple-element.41), channel_id=1, source_target_pairs={{0,16},{4,20},{8,24},{12,28},{16,0},{20,4},{24,8},{28,12},{1,17},{... | collective-permute-start | bytes 786440 | tf_op jit(solution)/shard_map/ppermute | solution.py:44
  41.2 0.2 collective-permute-start.9
  41.4 1.3 cut.2
  42.7 1.3 collective-permute-start.5
  44.0 0.8 collective-permute-start.6
  44.8 3.3 %collective-permute-done.7.refs_1_.refs_3_ = bf16[2,4,32,512]{3,2,1,0:T(8,128)(2,1)S(1)} collective-permute-done((bf16[2,4,32,512]{3,2,1,0:T(8,128)(2,1)S(1)}, bf16[2,4,32,512]{3,2,1,0:T(8,128)(2,1)S(1)}, u32[]{:S(2)}, u32[]{:S(2)}) %collective-permute-start.7) | collective-permute-done | bytes 262176 | tf_op jit(solution)/shard_map/ppermute | solution.py:44
  48.1 11.9 %collective-permute-done.8.refs_2_.refs_4_ = bf16[2,4,32,512]{3,2,1,0:T(8,128)(2,1)S(1)} collective-permute-done((bf16[2,4,32,512]{3,2,1,0:T(8,128)(2,1)S(1)}, bf16[2,4,32,512]{3,2,1,0:T(8,128)(2,1)S(1)}, u32[]{:S(2)}, u32[]{:S(2)}) %collective-permute-start.8) | collective-permute-done | bytes 262176 | tf_op jit(solution)/shard_map/ppermute | solution.py:44
  60.0 0.0 collective-permute-done.9.refs_3_.refs_5_
  60.0 0.1 collective-permute-start.10
  60.1 0.6 split.1
  60.7 1.3 collective-permute-start.14
  62.0 0.8 collective-permute-start.15
  62.9 1.1 slice_bitcast_fusion.1.refs_1_
  63.9 2.2 %forward.1.refs_2_ = f32[2,256,512]{2,1,0:T(8,128)S(1)} custom-call(s32[2]{0:T(128)S(1)} %pad_add_fusion.refs_0_, bf16[256,2048]{1,0:T(8,128)(2,1)S(1)} %bitcast.10, bf16[2,512,512]{2,1,0:T(8,128)(2,1)S(1)} %slice_bitcast_fusion.refs_2_, bf16[2,512,512]{2,1,0:T(8,128)(2,1)S(1)} %collective-permute-done.refs_3_.refs_1_, ...), custom_call_target="tpu_custom_call" | custom-call | tf_op jit(solution)/shard_map/forward/pallas_call | solution.py:140
  66.2 1.5 %collective-permute-start.16 = (bf16[256,512]{1,0:T(8,128)(2,1)S(1)}, bf16[256,512]{1,0:T(8,128)(2,1)S(1)}, u32[]{:S(2)}, u32[]{:S(2)}) collective-permute-start(bf16[256,512]{1,0:T(8,128)(2,1)S(1)} %get-tuple-element.49), channel_id=1, source_target_pairs={{0,3},{1,2},{2,1},{3,0},{4,7},{5,6},{6,5},{7,4},{8,11},{9,10},{10,... | collective-permute-start | bytes 786440 | tf_op jit(solution)/shard_map/ppermute | solution.py:38
  67.7 0.0 collective-permute-done.6.refs_4_.refs_6_
  67.7 1.0 rest.1.refs_7_.refs_0_
  68.7 1.3 back.1
  69.9 1.3 collective-permute-start.11
  71.2 0.8 collective-permute-start.12
  72.0 1.4 %collective-permute-start.13 = (bf16[256,512]{1,0:T(8,128)(2,1)S(1)}, bf16[256,512]{1,0:T(8,128)(2,1)S(1)}, u32[]{:S(2)}, u32[]{:S(2)}) collective-permute-start(bf16[256,512]{1,0:T(8,128)(2,1)S(1)} %get-tuple-element.46), channel_id=1, source_target_pairs={{0,3},{1,2},{2,1},{3,0},{4,7},{5,6},{6,5},{7,4},{8,11},{9,10},{10,... | collective-permute-start | bytes 786440 | tf_op jit(solution)/shard_map/ppermute | solution.py:38
  73.5 3.2 %collective-permute-done.15.refs_6_ = bf16[256,512]{1,0:T(8,128)(2,1)S(1)} collective-permute-done((bf16[256,512]{1,0:T(8,128)(2,1)S(1)}, bf16[256,512]{1,0:T(8,128)(2,1)S(1)}, u32[]{:S(2)}, u32[]{:S(2)}) %collective-permute-start.15) | collective-permute-done | bytes 262176 | tf_op jit(solution)/shard_map/ppermute | solution.py:38
  76.7 5.0 %collective-permute-done.11.refs_2_ = bf16[256,512]{1,0:T(8,128)(2,1)S(1)} collective-permute-done((bf16[256,512]{1,0:T(8,128)(2,1)S(1)}, bf16[256,512]{1,0:T(8,128)(2,1)S(1)}, u32[]{:S(2)}, u32[]{:S(2)}) %collective-permute-start.11) | collective-permute-done | bytes 262176 | tf_op jit(solution)/shard_map/ppermute | solution.py:38
  81.7 5.6 %collective-permute-done.12.refs_3_ = bf16[256,512]{1,0:T(8,128)(2,1)S(1)} collective-permute-done((bf16[256,512]{1,0:T(8,128)(2,1)S(1)}, bf16[256,512]{1,0:T(8,128)(2,1)S(1)}, u32[]{:S(2)}, u32[]{:S(2)}) %collective-permute-start.12) | collective-permute-done | bytes 262176 | tf_op jit(solution)/shard_map/ppermute | solution.py:38
  87.3 0.4 factors.1.refs_1_.refs_3_
  87.7 0.9 collective-permute-start.20
  88.6 1.0 collective-permute-start.21
  89.6 2.6 %slots.1 = (bf16[2,32,2048]{2,1,0:T(8,128)(2,1)S(1)}, bf16[2,32,2048]{2,1,0:T(8,128)(2,1)S(1)}, bf16[2,32,2048]{2,1,0:T(8,128)(2,1)S(1)}, bf16[2,32,2048]{2,1,0:T(8,128)(2,1)S(1)}) custom-call(s32[2]{0:T(128)S(1)} %pad_add_fusion.refs_0_, bf16[2,384,512]{2,1,0:T(8,128)(2,1)S(1)} %factors.1.refs_1_.refs_3_, ...), custom_call_target="tpu_custom_call" | custom-call | tf_op jit(solution)/shard_map/slots/pallas_call | solution.py:140
  92.1 3.9 %collective-permute-start.17 = (bf16[2,32,2048]{2,1,0:T(8,128)(2,1)S(1)}, bf16[2,32,2048]{2,1,0:T(8,128)(2,1)S(1)}, u32[]{:S(2)}, u32[]{:S(2)}) collective-permute-start(bf16[2,32,2048]{2,1,0:T(8,128)(2,1)S(1)} %get-tuple-element.51), channel_id=1, source_target_pairs={{0,8},{4,12},{8,0},{12,4},{16,24},{20,28},{24,16},{28,20},{1,9},{5... | collective-permute-start | bytes 786440 | tf_op jit(solution)/shard_map/ppermute | solution.py:44
  96.1 1.1 collective-permute-start.18
  97.2 1.4 %collective-permute-start.19 = (bf16[2,32,2048]{2,1,0:T(8,128)(2,1)S(1)}, bf16[2,32,2048]{2,1,0:T(8,128)(2,1)S(1)}, u32[]{:S(2)}, u32[]{:S(2)}) collective-permute-start(bf16[2,32,2048]{2,1,0:T(8,128)(2,1)S(1)} %get-tuple-element.53), channel_id=1, source_target_pairs={{0,24},{4,28},{8,16},{12,20},{16,8},{20,12},{24,0},{28,4},{1,25},{... | collective-permute-start | bytes 786440 | tf_op jit(solution)/shard_map/ppermute | solution.py:44
  98.5 8.2 %collective-permute-done.20.refs_5_.refs_1_ = bf16[2,384,512]{2,1,0:T(8,128)(2,1)S(1)} collective-permute-done((bf16[2,384,512]{2,1,0:T(8,128)(2,1)S(1)}, bf16[2,384,512]{2,1,0:T(8,128)(2,1)S(1)}, u32[]{:S(2)}, u32[]{:S(2)}) %collective-permute-start.20) | collective-permute-done | bytes 786464 | tf_op jit(solution)/shard_map/ppermute | solution.py:38
  106.7 1.0 collective-permute-done.21.refs_7_.refs_0_
  107.8 0.1 cut.3
  107.8 0.8 collective-permute-start.24
  108.6 1.3 collective-permute-start.25
  109.9 4.2 %gram.1 = (f32[3,3,512,512]{3,2,1,0:T(8,128)S(1)}, f32[16,128]{1,0:T(8,128)S(1)}) custom-call(s32[2]{0:T(128)S(1)} %pad_add_fusion.refs_0_, bf16[4,8,32,512]{3,2,1,0:T(8,128)(2,1)S(1)} %get-tuple-element.54.refs_1_.refs_3_, bf16[256,512]{1,0:T(8,128)(2,1)S(1)} %get-tuple-element.55.refs_2_, bf16[2,384,512]{2,1,0:T(8,128)(2,1)S(1)} %factors.1.refs_1_.refs_3_, ...), custom_call_target="tpu_custom_call" | custom-call | tf_op jit(solution)/shard_map/gram/pallas_call | solution.py:140
  114.1 3.3 %collective-permute-done.18.refs_2_.refs_4_ = bf16[2,32,2048]{2,1,0:T(8,128)(2,1)S(1)} collective-permute-done((bf16[2,32,2048]{2,1,0:T(8,128)(2,1)S(1)}, bf16[2,32,2048]{2,1,0:T(8,128)(2,1)S(1)}, u32[]{:S(2)}, u32[]{:S(2)}) %collective-permute-start.18) | collective-permute-done | bytes 262176 | tf_op jit(solution)/shard_map/ppermute | solution.py:44
  117.5 0.1 collective-permute-start.22
  117.6 0.5 collective-permute-start.23
  118.1 0.0 collective-permute-done.25.refs_6_
  118.1 2.7 %gram_late.1 = (f32[1,3,512,512]{3,2,1,0:T(8,128)S(1)}, f32[16,128]{1,0:T(8,128)S(1)}) custom-call(s32[2]{0:T(128)S(1)} %pad_add_fusion.refs_0_, f32[16,128]{1,0:T(8,128)S(1)} %get-tuple-element.56.refs_4_.refs_1_, f32[3,3,512,512]{3,2,1,0:T(8,128)S(1)} %get-tuple-element.59.refs_2_.refs_5_, bf16[4,8,32,512]{3,2,1,0:T(8,128)(2,1)S(1)} %get-tuple-element.54.refs_1_.refs_3_, ...), custom_call_target="tpu_custom_call" | custom-call | tf_op jit(solution)/shard_map/gram_late/pallas_call | solution.py:140
  120.8 1.5 %collective-permute-start.26 = (f32[16,128]{1,0:T(8,128)S(1)}, f32[16,128]{1,0:T(8,128)S(1)}, u32[]{:S(2)}, u32[]{:S(2)}) collective-permute-start(f32[16,128]{1,0:T(8,128)S(1)} %get-tuple-element.62.refs_8_.refs_1_), channel_id=1, source_target_pairs={{0,1},{1,0},{2,3},{3,2},{4,5},{5,4},{6,7},{7,6},{8,9},{9,8},{10,11... | collective-permute-start | bytes 24584 | tf_op jit(solution)/shard_map/ppermute | solution.py:38
  122.3 0.8 collective-permute-start.27
  123.1 1.2 collective-permute-start.28
  124.4 1.7 %unplace.1.refs_9_ = bf16[1,128,2048]{2,1,0:T(8,128)(2,1)} custom-call(s32[2]{0:T(128)S(1)} %pad_add_fusion.refs_0_, bf16[144,512]{1,0:T(8,128)(2,1)S(1)} %get-tuple-element.33.refs_1_, bf16[2,32,2048]{2,1,0:T(8,128)(2,1)S(1)} %get-tuple-element.50.refs_0_.refs_2_, bf16[2,32,2048]{2,1,0:T(8,128)(2,1)S(1)} %collective-permute-done.17.refs_1_.refs_3_, ...), custom_call_target="tpu_custom_call" | custom-call | tf_op jit(solution)/shard_map/unplace/pallas_call | solution.py:140
  126.1 1.6 %collective-permute-done.28.refs_4_ = f32[16,128]{1,0:T(8,128)S(1)} collective-permute-done((f32[16,128]{1,0:T(8,128)S(1)}, f32[16,128]{1,0:T(8,128)S(1)}, u32[]{:S(2)}, u32[]{:S(2)}) %collective-permute-start.28) | collective-permute-done | bytes 8224 | tf_op jit(solution)/shard_map/ppermute | solution.py:38
  127.7 1.0 copy-done.3
  128.7 4.9 %adam.1 = f32[1,3,512,512]{3,2,1,0:T(8,128)} custom-call(s32[2]{0:T(128)S(1)} %pad_add_fusion.refs_0_, f32[16,128]{1,0:T(8,128)S(1)} %get-tuple-element.62.refs_8_.refs_1_, f32[16,128]{1,0:T(8,128)S(1)} %collective-permute-done.26.refs_2_, f32[16,128]{1,0:T(8,128)S(1)} %collective-permute-done.27.refs_3_, f32[16,128]{1,0:T(8,128)S(1)} %collective-permute-done.28.refs_4_, ...), custom_call_target="tpu_custom_call" | custom-call | tf_op jit(solution)/shard_map/adam/pallas_call | solution.py:140
  (27 shorter events, 0.1 us)
Async XLA Ops:
  0.6 59.5 %copy-start = (bf16[1,1,256,2048]{3,2,1,0:T(8,128)(2,1)S(1)}, bf16[1,1,256,2048]{3,2,1,0:T(8,128)(2,1)}, u32[]{:S(2)}) copy-start(bf16[1,1,256,2048]{3,2,1,0:T(8,128)(2,1)} %param.15) | copy-start | bytes 3145732
  2.0 39.4 %collective-permute-start = (bf16[2,512,512]{2,1,0:T(8,128)(2,1)S(1)}, bf16[2,512,512]{2,1,0:T(8,128)(2,1)S(1)}, u32[]{:S(2)}, u32[]{:S(2)}) collective-permute-start(bf16[2,512,512]{2,1,0:T(8,128)(2,1)S(1)} %slice_bitcast_fusion.refs_2_), channel_id=1, source_target_pairs={{0,1},{1,0},{2,3},{3,2},{4,5},{5,4},{6,7},{7,6},{8,9},{9,8},{10,11... | collective-permute-start | bytes 3145736 | tf_op jit(solution)/shard_map/ppermute | solution.py:38
  5.0 36.4 %collective-permute-start.1 = (bf16[2,512,512]{2,1,0:T(8,128)(2,1)S(1)}, bf16[2,512,512]{2,1,0:T(8,128)(2,1)}, u32[]{:S(2)}, u32[]{:S(2)}) collective-permute-start(bf16[2,512,512]{2,1,0:T(8,128)(2,1)S(1)} %slice_bitcast_fusion.refs_2_), channel_id=1, source_target_pairs={{0,2},{1,3},{2,0},{3,1},{4,6},{5,7},{6,4},{7,5},{8,10},{9,11},{10,... | collective-permute-start | bytes 3145736 | tf_op jit(solution)/shard_map/ppermute | solution.py:38
  7.3 1.0 copy-start.4
  8.3 0.7 copy-start.5
  9.0 0.7 copy-start.6
  10.3 21.8 %collective-permute-start.2 = (bf16[144,512]{1,0:T(8,128)(2,1)S(1)}, bf16[144,512]{1,0:T(8,128)(2,1)S(1)}, u32[]{:S(2)}, u32[]{:S(2)}) collective-permute-start(bf16[144,512]{1,0:T(8,128)(2,1)S(1)} %get-tuple-element.34), channel_id=1, source_target_pairs={{0,1},{1,0},{2,3},{3,2},{4,5},{5,4},{6,7},{7,6},{8,9},{9,8},{10,11... | collective-permute-start | bytes 442376 | tf_op jit(solution)/shard_map/ppermute | solution.py:38
  10.9 25.0 %collective-permute-start.3 = (bf16[144,512]{1,0:T(8,128)(2,1)S(1)}, bf16[144,512]{1,0:T(8,128)(2,1)S(1)}, u32[]{:S(2)}, u32[]{:S(2)}) collective-permute-start(bf16[144,512]{1,0:T(8,128)(2,1)S(1)} %get-tuple-element.35), channel_id=1, source_target_pairs={{0,2},{1,3},{2,0},{3,1},{4,6},{5,7},{6,4},{7,5},{8,10},{9,11},{10,... | collective-permute-start | bytes 442376 | tf_op jit(solution)/shard_map/ppermute | solution.py:38
  11.0 25.0 %collective-permute-start.4 = (bf16[144,512]{1,0:T(8,128)(2,1)S(1)}, bf16[144,512]{1,0:T(8,128)(2,1)S(1)}, u32[]{:S(2)}, u32[]{:S(2)}) collective-permute-start(bf16[144,512]{1,0:T(8,128)(2,1)S(1)} %get-tuple-element.36), channel_id=1, source_target_pairs={{0,3},{1,2},{2,1},{3,0},{4,7},{5,6},{6,5},{7,4},{8,11},{9,10},{10,... | collective-permute-start | bytes 442376 | tf_op jit(solution)/shard_map/ppermute | solution.py:38
  37.0 11.2 %collective-permute-start.7 = (bf16[2,4,32,512]{3,2,1,0:T(8,128)(2,1)S(1)}, bf16[2,4,32,512]{3,2,1,0:T(8,128)(2,1)S(1)}, u32[]{:S(2)}, u32[]{:S(2)}) collective-permute-start(bf16[2,4,32,512]{3,2,1,0:T(8,128)(2,1)S(1)} %get-tuple-element.40), channel_id=1, source_target_pairs={{0,8},{4,12},{8,0},{12,4},{16,24},{20,28},{24,16},{28,20},{1,9},{5... | collective-permute-start | bytes 786440 | tf_op jit(solution)/shard_map/ppermute | solution.py:44
  38.6 21.4 %collective-permute-start.8 = (bf16[2,4,32,512]{3,2,1,0:T(8,128)(2,1)S(1)}, bf16[2,4,32,512]{3,2,1,0:T(8,128)(2,1)S(1)}, u32[]{:S(2)}, u32[]{:S(2)}) collective-permute-start(bf16[2,4,32,512]{3,2,1,0:T(8,128)(2,1)S(1)} %get-tuple-element.41), channel_id=1, source_target_pairs={{0,16},{4,20},{8,24},{12,28},{16,0},{20,4},{24,8},{28,12},{1,17},{... | collective-permute-start | bytes 786440 | tf_op jit(solution)/shard_map/ppermute | solution.py:44
  41.2 18.8 %collective-permute-start.9 = (bf16[2,4,32,512]{3,2,1,0:T(8,128)(2,1)S(1)}, bf16[2,4,32,512]{3,2,1,0:T(8,128)(2,1)S(1)}, u32[]{:S(2)}, u32[]{:S(2)}) collective-permute-start(bf16[2,4,32,512]{3,2,1,0:T(8,128)(2,1)S(1)} %get-tuple-element.42), channel_id=1, source_target_pairs={{0,24},{4,28},{8,16},{12,20},{16,8},{20,12},{24,0},{28,4},{1,25},{... | collective-permute-start | bytes 786440 | tf_op jit(solution)/shard_map/ppermute | solution.py:44
  42.7 23.4 %collective-permute-start.5 = (bf16[512,512]{1,0:T(8,128)(2,1)S(1)}, bf16[512,512]{1,0:T(8,128)(2,1)S(1)}, u32[]{:S(2)}, u32[]{:S(2)}) collective-permute-start(bf16[512,512]{1,0:T(8,128)(2,1)S(1)} %get-tuple-element.38), channel_id=1, source_target_pairs={{0,1},{1,0},{2,3},{3,2},{4,5},{5,4},{6,7},{7,6},{8,9},{9,8},{10,11... | collective-permute-start | bytes 1572872 | tf_op jit(solution)/shard_map/ppermute | solution.py:38
  44.0 23.6 %collective-permute-start.6 = (bf16[512,512]{1,0:T(8,128)(2,1)S(1)}, bf16[512,512]{1,0:T(8,128)(2,1)S(1)}, u32[]{:S(2)}, u32[]{:S(2)}) collective-permute-start(bf16[512,512]{1,0:T(8,128)(2,1)S(1)} %get-tuple-element.39), channel_id=1, source_target_pairs={{0,2},{1,3},{2,0},{3,1},{4,6},{5,7},{6,4},{7,5},{8,10},{9,11},{10,... | collective-permute-start | bytes 1572872 | tf_op jit(solution)/shard_map/ppermute | solution.py:38
  60.0 8.6 %collective-permute-start.10 = (bf16[4,4,32,512]{3,2,1,0:T(8,128)(2,1)S(1)}, bf16[4,4,32,512]{3,2,1,0:T(8,128)(2,1)S(1)}, u32[]{:S(2)}, u32[]{:S(2)}) collective-permute-start(bf16[4,4,32,512]{3,2,1,0:T(8,128)(2,1)S(1)} %pick.2), channel_id=1, source_target_pairs={{0,4},{4,0},{8,12},{12,8},{16,20},{20,16},{24,28},{28,24},{1,5},{5... | collective-permute-start | bytes 1572872 | tf_op jit(solution)/shard_map/ppermute | solution.py:68
  60.7 11.3 %collective-permute-start.14 = (bf16[256,512]{1,0:T(8,128)(2,1)S(1)}, bf16[256,512]{1,0:T(8,128)(2,1)S(1)}, u32[]{:S(2)}, u32[]{:S(2)}) collective-permute-start(bf16[256,512]{1,0:T(8,128)(2,1)S(1)} %get-tuple-element.47), channel_id=1, source_target_pairs={{0,1},{1,0},{2,3},{3,2},{4,5},{5,4},{6,7},{7,6},{8,9},{9,8},{10,11... | collective-permute-start | bytes 786440 | tf_op jit(solution)/shard_map/ppermute | solution.py:38
  62.0 14.6 %collective-permute-start.15 = (bf16[256,512]{1,0:T(8,128)(2,1)S(1)}, bf16[256,512]{1,0:T(8,128)(2,1)S(1)}, u32[]{:S(2)}, u32[]{:S(2)}) collective-permute-start(bf16[256,512]{1,0:T(8,128)(2,1)S(1)} %get-tuple-element.48), channel_id=1, source_target_pairs={{0,2},{1,3},{2,0},{3,1},{4,6},{5,7},{6,4},{7,5},{8,10},{9,11},{10,... | collective-permute-start | bytes 786440 | tf_op jit(solution)/shard_map/ppermute | solution.py:38
  66.2 10.5 %collective-permute-start.16 = (bf16[256,512]{1,0:T(8,128)(2,1)S(1)}, bf16[256,512]{1,0:T(8,128)(2,1)S(1)}, u32[]{:S(2)}, u32[]{:S(2)}) collective-permute-start(bf16[256,512]{1,0:T(8,128)(2,1)S(1)} %get-tuple-element.49), channel_id=1, source_target_pairs={{0,3},{1,2},{2,1},{3,0},{4,7},{5,6},{6,5},{7,4},{8,11},{9,10},{10,... | collective-permute-start | bytes 786440 | tf_op jit(solution)/shard_map/ppermute | solution.py:38
  69.9 11.8 %collective-permute-start.11 = (bf16[256,512]{1,0:T(8,128)(2,1)S(1)}, bf16[256,512]{1,0:T(8,128)(2,1)S(1)}, u32[]{:S(2)}, u32[]{:S(2)}) collective-permute-start(bf16[256,512]{1,0:T(8,128)(2,1)S(1)} %get-tuple-element.44), channel_id=1, source_target_pairs={{0,1},{1,0},{2,3},{3,2},{4,5},{5,4},{6,7},{7,6},{8,9},{9,8},{10,11... | collective-permute-start | bytes 786440 | tf_op jit(solution)/shard_map/ppermute | solution.py:38
  71.2 16.1 %collective-permute-start.12 = (bf16[256,512]{1,0:T(8,128)(2,1)S(1)}, bf16[256,512]{1,0:T(8,128)(2,1)S(1)}, u32[]{:S(2)}, u32[]{:S(2)}) collective-permute-start(bf16[256,512]{1,0:T(8,128)(2,1)S(1)} %get-tuple-element.45), channel_id=1, source_target_pairs={{0,2},{1,3},{2,0},{3,1},{4,6},{5,7},{6,4},{7,5},{8,10},{9,11},{10,... | collective-permute-start | bytes 786440 | tf_op jit(solution)/shard_map/ppermute | solution.py:38
  72.0 15.3 %collective-permute-start.13 = (bf16[256,512]{1,0:T(8,128)(2,1)S(1)}, bf16[256,512]{1,0:T(8,128)(2,1)S(1)}, u32[]{:S(2)}, u32[]{:S(2)}) collective-permute-start(bf16[256,512]{1,0:T(8,128)(2,1)S(1)} %get-tuple-element.46), channel_id=1, source_target_pairs={{0,3},{1,2},{2,1},{3,0},{4,7},{5,6},{6,5},{7,4},{8,11},{9,10},{10,... | collective-permute-start | bytes 786440 | tf_op jit(solution)/shard_map/ppermute | solution.py:38
  87.7 19.0 %collective-permute-start.20 = (bf16[2,384,512]{2,1,0:T(8,128)(2,1)S(1)}, bf16[2,384,512]{2,1,0:T(8,128)(2,1)S(1)}, u32[]{:S(2)}, u32[]{:S(2)}) collective-permute-start(bf16[2,384,512]{2,1,0:T(8,128)(2,1)S(1)} %factors.1.refs_1_.refs_3_), channel_id=1, source_target_pairs={{0,1},{1,0},{2,3},{3,2},{4,5},{5,4},{6,7},{7,6},{8,9},{9,8},{10,11... | collective-permute-start | bytes 2359304 | tf_op jit(solution)/shard_map/ppermute | solution.py:38
  88.6 19.2 %collective-permute-start.21 = (bf16[2,384,512]{2,1,0:T(8,128)(2,1)S(1)}, bf16[2,384,512]{2,1,0:T(8,128)(2,1)S(1)}, u32[]{:S(2)}, u32[]{:S(2)}) collective-permute-start(bf16[2,384,512]{2,1,0:T(8,128)(2,1)S(1)} %factors.1.refs_1_.refs_3_), channel_id=1, source_target_pairs={{0,2},{1,3},{2,0},{3,1},{4,6},{5,7},{6,4},{7,5},{8,10},{9,11},{10,... | collective-permute-start | bytes 2359304 | tf_op jit(solution)/shard_map/ppermute | solution.py:38
  92.1 22.0 %collective-permute-start.17 = (bf16[2,32,2048]{2,1,0:T(8,128)(2,1)S(1)}, bf16[2,32,2048]{2,1,0:T(8,128)(2,1)S(1)}, u32[]{:S(2)}, u32[]{:S(2)}) collective-permute-start(bf16[2,32,2048]{2,1,0:T(8,128)(2,1)S(1)} %get-tuple-element.51), channel_id=1, source_target_pairs={{0,8},{4,12},{8,0},{12,4},{16,24},{20,28},{24,16},{28,20},{1,9},{5... | collective-permute-start | bytes 786440 | tf_op jit(solution)/shard_map/ppermute | solution.py:44
  96.1 21.4 %collective-permute-start.18 = (bf16[2,32,2048]{2,1,0:T(8,128)(2,1)S(1)}, bf16[2,32,2048]{2,1,0:T(8,128)(2,1)S(1)}, u32[]{:S(2)}, u32[]{:S(2)}) collective-permute-start(bf16[2,32,2048]{2,1,0:T(8,128)(2,1)S(1)} %get-tuple-element.52), channel_id=1, source_target_pairs={{0,16},{4,20},{8,24},{12,28},{16,0},{20,4},{24,8},{28,12},{1,17},{... | collective-permute-start | bytes 786440 | tf_op jit(solution)/shard_map/ppermute | solution.py:44
  97.2 20.3 %collective-permute-start.19 = (bf16[2,32,2048]{2,1,0:T(8,128)(2,1)S(1)}, bf16[2,32,2048]{2,1,0:T(8,128)(2,1)S(1)}, u32[]{:S(2)}, u32[]{:S(2)}) collective-permute-start(bf16[2,32,2048]{2,1,0:T(8,128)(2,1)S(1)} %get-tuple-element.53), channel_id=1, source_target_pairs={{0,24},{4,28},{8,16},{12,20},{16,8},{20,12},{24,0},{28,4},{1,25},{... | collective-permute-start | bytes 786440 | tf_op jit(solution)/shard_map/ppermute | solution.py:44
  107.8 10.2 %collective-permute-start.24 = (bf16[384,512]{1,0:T(8,128)(2,1)S(1)}, bf16[384,512]{1,0:T(8,128)(2,1)S(1)}, u32[]{:S(2)}, u32[]{:S(2)}) collective-permute-start(bf16[384,512]{1,0:T(8,128)(2,1)S(1)} %get-tuple-element.60), channel_id=1, source_target_pairs={{0,1},{1,0},{2,3},{3,2},{4,5},{5,4},{6,7},{7,6},{8,9},{9,8},{10,11... | collective-permute-start | bytes 1179656 | tf_op jit(solution)/shard_map/ppermute | solution.py:38
  108.6 9.5 %collective-permute-start.25 = (bf16[384,512]{1,0:T(8,128)(2,1)S(1)}, bf16[384,512]{1,0:T(8,128)(2,1)S(1)}, u32[]{:S(2)}, u32[]{:S(2)}) collective-permute-start(bf16[384,512]{1,0:T(8,128)(2,1)S(1)} %get-tuple-element.61), channel_id=1, source_target_pairs={{0,2},{1,3},{2,0},{3,1},{4,6},{5,7},{6,4},{7,5},{8,10},{9,11},{10,... | collective-permute-start | bytes 1179656 | tf_op jit(solution)/shard_map/ppermute | solution.py:38
  117.5 6.9 %collective-permute-start.22 = (bf16[2,32,2048]{2,1,0:T(8,128)(2,1)S(1)}, bf16[2,32,2048]{2,1,0:T(8,128)(2,1)S(1)}, u32[]{:S(2)}, u32[]{:S(2)}) collective-permute-start(bf16[2,32,2048]{2,1,0:T(8,128)(2,1)S(1)} %get-tuple-element.57), channel_id=1, source_target_pairs={{0,4},{4,0},{8,12},{12,8},{16,20},{20,16},{24,28},{28,24},{1,5},{5... | collective-permute-start | bytes 786440 | tf_op jit(solution)/shard_map/ppermute | solution.py:68
  117.6 6.8 %collective-permute-start.23 = (bf16[2,32,2048]{2,1,0:T(8,128)(2,1)S(1)}, bf16[2,32,2048]{2,1,0:T(8,128)(2,1)S(1)}, u32[]{:S(2)}, u32[]{:S(2)}) collective-permute-start(bf16[2,32,2048]{2,1,0:T(8,128)(2,1)S(1)} %get-tuple-element.58), channel_id=1, source_target_pairs={{0,4},{4,0},{8,12},{12,8},{16,20},{20,16},{24,28},{28,24},{1,5},{5... | collective-permute-start | bytes 786440 | tf_op jit(solution)/shard_map/ppermute | solution.py:68
  118.1 9.6 %copy-start.1 = (f32[1,3,512,512]{3,2,1,0:T(8,128)S(1)}, f32[1,3,512,512]{3,2,1,0:T(8,128)}, u32[]{:S(2)}) copy-start(f32[1,3,512,512]{3,2,1,0:T(8,128)} %refs_7_.1) | copy-start | bytes 9437188
  118.1 9.6 %copy-start.2 = (f32[1,3,512,512]{3,2,1,0:T(8,128)S(1)}, f32[1,3,512,512]{3,2,1,0:T(8,128)}, u32[]{:S(2)}) copy-start(f32[1,3,512,512]{3,2,1,0:T(8,128)} %refs_8_.1) | copy-start | bytes 9437188
  120.8 5.3 %collective-permute-start.26 = (f32[16,128]{1,0:T(8,128)S(1)}, f32[16,128]{1,0:T(8,128)S(1)}, u32[]{:S(2)}, u32[]{:S(2)}) collective-permute-start(f32[16,128]{1,0:T(8,128)S(1)} %get-tuple-element.62.refs_8_.refs_1_), channel_id=1, source_target_pairs={{0,1},{1,0},{2,3},{3,2},{4,5},{5,4},{6,7},{7,6},{8,9},{9,8},{10,11... | collective-permute-start | bytes 24584 | tf_op jit(solution)/shard_map/ppermute | solution.py:38
  122.3 3.8 %collective-permute-start.27 = (f32[16,128]{1,0:T(8,128)S(1)}, f32[16,128]{1,0:T(8,128)S(1)}, u32[]{:S(2)}, u32[]{:S(2)}) collective-permute-start(f32[16,128]{1,0:T(8,128)S(1)} %get-tuple-element.62.refs_8_.refs_1_), channel_id=1, source_target_pairs={{0,2},{1,3},{2,0},{3,1},{4,6},{5,7},{6,4},{7,5},{8,10},{9,11},{10,... | collective-permute-start | bytes 24584 | tf_op jit(solution)/shard_map/ppermute | solution.py:38
  123.1 4.5 %collective-permute-start.28 = (f32[16,128]{1,0:T(8,128)S(1)}, f32[16,128]{1,0:T(8,128)S(1)}, u32[]{:S(2)}, u32[]{:S(2)}) collective-permute-start(f32[16,128]{1,0:T(8,128)S(1)} %get-tuple-element.62.refs_8_.refs_1_), channel_id=1, source_target_pairs={{0,3},{1,2},{2,1},{3,0},{4,7},{5,6},{6,5},{7,4},{8,11},{9,10},{10,... | collective-permute-start | bytes 24584 | tf_op jit(solution)/shard_map/ppermute | solution.py:38
  127.7 1.0 copy-start.3

commit v5 on v4

--- a/solution.py
+++ b/solution.py
@@ -80,6 +80,10 @@
     return [parts[0]] + [from_peer(part, k) for k, part in enumerate(parts) if k]
 
 
+def copy_kernel(weights_ref, out_ref):
+    out_ref[...] = weights_ref[0, pl.ds(0, out_ref.shape[0])]
+
+
 def cut_kernel(from_two_ref, from_one_ref, first_ref, second_ref):
     first_ref[...] = from_two_ref[0]
     second_ref[...] = from_one_ref[1]
@@ -129,7 +133,7 @@
 
 
 def call(
-    kernel, name, operands, specs, outs, out_specs=None, grid=(), scratch=(), after=(), cost=0
+    kernel, name, operands, specs, outs, out_specs=None, grid=(), scratch=(), after=(), cost=0, room=0
 ):
     size = sum(x.size * x.dtype.itemsize for x in list(operands) + list(outs))
     taken = len(operands)
@@ -140,13 +144,13 @@
     return pl.pallas_call(
         body,
         grid=grid,
-        in_specs=list(specs) + [pl.BlockSpec(memory_space=pl.ANY)] * len(after),
+        in_specs=list(specs) + [VMEM] * len(after),
         out_specs=out_specs if out_specs is not None else [VMEM for _ in outs],
         out_shape=outs,
         scratch_shapes=list(scratch),
         compiler_params=pltpu.CompilerParams(
             dimension_semantics=("arbitrary",) * len(grid),
-            vmem_limit_bytes=min(56 * MIB, size + 8 * MIB),
+            vmem_limit_bytes=max(room, min(56 * MIB, size + 8 * MIB)),
         ),
         cost_estimate=pl.CostEstimate(flops=0, bytes_accessed=cost, transcendentals=0),
         name=name,
@@ -157,7 +161,7 @@
     return pl.ds(pl.multiple_of((pos_ref[0] ^ offset) * width, width), width)
 
 
-def rows_kernel(expert_count, pos_ref, ids_ref, task_ref, row_ref, grads_ref, *out_refs):
+def rows_kernel(expert_count, pos_ref, ids_ref, task_ref, row_ref, grads_ref, inputs_ref, *out_refs):
     row_count = grads_ref.shape[0]
     seg_rows = out_refs[0].shape[1]
     block_count = ids_ref.shape[1]
@@ -188,11 +192,8 @@
                 (LABEL_ROWS, seg_rows), jnp.bfloat16
             )
         out_ref[pl.ds(row_count, LABEL_ROWS), pl.ds(0, row_count)] = labels
-
-
-def split_kernel(pos_ref, matrix_ref, *out_refs):
-    for offset, out_ref in enumerate(out_refs):
-        out_ref[...] = matrix_ref[:, segment(pos_ref, offset, out_ref.shape[1])]
+        head = row_count + LABEL_ROWS
+        out_ref[pl.ds(head, inputs_ref.shape[0]), :] = inputs_ref[:, columns]
 
 
 def one_hot(block_ref, row_count, slot_count, capacity):
@@ -202,11 +203,10 @@
     return jnp.where(places == slot, 1.0, 0.0).astype(jnp.bfloat16)
 
 
-def place_kernel(count, pos_ref, *refs):
+def place_kernel(count, row_count, pos_ref, *refs):
     block_refs, out_refs, placed_ref = refs[:count], refs[count:-1], refs[-1]
     _, expert_count, capacity, seg_rows = placed_ref.shape
     slot_count = expert_count * capacity
-    row_count = block_refs[0].shape[0] - LABEL_ROWS
     for offset, block_ref in enumerate(block_refs):
         placing = one_hot(block_ref, row_count, slot_count, capacity)
         placed = multiply(placing, block_ref[pl.ds(0, row_count), :])
@@ -304,15 +304,16 @@
     incoming_ref, operand_refs, grads_ref, gram_ref = refs[0], refs[1:-2], refs[-2], refs[-1]
     middle = incoming_ref.shape[1] // 2
     seg_rows, hidden_width = grads_ref.shape[2:]
+    slot_count = incoming_ref.shape[1] * incoming_ref.shape[2]
     groups = regroup(operand_refs, lengths)
     for at, offset in enumerate(offsets):
         (inputs_ref,), factor_refs = groups[2 * at : 2 * at + 2]
-        slot_count = inputs_ref.shape[0]
         rest = pl.ds(slot_count, slot_count // 2)
+        columns = inputs_ref[pl.ds(inputs_ref.shape[0] - slot_count, slot_count), :]
         gate_ref, up_ref = (ref.at[pl.ds(0, slot_count)] for ref in halves(factor_refs))
         first_ref, second_ref = (ref.at[rest] for ref in halves(factor_refs))
-        grads_ref[at, 0] = contract_first(inputs_ref[...], gate_ref[...])
-        grads_ref[at, 1] = contract_first(inputs_ref[...], up_ref[...])
+        grads_ref[at, 0] = contract_first(columns, gate_ref[...])
+        grads_ref[at, 1] = contract_first(columns, up_ref[...])
         grads_ref[at, 2] = contract_first(
             flat_rows(incoming_ref[offset, :middle]), first_ref[...]
         ) + contract_first(flat_rows(incoming_ref[offset, middle:]), second_ref[...])
@@ -375,7 +376,7 @@
     first_ref, second_ref, step_ref, coef_ref = refs[count + len(places) :]
     hidden_width = step_ref.shape[3]
 
-    @pl.when(pl.program_id(0) == 0)
+    @pl.when((pl.program_id(0) == 0) & (pl.program_id(1) == 0))
     def _():
         sums = gram_refs[0][...]
         for gram_ref in gram_refs[1:]:
@@ -390,10 +391,12 @@
 
     def step(index, _):
         rows = pl.ds(pl.multiple_of(index * lines, lines), lines)
+        start = pl.program_id(1) * step_ref.shape[2] + index * lines
+        grad_rows = pl.ds(pl.multiple_of(start, lines), lines)
         merged = None
         for grads_ref, offsets in zip(grads_refs, places):
             for at, offset in enumerate(offsets):
-                part = grads_ref[at, matrix, rows] * coef_ref[pos_ref[0] ^ offset]
+                part = grads_ref[at, matrix, grad_rows] * coef_ref[pos_ref[0] ^ offset]
                 merged = part if merged is None else merged + part
         first_new = (beta_first / first_fix) * first_ref[0, 0, rows] + (
             (1.0 - beta_first) / first_fix
@@ -480,7 +483,8 @@
     count = sum(len(group) for group in groups)
     seg_rows, hidden_width = first_moment.shape[2:]
     grams = exchange([gram] * count)
-    moment_spec = pl.BlockSpec((1, 1, seg_rows, hidden_width), lambda m: (0, m, 0, 0))
+    tile = min(seg_rows, 256)
+    moment_spec = pl.BlockSpec((1, 1, tile, hidden_width), lambda m, d: (0, m, d, 0))
     (adam_step,) = call(
         functools.partial(adam_kernel, count, groups),
         "adam",
@@ -488,7 +492,7 @@
         [SMEM] + [VMEM] * (len(grams) + len(grads)) + [moment_spec, moment_spec],
         [jax.ShapeDtypeStruct(first_moment.shape, jnp.float32)],
         out_specs=[moment_spec],
-        grid=(3,),
+        grid=(3, seg_rows // tile),
         scratch=[pltpu.VMEM((count, 1, hidden_width), jnp.float32)],
         after=after,
     )
@@ -512,33 +516,36 @@
     rep = jnp.stack([lax.axis_index("replica"), lax.axis_index("expert")]).astype(jnp.int32)
     shape = jax.ShapeDtypeStruct
 
-    block = shape((row_count + LABEL_ROWS, seg_rows), jnp.bfloat16)
+    inputs_home = saved_inputs[0, 0]
+    head = row_count + LABEL_ROWS
+    block = shape((head + slot_count, seg_rows), jnp.bfloat16)
+    small = [routes[0].reshape(1, row_count), out_grads[0], inputs_home]
     row_blocks = call(
         functools.partial(rows_kernel, expert_count),
         "rows",
-        [rep, task_ids, task_weights, routes[0].reshape(1, row_count), out_grads[0]],
-        [SMEM, SMEM, SMEM, VMEM, VMEM],
+        [rep, task_ids, task_weights, *small],
+        [SMEM] * 3 + [pl.BlockSpec(x.shape, lambda i: (0, 0)) for x in small],
         [block for _ in offsets],
+        grid=(1,),
+        room=56 * MIB,
     )
     routed = exchange(row_blocks)
 
-    near_projections = gather_near(weights[0, :2])
-
-    inputs_home = saved_inputs[0, 0]
-    inputs = exchange(
-        call(
-            split_kernel,
-            "split",
-            [rep, inputs_home],
-            [SMEM, VMEM],
-            [shape((slot_count, seg_rows), jnp.bfloat16) for _ in offsets],
-        )
-    )
+    pair = (2, seg_rows, hidden_width)
+    (own_projections,) = call(
+        copy_kernel,
+        "projections",
+        [weights],
+        [VMEM],
+        [shape(pair, jnp.bfloat16)],
+        after=routed[1:],
+    )
+    near_projections = gather_near(own_projections)
 
     part = shape((2, rep_count, capacity, seg_rows), jnp.bfloat16)
     placed = (
         call(
-            functools.partial(place_kernel, rep_count),
+            functools.partial(place_kernel, rep_count, row_count),
             "place",
             [rep, *routed],
             [SMEM] + [VMEM] * len(routed),
@@ -579,7 +586,6 @@
         [SMEM] + [VMEM] * (1 + len(came)),
         [shape((rep_count, expert_count, capacity, seg_rows), jnp.bfloat16)]
         + [shape(back_shape, jnp.bfloat16 if k else jnp.float32) for k in offsets],
-        after=[forward],
     )
     back = exchange(back)
     (own_factors,) = call(
@@ -588,7 +594,6 @@
         [forward, *back],
         [VMEM] * (1 + len(back)),
         [shape((2, slot_count + half, hidden_width), jnp.bfloat16)],
-        after=inputs[1:],
     )
     near_factors = gather_near(own_factors)
 
@@ -607,7 +612,7 @@
     )
     factors = gather_rest(near_factors, after=returning[:1])
     if rep_count <= 4:
-        *merging, first_gram = adasum(rep, inputs, incoming, factors)
+        *merging, first_gram = adasum(rep, routed, incoming, factors)
         returned = finish_spread(returning, [first_gram], pieces=2)
         unplace_after = merging[2:]
     else:
@@ -622,10 +627,10 @@
         after=unplace_after,
     )
     if rep_count <= 4:
-        adam_step = adam(rep, *merging, first_moment, second_moment, [input_grads])
+        adam_step = adam(rep, *merging, first_moment, second_moment, ())
     else:
         adam_step = adasum_adam_many(
-            rep, inputs, incoming, factors, first_moment, second_moment
+            rep, [x[head:] for x in routed], incoming, factors, first_moment, second_moment
         )
     return (input_grads, adam_step)
 

time: 135 us -> 127 us (0.941)
  starting transfers between devices: 36.3 us -> 31.3 us
  local copies, waits for them, and re-layouts: 5.86 us -> 2.51 us
    ppermute x20 -> x17, starting transfers between devices: 24.8 us -> 20.3 us  [from_peer(): lax.ppermute(array, 'replica', [(i, i ^ offset) for i in range(count)])]
    ppermute x6, waiting for transfers between devices: 18.5 us -> 21.4 us  [across_chips(): lax.ppermute(part, 'expert', [(i, i ^ 2 * k) for i in range(count)])]
    unnamed x14 -> x12, local copies, waits for them, and re-layouts: 3.41 us -> 1.43 us
    ppermute x20 -> x17, waiting for transfers between devices: 46.8 us -> 44.8 us  [from_peer(): lax.ppermute(array, 'replica', [(i, i ^ offset) for i in range(count)])]
    squeeze x1 -> x0, local copies, waits for them, and re-layouts: 1.38 us -> none  [shards(): near_projections = gather_near(weights[0, :2])]
  transfers between devices with their start and end apart: 29 -> 26, of which waited for: 11 -> 15; matrix products, arithmetic and copies ran while one was open for 1% -> 1% of each run, Pallas kernels for 14% -> 12%
where the time goes in v5:
time: 127 us; the launch traced here: 126 us
  waiting for transfers between devices  66.2 us (52%)
  starting transfers between devices  31.3 us (25%)
  Pallas kernels  23.9 us (19%)
  local copies, waits for them, and re-layouts  2.51 us (2%)
  between operations  1.44 us (1%)
    ppermute x17, waiting for transfers between devices, from_peer(): lax.ppermute(array, 'replica', [(i, i ^ offset) for i in range(count)])  44.8 us
    pallas_call x16, Pallas kernels, call(): pl.pallas_call(body, grid=grid, in_specs=list(specs) + [VMEM] * len(after...  23.9 us
    ppermute x6, waiting for transfers between devices, across_chips(): lax.ppermute(part, 'expert', [(i, i ^ 2 * k) for i in range(count)])  21.4 us
    ppermute x17, starting transfers between devices, from_peer(): lax.ppermute(array, 'replica', [(i, i ^ offset) for i in range(count)])  20.3 us
    ppermute x6, starting transfers between devices, across_chips(): lax.ppermute(part, 'expert', [(i, i ^ 2 * k) for i in range(count)])  10.4 us
  transfers between devices with their start and end apart: 26, of which 15 were waited for; matrix products, arithmetic and copies ran while one was open for 1% of the time, Pallas kernels for 12%

profile of v5, /device:TPU:0, one launch (start us, length us, event | category | flops | bytes accessed | tf_op | source)
XLA Modules:
  0.0 126.1 jit_solution(3370106930503299362)
XLA Ops:
  1.3 0.6 pad_add_fusion.refs_0_
  1.9 2.7 %rows.1 = (bf16[400,512]{1,0:T(8,128)(2,1)}, bf16[400,512]{1,0:T(8,128)(2,1)}, bf16[400,512]{1,0:T(8,128)(2,1)}, bf16[400,512]{1,0:T(8,128)(2,1)}) custom-call(s32[2]{0:T(128)} %pad_add_fusion.refs_0_, s32[1,1]{1,0:T(1,128)S(6)} %copy.10.refs_1_, f32[8]{0:T(128)} %refs_2_.1, s32[1,128]{1,0:T(1,128)} %bitcast.11, bf16[128,2048]{1,0:T(8,128)(2,1)} %bitcast.10, ...), custom_call_target="tpu_custom_call" | custom-call | tf_op jit(solution)/shard_map/rows/pallas_call | solution.py:144
  4.7 2.9 %collective-permute-start = (bf16[400,512]{1,0:T(8,128)(2,1)}, bf16[400,512]{1,0:T(8,128)(2,1)S(1)}, u32[]{:S(2)}, u32[]{:S(2)}) collective-permute-start(bf16[400,512]{1,0:T(8,128)(2,1)} %get-tuple-element.30), channel_id=1, source_target_pairs={{0,1},{1,0},{2,3},{3,2},{4,5},{5,4},{6,7},{7,6},{8,9},{9,8},{10,11... | collective-permute-start | bytes 1228808 | tf_op jit(solution)/shard_map/ppermute | solution.py:38
  7.6 1.5 %collective-permute-start.1 = (bf16[400,512]{1,0:T(8,128)(2,1)}, bf16[400,512]{1,0:T(8,128)(2,1)S(1)}, u32[]{:S(2)}, u32[]{:S(2)}) collective-permute-start(bf16[400,512]{1,0:T(8,128)(2,1)} %get-tuple-element.31), channel_id=1, source_target_pairs={{0,2},{1,3},{2,0},{3,1},{4,6},{5,7},{6,4},{7,5},{8,10},{9,11},{10,... | collective-permute-start | bytes 1228808 | tf_op jit(solution)/shard_map/ppermute | solution.py:38
  9.1 0.0 collective-permute-start.2
  9.1 9.0 %collective-permute-done.refs_1_.refs_2_.refs_4_ = bf16[400,512]{1,0:T(8,128)(2,1)S(1)} collective-permute-done((bf16[400,512]{1,0:T(8,128)(2,1)}, bf16[400,512]{1,0:T(8,128)(2,1)S(1)}, u32[]{:S(2)}, u32[]{:S(2)}) %collective-permute-start) | collective-permute-done | bytes 409632 | tf_op jit(solution)/shard_map/ppermute | solution.py:38
  18.1 9.4 %collective-permute-done.1.refs_2_.refs_3_.refs_6_ = bf16[400,512]{1,0:T(8,128)(2,1)S(1)} collective-permute-done((bf16[400,512]{1,0:T(8,128)(2,1)}, bf16[400,512]{1,0:T(8,128)(2,1)S(1)}, u32[]{:S(2)}, u32[]{:S(2)}) %collective-permute-start.1) | collective-permute-done | bytes 409632 | tf_op jit(solution)/shard_map/ppermute | solution.py:38
  27.5 0.0 collective-permute-done.2.refs_3_.refs_4_
  27.5 1.4 %copy-done.4 = bf16[1,3,512,512]{3,2,1,0:T(8,128)(2,1)S(1)} copy-done((bf16[1,3,512,512]{3,2,1,0:T(8,128)(2,1)S(1)}, bf16[1,3,512,512]{3,2,1,0:T(8,128)(2,1)}, u32[]{:S(2)}) %copy-start.4) | copy-done | bytes 1572888
  28.9 0.1 projections.1.refs_2_
  29.0 1.6 %collective-permute-start.4 = (bf16[2,512,512]{2,1,0:T(8,128)(2,1)S(1)}, bf16[2,512,512]{2,1,0:T(8,128)(2,1)S(1)}, u32[]{:S(2)}, u32[]{:S(2)}) collective-permute-start(bf16[2,512,512]{2,1,0:T(8,128)(2,1)S(1)} %projections.1.refs_2_), channel_id=1, source_target_pairs={{0,2},{1,3},{2,0},{3,1},{4,6},{5,7},{6,4},{7,5},{8,10},{9,11},{10,... | collective-permute-start | bytes 3145736 | tf_op jit(solution)/shard_map/ppermute | solution.py:38
  30.6 0.5 collective-permute-start.3
  31.1 1.0 place.1
  32.1 1.6 %collective-permute-start.7 = (bf16[2,4,32,512]{3,2,1,0:T(8,128)(2,1)S(1)}, bf16[2,4,32,512]{3,2,1,0:T(8,128)(2,1)S(1)}, u32[]{:S(2)}, u32[]{:S(2)}) collective-permute-start(bf16[2,4,32,512]{3,2,1,0:T(8,128)(2,1)S(1)} %get-tuple-element.36), channel_id=1, source_target_pairs={{0,8},{4,12},{8,0},{12,4},{16,24},{20,28},{24,16},{28,20},{1,9},{5... | collective-permute-start | bytes 786440 | tf_op jit(solution)/shard_map/ppermute | solution.py:44
  33.8 2.6 %collective-permute-start.8 = (bf16[2,4,32,512]{3,2,1,0:T(8,128)(2,1)S(1)}, bf16[2,4,32,512]{3,2,1,0:T(8,128)(2,1)S(1)}, u32[]{:S(2)}, u32[]{:S(2)}) collective-permute-start(bf16[2,4,32,512]{3,2,1,0:T(8,128)(2,1)S(1)} %get-tuple-element.37), channel_id=1, source_target_pairs={{0,16},{4,20},{8,24},{12,28},{16,0},{20,4},{24,8},{28,12},{1,17},{... | collective-permute-start | bytes 786440 | tf_op jit(solution)/shard_map/ppermute | solution.py:44
  36.3 0.2 collective-permute-start.9
  36.6 5.8 %collective-permute-done.7.refs_1_.refs_3_ = bf16[2,4,32,512]{3,2,1,0:T(8,128)(2,1)S(1)} collective-permute-done((bf16[2,4,32,512]{3,2,1,0:T(8,128)(2,1)S(1)}, bf16[2,4,32,512]{3,2,1,0:T(8,128)(2,1)S(1)}, u32[]{:S(2)}, u32[]{:S(2)}) %collective-permute-start.7) | collective-permute-done | bytes 262176 | tf_op jit(solution)/shard_map/ppermute | solution.py:44
  42.3 12.5 %collective-permute-done.8.refs_2_.refs_4_ = bf16[2,4,32,512]{3,2,1,0:T(8,128)(2,1)S(1)} collective-permute-done((bf16[2,4,32,512]{3,2,1,0:T(8,128)(2,1)S(1)}, bf16[2,4,32,512]{3,2,1,0:T(8,128)(2,1)S(1)}, u32[]{:S(2)}, u32[]{:S(2)}) %collective-permute-start.8) | collective-permute-done | bytes 262176 | tf_op jit(solution)/shard_map/ppermute | solution.py:44
  54.9 0.0 copy-start
  54.9 0.1 collective-permute-start.10
  55.0 0.0 collective-permute-done.3.refs_3_.refs_1_
  55.0 0.1 cut.2
  55.0 0.6 collective-permute-start.5
  55.6 1.5 %collective-permute-start.6 = (bf16[512,512]{1,0:T(8,128)(2,1)S(1)}, bf16[512,512]{1,0:T(8,128)(2,1)S(1)}, u32[]{:S(2)}, u32[]{:S(2)}) collective-permute-start(bf16[512,512]{1,0:T(8,128)(2,1)S(1)} %get-tuple-element.35), channel_id=1, source_target_pairs={{0,2},{1,3},{2,0},{3,1},{4,6},{5,7},{6,4},{7,5},{8,10},{9,11},{10,... | collective-permute-start | bytes 1572872 | tf_op jit(solution)/shard_map/ppermute | solution.py:38
  57.2 1.1 slice_bitcast_fusion.refs_1_
  58.2 0.0 collective-permute-done.10.refs_6_
  58.3 1.3 %back.1 = (bf16[4,8,32,512]{3,2,1,0:T(8,128)(2,1)S(1)}, f32[256,512]{1,0:T(8,128)S(1)}, bf16[256,512]{1,0:T(8,128)(2,1)S(1)}, bf16[256,512]{1,0:T(8,128)(2,1)S(1)}, bf16[256,512]{1,0:T(8,128)(2,1)S(1)}) custom-call(s32[2]{0:T(128)S(1)} %copy-done.5, bf16[512,512]{1,0:T(8,128)(2,1)S(1)} %slice_bitcast_fusion.refs_1_, ...), custom_call_target="tpu_custom_call" | custom-call | tf_op jit(solution)/shard_map/back/pallas_call | solution.py:144
  59.5 1.5 %collective-permute-start.11 = (bf16[256,512]{1,0:T(8,128)(2,1)S(1)}, bf16[256,512]{1,0:T(8,128)(2,1)S(1)}, u32[]{:S(2)}, u32[]{:S(2)}) collective-permute-start(bf16[256,512]{1,0:T(8,128)(2,1)S(1)} %get-tuple-element.40), channel_id=1, source_target_pairs={{0,1},{1,0},{2,3},{3,2},{4,5},{5,4},{6,7},{7,6},{8,9},{9,8},{10,11... | collective-permute-start | bytes 786440 | tf_op jit(solution)/shard_map/ppermute | solution.py:38
  61.0 0.6 collective-permute-start.12
  61.6 1.5 %collective-permute-start.13 = (bf16[256,512]{1,0:T(8,128)(2,1)S(1)}, bf16[256,512]{1,0:T(8,128)(2,1)S(1)}, u32[]{:S(2)}, u32[]{:S(2)}) collective-permute-start(bf16[256,512]{1,0:T(8,128)(2,1)S(1)} %get-tuple-element.42), channel_id=1, source_target_pairs={{0,3},{1,2},{2,1},{3,0},{4,7},{5,6},{6,5},{7,4},{8,11},{9,10},{10,... | collective-permute-start | bytes 786440 | tf_op jit(solution)/shard_map/ppermute | solution.py:38
  63.1 1.5 %forward.1.refs_2_ = f32[2,256,512]{2,1,0:T(8,128)S(1)} custom-call(s32[2]{0:T(128)S(1)} %copy-done.5, bf16[256,2048]{1,0:T(8,128)(2,1)S(1)} %bitcast.8, bf16[2,512,512]{2,1,0:T(8,128)(2,1)S(1)} %projections.1.refs_2_, bf16[2,512,512]{2,1,0:T(8,128)(2,1)S(1)} %collective-permute-done.3.refs_3_.refs_1_, ...), custom_call_target="tpu_custom_call" | custom-call | tf_op jit(solution)/shard_map/forward/pallas_call | solution.py:144
  64.6 5.2 %collective-permute-done.5.refs_3_.refs_5_ = bf16[512,512]{1,0:T(8,128)(2,1)S(1)} collective-permute-done((bf16[512,512]{1,0:T(8,128)(2,1)S(1)}, bf16[512,512]{1,0:T(8,128)(2,1)S(1)}, u32[]{:S(2)}, u32[]{:S(2)}) %collective-permute-start.5) | collective-permute-done | bytes 524320 | tf_op jit(solution)/shard_map/ppermute | solution.py:38
  69.8 0.6 collective-permute-done.6.refs_4_.refs_6_
  70.4 1.0 rest.1.refs_0_
  71.4 4.1 %collective-permute-done.11.refs_2_ = bf16[256,512]{1,0:T(8,128)(2,1)S(1)} collective-permute-done((bf16[256,512]{1,0:T(8,128)(2,1)S(1)}, bf16[256,512]{1,0:T(8,128)(2,1)S(1)}, u32[]{:S(2)}, u32[]{:S(2)}) %collective-permute-start.11) | collective-permute-done | bytes 262176 | tf_op jit(solution)/shard_map/ppermute | solution.py:38
  75.5 4.5 %collective-permute-done.12.refs_3_ = bf16[256,512]{1,0:T(8,128)(2,1)S(1)} collective-permute-done((bf16[256,512]{1,0:T(8,128)(2,1)S(1)}, bf16[256,512]{1,0:T(8,128)(2,1)S(1)}, u32[]{:S(2)}, u32[]{:S(2)}) %collective-permute-start.12) | collective-permute-done | bytes 262176 | tf_op jit(solution)/shard_map/ppermute | solution.py:38
  80.0 1.6 %collective-permute-done.13.refs_4_ = bf16[256,512]{1,0:T(8,128)(2,1)S(1)} collective-permute-done((bf16[256,512]{1,0:T(8,128)(2,1)S(1)}, bf16[256,512]{1,0:T(8,128)(2,1)S(1)}, u32[]{:S(2)}, u32[]{:S(2)}) %collective-permute-start.13) | collective-permute-done | bytes 262176 | tf_op jit(solution)/shard_map/ppermute | solution.py:38
  81.6 0.4 factors.1.refs_1_.refs_3_
  82.0 0.9 collective-permute-start.18
  82.9 1.4 %collective-permute-start.17 = (bf16[2,384,512]{2,1,0:T(8,128)(2,1)S(1)}, bf16[2,384,512]{2,1,0:T(8,128)(2,1)S(1)}, u32[]{:S(2)}, u32[]{:S(2)}) collective-permute-start(bf16[2,384,512]{2,1,0:T(8,128)(2,1)S(1)} %factors.1.refs_1_.refs_3_), channel_id=1, source_target_pairs={{0,1},{1,0},{2,3},{3,2},{4,5},{5,4},{6,7},{7,6},{8,9},{9,8},{10,11... | collective-permute-start | bytes 2359304 | tf_op jit(solution)/shard_map/ppermute | solution.py:38
  84.4 1.9 %slots.1 = (bf16[2,32,2048]{2,1,0:T(8,128)(2,1)S(1)}, bf16[2,32,2048]{2,1,0:T(8,128)(2,1)S(1)}, bf16[2,32,2048]{2,1,0:T(8,128)(2,1)S(1)}, bf16[2,32,2048]{2,1,0:T(8,128)(2,1)S(1)}) custom-call(s32[2]{0:T(128)S(1)} %copy-done.5, bf16[2,384,512]{2,1,0:T(8,128)(2,1)S(1)} %factors.1.refs_1_.refs_3_, bf16[2,512,512]{2,1,0:T(8,128)(2,1)S(1)} %projections.1.refs_2_, ...), custom_call_target="tpu_custom_call" | custom-call | tf_op jit(solution)/shard_map/slots/pallas_call | solution.py:144
  86.2 3.4 %collective-permute-start.14 = (bf16[2,32,2048]{2,1,0:T(8,128)(2,1)S(1)}, bf16[2,32,2048]{2,1,0:T(8,128)(2,1)S(1)}, u32[]{:S(2)}, u32[]{:S(2)}) collective-permute-start(bf16[2,32,2048]{2,1,0:T(8,128)(2,1)S(1)} %get-tuple-element.44), channel_id=1, source_target_pairs={{0,8},{4,12},{8,0},{12,4},{16,24},{20,28},{24,16},{28,20},{1,9},{5... | collective-permute-start | bytes 786440 | tf_op jit(solution)/shard_map/ppermute | solution.py:44
  89.7 1.1 collective-permute-start.15
  90.8 1.4 %collective-permute-start.16 = (bf16[2,32,2048]{2,1,0:T(8,128)(2,1)S(1)}, bf16[2,32,2048]{2,1,0:T(8,128)(2,1)S(1)}, u32[]{:S(2)}, u32[]{:S(2)}) collective-permute-start(bf16[2,32,2048]{2,1,0:T(8,128)(2,1)S(1)} %get-tuple-element.46), channel_id=1, source_target_pairs={{0,24},{4,28},{8,16},{12,20},{16,8},{20,12},{24,0},{28,4},{1,25},{... | collective-permute-start | bytes 786440 | tf_op jit(solution)/shard_map/ppermute | solution.py:44
  92.2 9.0 %collective-permute-done.18.refs_7_.refs_0_ = bf16[2,384,512]{2,1,0:T(8,128)(2,1)S(1)} collective-permute-done((bf16[2,384,512]{2,1,0:T(8,128)(2,1)S(1)}, bf16[2,384,512]{2,1,0:T(8,128)(2,1)S(1)}, u32[]{:S(2)}, u32[]{:S(2)}) %collective-permute-start.18) | collective-permute-done | bytes 786464 | tf_op jit(solution)/shard_map/ppermute | solution.py:38
  101.2 0.3 collective-permute-done.17.refs_5_.refs_1_
  101.5 0.1 cut.3
  101.6 1.5 %collective-permute-start.21 = (bf16[384,512]{1,0:T(8,128)(2,1)S(1)}, bf16[384,512]{1,0:T(8,128)(2,1)S(1)}, u32[]{:S(2)}, u32[]{:S(2)}) collective-permute-start(bf16[384,512]{1,0:T(8,128)(2,1)S(1)} %get-tuple-element.52), channel_id=1, source_target_pairs={{0,1},{1,0},{2,3},{3,2},{4,5},{5,4},{6,7},{7,6},{8,9},{9,8},{10,11... | collective-permute-start | bytes 1179656 | tf_op jit(solution)/shard_map/ppermute | solution.py:38
  103.0 0.7 collective-permute-start.22
  103.7 4.2 %gram.1 = (f32[3,3,512,512]{3,2,1,0:T(8,128)S(1)}, f32[16,128]{1,0:T(8,128)S(1)}) custom-call(s32[2]{0:T(128)S(1)} %copy-done.5, bf16[4,8,32,512]{3,2,1,0:T(8,128)(2,1)S(1)} %get-tuple-element.47.refs_1_.refs_3_, bf16[400,512]{1,0:T(8,128)(2,1)S(1)} %copy-done.1, bf16[2,384,512]{2,1,0:T(8,128)(2,1)S(1)} %factors.1.refs_1_.refs_3_, ...), custom_call_target="tpu_custom_call" | custom-call | tf_op jit(solution)/shard_map/gram/pallas_call | solution.py:144
  107.9 3.1 %collective-permute-done.15.refs_2_.refs_4_ = bf16[2,32,2048]{2,1,0:T(8,128)(2,1)S(1)} collective-permute-done((bf16[2,32,2048]{2,1,0:T(8,128)(2,1)S(1)}, bf16[2,32,2048]{2,1,0:T(8,128)(2,1)S(1)}, u32[]{:S(2)}, u32[]{:S(2)}) %collective-permute-start.15) | collective-permute-done | bytes 262176 | tf_op jit(solution)/shard_map/ppermute | solution.py:44
  111.1 0.1 collective-permute-start.19
  111.2 0.5 collective-permute-start.20
  111.7 0.0 collective-permute-done.21.refs_5_
  111.7 0.3 collective-permute-done.22.refs_6_
  112.0 2.7 %gram_late.1 = (f32[1,3,512,512]{3,2,1,0:T(8,128)S(1)}, f32[16,128]{1,0:T(8,128)S(1)}) custom-call(s32[2]{0:T(128)S(1)} %copy-done.5, f32[16,128]{1,0:T(8,128)S(1)} %get-tuple-element.48.refs_4_.refs_1_, f32[3,3,512,512]{3,2,1,0:T(8,128)S(1)} %get-tuple-element.51.refs_2_.refs_5_, bf16[4,8,32,512]{3,2,1,0:T(8,128)(2,1)S(1)} %get-tuple-element.47.refs_1_.refs_3_, ...), custom_call_target="tpu_custom_call" | custom-call | tf_op jit(solution)/shard_map/gram_late/pallas_call | solution.py:144
  114.7 1.9 %collective-permute-start.25 = (f32[16,128]{1,0:T(8,128)S(1)}, f32[16,128]{1,0:T(8,128)S(1)}, u32[]{:S(2)}, u32[]{:S(2)}) collective-permute-start(f32[16,128]{1,0:T(8,128)S(1)} %get-tuple-element.54.refs_8_.refs_1_), channel_id=1, source_target_pairs={{0,3},{1,2},{2,1},{3,0},{4,7},{5,6},{6,5},{7,4},{8,11},{9,10},{10,... | collective-permute-start | bytes 24584 | tf_op jit(solution)/shard_map/ppermute | solution.py:38
  116.5 0.6 collective-permute-start.24
  117.1 1.1 collective-permute-start.23
  118.2 0.0 collective-permute-done.20.refs_7_
  118.2 1.7 %unplace.1 = bf16[1,128,2048]{2,1,0:T(8,128)(2,1)} custom-call(s32[2]{0:T(128)S(1)} %copy-done.5, bf16[400,512]{1,0:T(8,128)(2,1)S(1)} %copy-done.1, bf16[2,32,2048]{2,1,0:T(8,128)(2,1)S(1)} %get-tuple-element.43.refs_0_.refs_2_, bf16[2,32,2048]{2,1,0:T(8,128)(2,1)S(1)} %collective-permute-done.14.refs_1_.refs_3_, ...), custom_call_target="tpu_custom_call" | custom-call | tf_op jit(solution)/shard_map/unplace/pallas_call | solution.py:144
  120.0 0.2 collective-permute-done.24.refs_3_
  120.2 0.6 collective-permute-done.23.refs_2_
  120.8 5.3 %adam.1 = f32[1,3,512,512]{3,2,1,0:T(8,128)} custom-call(s32[2]{0:T(128)S(1)} %copy-done.5, f32[16,128]{1,0:T(8,128)S(1)} %get-tuple-element.54.refs_8_.refs_1_, f32[16,128]{1,0:T(8,128)S(1)} %collective-permute-done.23.refs_2_, f32[16,128]{1,0:T(8,128)S(1)} %collective-permute-done.24.refs_3_, f32[16,128]{1,0:T(8,128)S(1)} %collective-permute-done.25.refs_4_, ...), custom_call_target="tpu_custom_call" | custom-call | tf_op jit(solution)/shard_map/adam/pallas_call | solution.py:144
  (18 shorter events, 0.1 us)
Async XLA Ops:
  1.9 29.2 %copy-start.5 = (s32[2]{0:T(128)S(1)}, s32[2]{0:T(128)}, u32[]{:S(2)}) copy-start(s32[2]{0:T(128)} %pad_add_fusion.refs_0_) | copy-start | bytes 28
  4.7 26.5 %copy-start.1 = (bf16[400,512]{1,0:T(8,128)(2,1)S(1)}, bf16[400,512]{1,0:T(8,128)(2,1)}, u32[]{:S(2)}) copy-start(bf16[400,512]{1,0:T(8,128)(2,1)} %get-tuple-element.29.refs_1_.refs_2_) | copy-start | bytes 1228804
  4.7 13.4 %collective-permute-start = (bf16[400,512]{1,0:T(8,128)(2,1)}, bf16[400,512]{1,0:T(8,128)(2,1)S(1)}, u32[]{:S(2)}, u32[]{:S(2)}) collective-permute-start(bf16[400,512]{1,0:T(8,128)(2,1)} %get-tuple-element.30), channel_id=1, source_target_pairs={{0,1},{1,0},{2,3},{3,2},{4,5},{5,4},{6,7},{7,6},{8,9},{9,8},{10,11... | collective-permute-start | bytes 1228808 | tf_op jit(solution)/shard_map/ppermute | solution.py:38
  7.6 19.9 %collective-permute-start.1 = (bf16[400,512]{1,0:T(8,128)(2,1)}, bf16[400,512]{1,0:T(8,128)(2,1)S(1)}, u32[]{:S(2)}, u32[]{:S(2)}) collective-permute-start(bf16[400,512]{1,0:T(8,128)(2,1)} %get-tuple-element.31), channel_id=1, source_target_pairs={{0,2},{1,3},{2,0},{3,1},{4,6},{5,7},{6,4},{7,5},{8,10},{9,11},{10,... | collective-permute-start | bytes 1228808 | tf_op jit(solution)/shard_map/ppermute | solution.py:38
  9.1 18.4 %collective-permute-start.2 = (bf16[400,512]{1,0:T(8,128)(2,1)}, bf16[400,512]{1,0:T(8,128)(2,1)S(1)}, u32[]{:S(2)}, u32[]{:S(2)}) collective-permute-start(bf16[400,512]{1,0:T(8,128)(2,1)} %get-tuple-element.32), channel_id=1, source_target_pairs={{0,3},{1,2},{2,1},{3,0},{4,7},{5,6},{6,5},{7,4},{8,11},{9,10},{10,... | collective-permute-start | bytes 1228808 | tf_op jit(solution)/shard_map/ppermute | solution.py:38
  27.5 1.4 %copy-start.4 = (bf16[1,3,512,512]{3,2,1,0:T(8,128)(2,1)S(1)}, bf16[1,3,512,512]{3,2,1,0:T(8,128)(2,1)}, u32[]{:S(2)}) copy-start(bf16[1,3,512,512]{3,2,1,0:T(8,128)(2,1)} %refs_0_.1) | copy-start | bytes 4718596
  29.0 25.9 %collective-permute-start.4 = (bf16[2,512,512]{2,1,0:T(8,128)(2,1)S(1)}, bf16[2,512,512]{2,1,0:T(8,128)(2,1)S(1)}, u32[]{:S(2)}, u32[]{:S(2)}) collective-permute-start(bf16[2,512,512]{2,1,0:T(8,128)(2,1)S(1)} %projections.1.refs_2_), channel_id=1, source_target_pairs={{0,2},{1,3},{2,0},{3,1},{4,6},{5,7},{6,4},{7,5},{8,10},{9,11},{10,... | collective-permute-start | bytes 3145736 | tf_op jit(solution)/shard_map/ppermute | solution.py:38
  30.6 24.4 %collective-permute-start.3 = (bf16[2,512,512]{2,1,0:T(8,128)(2,1)S(1)}, bf16[2,512,512]{2,1,0:T(8,128)(2,1)S(1)}, u32[]{:S(2)}, u32[]{:S(2)}) collective-permute-start(bf16[2,512,512]{2,1,0:T(8,128)(2,1)S(1)} %projections.1.refs_2_), channel_id=1, source_target_pairs={{0,1},{1,0},{2,3},{3,2},{4,5},{5,4},{6,7},{7,6},{8,9},{9,8},{10,11... | collective-permute-start | bytes 3145736 | tf_op jit(solution)/shard_map/ppermute | solution.py:38
  32.1 10.2 %collective-permute-start.7 = (bf16[2,4,32,512]{3,2,1,0:T(8,128)(2,1)S(1)}, bf16[2,4,32,512]{3,2,1,0:T(8,128)(2,1)S(1)}, u32[]{:S(2)}, u32[]{:S(2)}) collective-permute-start(bf16[2,4,32,512]{3,2,1,0:T(8,128)(2,1)S(1)} %get-tuple-element.36), channel_id=1, source_target_pairs={{0,8},{4,12},{8,0},{12,4},{16,24},{20,28},{24,16},{28,20},{1,9},{5... | collective-permute-start | bytes 786440 | tf_op jit(solution)/shard_map/ppermute | solution.py:44
  33.8 21.1 %collective-permute-start.8 = (bf16[2,4,32,512]{3,2,1,0:T(8,128)(2,1)S(1)}, bf16[2,4,32,512]{3,2,1,0:T(8,128)(2,1)S(1)}, u32[]{:S(2)}, u32[]{:S(2)}) collective-permute-start(bf16[2,4,32,512]{3,2,1,0:T(8,128)(2,1)S(1)} %get-tuple-element.37), channel_id=1, source_target_pairs={{0,16},{4,20},{8,24},{12,28},{16,0},{20,4},{24,8},{28,12},{1,17},{... | collective-permute-start | bytes 786440 | tf_op jit(solution)/shard_map/ppermute | solution.py:44
  36.3 18.5 %collective-permute-start.9 = (bf16[2,4,32,512]{3,2,1,0:T(8,128)(2,1)S(1)}, bf16[2,4,32,512]{3,2,1,0:T(8,128)(2,1)S(1)}, u32[]{:S(2)}, u32[]{:S(2)}) collective-permute-start(bf16[2,4,32,512]{3,2,1,0:T(8,128)(2,1)S(1)} %get-tuple-element.38), channel_id=1, source_target_pairs={{0,24},{4,28},{8,16},{12,20},{16,8},{20,12},{24,0},{28,4},{1,25},{... | collective-permute-start | bytes 786440 | tf_op jit(solution)/shard_map/ppermute | solution.py:44
  54.9 8.2 %copy-start = (bf16[1,1,256,2048]{3,2,1,0:T(8,128)(2,1)S(1)}, bf16[1,1,256,2048]{3,2,1,0:T(8,128)(2,1)}, u32[]{:S(2)}) copy-start(bf16[1,1,256,2048]{3,2,1,0:T(8,128)(2,1)} %param.15) | copy-start | bytes 3145732
  54.9 3.4 %collective-permute-start.10 = (bf16[4,4,32,512]{3,2,1,0:T(8,128)(2,1)S(1)}, bf16[4,4,32,512]{3,2,1,0:T(8,128)(2,1)S(1)}, u32[]{:S(2)}, u32[]{:S(2)}) collective-permute-start(bf16[4,4,32,512]{3,2,1,0:T(8,128)(2,1)S(1)} %pick.2), channel_id=1, source_target_pairs={{0,4},{4,0},{8,12},{12,8},{16,20},{20,16},{24,28},{28,24},{1,5},{5... | collective-permute-start | bytes 1572872 | tf_op jit(solution)/shard_map/ppermute | solution.py:68
  55.0 14.8 %collective-permute-start.5 = (bf16[512,512]{1,0:T(8,128)(2,1)S(1)}, bf16[512,512]{1,0:T(8,128)(2,1)S(1)}, u32[]{:S(2)}, u32[]{:S(2)}) collective-permute-start(bf16[512,512]{1,0:T(8,128)(2,1)S(1)} %get-tuple-element.34), channel_id=1, source_target_pairs={{0,1},{1,0},{2,3},{3,2},{4,5},{5,4},{6,7},{7,6},{8,9},{9,8},{10,11... | collective-permute-start | bytes 1572872 | tf_op jit(solution)/shard_map/ppermute | solution.py:38
  55.6 14.8 %collective-permute-start.6 = (bf16[512,512]{1,0:T(8,128)(2,1)S(1)}, bf16[512,512]{1,0:T(8,128)(2,1)S(1)}, u32[]{:S(2)}, u32[]{:S(2)}) collective-permute-start(bf16[512,512]{1,0:T(8,128)(2,1)S(1)} %get-tuple-element.35), channel_id=1, source_target_pairs={{0,2},{1,3},{2,0},{3,1},{4,6},{5,7},{6,4},{7,5},{8,10},{9,11},{10,... | collective-permute-start | bytes 1572872 | tf_op jit(solution)/shard_map/ppermute | solution.py:38
  59.5 15.9 %collective-permute-start.11 = (bf16[256,512]{1,0:T(8,128)(2,1)S(1)}, bf16[256,512]{1,0:T(8,128)(2,1)S(1)}, u32[]{:S(2)}, u32[]{:S(2)}) collective-permute-start(bf16[256,512]{1,0:T(8,128)(2,1)S(1)} %get-tuple-element.40), channel_id=1, source_target_pairs={{0,1},{1,0},{2,3},{3,2},{4,5},{5,4},{6,7},{7,6},{8,9},{9,8},{10,11... | collective-permute-start | bytes 786440 | tf_op jit(solution)/shard_map/ppermute | solution.py:38
  61.0 18.9 %collective-permute-start.12 = (bf16[256,512]{1,0:T(8,128)(2,1)S(1)}, bf16[256,512]{1,0:T(8,128)(2,1)S(1)}, u32[]{:S(2)}, u32[]{:S(2)}) collective-permute-start(bf16[256,512]{1,0:T(8,128)(2,1)S(1)} %get-tuple-element.41), channel_id=1, source_target_pairs={{0,2},{1,3},{2,0},{3,1},{4,6},{5,7},{6,4},{7,5},{8,10},{9,11},{10,... | collective-permute-start | bytes 786440 | tf_op jit(solution)/shard_map/ppermute | solution.py:38
  61.6 20.0 %collective-permute-start.13 = (bf16[256,512]{1,0:T(8,128)(2,1)S(1)}, bf16[256,512]{1,0:T(8,128)(2,1)S(1)}, u32[]{:S(2)}, u32[]{:S(2)}) collective-permute-start(bf16[256,512]{1,0:T(8,128)(2,1)S(1)} %get-tuple-element.42), channel_id=1, source_target_pairs={{0,3},{1,2},{2,1},{3,0},{4,7},{5,6},{6,5},{7,4},{8,11},{9,10},{10,... | collective-permute-start | bytes 786440 | tf_op jit(solution)/shard_map/ppermute | solution.py:38
  82.0 19.2 %collective-permute-start.18 = (bf16[2,384,512]{2,1,0:T(8,128)(2,1)S(1)}, bf16[2,384,512]{2,1,0:T(8,128)(2,1)S(1)}, u32[]{:S(2)}, u32[]{:S(2)}) collective-permute-start(bf16[2,384,512]{2,1,0:T(8,128)(2,1)S(1)} %factors.1.refs_1_.refs_3_), channel_id=1, source_target_pairs={{0,2},{1,3},{2,0},{3,1},{4,6},{5,7},{6,4},{7,5},{8,10},{9,11},{10,... | collective-permute-start | bytes 2359304 | tf_op jit(solution)/shard_map/ppermute | solution.py:38
  82.9 18.6 %collective-permute-start.17 = (bf16[2,384,512]{2,1,0:T(8,128)(2,1)S(1)}, bf16[2,384,512]{2,1,0:T(8,128)(2,1)S(1)}, u32[]{:S(2)}, u32[]{:S(2)}) collective-permute-start(bf16[2,384,512]{2,1,0:T(8,128)(2,1)S(1)} %factors.1.refs_1_.refs_3_), channel_id=1, source_target_pairs={{0,1},{1,0},{2,3},{3,2},{4,5},{5,4},{6,7},{7,6},{8,9},{9,8},{10,11... | collective-permute-start | bytes 2359304 | tf_op jit(solution)/shard_map/ppermute | solution.py:38
  86.2 21.7 %collective-permute-start.14 = (bf16[2,32,2048]{2,1,0:T(8,128)(2,1)S(1)}, bf16[2,32,2048]{2,1,0:T(8,128)(2,1)S(1)}, u32[]{:S(2)}, u32[]{:S(2)}) collective-permute-start(bf16[2,32,2048]{2,1,0:T(8,128)(2,1)S(1)} %get-tuple-element.44), channel_id=1, source_target_pairs={{0,8},{4,12},{8,0},{12,4},{16,24},{20,28},{24,16},{28,20},{1,9},{5... | collective-permute-start | bytes 786440 | tf_op jit(solution)/shard_map/ppermute | solution.py:44
  89.7 21.4 %collective-permute-start.15 = (bf16[2,32,2048]{2,1,0:T(8,128)(2,1)S(1)}, bf16[2,32,2048]{2,1,0:T(8,128)(2,1)S(1)}, u32[]{:S(2)}, u32[]{:S(2)}) collective-permute-start(bf16[2,32,2048]{2,1,0:T(8,128)(2,1)S(1)} %get-tuple-element.45), channel_id=1, source_target_pairs={{0,16},{4,20},{8,24},{12,28},{16,0},{20,4},{24,8},{28,12},{1,17},{... | collective-permute-start | bytes 786440 | tf_op jit(solution)/shard_map/ppermute | solution.py:44
  90.8 20.3 %collective-permute-start.16 = (bf16[2,32,2048]{2,1,0:T(8,128)(2,1)S(1)}, bf16[2,32,2048]{2,1,0:T(8,128)(2,1)S(1)}, u32[]{:S(2)}, u32[]{:S(2)}) collective-permute-start(bf16[2,32,2048]{2,1,0:T(8,128)(2,1)S(1)} %get-tuple-element.46), channel_id=1, source_target_pairs={{0,24},{4,28},{8,16},{12,20},{16,8},{20,12},{24,0},{28,4},{1,25},{... | collective-permute-start | bytes 786440 | tf_op jit(solution)/shard_map/ppermute | solution.py:44
  101.6 10.1 %collective-permute-start.21 = (bf16[384,512]{1,0:T(8,128)(2,1)S(1)}, bf16[384,512]{1,0:T(8,128)(2,1)S(1)}, u32[]{:S(2)}, u32[]{:S(2)}) collective-permute-start(bf16[384,512]{1,0:T(8,128)(2,1)S(1)} %get-tuple-element.52), channel_id=1, source_target_pairs={{0,1},{1,0},{2,3},{3,2},{4,5},{5,4},{6,7},{7,6},{8,9},{9,8},{10,11... | collective-permute-start | bytes 1179656 | tf_op jit(solution)/shard_map/ppermute | solution.py:38
  103.0 8.9 %collective-permute-start.22 = (bf16[384,512]{1,0:T(8,128)(2,1)S(1)}, bf16[384,512]{1,0:T(8,128)(2,1)S(1)}, u32[]{:S(2)}, u32[]{:S(2)}) collective-permute-start(bf16[384,512]{1,0:T(8,128)(2,1)S(1)} %get-tuple-element.53), channel_id=1, source_target_pairs={{0,2},{1,3},{2,0},{3,1},{4,6},{5,7},{6,4},{7,5},{8,10},{9,11},{10,... | collective-permute-start | bytes 1179656 | tf_op jit(solution)/shard_map/ppermute | solution.py:38
  111.1 7.1 %collective-permute-start.19 = (bf16[2,32,2048]{2,1,0:T(8,128)(2,1)S(1)}, bf16[2,32,2048]{2,1,0:T(8,128)(2,1)S(1)}, u32[]{:S(2)}, u32[]{:S(2)}) collective-permute-start(bf16[2,32,2048]{2,1,0:T(8,128)(2,1)S(1)} %get-tuple-element.49), channel_id=1, source_target_pairs={{0,4},{4,0},{8,12},{12,8},{16,20},{20,16},{24,28},{28,24},{1,5},{5... | collective-permute-start | bytes 786440 | tf_op jit(solution)/shard_map/ppermute | solution.py:68
  111.2 7.0 %collective-permute-start.20 = (bf16[2,32,2048]{2,1,0:T(8,128)(2,1)S(1)}, bf16[2,32,2048]{2,1,0:T(8,128)(2,1)S(1)}, u32[]{:S(2)}, u32[]{:S(2)}) collective-permute-start(bf16[2,32,2048]{2,1,0:T(8,128)(2,1)S(1)} %get-tuple-element.50), channel_id=1, source_target_pairs={{0,4},{4,0},{8,12},{12,8},{16,20},{20,16},{24,28},{28,24},{1,5},{5... | collective-permute-start | bytes 786440 | tf_op jit(solution)/shard_map/ppermute | solution.py:68
  111.9 8.8 %copy-start.2 = (f32[1,3,512,512]{3,2,1,0:T(8,128)S(1)}, f32[1,3,512,512]{3,2,1,0:T(8,128)}, u32[]{:S(2)}) copy-start(f32[1,3,512,512]{3,2,1,0:T(8,128)} %refs_7_.1) | copy-start | bytes 9437188
  112.0 8.8 %copy-start.3 = (f32[1,3,512,512]{3,2,1,0:T(8,128)S(1)}, f32[1,3,512,512]{3,2,1,0:T(8,128)}, u32[]{:S(2)}) copy-start(f32[1,3,512,512]{3,2,1,0:T(8,128)} %refs_8_.1) | copy-start | bytes 9437188
  114.7 5.3 %collective-permute-start.25 = (f32[16,128]{1,0:T(8,128)S(1)}, f32[16,128]{1,0:T(8,128)S(1)}, u32[]{:S(2)}, u32[]{:S(2)}) collective-permute-start(f32[16,128]{1,0:T(8,128)S(1)} %get-tuple-element.54.refs_8_.refs_1_), channel_id=1, source_target_pairs={{0,3},{1,2},{2,1},{3,0},{4,7},{5,6},{6,5},{7,4},{8,11},{9,10},{10,... | collective-permute-start | bytes 24584 | tf_op jit(solution)/shard_map/ppermute | solution.py:38
  116.5 3.7 %collective-permute-start.24 = (f32[16,128]{1,0:T(8,128)S(1)}, f32[16,128]{1,0:T(8,128)S(1)}, u32[]{:S(2)}, u32[]{:S(2)}) collective-permute-start(f32[16,128]{1,0:T(8,128)S(1)} %get-tuple-element.54.refs_8_.refs_1_), channel_id=1, source_target_pairs={{0,2},{1,3},{2,0},{3,1},{4,6},{5,7},{6,4},{7,5},{8,10},{9,11},{10,... | collective-permute-start | bytes 24584 | tf_op jit(solution)/shard_map/ppermute | solution.py:38
  117.1 3.7 %collective-permute-start.23 = (f32[16,128]{1,0:T(8,128)S(1)}, f32[16,128]{1,0:T(8,128)S(1)}, u32[]{:S(2)}, u32[]{:S(2)}) collective-permute-start(f32[16,128]{1,0:T(8,128)S(1)} %get-tuple-element.54.refs_8_.refs_1_), channel_id=1, source_target_pairs={{0,1},{1,0},{2,3},{3,2},{4,5},{5,4},{6,7},{7,6},{8,9},{9,8},{10,11... | collective-permute-start | bytes 24584 | tf_op jit(solution)/shard_map/ppermute | solution.py:38

commit v6 on v5

--- a/solution.py
+++ b/solution.py
@@ -80,8 +80,50 @@
     return [parts[0]] + [from_peer(part, k) for k, part in enumerate(parts) if k]
 
 
-def copy_kernel(weights_ref, out_ref):
-    out_ref[...] = weights_ref[0, pl.ds(0, out_ref.shape[0])]
+def split_kernel(rep_ref, matrix_ref, *out_refs):
+    for offset, out_ref in enumerate(out_refs):
+        out_ref[...] = matrix_ref[:, segment(rep_ref, offset, out_ref.shape[1])]
+
+
+def payload_kernel(rep_ref, pair_ref, inputs_ref, *out_refs):
+    seg_rows = pair_ref.shape[1]
+    slot_count = inputs_ref.shape[0]
+    half = slot_count // 2
+    for part, out_ref in enumerate(out_refs):
+        out_ref[pl.ds(0, seg_rows), :] = pair_ref[0]
+        out_ref[pl.ds(seg_rows, seg_rows), :] = pair_ref[1]
+        columns = segment(rep_ref, part + 1, seg_rows)
+        out_ref[pl.ds(2 * seg_rows, slot_count), :] = inputs_ref[:, columns]
+        columns = segment(rep_ref, 3, seg_rows)
+        out_ref[pl.ds(2 * seg_rows + slot_count, half), :] = inputs_ref[
+            pl.ds(part * half, half), columns
+        ]
+
+
+def pass_kernel(from_two_ref, from_one_ref, *out_refs):
+    for part, (near_ref, out_ref) in enumerate(zip((from_two_ref, from_one_ref), out_refs)):
+        seg_rows = near_ref.shape[1]
+        half = out_ref.shape[0] - seg_rows
+        out_ref[pl.ds(0, seg_rows), :] = near_ref[pl.ds(part * seg_rows, seg_rows), :]
+        out_ref[pl.ds(seg_rows, half), :] = near_ref[pl.ds(near_ref.shape[0] - half, half), :]
+
+
+def projection_rows(refs):
+    if len(refs) == 1 and len(refs[0].shape) == 3:
+        return refs[0].at[0], refs[0].at[1]
+    seg_rows = refs[0].shape[1]
+    start = 0 if len(refs) == 2 else seg_rows
+    return refs[0].at[pl.ds(0, seg_rows)], refs[-1].at[pl.ds(start, seg_rows)]
+
+
+def input_rows(rep_ref, refs, slot_count, seg_rows):
+    if len(refs) == 2:
+        rows = pl.ds(seg_rows, slot_count // 2)
+        return jnp.concatenate([refs[1][rows], refs[0][rows]], axis=0)
+    (ref,) = refs
+    if ref.shape[0] > slot_count:
+        return ref[pl.ds(2 * seg_rows, slot_count), :]
+    return ref[...] if ref.shape[1] == seg_rows else ref[:, segment(rep_ref, 0, seg_rows)]
 
 
 def cut_kernel(from_two_ref, from_one_ref, first_ref, second_ref):
@@ -161,7 +203,7 @@
     return pl.ds(pl.multiple_of((pos_ref[0] ^ offset) * width, width), width)
 
 
-def rows_kernel(expert_count, pos_ref, ids_ref, task_ref, row_ref, grads_ref, inputs_ref, *out_refs):
+def rows_kernel(expert_count, pos_ref, ids_ref, task_ref, row_ref, grads_ref, *out_refs):
     row_count = grads_ref.shape[0]
     seg_rows = out_refs[0].shape[1]
     block_count = ids_ref.shape[1]
@@ -192,8 +234,6 @@
                 (LABEL_ROWS, seg_rows), jnp.bfloat16
             )
         out_ref[pl.ds(row_count, LABEL_ROWS), pl.ds(0, row_count)] = labels
-        head = row_count + LABEL_ROWS
-        out_ref[pl.ds(head, inputs_ref.shape[0]), :] = inputs_ref[:, columns]
 
 
 def one_hot(block_ref, row_count, slot_count, capacity):
@@ -254,7 +294,7 @@
         gate, up = weight_refs[0][0], weight_refs[0][1]
         weight_refs = weight_refs[1:]
     for offset, group in zip(offsets, regroup(weight_refs, lengths)):
-        gate_ref, up_ref = halves(group)
+        gate_ref, up_ref = projection_rows(group)
         rows = inputs_ref[:, segment(pos_ref, offset, gate_ref.shape[0])]
         gate_part, up_part = multiply(rows, gate_ref[...]), multiply(rows, up_ref[...])
         gate = gate_part if gate is None else gate + gate_part
@@ -288,7 +328,7 @@
     rows = pl.ds(0, expert_count * capacity)
     gate_grad, up_grad = factor_ref[0, rows], factor_ref[1, rows]
     for offset, group in enumerate(regroup(weight_refs, lengths)):
-        gate_ref, up_ref = halves(group)
+        gate_ref, up_ref = projection_rows(group)
         total = contract_last(gate_grad, gate_ref[...]) + contract_last(up_grad, up_ref[...])
         total = total.reshape(expert_count, capacity, seg_rows)
         slots_ref[offset] = total.astype(jnp.bfloat16)
@@ -307,9 +347,9 @@
     slot_count = incoming_ref.shape[1] * incoming_ref.shape[2]
     groups = regroup(operand_refs, lengths)
     for at, offset in enumerate(offsets):
-        (inputs_ref,), factor_refs = groups[2 * at : 2 * at + 2]
+        input_refs, factor_refs = groups[2 * at : 2 * at + 2]
         rest = pl.ds(slot_count, slot_count // 2)
-        columns = inputs_ref[pl.ds(inputs_ref.shape[0] - slot_count, slot_count), :]
+        columns = input_rows(pos_ref, input_refs, slot_count, seg_rows)
         gate_ref, up_ref = (ref.at[pl.ds(0, slot_count)] for ref in halves(factor_refs))
         first_ref, second_ref = (ref.at[rest] for ref in halves(factor_refs))
         grads_ref[at, 0] = contract_first(columns, gate_ref[...])
@@ -404,7 +444,8 @@
         second_new = (beta_second / second_fix) * second_ref[0, 0, rows] + (
             (1.0 - beta_second) / second_fix
         ) * (merged * merged)
-        step_ref[0, 0, rows] = first_new / (jnp.sqrt(second_new) + adam_eps)
+        root = second_new * lax.rsqrt(second_new)
+        step_ref[0, 0, rows] = first_new / (root + adam_eps)
         return 0
 
     lax.fori_loop(0, step_ref.shape[2] // lines, step, 0, unroll=4)
@@ -453,14 +494,14 @@
 
 def adasum(rep, inputs, incoming, factors):
     count = len(inputs)
-    seg_rows, hidden_width = inputs[0].shape[1], factors[0][0].shape[2]
+    seg_rows, hidden_width = incoming.shape[3], factors[0][0].shape[2]
     shape = jax.ShapeDtypeStruct
     groups = [[k for k in range(count) if k < 3], [k for k in range(count) if k == 3]]
     groups = [group for group in groups if group]
     grads, gram, first_gram, place = [], None, None, 0
     for group in groups:
         operands = [rep] if gram is None else [rep, gram, grads[0]]
-        parts = [x for k in group for x in ((inputs[k],), factors[k])]
+        parts = [x for k in group for x in (inputs[k], factors[k])]
         operands += [incoming] + flatten(parts)
         more, gram = call(
             functools.partial(gram_kernel, count, group, [len(x) for x in parts], place),
@@ -516,10 +557,8 @@
     rep = jnp.stack([lax.axis_index("replica"), lax.axis_index("expert")]).astype(jnp.int32)
     shape = jax.ShapeDtypeStruct
 
-    inputs_home = saved_inputs[0, 0]
-    head = row_count + LABEL_ROWS
-    block = shape((head + slot_count, seg_rows), jnp.bfloat16)
-    small = [routes[0].reshape(1, row_count), out_grads[0], inputs_home]
+    block = shape((row_count + LABEL_ROWS, seg_rows), jnp.bfloat16)
+    small = [routes[0].reshape(1, row_count), out_grads[0]]
     row_blocks = call(
         functools.partial(rows_kernel, expert_count),
         "rows",
@@ -531,16 +570,27 @@
     )
     routed = exchange(row_blocks)
 
-    pair = (2, seg_rows, hidden_width)
-    (own_projections,) = call(
-        copy_kernel,
-        "projections",
-        [weights],
-        [VMEM],
-        [shape(pair, jnp.bfloat16)],
-        after=routed[1:],
-    )
-    near_projections = gather_near(own_projections)
+    inputs_home = saved_inputs[0, 0]
+    pair = weights[0, :2]
+    packed = rep_count == 4 and seg_rows == hidden_width
+    if packed:
+        payload = shape((2 * seg_rows + slot_count + half, seg_rows), jnp.bfloat16)
+        to_one, to_two = call(
+            payload_kernel,
+            "payload",
+            [rep, pair, inputs_home],
+            [SMEM, VMEM, VMEM],
+            [payload, payload],
+            after=routed[1:],
+        )
+        from_two, from_one = from_peer(to_two, 2), from_peer(to_one, 1)
+        projections = [(pair,), (from_one,), (from_two,)]
+        inputs = [(inputs_home,), (from_one,), (from_two,)]
+    else:
+        projections = [(x,) for x in exchange([pair] * rep_count)]
+        pieces = [shape((slot_count, seg_rows), jnp.bfloat16) for _ in offsets]
+        pieces = call(split_kernel, "split", [rep, inputs_home], [SMEM, VMEM], pieces)
+        inputs = [(x,) for x in exchange(pieces)]
 
     part = shape((2, rep_count, capacity, seg_rows), jnp.bfloat16)
     placed = (
@@ -557,10 +607,36 @@
     )
 
     came = across_chips(placed)
-    projections = gather_rest(near_projections, after=placed[:1])
+
+    came = finish_spread(came)
+
+    back_shape = (slot_count, hidden_width)
+    incoming, *back = call(
+        functools.partial(back_kernel, chips, len(came)),
+        "back",
+        [rep, weights[0, 2], *came],
+        [SMEM] + [VMEM] * (1 + len(came)),
+        [shape((rep_count, expert_count, capacity, seg_rows), jnp.bfloat16)]
+        + [shape(back_shape, jnp.bfloat16 if k else jnp.float32) for k in offsets],
+    )
+    own_back = back[:1]
+    back = exchange(back)
+    if packed:
+        passed = shape((seg_rows + half, seg_rows), jnp.bfloat16)
+        first, second = call(
+            pass_kernel,
+            "pass",
+            [from_two, from_one],
+            [VMEM, VMEM],
+            [passed, passed],
+            after=own_back,
+        )
+        last = (from_peer(first, 1), from_peer(second, 2))
+        projections.append(last)
+        inputs.append(last)
 
     forward = None
-    late = [3] if rep_count == 4 else []
+    late = [3] if packed else []
     for name, group in (("forward", [k for k in offsets if k not in late]), ("rest", late)):
         if not group:
             continue
@@ -576,18 +652,6 @@
             cost=0 if name == "rest" else 0,
         )
 
-    came = finish_spread(came)
-
-    back_shape = (slot_count, hidden_width)
-    incoming, *back = call(
-        functools.partial(back_kernel, chips, len(came)),
-        "back",
-        [rep, weights[0, 2], *came],
-        [SMEM] + [VMEM] * (1 + len(came)),
-        [shape((rep_count, expert_count, capacity, seg_rows), jnp.bfloat16)]
-        + [shape(back_shape, jnp.bfloat16 if k else jnp.float32) for k in offsets],
-    )
-    back = exchange(back)
     (own_factors,) = call(
         factor_kernel,
         "factors",
@@ -612,7 +676,7 @@
     )
     factors = gather_rest(near_factors, after=returning[:1])
     if rep_count <= 4:
-        *merging, first_gram = adasum(rep, routed, incoming, factors)
+        *merging, first_gram = adasum(rep, inputs, incoming, factors)
         returned = finish_spread(returning, [first_gram], pieces=2)
         unplace_after = merging[2:]
     else:
@@ -630,7 +694,7 @@
         adam_step = adam(rep, *merging, first_moment, second_moment, ())
     else:
         adam_step = adasum_adam_many(
-            rep, [x[head:] for x in routed], incoming, factors, first_moment, second_moment
+            rep, [x for (x,) in inputs], incoming, factors, first_moment, second_moment
         )
     return (input_grads, adam_step)
 

time: 127 us -> 118 us (0.929)
  waiting for transfers between devices: 66.2 us -> 59.5 us
    ppermute x17, waiting for transfers between devices: 44.8 us -> 39.9 us  [from_peer(): lax.ppermute(array, 'replica', [(i, i ^ offset) for i in range(count)])]
    ppermute x6, waiting for transfers between devices: 21.4 us -> 18.8 us  [across_chips(): lax.ppermute(part, 'expert', [(i, i ^ 2 * k) for i in range(count)])]
    unnamed x12 -> x10, local copies, waits for them, and re-layouts: 1.43 us -> 0.02 us
    squeeze x0 -> x1, local copies, waits for them, and re-layouts: none -> 1.29 us  [shards(): pair = weights[0, :2]]
  transfers between devices with their start and end apart: 26 -> 26, of which waited for: 15 -> 15; matrix products, arithmetic and copies ran while one was open for 1% -> 2% of each run, Pallas kernels for 12% -> 13%
where the time goes in v6:
time: 118 us
  waiting for transfers between devices  59.5 us (50%)
  starting transfers between devices  30.4 us (26%)
  Pallas kernels  23.6 us (20%)
  local copies, waits for them, and re-layouts  2.39 us (2%)
  between operations  1.52 us (1%)
    ppermute x17, waiting for transfers between devices, from_peer(): lax.ppermute(array, 'replica', [(i, i ^ offset) for i in range(count)])  39.9 us
    pallas_call x16, Pallas kernels, call(): pl.pallas_call(body, grid=grid, in_specs=list(specs) + [VMEM] * len(after...  23.6 us
    ppermute x17, starting transfers between devices, from_peer(): lax.ppermute(array, 'replica', [(i, i ^ offset) for i in range(count)])  20 us
    ppermute x6, waiting for transfers between devices, across_chips(): lax.ppermute(part, 'expert', [(i, i ^ 2 * k) for i in range(count)])  18.8 us
    ppermute x6, starting transfers between devices, across_chips(): lax.ppermute(part, 'expert', [(i, i ^ 2 * k) for i in range(count)])  9.77 us
  transfers between devices with their start and end apart: 26, of which 15 were waited for; matrix products, arithmetic and copies ran while one was open for 2% of the time, Pallas kernels for 13%

profile of v6, /device:TPU:0, one launch (start us, length us, event | category | flops | bytes accessed | tf_op | source)
XLA Modules:
  0.0 118.0 jit_solution(3569932235766398898)
XLA Ops:
  1.4 0.6 pad_add_fusion.refs_0_
  2.0 2.0 %rows.1 = (bf16[144,512]{1,0:T(8,128)(2,1)}, bf16[144,512]{1,0:T(8,128)(2,1)}, bf16[144,512]{1,0:T(8,128)(2,1)}, bf16[144,512]{1,0:T(8,128)(2,1)}) custom-call(s32[2]{0:T(128)} %pad_add_fusion.refs_0_, s32[1,1]{1,0:T(1,128)S(6)} %copy.10.refs_1_, f32[8]{0:T(128)} %refs_2_.1, s32[1,128]{1,0:T(1,128)} %bitcast.14, bf16[128,2048]{1,0:T(8,128)(2,1)} %bitcast.13), custom_call_target="tpu_custom_call" | custom-call | tf_op jit(solution)/shard_map/rows/pallas_call | solution.py:186
  4.0 2.9 %collective-permute-start = (bf16[144,512]{1,0:T(8,128)(2,1)}, bf16[144,512]{1,0:T(8,128)(2,1)S(1)}, u32[]{:S(2)}, u32[]{:S(2)}) collective-permute-start(bf16[144,512]{1,0:T(8,128)(2,1)} %get-tuple-element.32), channel_id=1, source_target_pairs={{0,1},{1,0},{2,3},{3,2},{4,5},{5,4},{6,7},{7,6},{8,9},{9,8},{10,11... | collective-permute-start | bytes 442376 | tf_op jit(solution)/shard_map/ppermute | solution.py:38
  6.9 1.5 %collective-permute-start.1 = (bf16[144,512]{1,0:T(8,128)(2,1)}, bf16[144,512]{1,0:T(8,128)(2,1)S(1)}, u32[]{:S(2)}, u32[]{:S(2)}) collective-permute-start(bf16[144,512]{1,0:T(8,128)(2,1)} %get-tuple-element.33), channel_id=1, source_target_pairs={{0,2},{1,3},{2,0},{3,1},{4,6},{5,7},{6,4},{7,5},{8,10},{9,11},{10,... | collective-permute-start | bytes 442376 | tf_op jit(solution)/shard_map/ppermute | solution.py:38
  8.5 0.0 collective-permute-start.2
  8.5 1.3 %slice_bitcast_fusion.refs_1_.refs_2_ = bf16[2,512,512]{2,1,0:T(8,128)(2,1)S(1)} fusion(bf16[1,3,512,512]{3,2,1,0:T(8,128)(2,1)} %param.8), kind=kLoop, calls=%fused_computation | loop fusion | bytes 2097152 | tf_op jit(solution)/shard_map/squeeze | solution.py:574
  9.8 0.0 copy-start.3
  9.8 1.7 %collective-permute-done.refs_3_.refs_2_ = bf16[144,512]{1,0:T(8,128)(2,1)S(1)} collective-permute-done((bf16[144,512]{1,0:T(8,128)(2,1)}, bf16[144,512]{1,0:T(8,128)(2,1)S(1)}, u32[]{:S(2)}, u32[]{:S(2)}) %collective-permute-start) | collective-permute-done | bytes 147488 | tf_op jit(solution)/shard_map/ppermute | solution.py:38
  11.5 4.1 %collective-permute-done.1.refs_4_.refs_3_ = bf16[144,512]{1,0:T(8,128)(2,1)S(1)} collective-permute-done((bf16[144,512]{1,0:T(8,128)(2,1)}, bf16[144,512]{1,0:T(8,128)(2,1)S(1)}, u32[]{:S(2)}, u32[]{:S(2)}) %collective-permute-start.1) | collective-permute-done | bytes 147488 | tf_op jit(solution)/shard_map/ppermute | solution.py:38
  15.6 0.7 payload.1
  16.4 1.3 %collective-permute-start.3 = (bf16[1408,512]{1,0:T(8,128)(2,1)S(1)}, bf16[1408,512]{1,0:T(8,128)(2,1)S(1)}, u32[]{:S(2)}, u32[]{:S(2)}) collective-permute-start(bf16[1408,512]{1,0:T(8,128)(2,1)S(1)} %get-tuple-element.35), channel_id=1, source_target_pairs={{0,1},{1,0},{2,3},{3,2},{4,5},{5,4},{6,7},{7,6},{8,9},{9,8},{10,11... | collective-permute-start | bytes 4325384 | tf_op jit(solution)/shard_map/ppermute | solution.py:38
  17.7 0.8 collective-permute-start.4
  18.5 1.0 place.1
  19.5 1.6 %collective-permute-start.5 = (bf16[2,4,32,512]{3,2,1,0:T(8,128)(2,1)S(1)}, bf16[2,4,32,512]{3,2,1,0:T(8,128)(2,1)S(1)}, u32[]{:S(2)}, u32[]{:S(2)}) collective-permute-start(bf16[2,4,32,512]{3,2,1,0:T(8,128)(2,1)S(1)} %get-tuple-element.38), channel_id=1, source_target_pairs={{0,8},{4,12},{8,0},{12,4},{16,24},{20,28},{24,16},{28,20},{1,9},{5... | collective-permute-start | bytes 786440 | tf_op jit(solution)/shard_map/ppermute | solution.py:44
  21.1 2.6 %collective-permute-start.6 = (bf16[2,4,32,512]{3,2,1,0:T(8,128)(2,1)S(1)}, bf16[2,4,32,512]{3,2,1,0:T(8,128)(2,1)S(1)}, u32[]{:S(2)}, u32[]{:S(2)}) collective-permute-start(bf16[2,4,32,512]{3,2,1,0:T(8,128)(2,1)S(1)} %get-tuple-element.39), channel_id=1, source_target_pairs={{0,16},{4,20},{8,24},{12,28},{16,0},{20,4},{24,8},{28,12},{1,17},{... | collective-permute-start | bytes 786440 | tf_op jit(solution)/shard_map/ppermute | solution.py:44
  23.7 0.2 collective-permute-start.7
  23.9 5.7 %collective-permute-done.5.refs_1_.refs_3_ = bf16[2,4,32,512]{3,2,1,0:T(8,128)(2,1)S(1)} collective-permute-done((bf16[2,4,32,512]{3,2,1,0:T(8,128)(2,1)S(1)}, bf16[2,4,32,512]{3,2,1,0:T(8,128)(2,1)S(1)}, u32[]{:S(2)}, u32[]{:S(2)}) %collective-permute-start.5) | collective-permute-done | bytes 262176 | tf_op jit(solution)/shard_map/ppermute | solution.py:44
  29.6 12.5 %collective-permute-done.6.refs_2_.refs_4_ = bf16[2,4,32,512]{3,2,1,0:T(8,128)(2,1)S(1)} collective-permute-done((bf16[2,4,32,512]{3,2,1,0:T(8,128)(2,1)S(1)}, bf16[2,4,32,512]{3,2,1,0:T(8,128)(2,1)S(1)}, u32[]{:S(2)}, u32[]{:S(2)}) %collective-permute-start.6) | collective-permute-done | bytes 262176 | tf_op jit(solution)/shard_map/ppermute | solution.py:44
  42.1 0.0 collective-permute-done.7.refs_3_.refs_5_
  42.2 0.1 collective-permute-start.8
  42.2 1.1 slice_bitcast_fusion.1.refs_1_
  43.3 0.8 collective-permute-done.8.refs_6_
  44.1 1.3 %back.1 = (bf16[4,8,32,512]{3,2,1,0:T(8,128)(2,1)S(1)}, f32[256,512]{1,0:T(8,128)S(1)}, bf16[256,512]{1,0:T(8,128)(2,1)S(1)}, bf16[256,512]{1,0:T(8,128)(2,1)S(1)}, bf16[256,512]{1,0:T(8,128)(2,1)S(1)}) custom-call(s32[2]{0:T(128)S(1)} %copy-done.4, bf16[512,512]{1,0:T(8,128)(2,1)S(1)} %slice_bitcast_fusion.1.refs_1_, ...), custom_call_target="tpu_custom_call" | custom-call | tf_op jit(solution)/shard_map/back/pallas_call | solution.py:186
  45.4 3.4 %collective-permute-done.3.refs_3_.refs_1_.refs_4_ = bf16[1408,512]{1,0:T(8,128)(2,1)S(1)} collective-permute-done((bf16[1408,512]{1,0:T(8,128)(2,1)S(1)}, bf16[1408,512]{1,0:T(8,128)(2,1)S(1)}, u32[]{:S(2)}, u32[]{:S(2)}) %collective-permute-start.3) | collective-permute-done | bytes 1441824 | tf_op jit(solution)/shard_map/ppermute | solution.py:38
  48.8 1.0 collective-permute-done.4.refs_4_.refs_0_.refs_6_
  49.8 0.1 pass.1
  49.9 0.8 collective-permute-start.9
  50.7 1.4 %collective-permute-start.10 = (bf16[640,512]{1,0:T(8,128)(2,1)S(1)}, bf16[640,512]{1,0:T(8,128)(2,1)S(1)}, u32[]{:S(2)}, u32[]{:S(2)}) collective-permute-start(bf16[640,512]{1,0:T(8,128)(2,1)S(1)} %get-tuple-element.43), channel_id=1, source_target_pairs={{0,2},{1,3},{2,0},{3,1},{4,6},{5,7},{6,4},{7,5},{8,10},{9,11},{10,... | collective-permute-start | bytes 1966088 | tf_op jit(solution)/shard_map/ppermute | solution.py:38
  52.1 0.4 collective-permute-start.11
  52.5 1.5 %collective-permute-start.12 = (bf16[256,512]{1,0:T(8,128)(2,1)S(1)}, bf16[256,512]{1,0:T(8,128)(2,1)S(1)}, u32[]{:S(2)}, u32[]{:S(2)}) collective-permute-start(bf16[256,512]{1,0:T(8,128)(2,1)S(1)} %get-tuple-element.45), channel_id=1, source_target_pairs={{0,2},{1,3},{2,0},{3,1},{4,6},{5,7},{6,4},{7,5},{8,10},{9,11},{10,... | collective-permute-start | bytes 786440 | tf_op jit(solution)/shard_map/ppermute | solution.py:38
  54.0 1.5 %collective-permute-start.13 = (bf16[256,512]{1,0:T(8,128)(2,1)S(1)}, bf16[256,512]{1,0:T(8,128)(2,1)S(1)}, u32[]{:S(2)}, u32[]{:S(2)}) collective-permute-start(bf16[256,512]{1,0:T(8,128)(2,1)S(1)} %get-tuple-element.46), channel_id=1, source_target_pairs={{0,3},{1,2},{2,1},{3,0},{4,7},{5,6},{6,5},{7,4},{8,11},{9,10},{10,... | collective-permute-start | bytes 786440 | tf_op jit(solution)/shard_map/ppermute | solution.py:38
  55.6 1.5 %forward.1.refs_2_ = f32[2,256,512]{2,1,0:T(8,128)S(1)} custom-call(s32[2]{0:T(128)S(1)} %copy-done.4, bf16[256,2048]{1,0:T(8,128)(2,1)S(1)} %bitcast.10, bf16[2,512,512]{2,1,0:T(8,128)(2,1)S(1)} %slice_bitcast_fusion.refs_1_.refs_2_, bf16[1408,512]{1,0:T(8,128)(2,1)S(1)} %collective-permute-done.3.refs_3_.refs_1_.refs_4_, ...), custom_call_target="tpu_custom_call" | custom-call | tf_op jit(solution)/shard_map/forward/pallas_call | solution.py:186
  57.1 10.6 %collective-permute-done.9.refs_3_.refs_5_.refs_4_ = bf16[640,512]{1,0:T(8,128)(2,1)S(1)} collective-permute-done((bf16[640,512]{1,0:T(8,128)(2,1)S(1)}, bf16[640,512]{1,0:T(8,128)(2,1)S(1)}, u32[]{:S(2)}, u32[]{:S(2)}) %collective-permute-start.9) | collective-permute-done | bytes 655392 | tf_op jit(solution)/shard_map/ppermute | solution.py:38
  67.7 1.0 collective-permute-done.10.refs_4_.refs_6_.refs_5_
  68.6 1.0 rest.1.refs_0_
  69.6 3.2 %collective-permute-done.11.refs_2_ = bf16[256,512]{1,0:T(8,128)(2,1)S(1)} collective-permute-done((bf16[256,512]{1,0:T(8,128)(2,1)S(1)}, bf16[256,512]{1,0:T(8,128)(2,1)S(1)}, u32[]{:S(2)}, u32[]{:S(2)}) %collective-permute-start.11) | collective-permute-done | bytes 262176 | tf_op jit(solution)/shard_map/ppermute | solution.py:38
  72.8 3.2 %collective-permute-done.12.refs_3_ = bf16[256,512]{1,0:T(8,128)(2,1)S(1)} collective-permute-done((bf16[256,512]{1,0:T(8,128)(2,1)S(1)}, bf16[256,512]{1,0:T(8,128)(2,1)S(1)}, u32[]{:S(2)}, u32[]{:S(2)}) %collective-permute-start.12) | collective-permute-done | bytes 262176 | tf_op jit(solution)/shard_map/ppermute | solution.py:38
  76.0 0.0 collective-permute-done.13.refs_4_
  76.0 0.4 factors.1.refs_1_.refs_3_
  76.5 1.7 %collective-permute-start.17 = (bf16[2,384,512]{2,1,0:T(8,128)(2,1)S(1)}, bf16[2,384,512]{2,1,0:T(8,128)(2,1)S(1)}, u32[]{:S(2)}, u32[]{:S(2)}) collective-permute-start(bf16[2,384,512]{2,1,0:T(8,128)(2,1)S(1)} %factors.1.refs_1_.refs_3_), channel_id=1, source_target_pairs={{0,1},{1,0},{2,3},{3,2},{4,5},{5,4},{6,7},{7,6},{8,9},{9,8},{10,11... | collective-permute-start | bytes 2359304 | tf_op jit(solution)/shard_map/ppermute | solution.py:38
  78.1 0.2 collective-permute-start.18
  78.3 1.8 %slots.1 = (bf16[2,32,2048]{2,1,0:T(8,128)(2,1)S(1)}, bf16[2,32,2048]{2,1,0:T(8,128)(2,1)S(1)}, bf16[2,32,2048]{2,1,0:T(8,128)(2,1)S(1)}, bf16[2,32,2048]{2,1,0:T(8,128)(2,1)S(1)}) custom-call(s32[2]{0:T(128)S(1)} %copy-done.4, bf16[2,384,512]{2,1,0:T(8,128)(2,1)S(1)} %factors.1.refs_1_.refs_3_, bf16[2,512,512]{2,1,0:T(8,128)(2,1)S(1)} %slice_bitcast_fusion.refs_1_.refs_2_, ...), custom_call_target="tpu_custom_call" | custom-call | tf_op jit(solution)/shard_map/slots/pallas_call | solution.py:186
  80.2 2.5 %collective-permute-start.14 = (bf16[2,32,2048]{2,1,0:T(8,128)(2,1)S(1)}, bf16[2,32,2048]{2,1,0:T(8,128)(2,1)S(1)}, u32[]{:S(2)}, u32[]{:S(2)}) collective-permute-start(bf16[2,32,2048]{2,1,0:T(8,128)(2,1)S(1)} %get-tuple-element.48), channel_id=1, source_target_pairs={{0,8},{4,12},{8,0},{12,4},{16,24},{20,28},{24,16},{28,20},{1,9},{5... | collective-permute-start | bytes 786440 | tf_op jit(solution)/shard_map/ppermute | solution.py:44
  82.6 2.8 %collective-permute-start.15 = (bf16[2,32,2048]{2,1,0:T(8,128)(2,1)S(1)}, bf16[2,32,2048]{2,1,0:T(8,128)(2,1)S(1)}, u32[]{:S(2)}, u32[]{:S(2)}) collective-permute-start(bf16[2,32,2048]{2,1,0:T(8,128)(2,1)S(1)} %get-tuple-element.49), channel_id=1, source_target_pairs={{0,16},{4,20},{8,24},{12,28},{16,0},{20,4},{24,8},{28,12},{1,17},{... | collective-permute-start | bytes 786440 | tf_op jit(solution)/shard_map/ppermute | solution.py:44
  85.5 0.0 collective-permute-start.16
  85.5 8.6 %collective-permute-done.17.refs_5_.refs_1_ = bf16[2,384,512]{2,1,0:T(8,128)(2,1)S(1)} collective-permute-done((bf16[2,384,512]{2,1,0:T(8,128)(2,1)S(1)}, bf16[2,384,512]{2,1,0:T(8,128)(2,1)S(1)}, u32[]{:S(2)}, u32[]{:S(2)}) %collective-permute-start.17) | collective-permute-done | bytes 786464 | tf_op jit(solution)/shard_map/ppermute | solution.py:38
  94.1 0.0 collective-permute-done.18.refs_7_.refs_0_
  94.1 0.1 cut.1
  94.2 1.7 %collective-permute-start.21 = (bf16[384,512]{1,0:T(8,128)(2,1)S(1)}, bf16[384,512]{1,0:T(8,128)(2,1)S(1)}, u32[]{:S(2)}, u32[]{:S(2)}) collective-permute-start(bf16[384,512]{1,0:T(8,128)(2,1)S(1)} %get-tuple-element.56), channel_id=1, source_target_pairs={{0,1},{1,0},{2,3},{3,2},{4,5},{5,4},{6,7},{7,6},{8,9},{9,8},{10,11... | collective-permute-start | bytes 1179656 | tf_op jit(solution)/shard_map/ppermute | solution.py:38
  95.9 0.6 collective-permute-start.22
  96.5 4.2 %gram.1 = (f32[3,3,512,512]{3,2,1,0:T(8,128)S(1)}, f32[16,128]{1,0:T(8,128)S(1)}) custom-call(s32[2]{0:T(128)S(1)} %copy-done.4, bf16[4,8,32,512]{3,2,1,0:T(8,128)(2,1)S(1)} %get-tuple-element.51.refs_1_.refs_3_, bf16[256,2048]{1,0:T(8,128)(2,1)S(1)} %bitcast.12, bf16[2,384,512]{2,1,0:T(8,128)(2,1)S(1)} %factors.1.refs_1_.refs_3_, ...), custom_call_target="tpu_custom_call" | custom-call | tf_op jit(solution)/shard_map/gram/pallas_call | solution.py:186
  100.7 0.0 collective-permute-done.14.refs_1_.refs_3_
  100.7 0.6 collective-permute-done.15.refs_2_.refs_4_
  101.4 0.1 collective-permute-start.19
  101.5 0.5 collective-permute-start.20
  102.0 0.0 collective-permute-done.21.refs_6_
  102.0 1.6 %collective-permute-done.22.refs_7_ = bf16[384,512]{1,0:T(8,128)(2,1)S(1)} collective-permute-done((bf16[384,512]{1,0:T(8,128)(2,1)S(1)}, bf16[384,512]{1,0:T(8,128)(2,1)S(1)}, u32[]{:S(2)}, u32[]{:S(2)}) %collective-permute-start.22) | collective-permute-done | bytes 393248 | tf_op jit(solution)/shard_map/ppermute | solution.py:38
  103.7 2.7 %gram_late.1 = (f32[1,3,512,512]{3,2,1,0:T(8,128)S(1)}, f32[16,128]{1,0:T(8,128)S(1)}) custom-call(s32[2]{0:T(128)S(1)} %copy-done.4, f32[16,128]{1,0:T(8,128)S(1)} %get-tuple-element.52.refs_4_.refs_1_, f32[3,3,512,512]{3,2,1,0:T(8,128)S(1)} %get-tuple-element.55.refs_2_.refs_5_, bf16[4,8,32,512]{3,2,1,0:T(8,128)(2,1)S(1)} %get-tuple-element.51.refs_1_.refs_3_, ...), custom_call_target="tpu_custom_call" | custom-call | tf_op jit(solution)/shard_map/gram_late/pallas_call | solution.py:186
  106.4 0.4 collective-permute-start.23
  106.8 1.6 %collective-permute-start.24 = (f32[16,128]{1,0:T(8,128)S(1)}, f32[16,128]{1,0:T(8,128)S(1)}, u32[]{:S(2)}, u32[]{:S(2)}) collective-permute-start(f32[16,128]{1,0:T(8,128)S(1)} %get-tuple-element.58.refs_8_.refs_1_), channel_id=1, source_target_pairs={{0,2},{1,3},{2,0},{3,1},{4,6},{5,7},{6,4},{7,5},{8,10},{9,11},{10,... | collective-permute-start | bytes 24584 | tf_op jit(solution)/shard_map/ppermute | solution.py:38
  108.5 1.5 %collective-permute-start.25 = (f32[16,128]{1,0:T(8,128)S(1)}, f32[16,128]{1,0:T(8,128)S(1)}, u32[]{:S(2)}, u32[]{:S(2)}) collective-permute-start(f32[16,128]{1,0:T(8,128)S(1)} %get-tuple-element.58.refs_8_.refs_1_), channel_id=1, source_target_pairs={{0,3},{1,2},{2,1},{3,0},{4,7},{5,6},{6,5},{7,4},{8,11},{9,10},{10,... | collective-permute-start | bytes 24584 | tf_op jit(solution)/shard_map/ppermute | solution.py:38
  109.9 1.7 %unplace.1 = bf16[1,128,2048]{2,1,0:T(8,128)(2,1)} custom-call(s32[2]{0:T(128)S(1)} %copy-done.4, bf16[144,512]{1,0:T(8,128)(2,1)S(1)} %copy-done.3, bf16[2,32,2048]{2,1,0:T(8,128)(2,1)S(1)} %get-tuple-element.47.refs_0_.refs_2_, bf16[2,32,2048]{2,1,0:T(8,128)(2,1)S(1)} %collective-permute-done.14.refs_1_.refs_3_, ...), custom_call_target="tpu_custom_call" | custom-call | tf_op jit(solution)/shard_map/unplace/pallas_call | solution.py:186
  111.6 1.4 %collective-permute-done.25.refs_4_ = f32[16,128]{1,0:T(8,128)S(1)} collective-permute-done((f32[16,128]{1,0:T(8,128)S(1)}, f32[16,128]{1,0:T(8,128)S(1)}, u32[]{:S(2)}, u32[]{:S(2)}) %collective-permute-start.25) | collective-permute-done | bytes 8224 | tf_op jit(solution)/shard_map/ppermute | solution.py:38
  113.0 5.0 %adam.1 = f32[1,3,512,512]{3,2,1,0:T(8,128)} custom-call(s32[2]{0:T(128)S(1)} %copy-done.4, f32[16,128]{1,0:T(8,128)S(1)} %get-tuple-element.58.refs_8_.refs_1_, f32[16,128]{1,0:T(8,128)S(1)} %collective-permute-done.23.refs_2_, f32[16,128]{1,0:T(8,128)S(1)} %collective-permute-done.24.refs_3_, f32[16,128]{1,0:T(8,128)S(1)} %collective-permute-done.25.refs_4_, ...), custom_call_target="tpu_custom_call" | custom-call | tf_op jit(solution)/shard_map/adam/pallas_call | solution.py:186
  (17 shorter events, 0.1 us)
Async XLA Ops:
  0.6 15.0 %copy-start = (bf16[1,1,256,2048]{3,2,1,0:T(8,128)(2,1)S(1)}, bf16[1,1,256,2048]{3,2,1,0:T(8,128)(2,1)}, u32[]{:S(2)}) copy-start(bf16[1,1,256,2048]{3,2,1,0:T(8,128)(2,1)} %param.15) | copy-start | bytes 3145732
  2.0 13.6 %copy-start.4 = (s32[2]{0:T(128)S(1)}, s32[2]{0:T(128)}, u32[]{:S(2)}) copy-start(s32[2]{0:T(128)} %pad_add_fusion.refs_0_) | copy-start | bytes 28
  4.0 7.5 %collective-permute-start = (bf16[144,512]{1,0:T(8,128)(2,1)}, bf16[144,512]{1,0:T(8,128)(2,1)S(1)}, u32[]{:S(2)}, u32[]{:S(2)}) collective-permute-start(bf16[144,512]{1,0:T(8,128)(2,1)} %get-tuple-element.32), channel_id=1, source_target_pairs={{0,1},{1,0},{2,3},{3,2},{4,5},{5,4},{6,7},{7,6},{8,9},{9,8},{10,11... | collective-permute-start | bytes 442376 | tf_op jit(solution)/shard_map/ppermute | solution.py:38
  6.9 8.7 %collective-permute-start.1 = (bf16[144,512]{1,0:T(8,128)(2,1)}, bf16[144,512]{1,0:T(8,128)(2,1)S(1)}, u32[]{:S(2)}, u32[]{:S(2)}) collective-permute-start(bf16[144,512]{1,0:T(8,128)(2,1)} %get-tuple-element.33), channel_id=1, source_target_pairs={{0,2},{1,3},{2,0},{3,1},{4,6},{5,7},{6,4},{7,5},{8,10},{9,11},{10,... | collective-permute-start | bytes 442376 | tf_op jit(solution)/shard_map/ppermute | solution.py:38
  8.5 7.2 %collective-permute-start.2 = (bf16[144,512]{1,0:T(8,128)(2,1)}, bf16[144,512]{1,0:T(8,128)(2,1)S(1)}, u32[]{:S(2)}, u32[]{:S(2)}) collective-permute-start(bf16[144,512]{1,0:T(8,128)(2,1)} %get-tuple-element.34), channel_id=1, source_target_pairs={{0,3},{1,2},{2,1},{3,0},{4,7},{5,6},{6,5},{7,4},{8,11},{9,10},{10,... | collective-permute-start | bytes 442376 | tf_op jit(solution)/shard_map/ppermute | solution.py:38
  9.8 8.7 %copy-start.3 = (bf16[144,512]{1,0:T(8,128)(2,1)S(1)}, bf16[144,512]{1,0:T(8,128)(2,1)}, u32[]{:S(2)}) copy-start(bf16[144,512]{1,0:T(8,128)(2,1)} %get-tuple-element.31.refs_1_) | copy-start | bytes 442372
  16.4 32.5 %collective-permute-start.3 = (bf16[1408,512]{1,0:T(8,128)(2,1)S(1)}, bf16[1408,512]{1,0:T(8,128)(2,1)S(1)}, u32[]{:S(2)}, u32[]{:S(2)}) collective-permute-start(bf16[1408,512]{1,0:T(8,128)(2,1)S(1)} %get-tuple-element.35), channel_id=1, source_target_pairs={{0,1},{1,0},{2,3},{3,2},{4,5},{5,4},{6,7},{7,6},{8,9},{9,8},{10,11... | collective-permute-start | bytes 4325384 | tf_op jit(solution)/shard_map/ppermute | solution.py:38
  17.7 32.2 %collective-permute-start.4 = (bf16[1408,512]{1,0:T(8,128)(2,1)S(1)}, bf16[1408,512]{1,0:T(8,128)(2,1)S(1)}, u32[]{:S(2)}, u32[]{:S(2)}) collective-permute-start(bf16[1408,512]{1,0:T(8,128)(2,1)S(1)} %get-tuple-element.36), channel_id=1, source_target_pairs={{0,2},{1,3},{2,0},{3,1},{4,6},{5,7},{6,4},{7,5},{8,10},{9,11},{10,... | collective-permute-start | bytes 4325384 | tf_op jit(solution)/shard_map/ppermute | solution.py:38
  19.5 10.1 %collective-permute-start.5 = (bf16[2,4,32,512]{3,2,1,0:T(8,128)(2,1)S(1)}, bf16[2,4,32,512]{3,2,1,0:T(8,128)(2,1)S(1)}, u32[]{:S(2)}, u32[]{:S(2)}) collective-permute-start(bf16[2,4,32,512]{3,2,1,0:T(8,128)(2,1)S(1)} %get-tuple-element.38), channel_id=1, source_target_pairs={{0,8},{4,12},{8,0},{12,4},{16,24},{20,28},{24,16},{28,20},{1,9},{5... | collective-permute-start | bytes 786440 | tf_op jit(solution)/shard_map/ppermute | solution.py:44
  21.1 21.0 %collective-permute-start.6 = (bf16[2,4,32,512]{3,2,1,0:T(8,128)(2,1)S(1)}, bf16[2,4,32,512]{3,2,1,0:T(8,128)(2,1)S(1)}, u32[]{:S(2)}, u32[]{:S(2)}) collective-permute-start(bf16[2,4,32,512]{3,2,1,0:T(8,128)(2,1)S(1)} %get-tuple-element.39), channel_id=1, source_target_pairs={{0,16},{4,20},{8,24},{12,28},{16,0},{20,4},{24,8},{28,12},{1,17},{... | collective-permute-start | bytes 786440 | tf_op jit(solution)/shard_map/ppermute | solution.py:44
  23.7 18.4 %collective-permute-start.7 = (bf16[2,4,32,512]{3,2,1,0:T(8,128)(2,1)S(1)}, bf16[2,4,32,512]{3,2,1,0:T(8,128)(2,1)S(1)}, u32[]{:S(2)}, u32[]{:S(2)}) collective-permute-start(bf16[2,4,32,512]{3,2,1,0:T(8,128)(2,1)S(1)} %get-tuple-element.40), channel_id=1, source_target_pairs={{0,24},{4,28},{8,16},{12,20},{16,8},{20,12},{24,0},{28,4},{1,25},{... | collective-permute-start | bytes 786440 | tf_op jit(solution)/shard_map/ppermute | solution.py:44
  42.2 2.0 %collective-permute-start.8 = (bf16[4,4,32,512]{3,2,1,0:T(8,128)(2,1)S(1)}, bf16[4,4,32,512]{3,2,1,0:T(8,128)(2,1)S(1)}, u32[]{:S(2)}, u32[]{:S(2)}) collective-permute-start(bf16[4,4,32,512]{3,2,1,0:T(8,128)(2,1)S(1)} %pick.2), channel_id=1, source_target_pairs={{0,4},{4,0},{8,12},{12,8},{16,20},{20,16},{24,28},{28,24},{1,5},{5... | collective-permute-start | bytes 1572872 | tf_op jit(solution)/shard_map/ppermute | solution.py:68
  49.9 17.7 %collective-permute-start.9 = (bf16[640,512]{1,0:T(8,128)(2,1)S(1)}, bf16[640,512]{1,0:T(8,128)(2,1)S(1)}, u32[]{:S(2)}, u32[]{:S(2)}) collective-permute-start(bf16[640,512]{1,0:T(8,128)(2,1)S(1)} %get-tuple-element.42), channel_id=1, source_target_pairs={{0,1},{1,0},{2,3},{3,2},{4,5},{5,4},{6,7},{7,6},{8,9},{9,8},{10,11... | collective-permute-start | bytes 1966088 | tf_op jit(solution)/shard_map/ppermute | solution.py:38
  50.7 17.9 %collective-permute-start.10 = (bf16[640,512]{1,0:T(8,128)(2,1)S(1)}, bf16[640,512]{1,0:T(8,128)(2,1)S(1)}, u32[]{:S(2)}, u32[]{:S(2)}) collective-permute-start(bf16[640,512]{1,0:T(8,128)(2,1)S(1)} %get-tuple-element.43), channel_id=1, source_target_pairs={{0,2},{1,3},{2,0},{3,1},{4,6},{5,7},{6,4},{7,5},{8,10},{9,11},{10,... | collective-permute-start | bytes 1966088 | tf_op jit(solution)/shard_map/ppermute | solution.py:38
  52.1 20.7 %collective-permute-start.11 = (bf16[256,512]{1,0:T(8,128)(2,1)S(1)}, bf16[256,512]{1,0:T(8,128)(2,1)S(1)}, u32[]{:S(2)}, u32[]{:S(2)}) collective-permute-start(bf16[256,512]{1,0:T(8,128)(2,1)S(1)} %get-tuple-element.44), channel_id=1, source_target_pairs={{0,1},{1,0},{2,3},{3,2},{4,5},{5,4},{6,7},{7,6},{8,9},{9,8},{10,11... | collective-permute-start | bytes 786440 | tf_op jit(solution)/shard_map/ppermute | solution.py:38
  52.5 23.5 %collective-permute-start.12 = (bf16[256,512]{1,0:T(8,128)(2,1)S(1)}, bf16[256,512]{1,0:T(8,128)(2,1)S(1)}, u32[]{:S(2)}, u32[]{:S(2)}) collective-permute-start(bf16[256,512]{1,0:T(8,128)(2,1)S(1)} %get-tuple-element.45), channel_id=1, source_target_pairs={{0,2},{1,3},{2,0},{3,1},{4,6},{5,7},{6,4},{7,5},{8,10},{9,11},{10,... | collective-permute-start | bytes 786440 | tf_op jit(solution)/shard_map/ppermute | solution.py:38
  54.0 22.0 %collective-permute-start.13 = (bf16[256,512]{1,0:T(8,128)(2,1)S(1)}, bf16[256,512]{1,0:T(8,128)(2,1)S(1)}, u32[]{:S(2)}, u32[]{:S(2)}) collective-permute-start(bf16[256,512]{1,0:T(8,128)(2,1)S(1)} %get-tuple-element.46), channel_id=1, source_target_pairs={{0,3},{1,2},{2,1},{3,0},{4,7},{5,6},{6,5},{7,4},{8,11},{9,10},{10,... | collective-permute-start | bytes 786440 | tf_op jit(solution)/shard_map/ppermute | solution.py:38
  76.5 17.6 %collective-permute-start.17 = (bf16[2,384,512]{2,1,0:T(8,128)(2,1)S(1)}, bf16[2,384,512]{2,1,0:T(8,128)(2,1)S(1)}, u32[]{:S(2)}, u32[]{:S(2)}) collective-permute-start(bf16[2,384,512]{2,1,0:T(8,128)(2,1)S(1)} %factors.1.refs_1_.refs_3_), channel_id=1, source_target_pairs={{0,1},{1,0},{2,3},{3,2},{4,5},{5,4},{6,7},{7,6},{8,9},{9,8},{10,11... | collective-permute-start | bytes 2359304 | tf_op jit(solution)/shard_map/ppermute | solution.py:38
  78.1 16.0 %collective-permute-start.18 = (bf16[2,384,512]{2,1,0:T(8,128)(2,1)S(1)}, bf16[2,384,512]{2,1,0:T(8,128)(2,1)S(1)}, u32[]{:S(2)}, u32[]{:S(2)}) collective-permute-start(bf16[2,384,512]{2,1,0:T(8,128)(2,1)S(1)} %factors.1.refs_1_.refs_3_), channel_id=1, source_target_pairs={{0,2},{1,3},{2,0},{3,1},{4,6},{5,7},{6,4},{7,5},{8,10},{9,11},{10,... | collective-permute-start | bytes 2359304 | tf_op jit(solution)/shard_map/ppermute | solution.py:38
  80.2 20.5 %collective-permute-start.14 = (bf16[2,32,2048]{2,1,0:T(8,128)(2,1)S(1)}, bf16[2,32,2048]{2,1,0:T(8,128)(2,1)S(1)}, u32[]{:S(2)}, u32[]{:S(2)}) collective-permute-start(bf16[2,32,2048]{2,1,0:T(8,128)(2,1)S(1)} %get-tuple-element.48), channel_id=1, source_target_pairs={{0,8},{4,12},{8,0},{12,4},{16,24},{20,28},{24,16},{28,20},{1,9},{5... | collective-permute-start | bytes 786440 | tf_op jit(solution)/shard_map/ppermute | solution.py:44
  82.6 18.7 %collective-permute-start.15 = (bf16[2,32,2048]{2,1,0:T(8,128)(2,1)S(1)}, bf16[2,32,2048]{2,1,0:T(8,128)(2,1)S(1)}, u32[]{:S(2)}, u32[]{:S(2)}) collective-permute-start(bf16[2,32,2048]{2,1,0:T(8,128)(2,1)S(1)} %get-tuple-element.49), channel_id=1, source_target_pairs={{0,16},{4,20},{8,24},{12,28},{16,0},{20,4},{24,8},{28,12},{1,17},{... | collective-permute-start | bytes 786440 | tf_op jit(solution)/shard_map/ppermute | solution.py:44
  85.5 15.9 %collective-permute-start.16 = (bf16[2,32,2048]{2,1,0:T(8,128)(2,1)S(1)}, bf16[2,32,2048]{2,1,0:T(8,128)(2,1)S(1)}, u32[]{:S(2)}, u32[]{:S(2)}) collective-permute-start(bf16[2,32,2048]{2,1,0:T(8,128)(2,1)S(1)} %get-tuple-element.50), channel_id=1, source_target_pairs={{0,24},{4,28},{8,16},{12,20},{16,8},{20,12},{24,0},{28,4},{1,25},{... | collective-permute-start | bytes 786440 | tf_op jit(solution)/shard_map/ppermute | solution.py:44
  94.2 7.8 %collective-permute-start.21 = (bf16[384,512]{1,0:T(8,128)(2,1)S(1)}, bf16[384,512]{1,0:T(8,128)(2,1)S(1)}, u32[]{:S(2)}, u32[]{:S(2)}) collective-permute-start(bf16[384,512]{1,0:T(8,128)(2,1)S(1)} %get-tuple-element.56), channel_id=1, source_target_pairs={{0,1},{1,0},{2,3},{3,2},{4,5},{5,4},{6,7},{7,6},{8,9},{9,8},{10,11... | collective-permute-start | bytes 1179656 | tf_op jit(solution)/shard_map/ppermute | solution.py:38
  95.9 7.8 %collective-permute-start.22 = (bf16[384,512]{1,0:T(8,128)(2,1)S(1)}, bf16[384,512]{1,0:T(8,128)(2,1)S(1)}, u32[]{:S(2)}, u32[]{:S(2)}) collective-permute-start(bf16[384,512]{1,0:T(8,128)(2,1)S(1)} %get-tuple-element.57), channel_id=1, source_target_pairs={{0,2},{1,3},{2,0},{3,1},{4,6},{5,7},{6,4},{7,5},{8,10},{9,11},{10,... | collective-permute-start | bytes 1179656 | tf_op jit(solution)/shard_map/ppermute | solution.py:38
  101.4 8.5 %collective-permute-start.19 = (bf16[2,32,2048]{2,1,0:T(8,128)(2,1)S(1)}, bf16[2,32,2048]{2,1,0:T(8,128)(2,1)S(1)}, u32[]{:S(2)}, u32[]{:S(2)}) collective-permute-start(bf16[2,32,2048]{2,1,0:T(8,128)(2,1)S(1)} %get-tuple-element.53), channel_id=1, source_target_pairs={{0,4},{4,0},{8,12},{12,8},{16,20},{20,16},{24,28},{28,24},{1,5},{5... | collective-permute-start | bytes 786440 | tf_op jit(solution)/shard_map/ppermute | solution.py:68
  101.5 8.4 %collective-permute-start.20 = (bf16[2,32,2048]{2,1,0:T(8,128)(2,1)S(1)}, bf16[2,32,2048]{2,1,0:T(8,128)(2,1)S(1)}, u32[]{:S(2)}, u32[]{:S(2)}) collective-permute-start(bf16[2,32,2048]{2,1,0:T(8,128)(2,1)S(1)} %get-tuple-element.54), channel_id=1, source_target_pairs={{0,4},{4,0},{8,12},{12,8},{16,20},{20,16},{24,28},{28,24},{1,5},{5... | collective-permute-start | bytes 786440 | tf_op jit(solution)/shard_map/ppermute | solution.py:68
  103.6 9.4 %copy-start.1 = (f32[1,3,512,512]{3,2,1,0:T(8,128)S(1)}, f32[1,3,512,512]{3,2,1,0:T(8,128)}, u32[]{:S(2)}) copy-start(f32[1,3,512,512]{3,2,1,0:T(8,128)} %refs_7_.1) | copy-start | bytes 9437188
  103.6 9.4 %copy-start.2 = (f32[1,3,512,512]{3,2,1,0:T(8,128)S(1)}, f32[1,3,512,512]{3,2,1,0:T(8,128)}, u32[]{:S(2)}) copy-start(f32[1,3,512,512]{3,2,1,0:T(8,128)} %refs_8_.1) | copy-start | bytes 9437188
  106.4 5.3 %collective-permute-start.23 = (f32[16,128]{1,0:T(8,128)S(1)}, f32[16,128]{1,0:T(8,128)S(1)}, u32[]{:S(2)}, u32[]{:S(2)}) collective-permute-start(f32[16,128]{1,0:T(8,128)S(1)} %get-tuple-element.58.refs_8_.refs_1_), channel_id=1, source_target_pairs={{0,1},{1,0},{2,3},{3,2},{4,5},{5,4},{6,7},{7,6},{8,9},{9,8},{10,11... | collective-permute-start | bytes 24584 | tf_op jit(solution)/shard_map/ppermute | solution.py:38
  106.8 4.8 %collective-permute-start.24 = (f32[16,128]{1,0:T(8,128)S(1)}, f32[16,128]{1,0:T(8,128)S(1)}, u32[]{:S(2)}, u32[]{:S(2)}) collective-permute-start(f32[16,128]{1,0:T(8,128)S(1)} %get-tuple-element.58.refs_8_.refs_1_), channel_id=1, source_target_pairs={{0,2},{1,3},{2,0},{3,1},{4,6},{5,7},{6,4},{7,5},{8,10},{9,11},{10,... | collective-permute-start | bytes 24584 | tf_op jit(solution)/shard_map/ppermute | solution.py:38
  108.5 4.5 %collective-permute-start.25 = (f32[16,128]{1,0:T(8,128)S(1)}, f32[16,128]{1,0:T(8,128)S(1)}, u32[]{:S(2)}, u32[]{:S(2)}) collective-permute-start(f32[16,128]{1,0:T(8,128)S(1)} %get-tuple-element.58.refs_8_.refs_1_), channel_id=1, source_target_pairs={{0,3},{1,2},{2,1},{3,0},{4,7},{5,6},{6,5},{7,4},{8,11},{9,10},{10,... | collective-permute-start | bytes 24584 | tf_op jit(solution)/shard_map/ppermute | solution.py:38

commit v7 on v6

--- a/solution.py
+++ b/solution.py
@@ -85,13 +85,13 @@
         out_ref[...] = matrix_ref[:, segment(rep_ref, offset, out_ref.shape[1])]
 
 
-def payload_kernel(rep_ref, pair_ref, inputs_ref, *out_refs):
-    seg_rows = pair_ref.shape[1]
+def payload_kernel(rep_ref, weights_ref, inputs_ref, *out_refs):
+    seg_rows = weights_ref.shape[2]
     slot_count = inputs_ref.shape[0]
     half = slot_count // 2
     for part, out_ref in enumerate(out_refs):
-        out_ref[pl.ds(0, seg_rows), :] = pair_ref[0]
-        out_ref[pl.ds(seg_rows, seg_rows), :] = pair_ref[1]
+        out_ref[pl.ds(0, seg_rows), :] = weights_ref[0, 0]
+        out_ref[pl.ds(seg_rows, seg_rows), :] = weights_ref[0, 1]
         columns = segment(rep_ref, part + 1, seg_rows)
         out_ref[pl.ds(2 * seg_rows, slot_count), :] = inputs_ref[:, columns]
         columns = segment(rep_ref, 3, seg_rows)
@@ -109,8 +109,9 @@
 
 
 def projection_rows(refs):
-    if len(refs) == 1 and len(refs[0].shape) == 3:
-        return refs[0].at[0], refs[0].at[1]
+    if len(refs) == 1 and len(refs[0].shape) > 2:
+        ref = refs[0] if len(refs[0].shape) == 3 else refs[0].at[0]
+        return ref.at[0], ref.at[1]
     seg_rows = refs[0].shape[1]
     start = 0 if len(refs) == 2 else seg_rows
     return refs[0].at[pl.ds(0, seg_rows)], refs[-1].at[pl.ds(start, seg_rows)]
@@ -199,11 +200,11 @@
     )(*operands, *after)
 
 
-def segment(pos_ref, offset, width):
-    return pl.ds(pl.multiple_of((pos_ref[0] ^ offset) * width, width), width)
-
-
-def rows_kernel(expert_count, pos_ref, ids_ref, task_ref, row_ref, grads_ref, *out_refs):
+def segment(rep_ref, offset, width):
+    return pl.ds(pl.multiple_of((rep_ref[0] ^ offset) * width, width), width)
+
+
+def rows_kernel(expert_count, rep_ref, ids_ref, task_ref, row_ref, grads_ref, *out_refs):
     row_count = grads_ref.shape[0]
     seg_rows = out_refs[0].shape[1]
     block_count = ids_ref.shape[1]
@@ -222,7 +223,7 @@
     labels = jnp.where(line == 0, row_ref[...].astype(jnp.float32), 0.0)
     labels = jnp.where(line == 1, rank, labels).astype(jnp.bfloat16)
     for offset, out_ref in enumerate(out_refs):
-        columns = segment(pos_ref, offset, seg_rows)
+        columns = segment(rep_ref, offset, seg_rows)
         for block in range(block_count):
             rows = pl.ds(block * block_rows, block_rows)
             weight = task_ref[ids_ref[0, block]]
@@ -243,7 +244,7 @@
     return jnp.where(places == slot, 1.0, 0.0).astype(jnp.bfloat16)
 
 
-def place_kernel(count, row_count, pos_ref, *refs):
+def place_kernel(count, row_count, spot_ref, *refs):
     block_refs, out_refs, placed_ref = refs[:count], refs[count:-1], refs[-1]
     _, expert_count, capacity, seg_rows = placed_ref.shape
     slot_count = expert_count * capacity
@@ -253,10 +254,10 @@
         placed = placed.reshape(expert_count, capacity, seg_rows)
         placed_ref[offset] = placed.astype(jnp.bfloat16)
         for expert in range(expert_count):
-            out_refs[expert // 2][expert % 2, offset] = placed_ref[offset, pos_ref[1] ^ expert]
-
-
-def unplace_kernel(pos_ref, block_ref, *refs):
+            out_refs[expert // 2][expert % 2, offset] = placed_ref[offset, spot_ref[0] ^ expert]
+
+
+def unplace_kernel(spot_ref, block_ref, *refs):
     returned_refs, out_ref, slots_ref = refs[:-2], refs[-2], refs[-1]
     expert_count, capacity, _ = slots_ref.shape
     slot_count = expert_count * capacity
@@ -264,7 +265,7 @@
     placing = one_hot(block_ref, row_count, slot_count, capacity)
     for expert in range(expert_count):
         block_ref = spread_block(expert_count // 2, returned_refs, expert)
-        slots_ref[pos_ref[1] ^ expert] = block_ref[...]
+        slots_ref[spot_ref[0] ^ expert] = block_ref[...]
     out_ref[0] = contract_first(placing, flat_rows(slots_ref[...])).astype(jnp.bfloat16)
 
 
@@ -276,17 +277,17 @@
     return blocks.reshape(rows, blocks.shape[2])
 
 
-def back_kernel(chips, arrays, pos_ref, weight_ref, *refs):
+def back_kernel(chips, arrays, spot_ref, weight_ref, *refs):
     came_refs, incoming_ref, out_refs = refs[:arrays], refs[arrays], refs[arrays + 1 :]
     for offset, out_ref in enumerate(out_refs):
         for expert in range(2 * chips):
             block_ref = spread_block(chips, came_refs, expert)
-            incoming_ref[offset, pos_ref[1] ^ expert] = block_ref[offset]
+            incoming_ref[offset, spot_ref[0] ^ expert] = block_ref[offset]
         rows = flat_rows(incoming_ref[offset])
-        out_ref[...] = multiply(rows, weight_ref[...]).astype(out_ref.dtype)
-
-
-def forward_kernel(offsets, lengths, has_start, pos_ref, inputs_ref, *refs):
+        out_ref[...] = multiply(rows, weight_ref[0, 2]).astype(out_ref.dtype)
+
+
+def forward_kernel(offsets, lengths, has_start, rep_ref, inputs_ref, *refs):
     out_ref = refs[-1]
     weight_refs = refs[:-1]
     gate = up = None
@@ -295,7 +296,7 @@
         weight_refs = weight_refs[1:]
     for offset, group in zip(offsets, regroup(weight_refs, lengths)):
         gate_ref, up_ref = projection_rows(group)
-        rows = inputs_ref[:, segment(pos_ref, offset, gate_ref.shape[0])]
+        rows = inputs_ref[:, segment(rep_ref, offset, gate_ref.shape[0])]
         gate_part, up_part = multiply(rows, gate_ref[...]), multiply(rows, up_ref[...])
         gate = gate_part if gate is None else gate + gate_part
         up = up_part if up is None else up + up_part
@@ -321,7 +322,7 @@
         out_ref[part, pl.ds(slot_count, half)] = hidden[part * half : (part + 1) * half]
 
 
-def slot_kernel(lengths, pos_ref, factor_ref, *refs):
+def slot_kernel(lengths, rep_ref, spot_ref, factor_ref, *refs):
     chips = refs[-1].shape[1] // 2
     weight_refs, out_refs, slots_ref = refs[: -chips - 1], refs[-chips - 1 : -1], refs[-1]
     _, expert_count, capacity, seg_rows = slots_ref.shape
@@ -332,13 +333,13 @@
         total = contract_last(gate_grad, gate_ref[...]) + contract_last(up_grad, up_ref[...])
         total = total.reshape(expert_count, capacity, seg_rows)
         slots_ref[offset] = total.astype(jnp.bfloat16)
-        columns = segment(pos_ref, offset, seg_rows)
+        columns = segment(rep_ref, offset, seg_rows)
         for expert in range(expert_count):
             out_ref = out_refs[expert // 2]
-            out_ref[expert % 2, :, columns] = slots_ref[offset, pos_ref[1] ^ expert]
-
-
-def gram_kernel(count, offsets, lengths, place, pos_ref, *refs):
+            out_ref[expert % 2, :, columns] = slots_ref[offset, spot_ref[0] ^ expert]
+
+
+def gram_kernel(count, offsets, lengths, place, rep_ref, *refs):
     if place:
         before_ref, earlier_ref, refs = refs[0], refs[1], refs[2:]
     incoming_ref, operand_refs, grads_ref, gram_ref = refs[0], refs[1:-2], refs[-2], refs[-1]
@@ -346,37 +347,48 @@
     seg_rows, hidden_width = grads_ref.shape[2:]
     slot_count = incoming_ref.shape[1] * incoming_ref.shape[2]
     groups = regroup(operand_refs, lengths)
+    known = list(range(place)) + list(offsets)
+    pairs = [(i, j) for i, j in pair_list(len(known)) if j >= place]
+    lines = 8
+    tile = min(seg_rows, 256)
+    sums = [jnp.zeros((lines, hidden_width), jnp.float32) for _ in pairs]
+    operands = []
     for at, offset in enumerate(offsets):
         input_refs, factor_refs = groups[2 * at : 2 * at + 2]
         rest = pl.ds(slot_count, slot_count // 2)
-        columns = input_rows(pos_ref, input_refs, slot_count, seg_rows)
+        columns = input_rows(rep_ref, input_refs, slot_count, seg_rows)
         gate_ref, up_ref = (ref.at[pl.ds(0, slot_count)] for ref in halves(factor_refs))
         first_ref, second_ref = (ref.at[rest] for ref in halves(factor_refs))
-        grads_ref[at, 0] = contract_first(columns, gate_ref[...])
-        grads_ref[at, 1] = contract_first(columns, up_ref[...])
-        grads_ref[at, 2] = contract_first(
-            flat_rows(incoming_ref[offset, :middle]), first_ref[...]
-        ) + contract_first(flat_rows(incoming_ref[offset, middle:]), second_ref[...])
+        upper = flat_rows(incoming_ref[offset, :middle])
+        lower = flat_rows(incoming_ref[offset, middle:])
+        operands.append(
+            [
+                [(columns, gate_ref)],
+                [(columns, up_ref)],
+                [(upper, first_ref), (lower, second_ref)],
+            ]
+        )
+    for matrix in range(3):
+        for start in range(0, seg_rows, tile):
+            rows = pl.ds(start, tile)
+            blocks = [earlier_ref[at, matrix, rows] for at in range(place)]
+            for at in range(len(offsets)):
+                block = None
+                for left, right_ref in operands[at][matrix]:
+                    part = contract_first(left[:, start : start + tile], right_ref[...])
+                    block = part if block is None else block + part
+                grads_ref[at, matrix, rows] = block
+                blocks.append(block)
+            for place_of, (i, j) in enumerate(pairs):
+                products = (blocks[i] * blocks[j]).reshape(tile // lines, lines, hidden_width)
+                sums[place_of] = sums[place_of] + jnp.sum(products, axis=0)
     gram_ref[...] = before_ref[...] if place else jnp.zeros_like(gram_ref)
-    known = list(range(place)) + list(offsets)
-    pairs = [(i, j) for i, j in pair_list(len(known)) if j >= place]
-    lines = 8
-
-    def add(step, sums):
-        rows = pl.ds(pl.multiple_of(lax.rem(step, seg_rows // lines) * lines, lines), lines)
-        matrix = lax.div(step, seg_rows // lines)
-        blocks = [earlier_ref[at, matrix, rows] for at in range(place)]
-        blocks += [grads_ref[at, matrix, rows] for at in range(len(offsets))]
-        return tuple(total + blocks[i] * blocks[j] for total, (i, j) in zip(sums, pairs))
-
-    zero = jnp.zeros((lines, hidden_width), jnp.float32)
-    sums = lax.fori_loop(0, 3 * (seg_rows // lines), add, tuple(zero for _ in pairs), unroll=4)
     for total, (i, j) in zip(sums, pairs):
         total = jnp.sum(total, axis=0, keepdims=True)
         part = total[:, :128]
         for lane in range(128, hidden_width, 128):
             part = part + total[:, lane : lane + 128]
-        first, second = pos_ref[0] ^ known[i], pos_ref[0] ^ known[j]
+        first, second = rep_ref[0] ^ known[i], rep_ref[0] ^ known[j]
         row = jnp.minimum(first, second) * count + jnp.maximum(first, second)
         gram_ref[pl.ds(row, 1), :] = part
 
@@ -411,10 +423,11 @@
     return [vectors[0][rep] for rep in range(count)]
 
 
-def adam_kernel(count, places, pos_ref, *refs):
+def adam_kernel(count, places, rep_ref, *refs):
     gram_refs, grads_refs = refs[:count], refs[count : count + len(places)]
     first_ref, second_ref, step_ref, coef_ref = refs[count + len(places) :]
-    hidden_width = step_ref.shape[3]
+    block_rows, hidden_width = step_ref.shape[2:]
+    lines = coef_ref.shape[1]
 
     @pl.when((pl.program_id(0) == 0) & (pl.program_id(1) == 0))
     def _():
@@ -427,28 +440,30 @@
             coef_ref[rep] = jnp.broadcast_to(coef, coef_ref.shape[1:])
 
     matrix = pl.program_id(0)
-    lines = 16
+    block = pl.program_id(1) * block_rows
+    coefs = [[coef_ref[rep_ref[0] ^ offset] for offset in offsets] for offsets in places]
 
     def step(index, _):
         rows = pl.ds(pl.multiple_of(index * lines, lines), lines)
-        start = pl.program_id(1) * step_ref.shape[2] + index * lines
-        grad_rows = pl.ds(pl.multiple_of(start, lines), lines)
-        merged = None
-        for grads_ref, offsets in zip(grads_refs, places):
-            for at, offset in enumerate(offsets):
-                part = grads_ref[at, matrix, grad_rows] * coef_ref[pos_ref[0] ^ offset]
-                merged = part if merged is None else merged + part
-        first_new = (beta_first / first_fix) * first_ref[0, 0, rows] + (
-            (1.0 - beta_first) / first_fix
-        ) * merged
-        second_new = (beta_second / second_fix) * second_ref[0, 0, rows] + (
-            (1.0 - beta_second) / second_fix
-        ) * (merged * merged)
-        root = second_new * lax.rsqrt(second_new)
-        step_ref[0, 0, rows] = first_new / (root + adam_eps)
+        all_rows = pl.ds(pl.multiple_of(block + index * lines, lines), lines)
+        for lane in range(0, hidden_width, 128):
+            columns = pl.ds(lane, 128)
+            merged = None
+            for grads_ref, group in zip(grads_refs, coefs):
+                for at, coef in enumerate(group):
+                    part = grads_ref[at, matrix, all_rows, columns] * coef
+                    merged = part if merged is None else merged + part
+            first_new = (beta_first / first_fix) * first_ref[0, matrix, all_rows, columns] + (
+                (1.0 - beta_first) / first_fix
+            ) * merged
+            second_new = (beta_second / second_fix) * second_ref[0, matrix, all_rows, columns] + (
+                (1.0 - beta_second) / second_fix
+            ) * (merged * merged)
+            root = second_new * lax.rsqrt(second_new)
+            step_ref[0, 0, rows, columns] = first_new / (root + adam_eps)
         return 0
 
-    lax.fori_loop(0, step_ref.shape[2] // lines, step, 0, unroll=4)
+    lax.fori_loop(0, block_rows // lines, step, 0, unroll=2)
 
 
 def adasum_adam_many(rep, inputs, incoming, factors, first_moment, second_moment):
@@ -530,11 +545,11 @@
         functools.partial(adam_kernel, count, groups),
         "adam",
         [rep, *grams, *grads, first_moment, second_moment],
-        [SMEM] + [VMEM] * (len(grams) + len(grads)) + [moment_spec, moment_spec],
+        [SMEM] + [VMEM] * (len(grams) + len(grads) + 2),
         [jax.ShapeDtypeStruct(first_moment.shape, jnp.float32)],
         out_specs=[moment_spec],
         grid=(3, seg_rows // tile),
-        scratch=[pltpu.VMEM((count, 1, hidden_width), jnp.float32)],
+        scratch=[pltpu.VMEM((count, 16, 128), jnp.float32)],
         after=after,
     )
     return adam_step
@@ -554,7 +569,8 @@
     half = slot_count // 2
     offsets = range(rep_count)
     chips = expert_count // 2
-    rep = jnp.stack([lax.axis_index("replica"), lax.axis_index("expert")]).astype(jnp.int32)
+    rep = lax.axis_index("replica").astype(jnp.int32).reshape(1)
+    spot = lax.axis_index("expert").astype(jnp.int32).reshape(1)
     shape = jax.ShapeDtypeStruct
 
     block = shape((row_count + LABEL_ROWS, seg_rows), jnp.bfloat16)
@@ -571,23 +587,22 @@
     routed = exchange(row_blocks)
 
     inputs_home = saved_inputs[0, 0]
-    pair = weights[0, :2]
     packed = rep_count == 4 and seg_rows == hidden_width
     if packed:
         payload = shape((2 * seg_rows + slot_count + half, seg_rows), jnp.bfloat16)
         to_one, to_two = call(
             payload_kernel,
             "payload",
-            [rep, pair, inputs_home],
+            [rep, weights, inputs_home],
             [SMEM, VMEM, VMEM],
             [payload, payload],
             after=routed[1:],
         )
         from_two, from_one = from_peer(to_two, 2), from_peer(to_one, 1)
-        projections = [(pair,), (from_one,), (from_two,)]
+        projections = [(weights,), (from_one,), (from_two,)]
         inputs = [(inputs_home,), (from_one,), (from_two,)]
     else:
-        projections = [(x,) for x in exchange([pair] * rep_count)]
+        projections = [(x,) for x in exchange([weights[0, :2]] * rep_count)]
         pieces = [shape((slot_count, seg_rows), jnp.bfloat16) for _ in offsets]
         pieces = call(split_kernel, "split", [rep, inputs_home], [SMEM, VMEM], pieces)
         inputs = [(x,) for x in exchange(pieces)]
@@ -597,7 +612,7 @@
         call(
             functools.partial(place_kernel, rep_count, row_count),
             "place",
-            [rep, *routed],
+            [spot, *routed],
             [SMEM] + [VMEM] * len(routed),
             [part] * chips,
             scratch=[
@@ -614,7 +629,7 @@
     incoming, *back = call(
         functools.partial(back_kernel, chips, len(came)),
         "back",
-        [rep, weights[0, 2], *came],
+        [spot, weights, *came],
         [SMEM] + [VMEM] * (1 + len(came)),
         [shape((rep_count, expert_count, capacity, seg_rows), jnp.bfloat16)]
         + [shape(back_shape, jnp.bfloat16 if k else jnp.float32) for k in offsets],
@@ -661,13 +676,13 @@
     )
     near_factors = gather_near(own_factors)
 
-    operands = [rep, own_factors] + flatten(projections)
+    operands = [rep, spot, own_factors] + flatten(projections)
     returning = across_chips(
         call(
             functools.partial(slot_kernel, [len(group) for group in projections]),
             "slots",
             operands,
-            [SMEM] + [VMEM] * (len(operands) - 1),
+            [SMEM] * 2 + [VMEM] * (len(operands) - 2),
             [shape((2, capacity, model_width), jnp.bfloat16)] * chips,
             scratch=[
                 pltpu.VMEM((rep_count, expert_count, capacity, seg_rows), jnp.bfloat16)
@@ -684,7 +699,7 @@
     (input_grads,) = call(
         unplace_kernel,
         "unplace",
-        [rep, routed[0], *returned],
+        [spot, routed[0], *returned],
         [SMEM] + [VMEM] * (1 + len(returned)),
         [shape((1, row_count, model_width), jnp.bfloat16)],
         scratch=[pltpu.VMEM((expert_count, capacity, model_width), jnp.bfloat16)],

time: 118 us -> 121 us (1.025)
  waiting for transfers between devices: 59.5 us -> 62.7 us
  local copies, waits for them, and re-layouts: 2.39 us -> 3.62 us
    unnamed x10 -> x18, local copies, waits for them, and re-layouts: 0.02 us -> 3.62 us
    squeeze x2 -> x0, local copies, waits for them, and re-layouts: 2.37 us -> none  [the longest x1 1.29 us: shards(): pair = weights[0, :2]]
  transfers between devices with their start and end apart: 26 -> 26, of which waited for: 15 -> 15; matrix products, arithmetic and copies ran while one was open for 2% -> 0% of each run, Pallas kernels for 13% -> 10%
where the time goes in v7:
time: 121 us
  waiting for transfers between devices  62.7 us (52%)
  starting transfers between devices  30.3 us (25%)
  Pallas kernels  22.6 us (19%)
  local copies, waits for them, and re-layouts  3.62 us (3%)
  between operations  1.43 us (1%)
    ppermute x17, waiting for transfers between devices, from_peer(): lax.ppermute(array, 'replica', [(i, i ^ offset) for i in range(count)])  40.9 us
    pallas_call x16, Pallas kernels, call(): pl.pallas_call(body, grid=grid, in_specs=list(specs) + [VMEM] * len(after...  22.6 us
    ppermute x6, waiting for transfers between devices, across_chips(): lax.ppermute(part, 'expert', [(i, i ^ 2 * k) for i in range(count)])  19.8 us
    ppermute x17, starting transfers between devices, from_peer(): lax.ppermute(array, 'replica', [(i, i ^ offset) for i in range(count)])  19.8 us
    ppermute x6, starting transfers between devices, across_chips(): lax.ppermute(part, 'expert', [(i, i ^ 2 * k) for i in range(count)])  9.83 us
    unnamed x18, local copies, waits for them, and re-layouts  3.62 us
  transfers between devices with their start and end apart: 26, of which 15 were waited for; matrix products, arithmetic and copies ran while one was open for 0% of the time, Pallas kernels for 10%

profile of v7, /device:TPU:0, one launch (start us, length us, event | category | flops | bytes accessed | tf_op | source)
XLA Modules:
  0.0 120.6 jit_solution(6459651095079741145)
XLA Ops:
  1.3 2.0 %rows.1 = (bf16[144,512]{1,0:T(8,128)(2,1)}, bf16[144,512]{1,0:T(8,128)(2,1)}, bf16[144,512]{1,0:T(8,128)(2,1)}, bf16[144,512]{1,0:T(8,128)(2,1)}) custom-call(s32[1]{0:T(128)} %bitcast.1.refs_0_, s32[1,1]{1,0:T(1,128)S(6)} %copy.10.refs_1_, f32[8]{0:T(128)} %refs_2_.2, s32[1,128]{1,0:T(1,128)} %bitcast.10, bf16[128,2048]{1,0:T(8,128)(2,1)} %bitcast.9), custom_call_target="tpu_custom_call" | custom-call | tf_op jit(solution)/shard_map/rows/pallas_call | solution.py:187
  3.3 2.9 %collective-permute-start = (bf16[144,512]{1,0:T(8,128)(2,1)}, bf16[144,512]{1,0:T(8,128)(2,1)S(1)}, u32[]{:S(2)}, u32[]{:S(2)}) collective-permute-start(bf16[144,512]{1,0:T(8,128)(2,1)} %get-tuple-element.32), channel_id=1, source_target_pairs={{0,1},{1,0},{2,3},{3,2},{4,5},{5,4},{6,7},{7,6},{8,9},{9,8},{10,11... | collective-permute-start | bytes 442376 | tf_op jit(solution)/shard_map/ppermute | solution.py:38
  6.2 1.5 %collective-permute-start.1 = (bf16[144,512]{1,0:T(8,128)(2,1)}, bf16[144,512]{1,0:T(8,128)(2,1)S(1)}, u32[]{:S(2)}, u32[]{:S(2)}) collective-permute-start(bf16[144,512]{1,0:T(8,128)(2,1)} %get-tuple-element.33), channel_id=1, source_target_pairs={{0,2},{1,3},{2,0},{3,1},{4,6},{5,7},{6,4},{7,5},{8,10},{9,11},{10,... | collective-permute-start | bytes 442376 | tf_op jit(solution)/shard_map/ppermute | solution.py:38
  7.8 0.0 collective-permute-start.2
  7.8 3.0 %collective-permute-done.refs_3_.refs_2_ = bf16[144,512]{1,0:T(8,128)(2,1)S(1)} collective-permute-done((bf16[144,512]{1,0:T(8,128)(2,1)}, bf16[144,512]{1,0:T(8,128)(2,1)S(1)}, u32[]{:S(2)}, u32[]{:S(2)}) %collective-permute-start) | collective-permute-done | bytes 147488 | tf_op jit(solution)/shard_map/ppermute | solution.py:38
  10.8 4.1 %collective-permute-done.1.refs_4_.refs_3_ = bf16[144,512]{1,0:T(8,128)(2,1)S(1)} collective-permute-done((bf16[144,512]{1,0:T(8,128)(2,1)}, bf16[144,512]{1,0:T(8,128)(2,1)S(1)}, u32[]{:S(2)}, u32[]{:S(2)}) %collective-permute-start.1) | collective-permute-done | bytes 147488 | tf_op jit(solution)/shard_map/ppermute | solution.py:38
  14.9 1.5 %copy-done = bf16[1,3,512,512]{3,2,1,0:T(8,128)(2,1)S(1)} copy-done((bf16[1,3,512,512]{3,2,1,0:T(8,128)(2,1)S(1)}, bf16[1,3,512,512]{3,2,1,0:T(8,128)(2,1)}, u32[]{:S(2)}) %copy-start) | copy-done | bytes 1572888
  16.4 1.2 %copy-done.2 = bf16[1,1,256,2048]{3,2,1,0:T(8,128)(2,1)S(1)} copy-done((bf16[1,1,256,2048]{3,2,1,0:T(8,128)(2,1)S(1)}, bf16[1,1,256,2048]{3,2,1,0:T(8,128)(2,1)}, u32[]{:S(2)}) %copy-start.2) | copy-done | bytes 1048600
  17.6 1.8 %payload.1 = (bf16[1408,512]{1,0:T(8,128)(2,1)}, bf16[1408,512]{1,0:T(8,128)(2,1)}) custom-call(s32[1]{0:T(128)} %bitcast.1.refs_0_, bf16[1,3,512,512]{3,2,1,0:T(8,128)(2,1)S(1)} %copy-done, bf16[256,2048]{1,0:T(8,128)(2,1)S(1)} %bitcast.5, bf16[144,512]{1,0:T(8,128)(2,1)S(1)} %collective-permute-done.refs_3_.refs_2_, ...), custom_call_target="tpu_custom_call" | custom-call | tf_op jit(solution)/shard_map/payload/pallas_call | solution.py:187
  19.4 1.2 %collective-permute-start.3 = (bf16[1408,512]{1,0:T(8,128)(2,1)}, bf16[1408,512]{1,0:T(8,128)(2,1)S(1)}, u32[]{:S(2)}, u32[]{:S(2)}) collective-permute-start(bf16[1408,512]{1,0:T(8,128)(2,1)} %get-tuple-element.35), channel_id=1, source_target_pairs={{0,1},{1,0},{2,3},{3,2},{4,5},{5,4},{6,7},{7,6},{8,9},{9,8},{10,11... | collective-permute-start | bytes 4325384 | tf_op jit(solution)/shard_map/ppermute | solution.py:38
  20.7 0.8 collective-permute-start.4
  21.5 0.9 copy-done.8
  22.4 0.4 place.1
  22.8 1.6 %collective-permute-start.5 = (bf16[2,4,32,512]{3,2,1,0:T(8,128)(2,1)S(1)}, bf16[2,4,32,512]{3,2,1,0:T(8,128)(2,1)S(1)}, u32[]{:S(2)}, u32[]{:S(2)}) collective-permute-start(bf16[2,4,32,512]{3,2,1,0:T(8,128)(2,1)S(1)} %get-tuple-element.38), channel_id=1, source_target_pairs={{0,8},{4,12},{8,0},{12,4},{16,24},{20,28},{24,16},{28,20},{1,9},{5... | collective-permute-start | bytes 786440 | tf_op jit(solution)/shard_map/ppermute | solution.py:44
  24.5 2.6 %collective-permute-start.6 = (bf16[2,4,32,512]{3,2,1,0:T(8,128)(2,1)S(1)}, bf16[2,4,32,512]{3,2,1,0:T(8,128)(2,1)S(1)}, u32[]{:S(2)}, u32[]{:S(2)}) collective-permute-start(bf16[2,4,32,512]{3,2,1,0:T(8,128)(2,1)S(1)} %get-tuple-element.39), channel_id=1, source_target_pairs={{0,16},{4,20},{8,24},{12,28},{16,0},{20,4},{24,8},{28,12},{1,17},{... | collective-permute-start | bytes 786440 | tf_op jit(solution)/shard_map/ppermute | solution.py:44
  27.1 0.2 collective-permute-start.7
  27.3 5.7 %collective-permute-done.5.refs_1_.refs_3_ = bf16[2,4,32,512]{3,2,1,0:T(8,128)(2,1)S(1)} collective-permute-done((bf16[2,4,32,512]{3,2,1,0:T(8,128)(2,1)S(1)}, bf16[2,4,32,512]{3,2,1,0:T(8,128)(2,1)S(1)}, u32[]{:S(2)}, u32[]{:S(2)}) %collective-permute-start.5) | collective-permute-done | bytes 262176 | tf_op jit(solution)/shard_map/ppermute | solution.py:44
  33.0 12.5 %collective-permute-done.6.refs_2_.refs_4_ = bf16[2,4,32,512]{3,2,1,0:T(8,128)(2,1)S(1)} collective-permute-done((bf16[2,4,32,512]{3,2,1,0:T(8,128)(2,1)S(1)}, bf16[2,4,32,512]{3,2,1,0:T(8,128)(2,1)S(1)}, u32[]{:S(2)}, u32[]{:S(2)}) %collective-permute-start.6) | collective-permute-done | bytes 262176 | tf_op jit(solution)/shard_map/ppermute | solution.py:44
  45.5 0.0 copy-start.3
  45.5 0.1 collective-permute-start.8
  45.6 1.9 %collective-permute-done.8.refs_6_ = bf16[4,4,32,512]{3,2,1,0:T(8,128)(2,1)S(1)} collective-permute-done((bf16[4,4,32,512]{3,2,1,0:T(8,128)(2,1)S(1)}, bf16[4,4,32,512]{3,2,1,0:T(8,128)(2,1)S(1)}, u32[]{:S(2)}, u32[]{:S(2)}) %collective-permute-start.8) | collective-permute-done | bytes 524320 | tf_op jit(solution)/shard_map/ppermute | solution.py:68
  47.5 0.7 back.1
  48.3 3.8 %collective-permute-done.3.refs_3_.refs_1_.refs_4_ = bf16[1408,512]{1,0:T(8,128)(2,1)S(1)} collective-permute-done((bf16[1408,512]{1,0:T(8,128)(2,1)}, bf16[1408,512]{1,0:T(8,128)(2,1)S(1)}, u32[]{:S(2)}, u32[]{:S(2)}) %collective-permute-start.3) | collective-permute-done | bytes 1441824 | tf_op jit(solution)/shard_map/ppermute | solution.py:38
  52.0 1.1 collective-permute-done.4.refs_4_.refs_0_.refs_5_.refs_6_
  53.1 1.4 %pass.1 = (bf16[640,512]{1,0:T(8,128)(2,1)S(1)}, bf16[640,512]{1,0:T(8,128)(2,1)S(1)}) custom-call(bf16[1408,512]{1,0:T(8,128)(2,1)} %collective-permute-done.4.refs_4_.refs_0_.refs_5_.refs_6_, bf16[1408,512]{1,0:T(8,128)(2,1)S(1)} %collective-permute-done.3.refs_3_.refs_1_.refs_4_, f32[256,512]{1,0:T(8,128)S(1)} %get-tuple-element.41.refs_2_.refs_1_), custom_call_target="tpu_custom_call" | custom-call | tf_op jit(solution)/shard_map/pass/pallas_call | solution.py:187
  54.6 0.8 collective-permute-start.9
  55.4 1.4 %collective-permute-start.10 = (bf16[640,512]{1,0:T(8,128)(2,1)S(1)}, bf16[640,512]{1,0:T(8,128)(2,1)S(1)}, u32[]{:S(2)}, u32[]{:S(2)}) collective-permute-start(bf16[640,512]{1,0:T(8,128)(2,1)S(1)} %get-tuple-element.43), channel_id=1, source_target_pairs={{0,2},{1,3},{2,0},{3,1},{4,6},{5,7},{6,4},{7,5},{8,10},{9,11},{10,... | collective-permute-start | bytes 1966088 | tf_op jit(solution)/shard_map/ppermute | solution.py:38
  56.8 0.4 collective-permute-start.11
  57.2 1.5 %collective-permute-start.12 = (bf16[256,512]{1,0:T(8,128)(2,1)S(1)}, bf16[256,512]{1,0:T(8,128)(2,1)S(1)}, u32[]{:S(2)}, u32[]{:S(2)}) collective-permute-start(bf16[256,512]{1,0:T(8,128)(2,1)S(1)} %get-tuple-element.45), channel_id=1, source_target_pairs={{0,2},{1,3},{2,0},{3,1},{4,6},{5,7},{6,4},{7,5},{8,10},{9,11},{10,... | collective-permute-start | bytes 786440 | tf_op jit(solution)/shard_map/ppermute | solution.py:38
  58.7 1.5 %collective-permute-start.13 = (bf16[256,512]{1,0:T(8,128)(2,1)S(1)}, bf16[256,512]{1,0:T(8,128)(2,1)S(1)}, u32[]{:S(2)}, u32[]{:S(2)}) collective-permute-start(bf16[256,512]{1,0:T(8,128)(2,1)S(1)} %get-tuple-element.46), channel_id=1, source_target_pairs={{0,3},{1,2},{2,1},{3,0},{4,7},{5,6},{6,5},{7,4},{8,11},{9,10},{10,... | collective-permute-start | bytes 786440 | tf_op jit(solution)/shard_map/ppermute | solution.py:38
  60.3 2.3 %forward.1.refs_2_ = f32[2,256,512]{2,1,0:T(8,128)S(1)} custom-call(s32[1]{0:T(128)} %bitcast.1.refs_0_, bf16[256,2048]{1,0:T(8,128)(2,1)S(1)} %bitcast.6, bf16[1,3,512,512]{3,2,1,0:T(8,128)(2,1)S(1)} %copy-done.1, bf16[1408,512]{1,0:T(8,128)(2,1)S(1)} %collective-permute-done.3.refs_3_.refs_1_.refs_4_, ...), custom_call_target="tpu_custom_call" | custom-call | tf_op jit(solution)/shard_map/forward/pallas_call | solution.py:187
  62.6 9.7 %collective-permute-done.9.refs_3_.refs_6_.refs_4_ = bf16[640,512]{1,0:T(8,128)(2,1)S(1)} collective-permute-done((bf16[640,512]{1,0:T(8,128)(2,1)S(1)}, bf16[640,512]{1,0:T(8,128)(2,1)S(1)}, u32[]{:S(2)}, u32[]{:S(2)}) %collective-permute-start.9) | collective-permute-done | bytes 655392 | tf_op jit(solution)/shard_map/ppermute | solution.py:38
  72.3 1.0 collective-permute-done.10.refs_4_.refs_7_.refs_5_
  73.3 0.4 rest.1.refs_0_
  73.8 3.7 %collective-permute-done.11.refs_2_ = bf16[256,512]{1,0:T(8,128)(2,1)S(1)} collective-permute-done((bf16[256,512]{1,0:T(8,128)(2,1)S(1)}, bf16[256,512]{1,0:T(8,128)(2,1)S(1)}, u32[]{:S(2)}, u32[]{:S(2)}) %collective-permute-start.11) | collective-permute-done | bytes 262176 | tf_op jit(solution)/shard_map/ppermute | solution.py:38
  77.5 3.2 %collective-permute-done.12.refs_3_ = bf16[256,512]{1,0:T(8,128)(2,1)S(1)} collective-permute-done((bf16[256,512]{1,0:T(8,128)(2,1)S(1)}, bf16[256,512]{1,0:T(8,128)(2,1)S(1)}, u32[]{:S(2)}, u32[]{:S(2)}) %collective-permute-start.12) | collective-permute-done | bytes 262176 | tf_op jit(solution)/shard_map/ppermute | solution.py:38
  80.7 0.0 collective-permute-done.13.refs_4_
  80.7 0.4 factors.1.refs_2_.refs_3_
  81.1 1.7 %collective-permute-start.17 = (bf16[2,384,512]{2,1,0:T(8,128)(2,1)S(1)}, bf16[2,384,512]{2,1,0:T(8,128)(2,1)S(1)}, u32[]{:S(2)}, u32[]{:S(2)}) collective-permute-start(bf16[2,384,512]{2,1,0:T(8,128)(2,1)S(1)} %factors.1.refs_2_.refs_3_), channel_id=1, source_target_pairs={{0,1},{1,0},{2,3},{3,2},{4,5},{5,4},{6,7},{7,6},{8,9},{9,8},{10,11... | collective-permute-start | bytes 2359304 | tf_op jit(solution)/shard_map/ppermute | solution.py:38
  82.7 0.2 collective-permute-start.18
  82.9 2.7 %slots.1 = (bf16[2,32,2048]{2,1,0:T(8,128)(2,1)S(1)}, bf16[2,32,2048]{2,1,0:T(8,128)(2,1)S(1)}, bf16[2,32,2048]{2,1,0:T(8,128)(2,1)S(1)}, bf16[2,32,2048]{2,1,0:T(8,128)(2,1)S(1)}) custom-call(s32[1]{0:T(128)} %bitcast.1.refs_0_, s32[1]{0:T(128)} %bitcast.refs_0_.refs_1_, bf16[2,384,512]{2,1,0:T(8,128)(2,1)S(1)} %factors.1.refs_2_.refs_3_, ...), custom_call_target="tpu_custom_call" | custom-call | tf_op jit(solution)/shard_map/slots/pallas_call | solution.py:187
  85.6 2.0 %collective-permute-start.14 = (bf16[2,32,2048]{2,1,0:T(8,128)(2,1)S(1)}, bf16[2,32,2048]{2,1,0:T(8,128)(2,1)S(1)}, u32[]{:S(2)}, u32[]{:S(2)}) collective-permute-start(bf16[2,32,2048]{2,1,0:T(8,128)(2,1)S(1)} %get-tuple-element.48), channel_id=1, source_target_pairs={{0,8},{4,12},{8,0},{12,4},{16,24},{20,28},{24,16},{28,20},{1,9},{5... | collective-permute-start | bytes 786440 | tf_op jit(solution)/shard_map/ppermute | solution.py:44
  87.6 3.4 %collective-permute-start.15 = (bf16[2,32,2048]{2,1,0:T(8,128)(2,1)S(1)}, bf16[2,32,2048]{2,1,0:T(8,128)(2,1)S(1)}, u32[]{:S(2)}, u32[]{:S(2)}) collective-permute-start(bf16[2,32,2048]{2,1,0:T(8,128)(2,1)S(1)} %get-tuple-element.49), channel_id=1, source_target_pairs={{0,16},{4,20},{8,24},{12,28},{16,0},{20,4},{24,8},{28,12},{1,17},{... | collective-permute-start | bytes 786440 | tf_op jit(solution)/shard_map/ppermute | solution.py:44
  91.0 7.7 %collective-permute-done.17.refs_5_.refs_1_ = bf16[2,384,512]{2,1,0:T(8,128)(2,1)S(1)} collective-permute-done((bf16[2,384,512]{2,1,0:T(8,128)(2,1)S(1)}, bf16[2,384,512]{2,1,0:T(8,128)(2,1)S(1)}, u32[]{:S(2)}, u32[]{:S(2)}) %collective-permute-start.17) | collective-permute-done | bytes 786464 | tf_op jit(solution)/shard_map/ppermute | solution.py:38
  98.7 0.0 collective-permute-done.18.refs_7_.refs_0_
  98.7 0.1 cut.1
  98.8 1.7 %collective-permute-start.21 = (bf16[384,512]{1,0:T(8,128)(2,1)S(1)}, bf16[384,512]{1,0:T(8,128)(2,1)S(1)}, u32[]{:S(2)}, u32[]{:S(2)}) collective-permute-start(bf16[384,512]{1,0:T(8,128)(2,1)S(1)} %get-tuple-element.56), channel_id=1, source_target_pairs={{0,1},{1,0},{2,3},{3,2},{4,5},{5,4},{6,7},{7,6},{8,9},{9,8},{10,11... | collective-permute-start | bytes 1179656 | tf_op jit(solution)/shard_map/ppermute | solution.py:38
  100.5 0.5 collective-permute-start.22
  101.0 3.4 %gram.1 = (f32[3,3,512,512]{3,2,1,0:T(8,128)S(1)}, f32[16,128]{1,0:T(8,128)S(1)}) custom-call(s32[1]{0:T(128)} %bitcast.1.refs_0_, bf16[4,8,32,512]{3,2,1,0:T(8,128)(2,1)S(1)} %get-tuple-element.51.refs_1_.refs_3_, bf16[256,2048]{1,0:T(8,128)(2,1)S(1)} %bitcast.8, bf16[2,384,512]{2,1,0:T(8,128)(2,1)S(1)} %factors.1.refs_2_.refs_3_, ...), custom_call_target="tpu_custom_call" | custom-call | tf_op jit(solution)/shard_map/gram/pallas_call | solution.py:187
  104.4 0.0 collective-permute-done.14.refs_1_.refs_3_
  104.4 1.6 %collective-permute-done.15.refs_2_.refs_4_ = bf16[2,32,2048]{2,1,0:T(8,128)(2,1)S(1)} collective-permute-done((bf16[2,32,2048]{2,1,0:T(8,128)(2,1)S(1)}, bf16[2,32,2048]{2,1,0:T(8,128)(2,1)S(1)}, u32[]{:S(2)}, u32[]{:S(2)}) %collective-permute-start.15) | collective-permute-done | bytes 262176 | tf_op jit(solution)/shard_map/ppermute | solution.py:44
  106.0 0.0 collective-permute-done.16.refs_3_.refs_5_
  106.1 0.1 collective-permute-start.19
  106.2 0.5 collective-permute-start.20
  106.7 1.6 %collective-permute-done.22.refs_7_ = bf16[384,512]{1,0:T(8,128)(2,1)S(1)} collective-permute-done((bf16[384,512]{1,0:T(8,128)(2,1)S(1)}, bf16[384,512]{1,0:T(8,128)(2,1)S(1)}, u32[]{:S(2)}, u32[]{:S(2)}) %collective-permute-start.22) | collective-permute-done | bytes 393248 | tf_op jit(solution)/shard_map/ppermute | solution.py:38
  108.3 1.2 %gram_late.1 = (f32[1,3,512,512]{3,2,1,0:T(8,128)S(1)}, f32[16,128]{1,0:T(8,128)S(1)}) custom-call(s32[1]{0:T(128)} %bitcast.1.refs_0_, f32[16,128]{1,0:T(8,128)S(1)} %get-tuple-element.52.refs_4_.refs_1_, f32[3,3,512,512]{3,2,1,0:T(8,128)S(1)} %get-tuple-element.55.refs_2_.refs_5_, bf16[4,8,32,512]{3,2,1,0:T(8,128)(2,1)S(1)} %get-tuple-element.51.refs_1_.refs_3_, ...), custom_call_target="tpu_custom_call" | custom-call | tf_op jit(solution)/shard_map/gram_late/pallas_call | solution.py:187
  109.5 0.4 collective-permute-start.23
  109.9 1.7 %collective-permute-start.24 = (f32[16,128]{1,0:T(8,128)S(1)}, f32[16,128]{1,0:T(8,128)S(1)}, u32[]{:S(2)}, u32[]{:S(2)}) collective-permute-start(f32[16,128]{1,0:T(8,128)S(1)} %get-tuple-element.58.refs_8_.refs_1_), channel_id=1, source_target_pairs={{0,2},{1,3},{2,0},{3,1},{4,6},{5,7},{6,4},{7,5},{8,10},{9,11},{10,... | collective-permute-start | bytes 24584 | tf_op jit(solution)/shard_map/ppermute | solution.py:38
  111.6 1.5 %collective-permute-start.25 = (f32[16,128]{1,0:T(8,128)S(1)}, f32[16,128]{1,0:T(8,128)S(1)}, u32[]{:S(2)}, u32[]{:S(2)}) collective-permute-start(f32[16,128]{1,0:T(8,128)S(1)} %get-tuple-element.58.refs_8_.refs_1_), channel_id=1, source_target_pairs={{0,3},{1,2},{2,1},{3,0},{4,7},{5,6},{6,5},{7,4},{8,11},{9,10},{10,... | collective-permute-start | bytes 24584 | tf_op jit(solution)/shard_map/ppermute | solution.py:38
  113.0 0.0 collective-permute-done.20.refs_7_
  113.0 1.2 unplace.1
  114.2 0.0 collective-permute-done.23.refs_2_
  114.2 1.9 %collective-permute-done.25.refs_4_ = f32[16,128]{1,0:T(8,128)S(1)} collective-permute-done((f32[16,128]{1,0:T(8,128)S(1)}, f32[16,128]{1,0:T(8,128)S(1)}, u32[]{:S(2)}, u32[]{:S(2)}) %collective-permute-start.25) | collective-permute-done | bytes 8224 | tf_op jit(solution)/shard_map/ppermute | solution.py:38
  116.1 4.5 %adam.1 = f32[1,3,512,512]{3,2,1,0:T(8,128)} custom-call(s32[1]{0:T(128)} %bitcast.1.refs_0_, f32[16,128]{1,0:T(8,128)S(1)} %get-tuple-element.58.refs_8_.refs_1_, f32[16,128]{1,0:T(8,128)S(1)} %collective-permute-done.23.refs_2_, f32[16,128]{1,0:T(8,128)S(1)} %collective-permute-done.24.refs_3_, f32[16,128]{1,0:T(8,128)S(1)} %collective-permute-done.25.refs_4_, ...), custom_call_target="tpu_custom_call" | custom-call | tf_op jit(solution)/shard_map/adam/pallas_call | solution.py:187
  (22 shorter events, 0.1 us)
Async XLA Ops:
  3.3 7.5 %collective-permute-start = (bf16[144,512]{1,0:T(8,128)(2,1)}, bf16[144,512]{1,0:T(8,128)(2,1)S(1)}, u32[]{:S(2)}, u32[]{:S(2)}) collective-permute-start(bf16[144,512]{1,0:T(8,128)(2,1)} %get-tuple-element.32), channel_id=1, source_target_pairs={{0,1},{1,0},{2,3},{3,2},{4,5},{5,4},{6,7},{7,6},{8,9},{9,8},{10,11... | collective-permute-start | bytes 442376 | tf_op jit(solution)/shard_map/ppermute | solution.py:38
  6.2 8.7 %collective-permute-start.1 = (bf16[144,512]{1,0:T(8,128)(2,1)}, bf16[144,512]{1,0:T(8,128)(2,1)S(1)}, u32[]{:S(2)}, u32[]{:S(2)}) collective-permute-start(bf16[144,512]{1,0:T(8,128)(2,1)} %get-tuple-element.33), channel_id=1, source_target_pairs={{0,2},{1,3},{2,0},{3,1},{4,6},{5,7},{6,4},{7,5},{8,10},{9,11},{10,... | collective-permute-start | bytes 442376 | tf_op jit(solution)/shard_map/ppermute | solution.py:38
  7.8 7.2 %collective-permute-start.2 = (bf16[144,512]{1,0:T(8,128)(2,1)}, bf16[144,512]{1,0:T(8,128)(2,1)S(1)}, u32[]{:S(2)}, u32[]{:S(2)}) collective-permute-start(bf16[144,512]{1,0:T(8,128)(2,1)} %get-tuple-element.34), channel_id=1, source_target_pairs={{0,3},{1,2},{2,1},{3,0},{4,7},{5,6},{6,5},{7,4},{8,11},{9,10},{10,... | collective-permute-start | bytes 442376 | tf_op jit(solution)/shard_map/ppermute | solution.py:38
  14.9 4.5 %copy-start.7 = (bf16[144,512]{1,0:T(8,128)(2,1)}, bf16[144,512]{1,0:T(8,128)(2,1)S(1)}, u32[]{:S(2)}) copy-start(bf16[144,512]{1,0:T(8,128)(2,1)S(1)} %collective-permute-done.2.refs_5_.refs_4_) | copy-start | bytes 442372
  14.9 1.5 %copy-start = (bf16[1,3,512,512]{3,2,1,0:T(8,128)(2,1)S(1)}, bf16[1,3,512,512]{3,2,1,0:T(8,128)(2,1)}, u32[]{:S(2)}) copy-start(bf16[1,3,512,512]{3,2,1,0:T(8,128)(2,1)} %refs_3_.1) | copy-start | bytes 4718596
  16.4 1.2 %copy-start.2 = (bf16[1,1,256,2048]{3,2,1,0:T(8,128)(2,1)S(1)}, bf16[1,1,256,2048]{3,2,1,0:T(8,128)(2,1)}, u32[]{:S(2)}) copy-start(bf16[1,1,256,2048]{3,2,1,0:T(8,128)(2,1)} %param.15) | copy-start | bytes 3145732
  17.6 3.9 %copy-start.6 = (bf16[144,512]{1,0:T(8,128)(2,1)S(1)}, bf16[144,512]{1,0:T(8,128)(2,1)}, u32[]{:S(2)}) copy-start(bf16[144,512]{1,0:T(8,128)(2,1)} %get-tuple-element.31.refs_1_) | copy-start | bytes 442372
  17.6 29.9 %copy-start.1 = (bf16[1,3,512,512]{3,2,1,0:T(8,128)(2,1)S(1)}, bf16[1,3,512,512]{3,2,1,0:T(8,128)(2,1)}, u32[]{:S(2)}) copy-start(bf16[1,3,512,512]{3,2,1,0:T(8,128)(2,1)} %refs_3_.1) | copy-start | bytes 4718596
  19.4 32.6 %collective-permute-start.3 = (bf16[1408,512]{1,0:T(8,128)(2,1)}, bf16[1408,512]{1,0:T(8,128)(2,1)S(1)}, u32[]{:S(2)}, u32[]{:S(2)}) collective-permute-start(bf16[1408,512]{1,0:T(8,128)(2,1)} %get-tuple-element.35), channel_id=1, source_target_pairs={{0,1},{1,0},{2,3},{3,2},{4,5},{5,4},{6,7},{7,6},{8,9},{9,8},{10,11... | collective-permute-start | bytes 4325384 | tf_op jit(solution)/shard_map/ppermute | solution.py:38
  20.7 32.5 %collective-permute-start.4 = (bf16[1408,512]{1,0:T(8,128)(2,1)}, bf16[1408,512]{1,0:T(8,128)(2,1)}, u32[]{:S(2)}, u32[]{:S(2)}) collective-permute-start(bf16[1408,512]{1,0:T(8,128)(2,1)} %get-tuple-element.36), channel_id=1, source_target_pairs={{0,2},{1,3},{2,0},{3,1},{4,6},{5,7},{6,4},{7,5},{8,10},{9,11},{10,... | collective-permute-start | bytes 4325384 | tf_op jit(solution)/shard_map/ppermute | solution.py:38
  21.5 0.9 copy-start.8
  22.8 10.2 %collective-permute-start.5 = (bf16[2,4,32,512]{3,2,1,0:T(8,128)(2,1)S(1)}, bf16[2,4,32,512]{3,2,1,0:T(8,128)(2,1)S(1)}, u32[]{:S(2)}, u32[]{:S(2)}) collective-permute-start(bf16[2,4,32,512]{3,2,1,0:T(8,128)(2,1)S(1)} %get-tuple-element.38), channel_id=1, source_target_pairs={{0,8},{4,12},{8,0},{12,4},{16,24},{20,28},{24,16},{28,20},{1,9},{5... | collective-permute-start | bytes 786440 | tf_op jit(solution)/shard_map/ppermute | solution.py:44
  24.5 21.0 %collective-permute-start.6 = (bf16[2,4,32,512]{3,2,1,0:T(8,128)(2,1)S(1)}, bf16[2,4,32,512]{3,2,1,0:T(8,128)(2,1)S(1)}, u32[]{:S(2)}, u32[]{:S(2)}) collective-permute-start(bf16[2,4,32,512]{3,2,1,0:T(8,128)(2,1)S(1)} %get-tuple-element.39), channel_id=1, source_target_pairs={{0,16},{4,20},{8,24},{12,28},{16,0},{20,4},{24,8},{28,12},{1,17},{... | collective-permute-start | bytes 786440 | tf_op jit(solution)/shard_map/ppermute | solution.py:44
  27.1 18.4 %collective-permute-start.7 = (bf16[2,4,32,512]{3,2,1,0:T(8,128)(2,1)S(1)}, bf16[2,4,32,512]{3,2,1,0:T(8,128)(2,1)S(1)}, u32[]{:S(2)}, u32[]{:S(2)}) collective-permute-start(bf16[2,4,32,512]{3,2,1,0:T(8,128)(2,1)S(1)} %get-tuple-element.40), channel_id=1, source_target_pairs={{0,24},{4,28},{8,16},{12,20},{16,8},{20,12},{24,0},{28,4},{1,25},{... | collective-permute-start | bytes 786440 | tf_op jit(solution)/shard_map/ppermute | solution.py:44
  45.5 14.7 %copy-start.3 = (bf16[1,1,256,2048]{3,2,1,0:T(8,128)(2,1)S(1)}, bf16[1,1,256,2048]{3,2,1,0:T(8,128)(2,1)}, u32[]{:S(2)}) copy-start(bf16[1,1,256,2048]{3,2,1,0:T(8,128)(2,1)} %param.15) | copy-start | bytes 3145732
  45.5 2.0 %collective-permute-start.8 = (bf16[4,4,32,512]{3,2,1,0:T(8,128)(2,1)S(1)}, bf16[4,4,32,512]{3,2,1,0:T(8,128)(2,1)S(1)}, u32[]{:S(2)}, u32[]{:S(2)}) collective-permute-start(bf16[4,4,32,512]{3,2,1,0:T(8,128)(2,1)S(1)} %pick.2), channel_id=1, source_target_pairs={{0,4},{4,0},{8,12},{12,8},{16,20},{20,16},{24,28},{28,24},{1,5},{5... | collective-permute-start | bytes 1572872 | tf_op jit(solution)/shard_map/ppermute | solution.py:68
  54.6 17.7 %collective-permute-start.9 = (bf16[640,512]{1,0:T(8,128)(2,1)S(1)}, bf16[640,512]{1,0:T(8,128)(2,1)S(1)}, u32[]{:S(2)}, u32[]{:S(2)}) collective-permute-start(bf16[640,512]{1,0:T(8,128)(2,1)S(1)} %get-tuple-element.42), channel_id=1, source_target_pairs={{0,1},{1,0},{2,3},{3,2},{4,5},{5,4},{6,7},{7,6},{8,9},{9,8},{10,11... | collective-permute-start | bytes 1966088 | tf_op jit(solution)/shard_map/ppermute | solution.py:38
  55.4 17.9 %collective-permute-start.10 = (bf16[640,512]{1,0:T(8,128)(2,1)S(1)}, bf16[640,512]{1,0:T(8,128)(2,1)S(1)}, u32[]{:S(2)}, u32[]{:S(2)}) collective-permute-start(bf16[640,512]{1,0:T(8,128)(2,1)S(1)} %get-tuple-element.43), channel_id=1, source_target_pairs={{0,2},{1,3},{2,0},{3,1},{4,6},{5,7},{6,4},{7,5},{8,10},{9,11},{10,... | collective-permute-start | bytes 1966088 | tf_op jit(solution)/shard_map/ppermute | solution.py:38
  56.8 20.7 %collective-permute-start.11 = (bf16[256,512]{1,0:T(8,128)(2,1)S(1)}, bf16[256,512]{1,0:T(8,128)(2,1)S(1)}, u32[]{:S(2)}, u32[]{:S(2)}) collective-permute-start(bf16[256,512]{1,0:T(8,128)(2,1)S(1)} %get-tuple-element.44), channel_id=1, source_target_pairs={{0,1},{1,0},{2,3},{3,2},{4,5},{5,4},{6,7},{7,6},{8,9},{9,8},{10,11... | collective-permute-start | bytes 786440 | tf_op jit(solution)/shard_map/ppermute | solution.py:38
  57.2 23.5 %collective-permute-start.12 = (bf16[256,512]{1,0:T(8,128)(2,1)S(1)}, bf16[256,512]{1,0:T(8,128)(2,1)S(1)}, u32[]{:S(2)}, u32[]{:S(2)}) collective-permute-start(bf16[256,512]{1,0:T(8,128)(2,1)S(1)} %get-tuple-element.45), channel_id=1, source_target_pairs={{0,2},{1,3},{2,0},{3,1},{4,6},{5,7},{6,4},{7,5},{8,10},{9,11},{10,... | collective-permute-start | bytes 786440 | tf_op jit(solution)/shard_map/ppermute | solution.py:38
  58.7 22.0 %collective-permute-start.13 = (bf16[256,512]{1,0:T(8,128)(2,1)S(1)}, bf16[256,512]{1,0:T(8,128)(2,1)S(1)}, u32[]{:S(2)}, u32[]{:S(2)}) collective-permute-start(bf16[256,512]{1,0:T(8,128)(2,1)S(1)} %get-tuple-element.46), channel_id=1, source_target_pairs={{0,3},{1,2},{2,1},{3,0},{4,7},{5,6},{6,5},{7,4},{8,11},{9,10},{10,... | collective-permute-start | bytes 786440 | tf_op jit(solution)/shard_map/ppermute | solution.py:38
  81.1 17.6 %collective-permute-start.17 = (bf16[2,384,512]{2,1,0:T(8,128)(2,1)S(1)}, bf16[2,384,512]{2,1,0:T(8,128)(2,1)S(1)}, u32[]{:S(2)}, u32[]{:S(2)}) collective-permute-start(bf16[2,384,512]{2,1,0:T(8,128)(2,1)S(1)} %factors.1.refs_2_.refs_3_), channel_id=1, source_target_pairs={{0,1},{1,0},{2,3},{3,2},{4,5},{5,4},{6,7},{7,6},{8,9},{9,8},{10,11... | collective-permute-start | bytes 2359304 | tf_op jit(solution)/shard_map/ppermute | solution.py:38
  82.7 16.0 %collective-permute-start.18 = (bf16[2,384,512]{2,1,0:T(8,128)(2,1)S(1)}, bf16[2,384,512]{2,1,0:T(8,128)(2,1)S(1)}, u32[]{:S(2)}, u32[]{:S(2)}) collective-permute-start(bf16[2,384,512]{2,1,0:T(8,128)(2,1)S(1)} %factors.1.refs_2_.refs_3_), channel_id=1, source_target_pairs={{0,2},{1,3},{2,0},{3,1},{4,6},{5,7},{6,4},{7,5},{8,10},{9,11},{10,... | collective-permute-start | bytes 2359304 | tf_op jit(solution)/shard_map/ppermute | solution.py:38
  85.6 18.8 %collective-permute-start.14 = (bf16[2,32,2048]{2,1,0:T(8,128)(2,1)S(1)}, bf16[2,32,2048]{2,1,0:T(8,128)(2,1)S(1)}, u32[]{:S(2)}, u32[]{:S(2)}) collective-permute-start(bf16[2,32,2048]{2,1,0:T(8,128)(2,1)S(1)} %get-tuple-element.48), channel_id=1, source_target_pairs={{0,8},{4,12},{8,0},{12,4},{16,24},{20,28},{24,16},{28,20},{1,9},{5... | collective-permute-start | bytes 786440 | tf_op jit(solution)/shard_map/ppermute | solution.py:44
  87.6 18.4 %collective-permute-start.15 = (bf16[2,32,2048]{2,1,0:T(8,128)(2,1)S(1)}, bf16[2,32,2048]{2,1,0:T(8,128)(2,1)S(1)}, u32[]{:S(2)}, u32[]{:S(2)}) collective-permute-start(bf16[2,32,2048]{2,1,0:T(8,128)(2,1)S(1)} %get-tuple-element.49), channel_id=1, source_target_pairs={{0,16},{4,20},{8,24},{12,28},{16,0},{20,4},{24,8},{28,12},{1,17},{... | collective-permute-start | bytes 786440 | tf_op jit(solution)/shard_map/ppermute | solution.py:44
  91.0 15.1 %collective-permute-start.16 = (bf16[2,32,2048]{2,1,0:T(8,128)(2,1)S(1)}, bf16[2,32,2048]{2,1,0:T(8,128)(2,1)S(1)}, u32[]{:S(2)}, u32[]{:S(2)}) collective-permute-start(bf16[2,32,2048]{2,1,0:T(8,128)(2,1)S(1)} %get-tuple-element.50), channel_id=1, source_target_pairs={{0,24},{4,28},{8,16},{12,20},{16,8},{20,12},{24,0},{28,4},{1,25},{... | collective-permute-start | bytes 786440 | tf_op jit(solution)/shard_map/ppermute | solution.py:44
  98.8 7.9 %collective-permute-start.21 = (bf16[384,512]{1,0:T(8,128)(2,1)S(1)}, bf16[384,512]{1,0:T(8,128)(2,1)S(1)}, u32[]{:S(2)}, u32[]{:S(2)}) collective-permute-start(bf16[384,512]{1,0:T(8,128)(2,1)S(1)} %get-tuple-element.56), channel_id=1, source_target_pairs={{0,1},{1,0},{2,3},{3,2},{4,5},{5,4},{6,7},{7,6},{8,9},{9,8},{10,11... | collective-permute-start | bytes 1179656 | tf_op jit(solution)/shard_map/ppermute | solution.py:38
  100.5 7.8 %collective-permute-start.22 = (bf16[384,512]{1,0:T(8,128)(2,1)S(1)}, bf16[384,512]{1,0:T(8,128)(2,1)S(1)}, u32[]{:S(2)}, u32[]{:S(2)}) collective-permute-start(bf16[384,512]{1,0:T(8,128)(2,1)S(1)} %get-tuple-element.57), channel_id=1, source_target_pairs={{0,2},{1,3},{2,0},{3,1},{4,6},{5,7},{6,4},{7,5},{8,10},{9,11},{10,... | collective-permute-start | bytes 1179656 | tf_op jit(solution)/shard_map/ppermute | solution.py:38
  106.1 7.0 %collective-permute-start.19 = (bf16[2,32,2048]{2,1,0:T(8,128)(2,1)S(1)}, bf16[2,32,2048]{2,1,0:T(8,128)(2,1)S(1)}, u32[]{:S(2)}, u32[]{:S(2)}) collective-permute-start(bf16[2,32,2048]{2,1,0:T(8,128)(2,1)S(1)} %get-tuple-element.53), channel_id=1, source_target_pairs={{0,4},{4,0},{8,12},{12,8},{16,20},{20,16},{24,28},{28,24},{1,5},{5... | collective-permute-start | bytes 786440 | tf_op jit(solution)/shard_map/ppermute | solution.py:68
  106.2 6.9 %collective-permute-start.20 = (bf16[2,32,2048]{2,1,0:T(8,128)(2,1)S(1)}, bf16[2,32,2048]{2,1,0:T(8,128)(2,1)S(1)}, u32[]{:S(2)}, u32[]{:S(2)}) collective-permute-start(bf16[2,32,2048]{2,1,0:T(8,128)(2,1)S(1)} %get-tuple-element.54), channel_id=1, source_target_pairs={{0,4},{4,0},{8,12},{12,8},{16,20},{20,16},{24,28},{28,24},{1,5},{5... | collective-permute-start | bytes 786440 | tf_op jit(solution)/shard_map/ppermute | solution.py:68
  108.3 7.9 %copy-start.4 = (f32[1,3,512,512]{3,2,1,0:T(8,128)S(1)}, f32[1,3,512,512]{3,2,1,0:T(8,128)}, u32[]{:S(2)}) copy-start(f32[1,3,512,512]{3,2,1,0:T(8,128)} %refs_7_.1) | copy-start | bytes 9437188
  108.3 7.9 %copy-start.5 = (f32[1,3,512,512]{3,2,1,0:T(8,128)S(1)}, f32[1,3,512,512]{3,2,1,0:T(8,128)}, u32[]{:S(2)}) copy-start(f32[1,3,512,512]{3,2,1,0:T(8,128)} %refs_8_.1) | copy-start | bytes 9437188
  109.5 4.7 %collective-permute-start.23 = (f32[16,128]{1,0:T(8,128)S(1)}, f32[16,128]{1,0:T(8,128)S(1)}, u32[]{:S(2)}, u32[]{:S(2)}) collective-permute-start(f32[16,128]{1,0:T(8,128)S(1)} %get-tuple-element.58.refs_8_.refs_1_), channel_id=1, source_target_pairs={{0,1},{1,0},{2,3},{3,2},{4,5},{5,4},{6,7},{7,6},{8,9},{9,8},{10,11... | collective-permute-start | bytes 24584 | tf_op jit(solution)/shard_map/ppermute | solution.py:38
  109.9 4.3 %collective-permute-start.24 = (f32[16,128]{1,0:T(8,128)S(1)}, f32[16,128]{1,0:T(8,128)S(1)}, u32[]{:S(2)}, u32[]{:S(2)}) collective-permute-start(f32[16,128]{1,0:T(8,128)S(1)} %get-tuple-element.58.refs_8_.refs_1_), channel_id=1, source_target_pairs={{0,2},{1,3},{2,0},{3,1},{4,6},{5,7},{6,4},{7,5},{8,10},{9,11},{10,... | collective-permute-start | bytes 24584 | tf_op jit(solution)/shard_map/ppermute | solution.py:38
  111.6 4.5 %collective-permute-start.25 = (f32[16,128]{1,0:T(8,128)S(1)}, f32[16,128]{1,0:T(8,128)S(1)}, u32[]{:S(2)}, u32[]{:S(2)}) collective-permute-start(f32[16,128]{1,0:T(8,128)S(1)} %get-tuple-element.58.refs_8_.refs_1_), channel_id=1, source_target_pairs={{0,3},{1,2},{2,1},{3,0},{4,7},{5,6},{6,5},{7,4},{8,11},{9,10},{10,... | collective-permute-start | bytes 24584 | tf_op jit(solution)/shard_map/ppermute | solution.py:38

commit v8 on v7

--- a/solution.py
+++ b/solution.py
@@ -85,51 +85,55 @@
         out_ref[...] = matrix_ref[:, segment(rep_ref, offset, out_ref.shape[1])]
 
 
-def payload_kernel(rep_ref, weights_ref, inputs_ref, *out_refs):
-    seg_rows = weights_ref.shape[2]
+def first_kernel(pair_ref, *out_refs):
+    for part, out_ref in enumerate(out_refs):
+        out_ref[...] = pair_ref[1 - part]
+
+
+def second_kernel(pos_ref, pair_ref, inputs_ref, *out_refs):
+    seg_rows = pair_ref.shape[1]
     slot_count = inputs_ref.shape[0]
     half = slot_count // 2
     for part, out_ref in enumerate(out_refs):
-        out_ref[pl.ds(0, seg_rows), :] = weights_ref[0, 0]
-        out_ref[pl.ds(seg_rows, seg_rows), :] = weights_ref[0, 1]
-        columns = segment(rep_ref, part + 1, seg_rows)
-        out_ref[pl.ds(2 * seg_rows, slot_count), :] = inputs_ref[:, columns]
-        columns = segment(rep_ref, 3, seg_rows)
-        out_ref[pl.ds(2 * seg_rows + slot_count, half), :] = inputs_ref[
+        out_ref[pl.ds(0, seg_rows), :] = pair_ref[part]
+        columns = segment(pos_ref, part + 1, seg_rows)
+        out_ref[pl.ds(seg_rows, slot_count), :] = inputs_ref[:, columns]
+        columns = segment(pos_ref, 3, seg_rows)
+        out_ref[pl.ds(seg_rows + slot_count, half), :] = inputs_ref[
             pl.ds(part * half, half), columns
         ]
 
 
-def pass_kernel(from_two_ref, from_one_ref, *out_refs):
-    for part, (near_ref, out_ref) in enumerate(zip((from_two_ref, from_one_ref), out_refs)):
-        seg_rows = near_ref.shape[1]
-        half = out_ref.shape[0] - seg_rows
-        out_ref[pl.ds(0, seg_rows), :] = near_ref[pl.ds(part * seg_rows, seg_rows), :]
-        out_ref[pl.ds(seg_rows, half), :] = near_ref[pl.ds(near_ref.shape[0] - half, half), :]
+def pass_kernel(from_two_ref, from_one_ref, first_ref, second_ref):
+    first_ref[...] = from_two_ref[...]
+    second_ref[...] = from_one_ref[...]
 
 
 def projection_rows(refs):
-    if len(refs) == 1 and len(refs[0].shape) > 2:
-        ref = refs[0] if len(refs[0].shape) == 3 else refs[0].at[0]
-        return ref.at[0], ref.at[1]
-    seg_rows = refs[0].shape[1]
-    start = 0 if len(refs) == 2 else seg_rows
-    return refs[0].at[pl.ds(0, seg_rows)], refs[-1].at[pl.ds(start, seg_rows)]
+    if len(refs) == 1:
+        return refs[0].at[0], refs[0].at[1]
+    return tuple(ref.at[pl.ds(0, ref.shape[1])] for ref in refs)
 
 
 def input_rows(rep_ref, refs, slot_count, seg_rows):
     if len(refs) == 2:
-        rows = pl.ds(seg_rows, slot_count // 2)
+        rows = pl.ds(slot_count + slot_count // 2, slot_count // 2)
         return jnp.concatenate([refs[1][rows], refs[0][rows]], axis=0)
     (ref,) = refs
     if ref.shape[0] > slot_count:
-        return ref[pl.ds(2 * seg_rows, slot_count), :]
+        return ref[pl.ds(seg_rows, slot_count), :]
     return ref[...] if ref.shape[1] == seg_rows else ref[:, segment(rep_ref, 0, seg_rows)]
 
 
-def cut_kernel(from_two_ref, from_one_ref, first_ref, second_ref):
-    first_ref[...] = from_two_ref[0]
-    second_ref[...] = from_one_ref[1]
+def cut_kernel(from_two_ref, from_one_ref, *refs):
+    tail_refs, out_refs = refs[:-2], refs[-2:]
+    for part, (near_ref, out_ref) in enumerate(zip((from_two_ref, from_one_ref), out_refs)):
+        rows = near_ref.shape[1]
+        out_ref[pl.ds(0, rows), :] = near_ref[part]
+        if tail_refs:
+            tail = out_ref.shape[0] - rows
+            tail_ref = tail_refs[part]
+            out_ref[pl.ds(rows, tail), :] = tail_ref[pl.ds(tail_ref.shape[0] - tail, tail), :]
 
 
 def gather_near(payload):
@@ -140,13 +144,14 @@
     return [payload, from_peer(payload, 1), from_two]
 
 
-def gather_rest(near, after):
+def gather_rest(near, after, tails=(), rows=0):
     whole = [(part,) for part in near]
     if lax.axis_size("replica") != 4:
         return whole
-    half = jax.ShapeDtypeStruct(near[0].shape[1:], near[0].dtype)
+    half = jax.ShapeDtypeStruct((near[0].shape[1] + rows, near[0].shape[2]), near[0].dtype)
+    operands = [near[2], near[1], *tails]
     first, second = call(
-        cut_kernel, "cut", [near[2], near[1]], [VMEM, VMEM], [half, half], after=after
+        cut_kernel, "cut", operands, [VMEM] * len(operands), [half, half], after=after
     )
     return whole + [(from_peer(first, 1), from_peer(second, 2))]
 
@@ -200,11 +205,11 @@
     )(*operands, *after)
 
 
-def segment(rep_ref, offset, width):
-    return pl.ds(pl.multiple_of((rep_ref[0] ^ offset) * width, width), width)
-
-
-def rows_kernel(expert_count, rep_ref, ids_ref, task_ref, row_ref, grads_ref, *out_refs):
+def segment(pos_ref, offset, width):
+    return pl.ds(pl.multiple_of((pos_ref[0] ^ offset) * width, width), width)
+
+
+def rows_kernel(expert_count, pos_ref, ids_ref, task_ref, row_ref, grads_ref, *out_refs):
     row_count = grads_ref.shape[0]
     seg_rows = out_refs[0].shape[1]
     block_count = ids_ref.shape[1]
@@ -223,7 +228,7 @@
     labels = jnp.where(line == 0, row_ref[...].astype(jnp.float32), 0.0)
     labels = jnp.where(line == 1, rank, labels).astype(jnp.bfloat16)
     for offset, out_ref in enumerate(out_refs):
-        columns = segment(rep_ref, offset, seg_rows)
+        columns = segment(pos_ref, offset, seg_rows)
         for block in range(block_count):
             rows = pl.ds(block * block_rows, block_rows)
             weight = task_ref[ids_ref[0, block]]
@@ -244,7 +249,7 @@
     return jnp.where(places == slot, 1.0, 0.0).astype(jnp.bfloat16)
 
 
-def place_kernel(count, row_count, spot_ref, *refs):
+def place_kernel(count, row_count, pos_ref, *refs):
     block_refs, out_refs, placed_ref = refs[:count], refs[count:-1], refs[-1]
     _, expert_count, capacity, seg_rows = placed_ref.shape
     slot_count = expert_count * capacity
@@ -254,10 +259,10 @@
         placed = placed.reshape(expert_count, capacity, seg_rows)
         placed_ref[offset] = placed.astype(jnp.bfloat16)
         for expert in range(expert_count):
-            out_refs[expert // 2][expert % 2, offset] = placed_ref[offset, spot_ref[0] ^ expert]
-
-
-def unplace_kernel(spot_ref, block_ref, *refs):
+            out_refs[expert // 2][expert % 2, offset] = placed_ref[offset, pos_ref[1] ^ expert]
+
+
+def unplace_kernel(pos_ref, block_ref, *refs):
     returned_refs, out_ref, slots_ref = refs[:-2], refs[-2], refs[-1]
     expert_count, capacity, _ = slots_ref.shape
     slot_count = expert_count * capacity
@@ -265,7 +270,7 @@
     placing = one_hot(block_ref, row_count, slot_count, capacity)
     for expert in range(expert_count):
         block_ref = spread_block(expert_count // 2, returned_refs, expert)
-        slots_ref[spot_ref[0] ^ expert] = block_ref[...]
+        slots_ref[pos_ref[1] ^ expert] = block_ref[...]
     out_ref[0] = contract_first(placing, flat_rows(slots_ref[...])).astype(jnp.bfloat16)
 
 
@@ -277,31 +282,31 @@
     return blocks.reshape(rows, blocks.shape[2])
 
 
-def back_kernel(chips, arrays, spot_ref, weight_ref, *refs):
+def back_kernel(chips, arrays, pos_ref, weight_ref, *refs):
     came_refs, incoming_ref, out_refs = refs[:arrays], refs[arrays], refs[arrays + 1 :]
     for offset, out_ref in enumerate(out_refs):
         for expert in range(2 * chips):
             block_ref = spread_block(chips, came_refs, expert)
-            incoming_ref[offset, spot_ref[0] ^ expert] = block_ref[offset]
+            incoming_ref[offset, pos_ref[1] ^ expert] = block_ref[offset]
         rows = flat_rows(incoming_ref[offset])
-        out_ref[...] = multiply(rows, weight_ref[0, 2]).astype(out_ref.dtype)
-
-
-def forward_kernel(offsets, lengths, has_start, rep_ref, inputs_ref, *refs):
-    out_ref = refs[-1]
-    weight_refs = refs[:-1]
-    gate = up = None
+        out_ref[...] = multiply(rows, weight_ref[...]).astype(out_ref.dtype)
+
+
+def forward_kernel(terms, count, has_start, pos_ref, inputs_ref, *refs):
+    weight_refs, out_ref = refs[:-1], refs[-1]
+    totals = [None, None]
     if has_start:
-        gate, up = weight_refs[0][0], weight_refs[0][1]
+        totals = [weight_refs[0][0], weight_refs[0][1]]
         weight_refs = weight_refs[1:]
-    for offset, group in zip(offsets, regroup(weight_refs, lengths)):
-        gate_ref, up_ref = projection_rows(group)
-        rows = inputs_ref[:, segment(rep_ref, offset, gate_ref.shape[0])]
-        gate_part, up_part = multiply(rows, gate_ref[...]), multiply(rows, up_ref[...])
-        gate = gate_part if gate is None else gate + gate_part
-        up = up_part if up is None else up + up_part
-    out_ref[0] = gate
-    out_ref[1] = up
+    for (offset, which), weight_ref in zip(terms, weight_refs):
+        if len(weight_ref.shape) == 3:
+            weight_ref = weight_ref.at[which]
+        seg_rows = inputs_ref.shape[1] // count
+        rows = inputs_ref[:, segment(pos_ref, offset, seg_rows)]
+        part = multiply(rows, weight_ref[pl.ds(0, seg_rows), :])
+        totals[which] = part if totals[which] is None else totals[which] + part
+    for which, total in enumerate(totals):
+        out_ref[which] = total
 
 
 def factor_kernel(forward_ref, *refs):
@@ -322,7 +327,7 @@
         out_ref[part, pl.ds(slot_count, half)] = hidden[part * half : (part + 1) * half]
 
 
-def slot_kernel(lengths, rep_ref, spot_ref, factor_ref, *refs):
+def slot_kernel(lengths, pos_ref, factor_ref, *refs):
     chips = refs[-1].shape[1] // 2
     weight_refs, out_refs, slots_ref = refs[: -chips - 1], refs[-chips - 1 : -1], refs[-1]
     _, expert_count, capacity, seg_rows = slots_ref.shape
@@ -333,10 +338,10 @@
         total = contract_last(gate_grad, gate_ref[...]) + contract_last(up_grad, up_ref[...])
         total = total.reshape(expert_count, capacity, seg_rows)
         slots_ref[offset] = total.astype(jnp.bfloat16)
-        columns = segment(rep_ref, offset, seg_rows)
+        columns = segment(pos_ref, offset, seg_rows)
         for expert in range(expert_count):
             out_ref = out_refs[expert // 2]
-            out_ref[expert % 2, :, columns] = slots_ref[offset, spot_ref[0] ^ expert]
+            out_ref[expert % 2, :, columns] = slots_ref[offset, pos_ref[1] ^ expert]
 
 
 def gram_kernel(count, offsets, lengths, place, rep_ref, *refs):
@@ -569,8 +574,7 @@
     half = slot_count // 2
     offsets = range(rep_count)
     chips = expert_count // 2
-    rep = lax.axis_index("replica").astype(jnp.int32).reshape(1)
-    spot = lax.axis_index("expert").astype(jnp.int32).reshape(1)
+    rep = jnp.stack([lax.axis_index("replica"), lax.axis_index("expert")]).astype(jnp.int32)
     shape = jax.ShapeDtypeStruct
 
     block = shape((row_count + LABEL_ROWS, seg_rows), jnp.bfloat16)
@@ -578,7 +582,7 @@
     row_blocks = call(
         functools.partial(rows_kernel, expert_count),
         "rows",
-        [rep, task_ids, task_weights, *small],
+        [lax.axis_index("replica").astype(jnp.int32).reshape(1), task_ids, task_weights, *small],
         [SMEM] * 3 + [pl.BlockSpec(x.shape, lambda i: (0, 0)) for x in small],
         [block for _ in offsets],
         grid=(1,),
@@ -587,32 +591,48 @@
     routed = exchange(row_blocks)
 
     inputs_home = saved_inputs[0, 0]
+    pair = weights[0, :2]
     packed = rep_count == 4 and seg_rows == hidden_width
     if packed:
-        payload = shape((2 * seg_rows + slot_count + half, seg_rows), jnp.bfloat16)
+        part = shape((seg_rows, hidden_width), jnp.bfloat16)
+        to_one, to_two = call(first_kernel, "first", [pair], [VMEM], [part, part])
+        up_one, gate_two = from_peer(to_one, 1), from_peer(to_two, 2)
         to_one, to_two = call(
-            payload_kernel,
-            "payload",
-            [rep, weights, inputs_home],
+            pass_kernel,
+            "pass",
+            [gate_two, up_one],
+            [VMEM, VMEM],
+            [part, part],
+            after=routed[1:],
+        )
+        last = (from_peer(to_one, 1), from_peer(to_two, 2))
+        part = shape((seg_rows + slot_count + half, seg_rows), jnp.bfloat16)
+        to_one, to_two = call(
+            second_kernel,
+            "second",
+            [rep, pair, inputs_home],
             [SMEM, VMEM, VMEM],
-            [payload, payload],
-            after=routed[1:],
-        )
-        from_two, from_one = from_peer(to_two, 2), from_peer(to_one, 1)
-        projections = [(weights,), (from_one,), (from_two,)]
-        inputs = [(inputs_home,), (from_one,), (from_two,)]
+            [part, part],
+            after=last,
+        )
+        gate_one, up_two = from_peer(to_one, 1), from_peer(to_two, 2)
+        projections = [(pair,), (gate_one, up_one), (gate_two, up_two), last]
+        inputs = [(inputs_home,), (gate_one,), (up_two,)]
+        late = [(1, 0), (2, 1)]
+        tails = [up_two, gate_one]
     else:
-        projections = [(x,) for x in exchange([weights[0, :2]] * rep_count)]
+        projections = [(x,) for x in exchange([pair] * rep_count)]
         pieces = [shape((slot_count, seg_rows), jnp.bfloat16) for _ in offsets]
         pieces = call(split_kernel, "split", [rep, inputs_home], [SMEM, VMEM], pieces)
         inputs = [(x,) for x in exchange(pieces)]
+        late, tails = [], []
 
     part = shape((2, rep_count, capacity, seg_rows), jnp.bfloat16)
     placed = (
         call(
             functools.partial(place_kernel, rep_count, row_count),
             "place",
-            [spot, *routed],
+            [rep, *routed],
             [SMEM] + [VMEM] * len(routed),
             [part] * chips,
             scratch=[
@@ -629,44 +649,27 @@
     incoming, *back = call(
         functools.partial(back_kernel, chips, len(came)),
         "back",
-        [spot, weights, *came],
+        [rep, weights[0, 2], *came],
         [SMEM] + [VMEM] * (1 + len(came)),
         [shape((rep_count, expert_count, capacity, seg_rows), jnp.bfloat16)]
         + [shape(back_shape, jnp.bfloat16 if k else jnp.float32) for k in offsets],
     )
     own_back = back[:1]
     back = exchange(back)
-    if packed:
-        passed = shape((seg_rows + half, seg_rows), jnp.bfloat16)
-        first, second = call(
-            pass_kernel,
-            "pass",
-            [from_two, from_one],
-            [VMEM, VMEM],
-            [passed, passed],
-            after=own_back,
-        )
-        last = (from_peer(first, 1), from_peer(second, 2))
-        projections.append(last)
-        inputs.append(last)
-
     forward = None
-    late = [3] if packed else []
-    for name, group in (("forward", [k for k in offsets if k not in late]), ("rest", late)):
+    terms = [(k, which) for k in offsets for which in range(2)]
+    for name, group in (("forward", [x for x in terms if x not in late]), ("rest", late)):
         if not group:
             continue
         operands = [rep, inputs_home] + ([] if forward is None else [forward])
-        operands += flatten(projections[k] for k in group)
-        lengths = [len(projections[k]) for k in group]
+        operands += [(projections[k] * 2)[which] if k else pair for k, which in group]
         (forward,) = call(
-            functools.partial(forward_kernel, group, lengths, forward is not None),
+            functools.partial(forward_kernel, group, rep_count, forward is not None),
             name,
             operands,
             [SMEM] + [VMEM] * (len(operands) - 1),
             [shape((2, slot_count, hidden_width), jnp.float32)],
-            cost=0 if name == "rest" else 0,
-        )
-
+        )
     (own_factors,) = call(
         factor_kernel,
         "factors",
@@ -676,30 +679,31 @@
     )
     near_factors = gather_near(own_factors)
 
-    operands = [rep, spot, own_factors] + flatten(projections)
+    operands = [rep, own_factors] + flatten(projections)
     returning = across_chips(
         call(
             functools.partial(slot_kernel, [len(group) for group in projections]),
             "slots",
             operands,
-            [SMEM] * 2 + [VMEM] * (len(operands) - 2),
+            [SMEM] + [VMEM] * (len(operands) - 1),
             [shape((2, capacity, model_width), jnp.bfloat16)] * chips,
             scratch=[
                 pltpu.VMEM((rep_count, expert_count, capacity, seg_rows), jnp.bfloat16)
             ],
         )
     )
-    factors = gather_rest(near_factors, after=returning[:1])
+    factors = gather_rest(near_factors, returning[:1], tails, half if tails else 0)
+    inputs += factors[3:] if tails else []
     if rep_count <= 4:
         *merging, first_gram = adasum(rep, inputs, incoming, factors)
-        returned = finish_spread(returning, [first_gram], pieces=2)
+        returned = finish_spread(returning, [first_gram])
         unplace_after = merging[2:]
     else:
         returned, unplace_after = finish_spread(returning), ()
     (input_grads,) = call(
         unplace_kernel,
         "unplace",
-        [spot, routed[0], *returned],
+        [rep, routed[0], *returned],
         [SMEM] + [VMEM] * (1 + len(returned)),
         [shape((1, row_count, model_width), jnp.bfloat16)],
         scratch=[pltpu.VMEM((expert_count, capacity, model_width), jnp.bfloat16)],

time: 121 us -> 120 us (level)
  waiting for transfers between devices: 62.7 us -> 55.7 us
  Pallas kernels: 22.6 us -> 25 us
  starting transfers between devices: 30.3 us -> 32.1 us
  local copies, waits for them, and re-layouts: 3.62 us -> 4.96 us
    ppermute x6, waiting for transfers between devices: 19.8 us -> 15.2 us  [across_chips(): lax.ppermute(part, 'expert', [(i, i ^ 2 * k) for i in range(count)])]
    squeeze x0 -> x2, local copies, waits for them, and re-layouts: none -> 2.46 us  [the longest x1 1.38 us: shards(): pair = weights[0, :2]]
    pallas_call x16 -> x17, Pallas kernels: 22.6 us -> 25 us  [call(): pl.pallas_call(body, grid=grid, in_specs=list(specs) + [VMEM] * len(after...]
    ppermute x17 -> x19, starting transfers between devices: 19.8 us -> 22.1 us  [from_peer(): lax.ppermute(array, 'replica', [(i, i ^ offset) for i in range(count)])]
    ppermute x17 -> x19, waiting for transfers between devices: 40.9 us -> 39.7 us  [from_peer(): lax.ppermute(array, 'replica', [(i, i ^ offset) for i in range(count)])]
    unnamed x18 -> x14, local copies, waits for them, and re-layouts: 3.62 us -> 2.5 us
  transfers between devices with their start and end apart: 26 -> 27, of which waited for: 15 -> 16; matrix products, arithmetic and copies ran while one was open for 0% -> 1% of each run, Pallas kernels for 10% -> 15%
where the time goes in v8:
time: 120 us; the launch traced here: 119 us
  waiting for transfers between devices  55.7 us (46%)
  starting transfers between devices  32.1 us (27%)
  Pallas kernels  25 us (21%)
  local copies, waits for them, and re-layouts  4.96 us (4%)
  between operations  1.43 us (1%)
    ppermute x19, waiting for transfers between devices, from_peer(): lax.ppermute(array, 'replica', [(i, i ^ offset) for i in range(count)])  39.7 us
    pallas_call x17, Pallas kernels, call(): pl.pallas_call(body, grid=grid, in_specs=list(specs) + [VMEM] * len(after...  25 us
    ppermute x19, starting transfers between devices, from_peer(): lax.ppermute(array, 'replica', [(i, i ^ offset) for i in range(count)])  22.1 us
    ppermute x6, waiting for transfers between devices, across_chips(): lax.ppermute(part, 'expert', [(i, i ^ 2 * k) for i in range(count)])  15.2 us
    ppermute x6, starting transfers between devices, across_chips(): lax.ppermute(part, 'expert', [(i, i ^ 2 * k) for i in range(count)])  9.78 us
    unnamed x14, local copies, waits for them, and re-layouts  2.5 us
  transfers between devices with their start and end apart: 27, of which 16 were waited for; matrix products, arithmetic and copies ran while one was open for 1% of the time, Pallas kernels for 15%

profile of v8, /device:TPU:0, one launch (start us, length us, event | category | flops | bytes accessed | tf_op | source)
XLA Modules:
  0.0 119.2 jit_solution(11821630598322823881)
XLA Ops:
  0.6 1.4 %slice_bitcast_fusion.refs_0_.refs_2_.refs_3_.refs_1_ = bf16[2,512,512]{2,1,0:T(8,128)(2,1)S(1)} fusion(bf16[1,3,512,512]{3,2,1,0:T(8,128)(2,1)} %param.8), kind=kLoop, calls=%fused_computation | loop fusion | bytes 2097152 | tf_op jit(solution)/shard_map/squeeze | solution.py:594
  2.0 1.0 first.1
  3.1 2.9 %collective-permute-start = (bf16[512,512]{1,0:T(8,128)(2,1)}, bf16[512,512]{1,0:T(8,128)(2,1)S(1)}, u32[]{:S(2)}, u32[]{:S(2)}) collective-permute-start(bf16[512,512]{1,0:T(8,128)(2,1)} %get-tuple-element.32), channel_id=1, source_target_pairs={{0,1},{1,0},{2,3},{3,2},{4,5},{5,4},{6,7},{7,6},{8,9},{9,8},{10,11... | collective-permute-start | bytes 1572872 | tf_op jit(solution)/shard_map/ppermute | solution.py:38
  6.0 1.5 %collective-permute-start.1 = (bf16[512,512]{1,0:T(8,128)(2,1)}, bf16[512,512]{1,0:T(8,128)(2,1)S(1)}, u32[]{:S(2)}, u32[]{:S(2)}) collective-permute-start(bf16[512,512]{1,0:T(8,128)(2,1)} %get-tuple-element.33), channel_id=1, source_target_pairs={{0,2},{1,3},{2,0},{3,1},{4,6},{5,7},{6,4},{7,5},{8,10},{9,11},{10,... | collective-permute-start | bytes 1572872 | tf_op jit(solution)/shard_map/ppermute | solution.py:38
  8.2 2.0 %rows.1 = (bf16[144,512]{1,0:T(8,128)(2,1)}, bf16[144,512]{1,0:T(8,128)(2,1)}, bf16[144,512]{1,0:T(8,128)(2,1)}, bf16[144,512]{1,0:T(8,128)(2,1)}) custom-call(s32[1]{0:T(128)} %bitcast.refs_0_, s32[1,1]{1,0:T(1,128)S(6)} %copy.10.refs_1_, f32[8]{0:T(128)} %refs_2_.1, s32[1,128]{1,0:T(1,128)} %bitcast.14, bf16[128,2048]{1,0:T(8,128)(2,1)} %bitcast.13), custom_call_target="tpu_custom_call" | custom-call | tf_op jit(solution)/shard_map/rows/pallas_call | solution.py:192
  10.2 0.5 collective-permute-start.2
  10.8 0.0 collective-permute-start.3
  10.8 3.0 %collective-permute-start.4 = (bf16[144,512]{1,0:T(8,128)(2,1)}, bf16[144,512]{1,0:T(8,128)(2,1)S(1)}, u32[]{:S(2)}, u32[]{:S(2)}) collective-permute-start(bf16[144,512]{1,0:T(8,128)(2,1)} %get-tuple-element.36), channel_id=1, source_target_pairs={{0,3},{1,2},{2,1},{3,0},{4,7},{5,6},{6,5},{7,4},{8,11},{9,10},{10,... | collective-permute-start | bytes 442376 | tf_op jit(solution)/shard_map/ppermute | solution.py:38
  13.7 8.4 %collective-permute-done.2.refs_2_ = bf16[144,512]{1,0:T(8,128)(2,1)S(1)} collective-permute-done((bf16[144,512]{1,0:T(8,128)(2,1)}, bf16[144,512]{1,0:T(8,128)(2,1)S(1)}, u32[]{:S(2)}, u32[]{:S(2)}) %collective-permute-start.2) | collective-permute-done | bytes 147488 | tf_op jit(solution)/shard_map/ppermute | solution.py:38
  22.1 3.8 %collective-permute-done.3.refs_3_ = bf16[144,512]{1,0:T(8,128)(2,1)S(1)} collective-permute-done((bf16[144,512]{1,0:T(8,128)(2,1)}, bf16[144,512]{1,0:T(8,128)(2,1)S(1)}, u32[]{:S(2)}, u32[]{:S(2)}) %collective-permute-start.3) | collective-permute-done | bytes 147488 | tf_op jit(solution)/shard_map/ppermute | solution.py:38
  25.9 1.0 pass.1
  27.0 0.7 copy-done.5
  27.6 1.2 %collective-permute-start.5 = (bf16[512,512]{1,0:T(8,128)(2,1)}, bf16[512,512]{1,0:T(8,128)(2,1)}, u32[]{:S(2)}, u32[]{:S(2)}) collective-permute-start(bf16[512,512]{1,0:T(8,128)(2,1)} %get-tuple-element.37), channel_id=1, source_target_pairs={{0,1},{1,0},{2,3},{3,2},{4,5},{5,4},{6,7},{7,6},{8,9},{9,8},{10,11... | collective-permute-start | bytes 1572872 | tf_op jit(solution)/shard_map/ppermute | solution.py:38
  28.9 0.8 collective-permute-start.6
  29.7 0.1 pad_add_fusion.refs_0_
  29.8 0.9 copy-done.3
  30.7 0.9 copy-done.6
  31.6 1.0 place.1
  32.6 1.6 %collective-permute-start.9 = (bf16[2,4,32,512]{3,2,1,0:T(8,128)(2,1)S(1)}, bf16[2,4,32,512]{3,2,1,0:T(8,128)(2,1)S(1)}, u32[]{:S(2)}, u32[]{:S(2)}) collective-permute-start(bf16[2,4,32,512]{3,2,1,0:T(8,128)(2,1)S(1)} %get-tuple-element.42), channel_id=1, source_target_pairs={{0,8},{4,12},{8,0},{12,4},{16,24},{20,28},{24,16},{28,20},{1,9},{5... | collective-permute-start | bytes 786440 | tf_op jit(solution)/shard_map/ppermute | solution.py:44
  34.2 2.6 %collective-permute-start.10 = (bf16[2,4,32,512]{3,2,1,0:T(8,128)(2,1)S(1)}, bf16[2,4,32,512]{3,2,1,0:T(8,128)(2,1)S(1)}, u32[]{:S(2)}, u32[]{:S(2)}) collective-permute-start(bf16[2,4,32,512]{3,2,1,0:T(8,128)(2,1)S(1)} %get-tuple-element.43), channel_id=1, source_target_pairs={{0,16},{4,20},{8,24},{12,28},{16,0},{20,4},{24,8},{28,12},{1,17},{... | collective-permute-start | bytes 786440 | tf_op jit(solution)/shard_map/ppermute | solution.py:44
  36.8 0.2 collective-permute-start.11
  37.0 3.5 %collective-permute-done.5.refs_6_.refs_3_.refs_7_ = bf16[512,512]{1,0:T(8,128)(2,1)} collective-permute-done((bf16[512,512]{1,0:T(8,128)(2,1)}, bf16[512,512]{1,0:T(8,128)(2,1)}, u32[]{:S(2)}, u32[]{:S(2)}) %collective-permute-start.5) | collective-permute-done | bytes 524320 | tf_op jit(solution)/shard_map/ppermute | solution.py:38
  40.5 1.2 %collective-permute-done.6.refs_7_.refs_4_.refs_8_ = bf16[512,512]{1,0:T(8,128)(2,1)} collective-permute-done((bf16[512,512]{1,0:T(8,128)(2,1)}, bf16[512,512]{1,0:T(8,128)(2,1)}, u32[]{:S(2)}, u32[]{:S(2)}) %collective-permute-start.6) | collective-permute-done | bytes 524320 | tf_op jit(solution)/shard_map/ppermute | solution.py:38
  41.7 1.3 %second.1 = (bf16[896,512]{1,0:T(8,128)(2,1)S(1)}, bf16[896,512]{1,0:T(8,128)(2,1)S(1)}) custom-call(s32[2]{0:T(128)S(1)} %pad_add_fusion.refs_0_, bf16[2,512,512]{2,1,0:T(8,128)(2,1)S(1)} %slice_bitcast_fusion.refs_0_.refs_2_.refs_3_.refs_1_, bf16[256,2048]{1,0:T(8,128)(2,1)S(1)} %bitcast.9, ...), custom_call_target="tpu_custom_call" | custom-call | tf_op jit(solution)/shard_map/second/pallas_call | solution.py:192
  43.0 0.6 collective-permute-start.7
  43.6 0.6 collective-permute-start.8
  44.2 11.0 %collective-permute-done.10.refs_2_.refs_4_ = bf16[2,4,32,512]{3,2,1,0:T(8,128)(2,1)S(1)} collective-permute-done((bf16[2,4,32,512]{3,2,1,0:T(8,128)(2,1)S(1)}, bf16[2,4,32,512]{3,2,1,0:T(8,128)(2,1)S(1)}, u32[]{:S(2)}, u32[]{:S(2)}) %collective-permute-start.10) | collective-permute-done | bytes 262176 | tf_op jit(solution)/shard_map/ppermute | solution.py:44
  55.3 0.1 collective-permute-start.12
  55.3 1.1 slice_bitcast_fusion.1.refs_1_
  56.4 0.8 collective-permute-done.12.refs_6_
  57.2 1.3 %back.1 = (bf16[4,8,32,512]{3,2,1,0:T(8,128)(2,1)S(1)}, f32[256,512]{1,0:T(8,128)S(1)}, bf16[256,512]{1,0:T(8,128)(2,1)S(1)}, bf16[256,512]{1,0:T(8,128)(2,1)S(1)}, bf16[256,512]{1,0:T(8,128)(2,1)S(1)}) custom-call(s32[2]{0:T(128)S(1)} %pad_add_fusion.refs_0_, bf16[512,512]{1,0:T(8,128)(2,1)S(1)} %slice_bitcast_fusion.1.refs_1_, ...), custom_call_target="tpu_custom_call" | custom-call | tf_op jit(solution)/shard_map/back/pallas_call | solution.py:192
  58.5 0.6 collective-permute-start.13
  59.1 1.5 %collective-permute-start.14 = (bf16[256,512]{1,0:T(8,128)(2,1)S(1)}, bf16[256,512]{1,0:T(8,128)(2,1)S(1)}, u32[]{:S(2)}, u32[]{:S(2)}) collective-permute-start(bf16[256,512]{1,0:T(8,128)(2,1)S(1)} %get-tuple-element.47), channel_id=1, source_target_pairs={{0,2},{1,3},{2,0},{3,1},{4,6},{5,7},{6,4},{7,5},{8,10},{9,11},{10,... | collective-permute-start | bytes 786440 | tf_op jit(solution)/shard_map/ppermute | solution.py:38
  60.6 1.4 %collective-permute-start.15 = (bf16[256,512]{1,0:T(8,128)(2,1)S(1)}, bf16[256,512]{1,0:T(8,128)(2,1)S(1)}, u32[]{:S(2)}, u32[]{:S(2)}) collective-permute-start(bf16[256,512]{1,0:T(8,128)(2,1)S(1)} %get-tuple-element.48), channel_id=1, source_target_pairs={{0,3},{1,2},{2,1},{3,0},{4,7},{5,6},{6,5},{7,4},{8,11},{9,10},{10,... | collective-permute-start | bytes 786440 | tf_op jit(solution)/shard_map/ppermute | solution.py:38
  62.1 2.2 %forward.1.refs_2_ = f32[2,256,512]{2,1,0:T(8,128)S(1)} custom-call(s32[2]{0:T(128)S(1)} %pad_add_fusion.refs_0_, bf16[256,2048]{1,0:T(8,128)(2,1)S(1)} %bitcast.10, bf16[2,512,512]{2,1,0:T(8,128)(2,1)S(1)} %slice_bitcast_fusion.refs_0_.refs_2_.refs_3_.refs_1_, bf16[2,512,512]{2,1,0:T(8,128)(2,1)S(1)} %slice_bitcast_fusion.refs_0_.refs_2_.refs_3_.refs_1_, ...), custom_call_target="tpu_custom_call" | custom-call | tf_op jit(solution)/shard_map/forward/pallas_call | solution.py:192
  64.2 0.6 collective-permute-done.7.refs_3_.refs_4_
  64.9 0.3 collective-permute-done.8.refs_4_.refs_6_.refs_2_
  65.2 1.0 rest.1.refs_0_
  66.2 4.3 %collective-permute-done.13.refs_2_ = bf16[256,512]{1,0:T(8,128)(2,1)S(1)} collective-permute-done((bf16[256,512]{1,0:T(8,128)(2,1)S(1)}, bf16[256,512]{1,0:T(8,128)(2,1)S(1)}, u32[]{:S(2)}, u32[]{:S(2)}) %collective-permute-start.13) | collective-permute-done | bytes 262176 | tf_op jit(solution)/shard_map/ppermute | solution.py:38
  70.5 4.2 %collective-permute-done.14.refs_3_ = bf16[256,512]{1,0:T(8,128)(2,1)S(1)} collective-permute-done((bf16[256,512]{1,0:T(8,128)(2,1)S(1)}, bf16[256,512]{1,0:T(8,128)(2,1)S(1)}, u32[]{:S(2)}, u32[]{:S(2)}) %collective-permute-start.14) | collective-permute-done | bytes 262176 | tf_op jit(solution)/shard_map/ppermute | solution.py:38
  74.6 0.4 factors.1.refs_1_.refs_3_
  75.1 1.5 %collective-permute-start.19 = (bf16[2,384,512]{2,1,0:T(8,128)(2,1)S(1)}, bf16[2,384,512]{2,1,0:T(8,128)(2,1)S(1)}, u32[]{:S(2)}, u32[]{:S(2)}) collective-permute-start(bf16[2,384,512]{2,1,0:T(8,128)(2,1)S(1)} %factors.1.refs_1_.refs_3_), channel_id=1, source_target_pairs={{0,1},{1,0},{2,3},{3,2},{4,5},{5,4},{6,7},{7,6},{8,9},{9,8},{10,11... | collective-permute-start | bytes 2359304 | tf_op jit(solution)/shard_map/ppermute | solution.py:38
  76.6 0.3 collective-permute-start.20
  76.9 2.5 %slots.1 = (bf16[2,32,2048]{2,1,0:T(8,128)(2,1)S(1)}, bf16[2,32,2048]{2,1,0:T(8,128)(2,1)S(1)}, bf16[2,32,2048]{2,1,0:T(8,128)(2,1)S(1)}, bf16[2,32,2048]{2,1,0:T(8,128)(2,1)S(1)}) custom-call(s32[2]{0:T(128)S(1)} %pad_add_fusion.refs_0_, bf16[2,384,512]{2,1,0:T(8,128)(2,1)S(1)} %factors.1.refs_1_.refs_3_, ...), custom_call_target="tpu_custom_call" | custom-call | tf_op jit(solution)/shard_map/slots/pallas_call | solution.py:192
  79.4 2.8 %collective-permute-start.16 = (bf16[2,32,2048]{2,1,0:T(8,128)(2,1)S(1)}, bf16[2,32,2048]{2,1,0:T(8,128)(2,1)S(1)}, u32[]{:S(2)}, u32[]{:S(2)}) collective-permute-start(bf16[2,32,2048]{2,1,0:T(8,128)(2,1)S(1)} %get-tuple-element.50), channel_id=1, source_target_pairs={{0,8},{4,12},{8,0},{12,4},{16,24},{20,28},{24,16},{28,20},{1,9},{5... | collective-permute-start | bytes 786440 | tf_op jit(solution)/shard_map/ppermute | solution.py:44
  82.2 1.4 %collective-permute-start.17 = (bf16[2,32,2048]{2,1,0:T(8,128)(2,1)S(1)}, bf16[2,32,2048]{2,1,0:T(8,128)(2,1)S(1)}, u32[]{:S(2)}, u32[]{:S(2)}) collective-permute-start(bf16[2,32,2048]{2,1,0:T(8,128)(2,1)S(1)} %get-tuple-element.51), channel_id=1, source_target_pairs={{0,16},{4,20},{8,24},{12,28},{16,0},{20,4},{24,8},{28,12},{1,17},{... | collective-permute-start | bytes 786440 | tf_op jit(solution)/shard_map/ppermute | solution.py:44
  83.6 1.1 collective-permute-start.18
  84.7 8.9 %collective-permute-done.19.refs_5_.refs_1_ = bf16[2,384,512]{2,1,0:T(8,128)(2,1)S(1)} collective-permute-done((bf16[2,384,512]{2,1,0:T(8,128)(2,1)S(1)}, bf16[2,384,512]{2,1,0:T(8,128)(2,1)S(1)}, u32[]{:S(2)}, u32[]{:S(2)}) %collective-permute-start.19) | collective-permute-done | bytes 786464 | tf_op jit(solution)/shard_map/ppermute | solution.py:38
  93.6 0.3 collective-permute-done.20.refs_7_.refs_0_
  93.9 0.1 cut.1
  94.0 1.6 %collective-permute-start.22 = (bf16[512,512]{1,0:T(8,128)(2,1)S(1)}, bf16[512,512]{1,0:T(8,128)(2,1)S(1)}, u32[]{:S(2)}, u32[]{:S(2)}) collective-permute-start(bf16[512,512]{1,0:T(8,128)(2,1)S(1)} %get-tuple-element.56), channel_id=1, source_target_pairs={{0,1},{1,0},{2,3},{3,2},{4,5},{5,4},{6,7},{7,6},{8,9},{9,8},{10,11... | collective-permute-start | bytes 1572872 | tf_op jit(solution)/shard_map/ppermute | solution.py:38
  95.5 0.5 collective-permute-start.23
  96.0 2.6 %gram.1 = (f32[3,3,512,512]{3,2,1,0:T(8,128)S(1)}, f32[16,128]{1,0:T(8,128)S(1)}) custom-call(s32[2]{0:T(128)S(1)} %pad_add_fusion.refs_0_, bf16[4,8,32,512]{3,2,1,0:T(8,128)(2,1)S(1)} %get-tuple-element.53.refs_1_.refs_3_, bf16[256,2048]{1,0:T(8,128)(2,1)S(1)} %bitcast.12, bf16[2,384,512]{2,1,0:T(8,128)(2,1)S(1)} %factors.1.refs_1_.refs_3_, ...), custom_call_target="tpu_custom_call" | custom-call | tf_op jit(solution)/shard_map/gram/pallas_call | solution.py:192
  98.6 4.2 %collective-permute-done.17.refs_2_.refs_4_ = bf16[2,32,2048]{2,1,0:T(8,128)(2,1)S(1)} collective-permute-done((bf16[2,32,2048]{2,1,0:T(8,128)(2,1)S(1)}, bf16[2,32,2048]{2,1,0:T(8,128)(2,1)S(1)}, u32[]{:S(2)}, u32[]{:S(2)}) %collective-permute-start.17) | collective-permute-done | bytes 262176 | tf_op jit(solution)/shard_map/ppermute | solution.py:44
  102.9 0.1 collective-permute-start.21
  102.9 2.8 %collective-permute-done.22.refs_4_.refs_6_ = bf16[512,512]{1,0:T(8,128)(2,1)S(1)} collective-permute-done((bf16[512,512]{1,0:T(8,128)(2,1)S(1)}, bf16[512,512]{1,0:T(8,128)(2,1)S(1)}, u32[]{:S(2)}, u32[]{:S(2)}) %collective-permute-start.22) | collective-permute-done | bytes 524320 | tf_op jit(solution)/shard_map/ppermute | solution.py:38
  105.8 1.2 collective-permute-done.23.refs_5_.refs_7_
  107.0 1.7 %gram_late.1 = (f32[1,3,512,512]{3,2,1,0:T(8,128)S(1)}, f32[16,128]{1,0:T(8,128)S(1)}) custom-call(s32[2]{0:T(128)S(1)} %pad_add_fusion.refs_0_, f32[16,128]{1,0:T(8,128)S(1)} %get-tuple-element.54.refs_4_.refs_1_, f32[3,3,512,512]{3,2,1,0:T(8,128)S(1)} %get-tuple-element.55.refs_2_.refs_5_, bf16[4,8,32,512]{3,2,1,0:T(8,128)(2,1)S(1)} %get-tuple-element.53.refs_1_.refs_3_, ...), custom_call_target="tpu_custom_call" | custom-call | tf_op jit(solution)/shard_map/gram_late/pallas_call | solution.py:192
  108.7 0.6 collective-permute-start.24
  109.3 0.3 collective-permute-start.25
  109.6 2.6 %collective-permute-start.26 = (f32[16,128]{1,0:T(8,128)S(1)}, f32[16,128]{1,0:T(8,128)S(1)}, u32[]{:S(2)}, u32[]{:S(2)}) collective-permute-start(f32[16,128]{1,0:T(8,128)S(1)} %get-tuple-element.58.refs_7_.refs_1_), channel_id=1, source_target_pairs={{0,3},{1,2},{2,1},{3,0},{4,7},{5,6},{6,5},{7,4},{8,11},{9,10},{10,... | collective-permute-start | bytes 24584 | tf_op jit(solution)/shard_map/ppermute | solution.py:38
  112.3 1.7 %unplace.1 = bf16[1,128,2048]{2,1,0:T(8,128)(2,1)} custom-call(s32[2]{0:T(128)S(1)} %pad_add_fusion.refs_0_, bf16[144,512]{1,0:T(8,128)(2,1)S(1)} %copy-done.4, bf16[2,32,2048]{2,1,0:T(8,128)(2,1)S(1)} %get-tuple-element.49.refs_0_.refs_4_.refs_2_, bf16[2,32,2048]{2,1,0:T(8,128)(2,1)S(1)} %collective-permute-done.16.refs_1_.refs_3_, ...), custom_call_target="tpu_custom_call" | custom-call | tf_op jit(solution)/shard_map/unplace/pallas_call | solution.py:192
  114.0 0.2 collective-permute-done.26.refs_4_
  114.2 5.1 %adam.1 = f32[1,3,512,512]{3,2,1,0:T(8,128)} custom-call(s32[2]{0:T(128)S(1)} %pad_add_fusion.refs_0_, f32[16,128]{1,0:T(8,128)S(1)} %get-tuple-element.58.refs_7_.refs_1_, f32[16,128]{1,0:T(8,128)S(1)} %collective-permute-done.24.refs_2_, f32[16,128]{1,0:T(8,128)S(1)} %collective-permute-done.25.refs_3_, f32[16,128]{1,0:T(8,128)S(1)} %collective-permute-done.26.refs_4_, ...), custom_call_target="tpu_custom_call" | custom-call | tf_op jit(solution)/shard_map/adam/pallas_call | solution.py:192
  (24 shorter events, 0.1 us)
Async XLA Ops:
  0.6 41.1 %copy-start = (bf16[1,1,256,2048]{3,2,1,0:T(8,128)(2,1)S(1)}, bf16[1,1,256,2048]{3,2,1,0:T(8,128)(2,1)}, u32[]{:S(2)}) copy-start(bf16[1,1,256,2048]{3,2,1,0:T(8,128)(2,1)} %param.15) | copy-start | bytes 3145732
  3.1 22.9 %collective-permute-start = (bf16[512,512]{1,0:T(8,128)(2,1)}, bf16[512,512]{1,0:T(8,128)(2,1)S(1)}, u32[]{:S(2)}, u32[]{:S(2)}) collective-permute-start(bf16[512,512]{1,0:T(8,128)(2,1)} %get-tuple-element.32), channel_id=1, source_target_pairs={{0,1},{1,0},{2,3},{3,2},{4,5},{5,4},{6,7},{7,6},{8,9},{9,8},{10,11... | collective-permute-start | bytes 1572872 | tf_op jit(solution)/shard_map/ppermute | solution.py:38
  6.0 19.9 %collective-permute-start.1 = (bf16[512,512]{1,0:T(8,128)(2,1)}, bf16[512,512]{1,0:T(8,128)(2,1)S(1)}, u32[]{:S(2)}, u32[]{:S(2)}) collective-permute-start(bf16[512,512]{1,0:T(8,128)(2,1)} %get-tuple-element.33), channel_id=1, source_target_pairs={{0,2},{1,3},{2,0},{3,1},{4,6},{5,7},{6,4},{7,5},{8,10},{9,11},{10,... | collective-permute-start | bytes 1572872 | tf_op jit(solution)/shard_map/ppermute | solution.py:38
  10.2 11.9 %collective-permute-start.2 = (bf16[144,512]{1,0:T(8,128)(2,1)}, bf16[144,512]{1,0:T(8,128)(2,1)S(1)}, u32[]{:S(2)}, u32[]{:S(2)}) collective-permute-start(bf16[144,512]{1,0:T(8,128)(2,1)} %get-tuple-element.34), channel_id=1, source_target_pairs={{0,1},{1,0},{2,3},{3,2},{4,5},{5,4},{6,7},{7,6},{8,9},{9,8},{10,11... | collective-permute-start | bytes 442376 | tf_op jit(solution)/shard_map/ppermute | solution.py:38
  10.8 15.2 %collective-permute-start.3 = (bf16[144,512]{1,0:T(8,128)(2,1)}, bf16[144,512]{1,0:T(8,128)(2,1)S(1)}, u32[]{:S(2)}, u32[]{:S(2)}) collective-permute-start(bf16[144,512]{1,0:T(8,128)(2,1)} %get-tuple-element.35), channel_id=1, source_target_pairs={{0,2},{1,3},{2,0},{3,1},{4,6},{5,7},{6,4},{7,5},{8,10},{9,11},{10,... | collective-permute-start | bytes 442376 | tf_op jit(solution)/shard_map/ppermute | solution.py:38
  10.8 15.2 %collective-permute-start.4 = (bf16[144,512]{1,0:T(8,128)(2,1)}, bf16[144,512]{1,0:T(8,128)(2,1)S(1)}, u32[]{:S(2)}, u32[]{:S(2)}) collective-permute-start(bf16[144,512]{1,0:T(8,128)(2,1)} %get-tuple-element.36), channel_id=1, source_target_pairs={{0,3},{1,2},{2,1},{3,0},{4,7},{5,6},{6,5},{7,4},{8,11},{9,10},{10,... | collective-permute-start | bytes 442376 | tf_op jit(solution)/shard_map/ppermute | solution.py:38
  27.0 0.7 copy-start.5
  27.6 12.8 %collective-permute-start.5 = (bf16[512,512]{1,0:T(8,128)(2,1)}, bf16[512,512]{1,0:T(8,128)(2,1)}, u32[]{:S(2)}, u32[]{:S(2)}) collective-permute-start(bf16[512,512]{1,0:T(8,128)(2,1)} %get-tuple-element.37), channel_id=1, source_target_pairs={{0,1},{1,0},{2,3},{3,2},{4,5},{5,4},{6,7},{7,6},{8,9},{9,8},{10,11... | collective-permute-start | bytes 1572872 | tf_op jit(solution)/shard_map/ppermute | solution.py:38
  28.9 12.8 %collective-permute-start.6 = (bf16[512,512]{1,0:T(8,128)(2,1)}, bf16[512,512]{1,0:T(8,128)(2,1)}, u32[]{:S(2)}, u32[]{:S(2)}) collective-permute-start(bf16[512,512]{1,0:T(8,128)(2,1)} %get-tuple-element.38), channel_id=1, source_target_pairs={{0,2},{1,3},{2,0},{3,1},{4,6},{5,7},{6,4},{7,5},{8,10},{9,11},{10,... | collective-permute-start | bytes 1572872 | tf_op jit(solution)/shard_map/ppermute | solution.py:38
  29.8 0.9 copy-start.3
  30.7 0.9 copy-start.6
  32.6 11.7 %collective-permute-start.9 = (bf16[2,4,32,512]{3,2,1,0:T(8,128)(2,1)S(1)}, bf16[2,4,32,512]{3,2,1,0:T(8,128)(2,1)S(1)}, u32[]{:S(2)}, u32[]{:S(2)}) collective-permute-start(bf16[2,4,32,512]{3,2,1,0:T(8,128)(2,1)S(1)} %get-tuple-element.42), channel_id=1, source_target_pairs={{0,8},{4,12},{8,0},{12,4},{16,24},{20,28},{24,16},{28,20},{1,9},{5... | collective-permute-start | bytes 786440 | tf_op jit(solution)/shard_map/ppermute | solution.py:44
  34.2 21.0 %collective-permute-start.10 = (bf16[2,4,32,512]{3,2,1,0:T(8,128)(2,1)S(1)}, bf16[2,4,32,512]{3,2,1,0:T(8,128)(2,1)S(1)}, u32[]{:S(2)}, u32[]{:S(2)}) collective-permute-start(bf16[2,4,32,512]{3,2,1,0:T(8,128)(2,1)S(1)} %get-tuple-element.43), channel_id=1, source_target_pairs={{0,16},{4,20},{8,24},{12,28},{16,0},{20,4},{24,8},{28,12},{1,17},{... | collective-permute-start | bytes 786440 | tf_op jit(solution)/shard_map/ppermute | solution.py:44
  36.8 18.4 %collective-permute-start.11 = (bf16[2,4,32,512]{3,2,1,0:T(8,128)(2,1)S(1)}, bf16[2,4,32,512]{3,2,1,0:T(8,128)(2,1)S(1)}, u32[]{:S(2)}, u32[]{:S(2)}) collective-permute-start(bf16[2,4,32,512]{3,2,1,0:T(8,128)(2,1)S(1)} %get-tuple-element.44), channel_id=1, source_target_pairs={{0,24},{4,28},{8,16},{12,20},{16,8},{20,12},{24,0},{28,4},{1,25},{... | collective-permute-start | bytes 786440 | tf_op jit(solution)/shard_map/ppermute | solution.py:44
  43.0 21.8 %collective-permute-start.7 = (bf16[896,512]{1,0:T(8,128)(2,1)S(1)}, bf16[896,512]{1,0:T(8,128)(2,1)S(1)}, u32[]{:S(2)}, u32[]{:S(2)}) collective-permute-start(bf16[896,512]{1,0:T(8,128)(2,1)S(1)} %get-tuple-element.39), channel_id=1, source_target_pairs={{0,1},{1,0},{2,3},{3,2},{4,5},{5,4},{6,7},{7,6},{8,9},{9,8},{10,11... | collective-permute-start | bytes 2752520 | tf_op jit(solution)/shard_map/ppermute | solution.py:38
  43.6 21.5 %collective-permute-start.8 = (bf16[896,512]{1,0:T(8,128)(2,1)S(1)}, bf16[896,512]{1,0:T(8,128)(2,1)S(1)}, u32[]{:S(2)}, u32[]{:S(2)}) collective-permute-start(bf16[896,512]{1,0:T(8,128)(2,1)S(1)} %get-tuple-element.40), channel_id=1, source_target_pairs={{0,2},{1,3},{2,0},{3,1},{4,6},{5,7},{6,4},{7,5},{8,10},{9,11},{10,... | collective-permute-start | bytes 2752520 | tf_op jit(solution)/shard_map/ppermute | solution.py:38
  55.3 2.0 %collective-permute-start.12 = (bf16[4,4,32,512]{3,2,1,0:T(8,128)(2,1)S(1)}, bf16[4,4,32,512]{3,2,1,0:T(8,128)(2,1)S(1)}, u32[]{:S(2)}, u32[]{:S(2)}) collective-permute-start(bf16[4,4,32,512]{3,2,1,0:T(8,128)(2,1)S(1)} %pick.2), channel_id=1, source_target_pairs={{0,4},{4,0},{8,12},{12,8},{16,20},{20,16},{24,28},{28,24},{1,5},{5... | collective-permute-start | bytes 1572872 | tf_op jit(solution)/shard_map/ppermute | solution.py:68
  58.5 12.0 %collective-permute-start.13 = (bf16[256,512]{1,0:T(8,128)(2,1)S(1)}, bf16[256,512]{1,0:T(8,128)(2,1)S(1)}, u32[]{:S(2)}, u32[]{:S(2)}) collective-permute-start(bf16[256,512]{1,0:T(8,128)(2,1)S(1)} %get-tuple-element.46), channel_id=1, source_target_pairs={{0,1},{1,0},{2,3},{3,2},{4,5},{5,4},{6,7},{7,6},{8,9},{9,8},{10,11... | collective-permute-start | bytes 786440 | tf_op jit(solution)/shard_map/ppermute | solution.py:38
  59.1 15.5 %collective-permute-start.14 = (bf16[256,512]{1,0:T(8,128)(2,1)S(1)}, bf16[256,512]{1,0:T(8,128)(2,1)S(1)}, u32[]{:S(2)}, u32[]{:S(2)}) collective-permute-start(bf16[256,512]{1,0:T(8,128)(2,1)S(1)} %get-tuple-element.47), channel_id=1, source_target_pairs={{0,2},{1,3},{2,0},{3,1},{4,6},{5,7},{6,4},{7,5},{8,10},{9,11},{10,... | collective-permute-start | bytes 786440 | tf_op jit(solution)/shard_map/ppermute | solution.py:38
  60.6 14.0 %collective-permute-start.15 = (bf16[256,512]{1,0:T(8,128)(2,1)S(1)}, bf16[256,512]{1,0:T(8,128)(2,1)S(1)}, u32[]{:S(2)}, u32[]{:S(2)}) collective-permute-start(bf16[256,512]{1,0:T(8,128)(2,1)S(1)} %get-tuple-element.48), channel_id=1, source_target_pairs={{0,3},{1,2},{2,1},{3,0},{4,7},{5,6},{6,5},{7,4},{8,11},{9,10},{10,... | collective-permute-start | bytes 786440 | tf_op jit(solution)/shard_map/ppermute | solution.py:38
  75.1 18.6 %collective-permute-start.19 = (bf16[2,384,512]{2,1,0:T(8,128)(2,1)S(1)}, bf16[2,384,512]{2,1,0:T(8,128)(2,1)S(1)}, u32[]{:S(2)}, u32[]{:S(2)}) collective-permute-start(bf16[2,384,512]{2,1,0:T(8,128)(2,1)S(1)} %factors.1.refs_1_.refs_3_), channel_id=1, source_target_pairs={{0,1},{1,0},{2,3},{3,2},{4,5},{5,4},{6,7},{7,6},{8,9},{9,8},{10,11... | collective-permute-start | bytes 2359304 | tf_op jit(solution)/shard_map/ppermute | solution.py:38
  76.6 17.3 %collective-permute-start.20 = (bf16[2,384,512]{2,1,0:T(8,128)(2,1)S(1)}, bf16[2,384,512]{2,1,0:T(8,128)(2,1)S(1)}, u32[]{:S(2)}, u32[]{:S(2)}) collective-permute-start(bf16[2,384,512]{2,1,0:T(8,128)(2,1)S(1)} %factors.1.refs_1_.refs_3_), channel_id=1, source_target_pairs={{0,2},{1,3},{2,0},{3,1},{4,6},{5,7},{6,4},{7,5},{8,10},{9,11},{10,... | collective-permute-start | bytes 2359304 | tf_op jit(solution)/shard_map/ppermute | solution.py:38
  79.4 19.2 %collective-permute-start.16 = (bf16[2,32,2048]{2,1,0:T(8,128)(2,1)S(1)}, bf16[2,32,2048]{2,1,0:T(8,128)(2,1)S(1)}, u32[]{:S(2)}, u32[]{:S(2)}) collective-permute-start(bf16[2,32,2048]{2,1,0:T(8,128)(2,1)S(1)} %get-tuple-element.50), channel_id=1, source_target_pairs={{0,8},{4,12},{8,0},{12,4},{16,24},{20,28},{24,16},{28,20},{1,9},{5... | collective-permute-start | bytes 786440 | tf_op jit(solution)/shard_map/ppermute | solution.py:44
  82.2 20.6 %collective-permute-start.17 = (bf16[2,32,2048]{2,1,0:T(8,128)(2,1)S(1)}, bf16[2,32,2048]{2,1,0:T(8,128)(2,1)S(1)}, u32[]{:S(2)}, u32[]{:S(2)}) collective-permute-start(bf16[2,32,2048]{2,1,0:T(8,128)(2,1)S(1)} %get-tuple-element.51), channel_id=1, source_target_pairs={{0,16},{4,20},{8,24},{12,28},{16,0},{20,4},{24,8},{28,12},{1,17},{... | collective-permute-start | bytes 786440 | tf_op jit(solution)/shard_map/ppermute | solution.py:44
  83.6 19.2 %collective-permute-start.18 = (bf16[2,32,2048]{2,1,0:T(8,128)(2,1)S(1)}, bf16[2,32,2048]{2,1,0:T(8,128)(2,1)S(1)}, u32[]{:S(2)}, u32[]{:S(2)}) collective-permute-start(bf16[2,32,2048]{2,1,0:T(8,128)(2,1)S(1)} %get-tuple-element.52), channel_id=1, source_target_pairs={{0,24},{4,28},{8,16},{12,20},{16,8},{20,12},{24,0},{28,4},{1,25},{... | collective-permute-start | bytes 786440 | tf_op jit(solution)/shard_map/ppermute | solution.py:44
  94.0 11.8 %collective-permute-start.22 = (bf16[512,512]{1,0:T(8,128)(2,1)S(1)}, bf16[512,512]{1,0:T(8,128)(2,1)S(1)}, u32[]{:S(2)}, u32[]{:S(2)}) collective-permute-start(bf16[512,512]{1,0:T(8,128)(2,1)S(1)} %get-tuple-element.56), channel_id=1, source_target_pairs={{0,1},{1,0},{2,3},{3,2},{4,5},{5,4},{6,7},{7,6},{8,9},{9,8},{10,11... | collective-permute-start | bytes 1572872 | tf_op jit(solution)/shard_map/ppermute | solution.py:38
  95.5 11.4 %collective-permute-start.23 = (bf16[512,512]{1,0:T(8,128)(2,1)S(1)}, bf16[512,512]{1,0:T(8,128)(2,1)S(1)}, u32[]{:S(2)}, u32[]{:S(2)}) collective-permute-start(bf16[512,512]{1,0:T(8,128)(2,1)S(1)} %get-tuple-element.57), channel_id=1, source_target_pairs={{0,2},{1,3},{2,0},{3,1},{4,6},{5,7},{6,4},{7,5},{8,10},{9,11},{10,... | collective-permute-start | bytes 1572872 | tf_op jit(solution)/shard_map/ppermute | solution.py:38
  102.9 9.4 %collective-permute-start.21 = (bf16[4,32,2048]{2,1,0:T(8,128)(2,1)S(1)}, bf16[4,32,2048]{2,1,0:T(8,128)(2,1)S(1)}, u32[]{:S(2)}, u32[]{:S(2)}) collective-permute-start(bf16[4,32,2048]{2,1,0:T(8,128)(2,1)S(1)} %pick.3), channel_id=1, source_target_pairs={{0,4},{4,0},{8,12},{12,8},{16,20},{20,16},{24,28},{28,24},{1,5},{5... | collective-permute-start | bytes 1572872 | tf_op jit(solution)/shard_map/ppermute | solution.py:68
  106.9 5.3 %copy-start.4 = (bf16[144,512]{1,0:T(8,128)(2,1)S(1)}, bf16[144,512]{1,0:T(8,128)(2,1)}, u32[]{:S(2)}) copy-start(bf16[144,512]{1,0:T(8,128)(2,1)} %get-tuple-element.31.refs_1_) | copy-start | bytes 442372
  107.0 7.2 %copy-start.1 = (f32[1,3,512,512]{3,2,1,0:T(8,128)S(1)}, f32[1,3,512,512]{3,2,1,0:T(8,128)}, u32[]{:S(2)}) copy-start(f32[1,3,512,512]{3,2,1,0:T(8,128)} %refs_7_.1) | copy-start | bytes 9437188
  107.0 7.2 %copy-start.2 = (f32[1,3,512,512]{3,2,1,0:T(8,128)S(1)}, f32[1,3,512,512]{3,2,1,0:T(8,128)}, u32[]{:S(2)}) copy-start(f32[1,3,512,512]{3,2,1,0:T(8,128)} %refs_8_.1) | copy-start | bytes 9437188
  108.7 5.3 %collective-permute-start.24 = (f32[16,128]{1,0:T(8,128)S(1)}, f32[16,128]{1,0:T(8,128)S(1)}, u32[]{:S(2)}, u32[]{:S(2)}) collective-permute-start(f32[16,128]{1,0:T(8,128)S(1)} %get-tuple-element.58.refs_7_.refs_1_), channel_id=1, source_target_pairs={{0,1},{1,0},{2,3},{3,2},{4,5},{5,4},{6,7},{7,6},{8,9},{9,8},{10,11... | collective-permute-start | bytes 24584 | tf_op jit(solution)/shard_map/ppermute | solution.py:38
  109.3 4.7 %collective-permute-start.25 = (f32[16,128]{1,0:T(8,128)S(1)}, f32[16,128]{1,0:T(8,128)S(1)}, u32[]{:S(2)}, u32[]{:S(2)}) collective-permute-start(f32[16,128]{1,0:T(8,128)S(1)} %get-tuple-element.58.refs_7_.refs_1_), channel_id=1, source_target_pairs={{0,2},{1,3},{2,0},{3,1},{4,6},{5,7},{6,4},{7,5},{8,10},{9,11},{10,... | collective-permute-start | bytes 24584 | tf_op jit(solution)/shard_map/ppermute | solution.py:38
  109.6 4.5 %collective-permute-start.26 = (f32[16,128]{1,0:T(8,128)S(1)}, f32[16,128]{1,0:T(8,128)S(1)}, u32[]{:S(2)}, u32[]{:S(2)}) collective-permute-start(f32[16,128]{1,0:T(8,128)S(1)} %get-tuple-element.58.refs_7_.refs_1_), channel_id=1, source_target_pairs={{0,3},{1,2},{2,1},{3,0},{4,7},{5,6},{6,5},{7,4},{8,11},{9,10},{10,... | collective-permute-start | bytes 24584 | tf_op jit(solution)/shard_map/ppermute | solution.py:38

commit v9 on v7

--- a/solution.py
+++ b/solution.py
@@ -85,13 +85,13 @@
         out_ref[...] = matrix_ref[:, segment(rep_ref, offset, out_ref.shape[1])]
 
 
-def payload_kernel(rep_ref, weights_ref, inputs_ref, *out_refs):
-    seg_rows = weights_ref.shape[2]
+def payload_kernel(rep_ref, pair_ref, inputs_ref, *out_refs):
+    seg_rows = pair_ref.shape[1]
     slot_count = inputs_ref.shape[0]
     half = slot_count // 2
     for part, out_ref in enumerate(out_refs):
-        out_ref[pl.ds(0, seg_rows), :] = weights_ref[0, 0]
-        out_ref[pl.ds(seg_rows, seg_rows), :] = weights_ref[0, 1]
+        out_ref[pl.ds(0, seg_rows), :] = pair_ref[0]
+        out_ref[pl.ds(seg_rows, seg_rows), :] = pair_ref[1]
         columns = segment(rep_ref, part + 1, seg_rows)
         out_ref[pl.ds(2 * seg_rows, slot_count), :] = inputs_ref[:, columns]
         columns = segment(rep_ref, 3, seg_rows)
@@ -109,9 +109,8 @@
 
 
 def projection_rows(refs):
-    if len(refs) == 1 and len(refs[0].shape) > 2:
-        ref = refs[0] if len(refs[0].shape) == 3 else refs[0].at[0]
-        return ref.at[0], ref.at[1]
+    if len(refs) == 1 and len(refs[0].shape) == 3:
+        return refs[0].at[0], refs[0].at[1]
     seg_rows = refs[0].shape[1]
     start = 0 if len(refs) == 2 else seg_rows
     return refs[0].at[pl.ds(0, seg_rows)], refs[-1].at[pl.ds(start, seg_rows)]
@@ -284,7 +283,7 @@
             block_ref = spread_block(chips, came_refs, expert)
             incoming_ref[offset, spot_ref[0] ^ expert] = block_ref[offset]
         rows = flat_rows(incoming_ref[offset])
-        out_ref[...] = multiply(rows, weight_ref[0, 2]).astype(out_ref.dtype)
+        out_ref[...] = multiply(rows, weight_ref[...]).astype(out_ref.dtype)
 
 
 def forward_kernel(offsets, lengths, has_start, rep_ref, inputs_ref, *refs):
@@ -538,7 +537,7 @@
 def adam(rep, groups, grads, gram, first_moment, second_moment, after):
     count = sum(len(group) for group in groups)
     seg_rows, hidden_width = first_moment.shape[2:]
-    grams = exchange([gram] * count)
+    grams = [gram] + [from_peer(gram, k) for k in reversed(range(1, count))]
     tile = min(seg_rows, 256)
     moment_spec = pl.BlockSpec((1, 1, tile, hidden_width), lambda m, d: (0, m, d, 0))
     (adam_step,) = call(
@@ -587,22 +586,23 @@
     routed = exchange(row_blocks)
 
     inputs_home = saved_inputs[0, 0]
+    pair = weights[0, :2]
     packed = rep_count == 4 and seg_rows == hidden_width
     if packed:
         payload = shape((2 * seg_rows + slot_count + half, seg_rows), jnp.bfloat16)
         to_one, to_two = call(
             payload_kernel,
             "payload",
-            [rep, weights, inputs_home],
+            [rep, pair, inputs_home],
             [SMEM, VMEM, VMEM],
             [payload, payload],
             after=routed[1:],
         )
         from_two, from_one = from_peer(to_two, 2), from_peer(to_one, 1)
-        projections = [(weights,), (from_one,), (from_two,)]
+        projections = [(to_one,), (from_one,), (from_two,)]
         inputs = [(inputs_home,), (from_one,), (from_two,)]
     else:
-        projections = [(x,) for x in exchange([weights[0, :2]] * rep_count)]
+        projections = [(x,) for x in exchange([pair] * rep_count)]
         pieces = [shape((slot_count, seg_rows), jnp.bfloat16) for _ in offsets]
         pieces = call(split_kernel, "split", [rep, inputs_home], [SMEM, VMEM], pieces)
         inputs = [(x,) for x in exchange(pieces)]
@@ -629,7 +629,7 @@
     incoming, *back = call(
         functools.partial(back_kernel, chips, len(came)),
         "back",
-        [spot, weights, *came],
+        [spot, weights[0, 2], *came],
         [SMEM] + [VMEM] * (1 + len(came)),
         [shape((rep_count, expert_count, capacity, seg_rows), jnp.bfloat16)]
         + [shape(back_shape, jnp.bfloat16 if k else jnp.float32) for k in offsets],

time: 121 us -> 116 us (0.959)
  Pallas kernels: 22.6 us -> 19.9 us
  waiting for transfers between devices: 62.7 us -> 61.4 us
  local copies, waits for them, and re-layouts: 3.62 us -> 2.4 us
    unnamed x18 -> x10, local copies, waits for them, and re-layouts: 3.62 us -> 0.02 us
    pallas_call x16, Pallas kernels: 22.6 us -> 19.9 us  [call(): pl.pallas_call(body, grid=grid, in_specs=list(specs) + [VMEM] * len(after...]
    squeeze x0 -> x2, local copies, waits for them, and re-layouts: none -> 2.37 us  [the longest x1 1.29 us: shards(): pair = weights[0, :2]]
    ppermute x17, waiting for transfers between devices: 40.9 us -> 39.4 us  [from_peer(): lax.ppermute(array, 'replica', [(i, i ^ offset) for i in range(count)])]
    ppermute x6, waiting for transfers between devices: 19.8 us -> 21.2 us  [across_chips(): lax.ppermute(part, 'expert', [(i, i ^ 2 * k) for i in range(count)])]
  transfers between devices with their start and end apart: 26 -> 26, of which waited for: 15 -> 16; matrix products, arithmetic and copies ran while one was open for 0% -> 2% of each run, Pallas kernels for 10% -> 10%
where the time goes in v9:
time: 116 us; the launch traced here: 115 us
  waiting for transfers between devices  61.4 us (53%)
  starting transfers between devices  30.3 us (26%)
  Pallas kernels  19.9 us (17%)
  local copies, waits for them, and re-layouts  2.4 us (2%)
  between operations  1.52 us (1%)
    ppermute x17, waiting for transfers between devices, from_peer(): lax.ppermute(array, 'replica', [(i, i ^ offset) for i in range(count)])  39.4 us
    ppermute x6, waiting for transfers between devices, across_chips(): lax.ppermute(part, 'expert', [(i, i ^ 2 * k) for i in range(count)])  21.2 us
    pallas_call x16, Pallas kernels, call(): pl.pallas_call(body, grid=grid, in_specs=list(specs) + [VMEM] * len(after...  19.9 us
    ppermute x17, starting transfers between devices, from_peer(): lax.ppermute(array, 'replica', [(i, i ^ offset) for i in range(count)])  19.8 us
    ppermute x6, starting transfers between devices, across_chips(): lax.ppermute(part, 'expert', [(i, i ^ 2 * k) for i in range(count)])  9.82 us
  transfers between devices with their start and end apart: 26, of which 16 were waited for; matrix products, arithmetic and copies ran while one was open for 2% of the time, Pallas kernels for 10%

profile of v9, /device:TPU:0, one launch (start us, length us, event | category | flops | bytes accessed | tf_op | source)
XLA Modules:
  0.0 115.5 jit_solution(12567805663619861692)
XLA Ops:
  0.6 0.0 copy-start
  1.4 2.0 %rows.1 = (bf16[144,512]{1,0:T(8,128)(2,1)}, bf16[144,512]{1,0:T(8,128)(2,1)}, bf16[144,512]{1,0:T(8,128)(2,1)}, bf16[144,512]{1,0:T(8,128)(2,1)}) custom-call(s32[1]{0:T(128)} %bitcast.1.refs_0_, s32[1,1]{1,0:T(1,128)S(6)} %copy.10.refs_1_, f32[8]{0:T(128)} %refs_2_.1, s32[1,128]{1,0:T(1,128)} %bitcast.14, bf16[128,2048]{1,0:T(8,128)(2,1)} %bitcast.13), custom_call_target="tpu_custom_call" | custom-call | tf_op jit(solution)/shard_map/rows/pallas_call | solution.py:186
  3.4 2.9 %collective-permute-start = (bf16[144,512]{1,0:T(8,128)(2,1)}, bf16[144,512]{1,0:T(8,128)(2,1)S(1)}, u32[]{:S(2)}, u32[]{:S(2)}) collective-permute-start(bf16[144,512]{1,0:T(8,128)(2,1)} %get-tuple-element.32), channel_id=1, source_target_pairs={{0,1},{1,0},{2,3},{3,2},{4,5},{5,4},{6,7},{7,6},{8,9},{9,8},{10,11... | collective-permute-start | bytes 442376 | tf_op jit(solution)/shard_map/ppermute | solution.py:38
  6.3 1.5 %collective-permute-start.1 = (bf16[144,512]{1,0:T(8,128)(2,1)}, bf16[144,512]{1,0:T(8,128)(2,1)S(1)}, u32[]{:S(2)}, u32[]{:S(2)}) collective-permute-start(bf16[144,512]{1,0:T(8,128)(2,1)} %get-tuple-element.33), channel_id=1, source_target_pairs={{0,2},{1,3},{2,0},{3,1},{4,6},{5,7},{6,4},{7,5},{8,10},{9,11},{10,... | collective-permute-start | bytes 442376 | tf_op jit(solution)/shard_map/ppermute | solution.py:38
  7.8 0.0 collective-permute-start.2
  7.9 1.3 %slice_bitcast_fusion.refs_1_ = bf16[2,512,512]{2,1,0:T(8,128)(2,1)S(1)} fusion(bf16[1,3,512,512]{3,2,1,0:T(8,128)(2,1)} %param.8), kind=kLoop, calls=%fused_computation | loop fusion | bytes 2097152 | tf_op jit(solution)/shard_map/squeeze | solution.py:589
  9.1 0.0 copy-start.4
  9.2 1.7 %collective-permute-done.refs_3_.refs_2_ = bf16[144,512]{1,0:T(8,128)(2,1)S(1)} collective-permute-done((bf16[144,512]{1,0:T(8,128)(2,1)}, bf16[144,512]{1,0:T(8,128)(2,1)S(1)}, u32[]{:S(2)}, u32[]{:S(2)}) %collective-permute-start) | collective-permute-done | bytes 147488 | tf_op jit(solution)/shard_map/ppermute | solution.py:38
  10.9 4.1 %collective-permute-done.1.refs_4_.refs_3_ = bf16[144,512]{1,0:T(8,128)(2,1)S(1)} collective-permute-done((bf16[144,512]{1,0:T(8,128)(2,1)}, bf16[144,512]{1,0:T(8,128)(2,1)S(1)}, u32[]{:S(2)}, u32[]{:S(2)}) %collective-permute-start.1) | collective-permute-done | bytes 147488 | tf_op jit(solution)/shard_map/ppermute | solution.py:38
  15.0 1.8 %payload.1 = (bf16[1408,512]{1,0:T(8,128)(2,1)}, bf16[1408,512]{1,0:T(8,128)(2,1)}) custom-call(s32[1]{0:T(128)} %bitcast.1.refs_0_, bf16[2,512,512]{2,1,0:T(8,128)(2,1)S(1)} %slice_bitcast_fusion.refs_1_, bf16[256,2048]{1,0:T(8,128)(2,1)S(1)} %bitcast.9, bf16[144,512]{1,0:T(8,128)(2,1)S(1)} %collective-permute-done.refs_3_.refs_2_, ...), custom_call_target="tpu_custom_call" | custom-call | tf_op jit(solution)/shard_map/payload/pallas_call | solution.py:186
  16.8 1.2 %collective-permute-start.3 = (bf16[1408,512]{1,0:T(8,128)(2,1)}, bf16[1408,512]{1,0:T(8,128)(2,1)S(1)}, u32[]{:S(2)}, u32[]{:S(2)}) collective-permute-start(bf16[1408,512]{1,0:T(8,128)(2,1)} %get-tuple-element.35.refs_2_.refs_3_), channel_id=1, source_target_pairs={{0,1},{1,0},{2,3},{3,2},{4,5},{5,4},{6,7},{7,6},{8,9},{9,8},{10,11... | collective-permute-start | bytes 4325384 | tf_op jit(solution)/shard_map/ppermute | solution.py:38
  18.1 0.8 collective-permute-start.4
  18.9 0.4 place.1
  19.3 1.6 %collective-permute-start.5 = (bf16[2,4,32,512]{3,2,1,0:T(8,128)(2,1)S(1)}, bf16[2,4,32,512]{3,2,1,0:T(8,128)(2,1)S(1)}, u32[]{:S(2)}, u32[]{:S(2)}) collective-permute-start(bf16[2,4,32,512]{3,2,1,0:T(8,128)(2,1)S(1)} %get-tuple-element.38), channel_id=1, source_target_pairs={{0,8},{4,12},{8,0},{12,4},{16,24},{20,28},{24,16},{28,20},{1,9},{5... | collective-permute-start | bytes 786440 | tf_op jit(solution)/shard_map/ppermute | solution.py:44
  21.0 2.6 %collective-permute-start.6 = (bf16[2,4,32,512]{3,2,1,0:T(8,128)(2,1)S(1)}, bf16[2,4,32,512]{3,2,1,0:T(8,128)(2,1)S(1)}, u32[]{:S(2)}, u32[]{:S(2)}) collective-permute-start(bf16[2,4,32,512]{3,2,1,0:T(8,128)(2,1)S(1)} %get-tuple-element.39), channel_id=1, source_target_pairs={{0,16},{4,20},{8,24},{12,28},{16,0},{20,4},{24,8},{28,12},{1,17},{... | collective-permute-start | bytes 786440 | tf_op jit(solution)/shard_map/ppermute | solution.py:44
  23.6 0.2 collective-permute-start.7
  23.8 5.7 %collective-permute-done.5.refs_1_.refs_3_ = bf16[2,4,32,512]{3,2,1,0:T(8,128)(2,1)S(1)} collective-permute-done((bf16[2,4,32,512]{3,2,1,0:T(8,128)(2,1)S(1)}, bf16[2,4,32,512]{3,2,1,0:T(8,128)(2,1)S(1)}, u32[]{:S(2)}, u32[]{:S(2)}) %collective-permute-start.5) | collective-permute-done | bytes 262176 | tf_op jit(solution)/shard_map/ppermute | solution.py:44
  29.5 12.5 %collective-permute-done.6.refs_2_.refs_4_ = bf16[2,4,32,512]{3,2,1,0:T(8,128)(2,1)S(1)} collective-permute-done((bf16[2,4,32,512]{3,2,1,0:T(8,128)(2,1)S(1)}, bf16[2,4,32,512]{3,2,1,0:T(8,128)(2,1)S(1)}, u32[]{:S(2)}, u32[]{:S(2)}) %collective-permute-start.6) | collective-permute-done | bytes 262176 | tf_op jit(solution)/shard_map/ppermute | solution.py:44
  42.0 0.0 collective-permute-done.7.refs_3_.refs_5_
  42.0 0.1 collective-permute-start.8
  42.1 1.1 slice_bitcast_fusion.1.refs_1_
  43.2 0.8 collective-permute-done.8.refs_6_
  44.0 0.7 back.1
  44.7 4.7 %collective-permute-done.3.refs_3_.refs_1_.refs_4_ = bf16[1408,512]{1,0:T(8,128)(2,1)S(1)} collective-permute-done((bf16[1408,512]{1,0:T(8,128)(2,1)}, bf16[1408,512]{1,0:T(8,128)(2,1)S(1)}, u32[]{:S(2)}, u32[]{:S(2)}) %collective-permute-start.3) | collective-permute-done | bytes 1441824 | tf_op jit(solution)/shard_map/ppermute | solution.py:38
  49.4 1.0 collective-permute-done.4.refs_4_.refs_0_.refs_5_.refs_6_
  50.5 0.1 pass.1
  50.5 0.8 collective-permute-start.9
  51.3 1.4 %collective-permute-start.10 = (bf16[640,512]{1,0:T(8,128)(2,1)S(1)}, bf16[640,512]{1,0:T(8,128)(2,1)S(1)}, u32[]{:S(2)}, u32[]{:S(2)}) collective-permute-start(bf16[640,512]{1,0:T(8,128)(2,1)S(1)} %get-tuple-element.43), channel_id=1, source_target_pairs={{0,2},{1,3},{2,0},{3,1},{4,6},{5,7},{6,4},{7,5},{8,10},{9,11},{10,... | collective-permute-start | bytes 1966088 | tf_op jit(solution)/shard_map/ppermute | solution.py:38
  52.7 0.4 collective-permute-start.11
  53.1 1.5 %collective-permute-start.12 = (bf16[256,512]{1,0:T(8,128)(2,1)S(1)}, bf16[256,512]{1,0:T(8,128)(2,1)S(1)}, u32[]{:S(2)}, u32[]{:S(2)}) collective-permute-start(bf16[256,512]{1,0:T(8,128)(2,1)S(1)} %get-tuple-element.45), channel_id=1, source_target_pairs={{0,2},{1,3},{2,0},{3,1},{4,6},{5,7},{6,4},{7,5},{8,10},{9,11},{10,... | collective-permute-start | bytes 786440 | tf_op jit(solution)/shard_map/ppermute | solution.py:38
  54.7 1.5 %collective-permute-start.13 = (bf16[256,512]{1,0:T(8,128)(2,1)S(1)}, bf16[256,512]{1,0:T(8,128)(2,1)S(1)}, u32[]{:S(2)}, u32[]{:S(2)}) collective-permute-start(bf16[256,512]{1,0:T(8,128)(2,1)S(1)} %get-tuple-element.46), channel_id=1, source_target_pairs={{0,3},{1,2},{2,1},{3,0},{4,7},{5,6},{6,5},{7,4},{8,11},{9,10},{10,... | collective-permute-start | bytes 786440 | tf_op jit(solution)/shard_map/ppermute | solution.py:38
  56.2 2.3 %forward.1.refs_2_ = f32[2,256,512]{2,1,0:T(8,128)S(1)} custom-call(s32[1]{0:T(128)} %bitcast.1.refs_0_, bf16[256,2048]{1,0:T(8,128)(2,1)S(1)} %bitcast.10, bf16[1408,512]{1,0:T(8,128)(2,1)} %get-tuple-element.35.refs_2_.refs_3_, bf16[1408,512]{1,0:T(8,128)(2,1)S(1)} %collective-permute-done.3.refs_3_.refs_1_.refs_4_, ...), custom_call_target="tpu_custom_call" | custom-call | tf_op jit(solution)/shard_map/forward/pallas_call | solution.py:186
  58.5 9.7 %collective-permute-done.9.refs_3_.refs_6_.refs_4_ = bf16[640,512]{1,0:T(8,128)(2,1)S(1)} collective-permute-done((bf16[640,512]{1,0:T(8,128)(2,1)S(1)}, bf16[640,512]{1,0:T(8,128)(2,1)S(1)}, u32[]{:S(2)}, u32[]{:S(2)}) %collective-permute-start.9) | collective-permute-done | bytes 655392 | tf_op jit(solution)/shard_map/ppermute | solution.py:38
  68.3 1.0 collective-permute-done.10.refs_4_.refs_7_.refs_5_
  69.3 0.4 rest.1.refs_0_
  69.7 3.7 %collective-permute-done.11.refs_2_ = bf16[256,512]{1,0:T(8,128)(2,1)S(1)} collective-permute-done((bf16[256,512]{1,0:T(8,128)(2,1)S(1)}, bf16[256,512]{1,0:T(8,128)(2,1)S(1)}, u32[]{:S(2)}, u32[]{:S(2)}) %collective-permute-start.11) | collective-permute-done | bytes 262176 | tf_op jit(solution)/shard_map/ppermute | solution.py:38
  73.4 3.2 %collective-permute-done.12.refs_3_ = bf16[256,512]{1,0:T(8,128)(2,1)S(1)} collective-permute-done((bf16[256,512]{1,0:T(8,128)(2,1)S(1)}, bf16[256,512]{1,0:T(8,128)(2,1)S(1)}, u32[]{:S(2)}, u32[]{:S(2)}) %collective-permute-start.12) | collective-permute-done | bytes 262176 | tf_op jit(solution)/shard_map/ppermute | solution.py:38
  76.6 0.0 collective-permute-done.13.refs_4_
  76.6 0.4 factors.1.refs_2_.refs_3_
  77.0 1.7 %collective-permute-start.17 = (bf16[2,384,512]{2,1,0:T(8,128)(2,1)S(1)}, bf16[2,384,512]{2,1,0:T(8,128)(2,1)S(1)}, u32[]{:S(2)}, u32[]{:S(2)}) collective-permute-start(bf16[2,384,512]{2,1,0:T(8,128)(2,1)S(1)} %factors.1.refs_2_.refs_3_), channel_id=1, source_target_pairs={{0,1},{1,0},{2,3},{3,2},{4,5},{5,4},{6,7},{7,6},{8,9},{9,8},{10,11... | collective-permute-start | bytes 2359304 | tf_op jit(solution)/shard_map/ppermute | solution.py:38
  78.7 0.2 collective-permute-start.18
  78.9 2.7 %slots.1 = (bf16[2,32,2048]{2,1,0:T(8,128)(2,1)S(1)}, bf16[2,32,2048]{2,1,0:T(8,128)(2,1)S(1)}, bf16[2,32,2048]{2,1,0:T(8,128)(2,1)S(1)}, bf16[2,32,2048]{2,1,0:T(8,128)(2,1)S(1)}) custom-call(s32[1]{0:T(128)} %bitcast.1.refs_0_, s32[1]{0:T(128)} %bitcast.refs_0_.refs_1_, bf16[2,384,512]{2,1,0:T(8,128)(2,1)S(1)} %factors.1.refs_2_.refs_3_, ...), custom_call_target="tpu_custom_call" | custom-call | tf_op jit(solution)/shard_map/slots/pallas_call | solution.py:186
  81.6 2.8 %collective-permute-start.14 = (bf16[2,32,2048]{2,1,0:T(8,128)(2,1)S(1)}, bf16[2,32,2048]{2,1,0:T(8,128)(2,1)S(1)}, u32[]{:S(2)}, u32[]{:S(2)}) collective-permute-start(bf16[2,32,2048]{2,1,0:T(8,128)(2,1)S(1)} %get-tuple-element.48), channel_id=1, source_target_pairs={{0,8},{4,12},{8,0},{12,4},{16,24},{20,28},{24,16},{28,20},{1,9},{5... | collective-permute-start | bytes 786440 | tf_op jit(solution)/shard_map/ppermute | solution.py:44
  84.3 2.6 %collective-permute-start.15 = (bf16[2,32,2048]{2,1,0:T(8,128)(2,1)S(1)}, bf16[2,32,2048]{2,1,0:T(8,128)(2,1)S(1)}, u32[]{:S(2)}, u32[]{:S(2)}) collective-permute-start(bf16[2,32,2048]{2,1,0:T(8,128)(2,1)S(1)} %get-tuple-element.49), channel_id=1, source_target_pairs={{0,16},{4,20},{8,24},{12,28},{16,0},{20,4},{24,8},{28,12},{1,17},{... | collective-permute-start | bytes 786440 | tf_op jit(solution)/shard_map/ppermute | solution.py:44
  86.9 7.7 %collective-permute-done.17.refs_5_.refs_1_ = bf16[2,384,512]{2,1,0:T(8,128)(2,1)S(1)} collective-permute-done((bf16[2,384,512]{2,1,0:T(8,128)(2,1)S(1)}, bf16[2,384,512]{2,1,0:T(8,128)(2,1)S(1)}, u32[]{:S(2)}, u32[]{:S(2)}) %collective-permute-start.17) | collective-permute-done | bytes 786464 | tf_op jit(solution)/shard_map/ppermute | solution.py:38
  94.7 0.0 collective-permute-done.18.refs_7_.refs_0_
  94.7 0.1 cut.1
  94.7 1.7 %collective-permute-start.21 = (bf16[384,512]{1,0:T(8,128)(2,1)S(1)}, bf16[384,512]{1,0:T(8,128)(2,1)S(1)}, u32[]{:S(2)}, u32[]{:S(2)}) collective-permute-start(bf16[384,512]{1,0:T(8,128)(2,1)S(1)} %get-tuple-element.56), channel_id=1, source_target_pairs={{0,1},{1,0},{2,3},{3,2},{4,5},{5,4},{6,7},{7,6},{8,9},{9,8},{10,11... | collective-permute-start | bytes 1179656 | tf_op jit(solution)/shard_map/ppermute | solution.py:38
  96.5 0.5 collective-permute-start.22
  97.0 2.1 %gram.1 = (f32[3,3,512,512]{3,2,1,0:T(8,128)S(1)}, f32[16,128]{1,0:T(8,128)S(1)}) custom-call(s32[1]{0:T(128)} %bitcast.1.refs_0_, bf16[4,8,32,512]{3,2,1,0:T(8,128)(2,1)S(1)} %get-tuple-element.51.refs_1_.refs_3_, bf16[256,2048]{1,0:T(8,128)(2,1)S(1)} %bitcast.12, bf16[2,384,512]{2,1,0:T(8,128)(2,1)S(1)} %factors.1.refs_2_.refs_3_, ...), custom_call_target="tpu_custom_call" | custom-call | tf_op jit(solution)/shard_map/gram/pallas_call | solution.py:186
  99.0 0.0 collective-permute-done.14.refs_1_.refs_3_
  99.0 3.0 %collective-permute-done.15.refs_2_.refs_4_ = bf16[2,32,2048]{2,1,0:T(8,128)(2,1)S(1)} collective-permute-done((bf16[2,32,2048]{2,1,0:T(8,128)(2,1)S(1)}, bf16[2,32,2048]{2,1,0:T(8,128)(2,1)S(1)}, u32[]{:S(2)}, u32[]{:S(2)}) %collective-permute-start.15) | collective-permute-done | bytes 262176 | tf_op jit(solution)/shard_map/ppermute | solution.py:44
  102.1 0.1 collective-permute-start.19
  102.1 0.5 collective-permute-start.20
  102.6 0.0 collective-permute-done.21.refs_6_
  102.6 1.6 %collective-permute-done.22.refs_7_ = bf16[384,512]{1,0:T(8,128)(2,1)S(1)} collective-permute-done((bf16[384,512]{1,0:T(8,128)(2,1)S(1)}, bf16[384,512]{1,0:T(8,128)(2,1)S(1)}, u32[]{:S(2)}, u32[]{:S(2)}) %collective-permute-start.22) | collective-permute-done | bytes 393248 | tf_op jit(solution)/shard_map/ppermute | solution.py:38
  104.2 1.2 %gram_late.1 = (f32[1,3,512,512]{3,2,1,0:T(8,128)S(1)}, f32[16,128]{1,0:T(8,128)S(1)}) custom-call(s32[1]{0:T(128)} %bitcast.1.refs_0_, f32[16,128]{1,0:T(8,128)S(1)} %get-tuple-element.52.refs_4_.refs_1_, f32[3,3,512,512]{3,2,1,0:T(8,128)S(1)} %get-tuple-element.55.refs_2_.refs_5_, bf16[4,8,32,512]{3,2,1,0:T(8,128)(2,1)S(1)} %get-tuple-element.51.refs_1_.refs_3_, ...), custom_call_target="tpu_custom_call" | custom-call | tf_op jit(solution)/shard_map/gram_late/pallas_call | solution.py:186
  105.5 1.5 %collective-permute-start.23 = (f32[16,128]{1,0:T(8,128)S(1)}, f32[16,128]{1,0:T(8,128)S(1)}, u32[]{:S(2)}, u32[]{:S(2)}) collective-permute-start(f32[16,128]{1,0:T(8,128)S(1)} %get-tuple-element.58.refs_8_.refs_1_), channel_id=1, source_target_pairs={{0,3},{1,2},{2,1},{3,0},{4,7},{5,6},{6,5},{7,4},{8,11},{9,10},{10,... | collective-permute-start | bytes 24584 | tf_op jit(solution)/shard_map/ppermute | solution.py:38
  107.0 0.4 collective-permute-start.24
  107.4 1.7 %collective-permute-start.25 = (f32[16,128]{1,0:T(8,128)S(1)}, f32[16,128]{1,0:T(8,128)S(1)}, u32[]{:S(2)}, u32[]{:S(2)}) collective-permute-start(f32[16,128]{1,0:T(8,128)S(1)} %get-tuple-element.58.refs_8_.refs_1_), channel_id=1, source_target_pairs={{0,1},{1,0},{2,3},{3,2},{4,5},{5,4},{6,7},{7,6},{8,9},{9,8},{10,11... | collective-permute-start | bytes 24584 | tf_op jit(solution)/shard_map/ppermute | solution.py:38
  109.0 1.2 %unplace.1 = bf16[1,128,2048]{2,1,0:T(8,128)(2,1)} custom-call(s32[1]{0:T(128)} %bitcast.refs_0_.refs_1_, bf16[144,512]{1,0:T(8,128)(2,1)S(1)} %copy-done.4, bf16[2,32,2048]{2,1,0:T(8,128)(2,1)S(1)} %get-tuple-element.47.refs_0_.refs_2_, bf16[2,32,2048]{2,1,0:T(8,128)(2,1)S(1)} %collective-permute-done.14.refs_1_.refs_3_, ...), custom_call_target="tpu_custom_call" | custom-call | tf_op jit(solution)/shard_map/unplace/pallas_call | solution.py:186
  110.2 0.4 collective-permute-done.24.refs_3_
  110.6 0.4 collective-permute-done.25.refs_4_
  111.0 4.5 %adam.1 = f32[1,3,512,512]{3,2,1,0:T(8,128)} custom-call(s32[1]{0:T(128)} %bitcast.1.refs_0_, f32[16,128]{1,0:T(8,128)S(1)} %get-tuple-element.58.refs_8_.refs_1_, f32[16,128]{1,0:T(8,128)S(1)} %collective-permute-done.23.refs_2_, f32[16,128]{1,0:T(8,128)S(1)} %collective-permute-done.24.refs_3_, f32[16,128]{1,0:T(8,128)S(1)} %collective-permute-done.25.refs_4_, ...), custom_call_target="tpu_custom_call" | custom-call | tf_op jit(solution)/shard_map/adam/pallas_call | solution.py:186
  (16 shorter events, 0.1 us)
Async XLA Ops:
  0.6 14.4 %copy-start = (bf16[1,1,256,2048]{3,2,1,0:T(8,128)(2,1)S(1)}, bf16[1,1,256,2048]{3,2,1,0:T(8,128)(2,1)}, u32[]{:S(2)}) copy-start(bf16[1,1,256,2048]{3,2,1,0:T(8,128)(2,1)} %param.15) | copy-start | bytes 3145732
  3.4 7.5 %collective-permute-start = (bf16[144,512]{1,0:T(8,128)(2,1)}, bf16[144,512]{1,0:T(8,128)(2,1)S(1)}, u32[]{:S(2)}, u32[]{:S(2)}) collective-permute-start(bf16[144,512]{1,0:T(8,128)(2,1)} %get-tuple-element.32), channel_id=1, source_target_pairs={{0,1},{1,0},{2,3},{3,2},{4,5},{5,4},{6,7},{7,6},{8,9},{9,8},{10,11... | collective-permute-start | bytes 442376 | tf_op jit(solution)/shard_map/ppermute | solution.py:38
  6.3 8.7 %collective-permute-start.1 = (bf16[144,512]{1,0:T(8,128)(2,1)}, bf16[144,512]{1,0:T(8,128)(2,1)S(1)}, u32[]{:S(2)}, u32[]{:S(2)}) collective-permute-start(bf16[144,512]{1,0:T(8,128)(2,1)} %get-tuple-element.33), channel_id=1, source_target_pairs={{0,2},{1,3},{2,0},{3,1},{4,6},{5,7},{6,4},{7,5},{8,10},{9,11},{10,... | collective-permute-start | bytes 442376 | tf_op jit(solution)/shard_map/ppermute | solution.py:38
  7.8 7.2 %collective-permute-start.2 = (bf16[144,512]{1,0:T(8,128)(2,1)}, bf16[144,512]{1,0:T(8,128)(2,1)S(1)}, u32[]{:S(2)}, u32[]{:S(2)}) collective-permute-start(bf16[144,512]{1,0:T(8,128)(2,1)} %get-tuple-element.34), channel_id=1, source_target_pairs={{0,3},{1,2},{2,1},{3,0},{4,7},{5,6},{6,5},{7,4},{8,11},{9,10},{10,... | collective-permute-start | bytes 442376 | tf_op jit(solution)/shard_map/ppermute | solution.py:38
  9.1 9.7 %copy-start.4 = (bf16[144,512]{1,0:T(8,128)(2,1)S(1)}, bf16[144,512]{1,0:T(8,128)(2,1)}, u32[]{:S(2)}) copy-start(bf16[144,512]{1,0:T(8,128)(2,1)} %get-tuple-element.31.refs_1_) | copy-start | bytes 442372
  16.8 32.6 %collective-permute-start.3 = (bf16[1408,512]{1,0:T(8,128)(2,1)}, bf16[1408,512]{1,0:T(8,128)(2,1)S(1)}, u32[]{:S(2)}, u32[]{:S(2)}) collective-permute-start(bf16[1408,512]{1,0:T(8,128)(2,1)} %get-tuple-element.35.refs_2_.refs_3_), channel_id=1, source_target_pairs={{0,1},{1,0},{2,3},{3,2},{4,5},{5,4},{6,7},{7,6},{8,9},{9,8},{10,11... | collective-permute-start | bytes 4325384 | tf_op jit(solution)/shard_map/ppermute | solution.py:38
  18.1 32.4 %collective-permute-start.4 = (bf16[1408,512]{1,0:T(8,128)(2,1)}, bf16[1408,512]{1,0:T(8,128)(2,1)S(1)}, u32[]{:S(2)}, u32[]{:S(2)}) collective-permute-start(bf16[1408,512]{1,0:T(8,128)(2,1)} %get-tuple-element.36), channel_id=1, source_target_pairs={{0,2},{1,3},{2,0},{3,1},{4,6},{5,7},{6,4},{7,5},{8,10},{9,11},{10,... | collective-permute-start | bytes 4325384 | tf_op jit(solution)/shard_map/ppermute | solution.py:38
  19.3 10.2 %collective-permute-start.5 = (bf16[2,4,32,512]{3,2,1,0:T(8,128)(2,1)S(1)}, bf16[2,4,32,512]{3,2,1,0:T(8,128)(2,1)S(1)}, u32[]{:S(2)}, u32[]{:S(2)}) collective-permute-start(bf16[2,4,32,512]{3,2,1,0:T(8,128)(2,1)S(1)} %get-tuple-element.38), channel_id=1, source_target_pairs={{0,8},{4,12},{8,0},{12,4},{16,24},{20,28},{24,16},{28,20},{1,9},{5... | collective-permute-start | bytes 786440 | tf_op jit(solution)/shard_map/ppermute | solution.py:44
  21.0 21.0 %collective-permute-start.6 = (bf16[2,4,32,512]{3,2,1,0:T(8,128)(2,1)S(1)}, bf16[2,4,32,512]{3,2,1,0:T(8,128)(2,1)S(1)}, u32[]{:S(2)}, u32[]{:S(2)}) collective-permute-start(bf16[2,4,32,512]{3,2,1,0:T(8,128)(2,1)S(1)} %get-tuple-element.39), channel_id=1, source_target_pairs={{0,16},{4,20},{8,24},{12,28},{16,0},{20,4},{24,8},{28,12},{1,17},{... | collective-permute-start | bytes 786440 | tf_op jit(solution)/shard_map/ppermute | solution.py:44
  23.6 18.4 %collective-permute-start.7 = (bf16[2,4,32,512]{3,2,1,0:T(8,128)(2,1)S(1)}, bf16[2,4,32,512]{3,2,1,0:T(8,128)(2,1)S(1)}, u32[]{:S(2)}, u32[]{:S(2)}) collective-permute-start(bf16[2,4,32,512]{3,2,1,0:T(8,128)(2,1)S(1)} %get-tuple-element.40), channel_id=1, source_target_pairs={{0,24},{4,28},{8,16},{12,20},{16,8},{20,12},{24,0},{28,4},{1,25},{... | collective-permute-start | bytes 786440 | tf_op jit(solution)/shard_map/ppermute | solution.py:44
  42.0 2.0 %collective-permute-start.8 = (bf16[4,4,32,512]{3,2,1,0:T(8,128)(2,1)S(1)}, bf16[4,4,32,512]{3,2,1,0:T(8,128)(2,1)S(1)}, u32[]{:S(2)}, u32[]{:S(2)}) collective-permute-start(bf16[4,4,32,512]{3,2,1,0:T(8,128)(2,1)S(1)} %pick.2), channel_id=1, source_target_pairs={{0,4},{4,0},{8,12},{12,8},{16,20},{20,16},{24,28},{28,24},{1,5},{5... | collective-permute-start | bytes 1572872 | tf_op jit(solution)/shard_map/ppermute | solution.py:68
  50.5 5.8 %copy-start.1 = (bf16[1,1,256,2048]{3,2,1,0:T(8,128)(2,1)S(1)}, bf16[1,1,256,2048]{3,2,1,0:T(8,128)(2,1)}, u32[]{:S(2)}) copy-start(bf16[1,1,256,2048]{3,2,1,0:T(8,128)(2,1)} %param.15) | copy-start | bytes 3145732
  50.5 17.7 %collective-permute-start.9 = (bf16[640,512]{1,0:T(8,128)(2,1)S(1)}, bf16[640,512]{1,0:T(8,128)(2,1)S(1)}, u32[]{:S(2)}, u32[]{:S(2)}) collective-permute-start(bf16[640,512]{1,0:T(8,128)(2,1)S(1)} %get-tuple-element.42), channel_id=1, source_target_pairs={{0,1},{1,0},{2,3},{3,2},{4,5},{5,4},{6,7},{7,6},{8,9},{9,8},{10,11... | collective-permute-start | bytes 1966088 | tf_op jit(solution)/shard_map/ppermute | solution.py:38
  51.3 17.9 %collective-permute-start.10 = (bf16[640,512]{1,0:T(8,128)(2,1)S(1)}, bf16[640,512]{1,0:T(8,128)(2,1)S(1)}, u32[]{:S(2)}, u32[]{:S(2)}) collective-permute-start(bf16[640,512]{1,0:T(8,128)(2,1)S(1)} %get-tuple-element.43), channel_id=1, source_target_pairs={{0,2},{1,3},{2,0},{3,1},{4,6},{5,7},{6,4},{7,5},{8,10},{9,11},{10,... | collective-permute-start | bytes 1966088 | tf_op jit(solution)/shard_map/ppermute | solution.py:38
  52.7 20.7 %collective-permute-start.11 = (bf16[256,512]{1,0:T(8,128)(2,1)S(1)}, bf16[256,512]{1,0:T(8,128)(2,1)S(1)}, u32[]{:S(2)}, u32[]{:S(2)}) collective-permute-start(bf16[256,512]{1,0:T(8,128)(2,1)S(1)} %get-tuple-element.44), channel_id=1, source_target_pairs={{0,1},{1,0},{2,3},{3,2},{4,5},{5,4},{6,7},{7,6},{8,9},{9,8},{10,11... | collective-permute-start | bytes 786440 | tf_op jit(solution)/shard_map/ppermute | solution.py:38
  53.1 23.5 %collective-permute-start.12 = (bf16[256,512]{1,0:T(8,128)(2,1)S(1)}, bf16[256,512]{1,0:T(8,128)(2,1)S(1)}, u32[]{:S(2)}, u32[]{:S(2)}) collective-permute-start(bf16[256,512]{1,0:T(8,128)(2,1)S(1)} %get-tuple-element.45), channel_id=1, source_target_pairs={{0,2},{1,3},{2,0},{3,1},{4,6},{5,7},{6,4},{7,5},{8,10},{9,11},{10,... | collective-permute-start | bytes 786440 | tf_op jit(solution)/shard_map/ppermute | solution.py:38
  54.7 22.0 %collective-permute-start.13 = (bf16[256,512]{1,0:T(8,128)(2,1)S(1)}, bf16[256,512]{1,0:T(8,128)(2,1)S(1)}, u32[]{:S(2)}, u32[]{:S(2)}) collective-permute-start(bf16[256,512]{1,0:T(8,128)(2,1)S(1)} %get-tuple-element.46), channel_id=1, source_target_pairs={{0,3},{1,2},{2,1},{3,0},{4,7},{5,6},{6,5},{7,4},{8,11},{9,10},{10,... | collective-permute-start | bytes 786440 | tf_op jit(solution)/shard_map/ppermute | solution.py:38
  77.0 17.7 %collective-permute-start.17 = (bf16[2,384,512]{2,1,0:T(8,128)(2,1)S(1)}, bf16[2,384,512]{2,1,0:T(8,128)(2,1)S(1)}, u32[]{:S(2)}, u32[]{:S(2)}) collective-permute-start(bf16[2,384,512]{2,1,0:T(8,128)(2,1)S(1)} %factors.1.refs_2_.refs_3_), channel_id=1, source_target_pairs={{0,1},{1,0},{2,3},{3,2},{4,5},{5,4},{6,7},{7,6},{8,9},{9,8},{10,11... | collective-permute-start | bytes 2359304 | tf_op jit(solution)/shard_map/ppermute | solution.py:38
  78.7 16.0 %collective-permute-start.18 = (bf16[2,384,512]{2,1,0:T(8,128)(2,1)S(1)}, bf16[2,384,512]{2,1,0:T(8,128)(2,1)S(1)}, u32[]{:S(2)}, u32[]{:S(2)}) collective-permute-start(bf16[2,384,512]{2,1,0:T(8,128)(2,1)S(1)} %factors.1.refs_2_.refs_3_), channel_id=1, source_target_pairs={{0,2},{1,3},{2,0},{3,1},{4,6},{5,7},{6,4},{7,5},{8,10},{9,11},{10,... | collective-permute-start | bytes 2359304 | tf_op jit(solution)/shard_map/ppermute | solution.py:38
  81.6 17.5 %collective-permute-start.14 = (bf16[2,32,2048]{2,1,0:T(8,128)(2,1)S(1)}, bf16[2,32,2048]{2,1,0:T(8,128)(2,1)S(1)}, u32[]{:S(2)}, u32[]{:S(2)}) collective-permute-start(bf16[2,32,2048]{2,1,0:T(8,128)(2,1)S(1)} %get-tuple-element.48), channel_id=1, source_target_pairs={{0,8},{4,12},{8,0},{12,4},{16,24},{20,28},{24,16},{28,20},{1,9},{5... | collective-permute-start | bytes 786440 | tf_op jit(solution)/shard_map/ppermute | solution.py:44
  84.3 17.7 %collective-permute-start.15 = (bf16[2,32,2048]{2,1,0:T(8,128)(2,1)S(1)}, bf16[2,32,2048]{2,1,0:T(8,128)(2,1)S(1)}, u32[]{:S(2)}, u32[]{:S(2)}) collective-permute-start(bf16[2,32,2048]{2,1,0:T(8,128)(2,1)S(1)} %get-tuple-element.49), channel_id=1, source_target_pairs={{0,16},{4,20},{8,24},{12,28},{16,0},{20,4},{24,8},{28,12},{1,17},{... | collective-permute-start | bytes 786440 | tf_op jit(solution)/shard_map/ppermute | solution.py:44
  86.9 15.1 %collective-permute-start.16 = (bf16[2,32,2048]{2,1,0:T(8,128)(2,1)S(1)}, bf16[2,32,2048]{2,1,0:T(8,128)(2,1)S(1)}, u32[]{:S(2)}, u32[]{:S(2)}) collective-permute-start(bf16[2,32,2048]{2,1,0:T(8,128)(2,1)S(1)} %get-tuple-element.50), channel_id=1, source_target_pairs={{0,24},{4,28},{8,16},{12,20},{16,8},{20,12},{24,0},{28,4},{1,25},{... | collective-permute-start | bytes 786440 | tf_op jit(solution)/shard_map/ppermute | solution.py:44
  94.7 7.9 %collective-permute-start.21 = (bf16[384,512]{1,0:T(8,128)(2,1)S(1)}, bf16[384,512]{1,0:T(8,128)(2,1)S(1)}, u32[]{:S(2)}, u32[]{:S(2)}) collective-permute-start(bf16[384,512]{1,0:T(8,128)(2,1)S(1)} %get-tuple-element.56), channel_id=1, source_target_pairs={{0,1},{1,0},{2,3},{3,2},{4,5},{5,4},{6,7},{7,6},{8,9},{9,8},{10,11... | collective-permute-start | bytes 1179656 | tf_op jit(solution)/shard_map/ppermute | solution.py:38
  96.5 7.8 %collective-permute-start.22 = (bf16[384,512]{1,0:T(8,128)(2,1)S(1)}, bf16[384,512]{1,0:T(8,128)(2,1)S(1)}, u32[]{:S(2)}, u32[]{:S(2)}) collective-permute-start(bf16[384,512]{1,0:T(8,128)(2,1)S(1)} %get-tuple-element.57), channel_id=1, source_target_pairs={{0,2},{1,3},{2,0},{3,1},{4,6},{5,7},{6,4},{7,5},{8,10},{9,11},{10,... | collective-permute-start | bytes 1179656 | tf_op jit(solution)/shard_map/ppermute | solution.py:38
  102.1 7.0 %collective-permute-start.19 = (bf16[2,32,2048]{2,1,0:T(8,128)(2,1)S(1)}, bf16[2,32,2048]{2,1,0:T(8,128)(2,1)S(1)}, u32[]{:S(2)}, u32[]{:S(2)}) collective-permute-start(bf16[2,32,2048]{2,1,0:T(8,128)(2,1)S(1)} %get-tuple-element.53), channel_id=1, source_target_pairs={{0,4},{4,0},{8,12},{12,8},{16,20},{20,16},{24,28},{28,24},{1,5},{5... | collective-permute-start | bytes 786440 | tf_op jit(solution)/shard_map/ppermute | solution.py:68
  102.1 6.9 %collective-permute-start.20 = (bf16[2,32,2048]{2,1,0:T(8,128)(2,1)S(1)}, bf16[2,32,2048]{2,1,0:T(8,128)(2,1)S(1)}, u32[]{:S(2)}, u32[]{:S(2)}) collective-permute-start(bf16[2,32,2048]{2,1,0:T(8,128)(2,1)S(1)} %get-tuple-element.54), channel_id=1, source_target_pairs={{0,4},{4,0},{8,12},{12,8},{16,20},{20,16},{24,28},{28,24},{1,5},{5... | collective-permute-start | bytes 786440 | tf_op jit(solution)/shard_map/ppermute | solution.py:68
  104.2 6.8 %copy-start.2 = (f32[1,3,512,512]{3,2,1,0:T(8,128)S(1)}, f32[1,3,512,512]{3,2,1,0:T(8,128)}, u32[]{:S(2)}) copy-start(f32[1,3,512,512]{3,2,1,0:T(8,128)} %refs_7_.1) | copy-start | bytes 9437188
  104.2 6.8 %copy-start.3 = (f32[1,3,512,512]{3,2,1,0:T(8,128)S(1)}, f32[1,3,512,512]{3,2,1,0:T(8,128)}, u32[]{:S(2)}) copy-start(f32[1,3,512,512]{3,2,1,0:T(8,128)} %refs_8_.1) | copy-start | bytes 9437188
  105.5 4.7 %collective-permute-start.23 = (f32[16,128]{1,0:T(8,128)S(1)}, f32[16,128]{1,0:T(8,128)S(1)}, u32[]{:S(2)}, u32[]{:S(2)}) collective-permute-start(f32[16,128]{1,0:T(8,128)S(1)} %get-tuple-element.58.refs_8_.refs_1_), channel_id=1, source_target_pairs={{0,3},{1,2},{2,1},{3,0},{4,7},{5,6},{6,5},{7,4},{8,11},{9,10},{10,... | collective-permute-start | bytes 24584 | tf_op jit(solution)/shard_map/ppermute | solution.py:38
  107.0 3.7 %collective-permute-start.24 = (f32[16,128]{1,0:T(8,128)S(1)}, f32[16,128]{1,0:T(8,128)S(1)}, u32[]{:S(2)}, u32[]{:S(2)}) collective-permute-start(f32[16,128]{1,0:T(8,128)S(1)} %get-tuple-element.58.refs_8_.refs_1_), channel_id=1, source_target_pairs={{0,2},{1,3},{2,0},{3,1},{4,6},{5,7},{6,4},{7,5},{8,10},{9,11},{10,... | collective-permute-start | bytes 24584 | tf_op jit(solution)/shard_map/ppermute | solution.py:38
  107.4 3.7 %collective-permute-start.25 = (f32[16,128]{1,0:T(8,128)S(1)}, f32[16,128]{1,0:T(8,128)S(1)}, u32[]{:S(2)}, u32[]{:S(2)}) collective-permute-start(f32[16,128]{1,0:T(8,128)S(1)} %get-tuple-element.58.refs_8_.refs_1_), channel_id=1, source_target_pairs={{0,1},{1,0},{2,3},{3,2},{4,5},{5,4},{6,7},{7,6},{8,9},{9,8},{10,11... | collective-permute-start | bytes 24584 | tf_op jit(solution)/shard_map/ppermute | solution.py:38

commit v10 on v9

--- a/solution.py
+++ b/solution.py
@@ -462,7 +462,7 @@
             step_ref[0, 0, rows, columns] = first_new / (root + adam_eps)
         return 0
 
-    lax.fori_loop(0, block_rows // lines, step, 0, unroll=2)
+    lax.fori_loop(0, block_rows // lines, step, 0, unroll=4)
 
 
 def adasum_adam_many(rep, inputs, incoming, factors, first_moment, second_moment):
@@ -593,13 +593,13 @@
         to_one, to_two = call(
             payload_kernel,
             "payload",
-            [rep, pair, inputs_home],
+            [jnp.concatenate([rep, spot]), pair, inputs_home],
             [SMEM, VMEM, VMEM],
             [payload, payload],
             after=routed[1:],
         )
         from_two, from_one = from_peer(to_two, 2), from_peer(to_one, 1)
-        projections = [(to_one,), (from_one,), (from_two,)]
+        projections = [(pair,), (from_one,), (from_two,)]
         inputs = [(inputs_home,), (from_one,), (from_two,)]
     else:
         projections = [(x,) for x in exchange([pair] * rep_count)]

time: 116 us -> 114 us (0.983)
  Pallas kernels: 19.9 us -> 16 us
  waiting for transfers between devices: 61.4 us -> 63.7 us
    pallas_call x16, Pallas kernels: 19.9 us -> 16 us  [call(): pl.pallas_call(body, grid=grid, in_specs=list(specs) + [VMEM] * len(after...]
    ppermute x17, waiting for transfers between devices: 39.4 us -> 43.2 us  [from_peer(): lax.ppermute(array, 'replica', [(i, i ^ offset) for i in range(count)])]
    ppermute x6, waiting for transfers between devices: 21.2 us -> 19.7 us  [across_chips(): lax.ppermute(part, 'expert', [(i, i ^ 2 * k) for i in range(count)])]
  transfers between devices with their start and end apart: 26 -> 26, of which waited for: 16 -> 17; matrix products, arithmetic and copies ran while one was open for 2% -> 2% of each run, Pallas kernels for 10% -> 7%
where the time goes in v10:
time: 114 us
  waiting for transfers between devices  63.7 us (56%)
  starting transfers between devices  30.3 us (27%)
  Pallas kernels  16 us (14%)
  local copies, waits for them, and re-layouts  2.39 us (2%)
  between operations  1.53 us (1%)
    ppermute x17, waiting for transfers between devices, from_peer(): lax.ppermute(array, 'replica', [(i, i ^ offset) for i in range(count)])  43.2 us
    ppermute x17, starting transfers between devices, from_peer(): lax.ppermute(array, 'replica', [(i, i ^ offset) for i in range(count)])  19.9 us
    ppermute x6, waiting for transfers between devices, across_chips(): lax.ppermute(part, 'expert', [(i, i ^ 2 * k) for i in range(count)])  19.7 us
    pallas_call x16, Pallas kernels, call(): pl.pallas_call(body, grid=grid, in_specs=list(specs) + [VMEM] * len(after...  16 us
    ppermute x6, starting transfers between devices, across_chips(): lax.ppermute(part, 'expert', [(i, i ^ 2 * k) for i in range(count)])  9.8 us
  transfers between devices with their start and end apart: 26, of which 17 were waited for; matrix products, arithmetic and copies ran while one was open for 2% of the time, Pallas kernels for 7%

profile of v10, /device:TPU:0, one launch (start us, length us, event | category | flops | bytes accessed | tf_op | source)
XLA Modules:
  0.0 114.0 jit_solution(14757062323781895351)
XLA Ops:
  1.4 2.0 %rows.1 = (bf16[144,512]{1,0:T(8,128)(2,1)}, bf16[144,512]{1,0:T(8,128)(2,1)}, bf16[144,512]{1,0:T(8,128)(2,1)}, bf16[144,512]{1,0:T(8,128)(2,1)}) custom-call(s32[1]{0:T(128)} %bitcast.1.refs_0_, s32[1,1]{1,0:T(1,128)S(6)} %copy.10.refs_1_, f32[8]{0:T(128)} %refs_2_.1, s32[1,128]{1,0:T(1,128)} %bitcast.14, bf16[128,2048]{1,0:T(8,128)(2,1)} %bitcast.13), custom_call_target="tpu_custom_call" | custom-call | tf_op jit(solution)/shard_map/rows/pallas_call | solution.py:186
  3.4 2.9 %collective-permute-start = (bf16[144,512]{1,0:T(8,128)(2,1)}, bf16[144,512]{1,0:T(8,128)(2,1)S(1)}, u32[]{:S(2)}, u32[]{:S(2)}) collective-permute-start(bf16[144,512]{1,0:T(8,128)(2,1)} %get-tuple-element.32), channel_id=1, source_target_pairs={{0,1},{1,0},{2,3},{3,2},{4,5},{5,4},{6,7},{7,6},{8,9},{9,8},{10,11... | collective-permute-start | bytes 442376 | tf_op jit(solution)/shard_map/ppermute | solution.py:38
  6.3 1.5 %collective-permute-start.1 = (bf16[144,512]{1,0:T(8,128)(2,1)}, bf16[144,512]{1,0:T(8,128)(2,1)S(1)}, u32[]{:S(2)}, u32[]{:S(2)}) collective-permute-start(bf16[144,512]{1,0:T(8,128)(2,1)} %get-tuple-element.33), channel_id=1, source_target_pairs={{0,2},{1,3},{2,0},{3,1},{4,6},{5,7},{6,4},{7,5},{8,10},{9,11},{10,... | collective-permute-start | bytes 442376 | tf_op jit(solution)/shard_map/ppermute | solution.py:38
  7.9 0.0 collective-permute-start.2
  7.9 1.3 %slice_bitcast_fusion.refs_1_.refs_2_.refs_3_ = bf16[2,512,512]{2,1,0:T(8,128)(2,1)S(1)} fusion(bf16[1,3,512,512]{3,2,1,0:T(8,128)(2,1)} %param.8), kind=kLoop, calls=%fused_computation | loop fusion | bytes 2097152 | tf_op jit(solution)/shard_map/squeeze | solution.py:589
  9.2 0.0 copy-start.3
  9.2 0.1 pad_add_fusion.refs_0_
  9.3 1.7 %collective-permute-done.refs_3_.refs_2_ = bf16[144,512]{1,0:T(8,128)(2,1)S(1)} collective-permute-done((bf16[144,512]{1,0:T(8,128)(2,1)}, bf16[144,512]{1,0:T(8,128)(2,1)S(1)}, u32[]{:S(2)}, u32[]{:S(2)}) %collective-permute-start) | collective-permute-done | bytes 147488 | tf_op jit(solution)/shard_map/ppermute | solution.py:38
  10.9 4.1 %collective-permute-done.1.refs_4_.refs_3_ = bf16[144,512]{1,0:T(8,128)(2,1)S(1)} collective-permute-done((bf16[144,512]{1,0:T(8,128)(2,1)}, bf16[144,512]{1,0:T(8,128)(2,1)S(1)}, u32[]{:S(2)}, u32[]{:S(2)}) %collective-permute-start.1) | collective-permute-done | bytes 147488 | tf_op jit(solution)/shard_map/ppermute | solution.py:38
  15.0 0.7 payload.1
  15.8 1.3 %collective-permute-start.3 = (bf16[1408,512]{1,0:T(8,128)(2,1)S(1)}, bf16[1408,512]{1,0:T(8,128)(2,1)S(1)}, u32[]{:S(2)}, u32[]{:S(2)}) collective-permute-start(bf16[1408,512]{1,0:T(8,128)(2,1)S(1)} %get-tuple-element.35), channel_id=1, source_target_pairs={{0,1},{1,0},{2,3},{3,2},{4,5},{5,4},{6,7},{7,6},{8,9},{9,8},{10,11... | collective-permute-start | bytes 4325384 | tf_op jit(solution)/shard_map/ppermute | solution.py:38
  17.1 0.8 collective-permute-start.4
  17.9 0.4 place.1
  18.3 1.6 %collective-permute-start.5 = (bf16[2,4,32,512]{3,2,1,0:T(8,128)(2,1)S(1)}, bf16[2,4,32,512]{3,2,1,0:T(8,128)(2,1)S(1)}, u32[]{:S(2)}, u32[]{:S(2)}) collective-permute-start(bf16[2,4,32,512]{3,2,1,0:T(8,128)(2,1)S(1)} %get-tuple-element.38), channel_id=1, source_target_pairs={{0,8},{4,12},{8,0},{12,4},{16,24},{20,28},{24,16},{28,20},{1,9},{5... | collective-permute-start | bytes 786440 | tf_op jit(solution)/shard_map/ppermute | solution.py:44
  20.0 2.6 %collective-permute-start.6 = (bf16[2,4,32,512]{3,2,1,0:T(8,128)(2,1)S(1)}, bf16[2,4,32,512]{3,2,1,0:T(8,128)(2,1)S(1)}, u32[]{:S(2)}, u32[]{:S(2)}) collective-permute-start(bf16[2,4,32,512]{3,2,1,0:T(8,128)(2,1)S(1)} %get-tuple-element.39), channel_id=1, source_target_pairs={{0,16},{4,20},{8,24},{12,28},{16,0},{20,4},{24,8},{28,12},{1,17},{... | collective-permute-start | bytes 786440 | tf_op jit(solution)/shard_map/ppermute | solution.py:44
  22.6 0.2 collective-permute-start.7
  22.8 5.7 %collective-permute-done.5.refs_1_.refs_3_ = bf16[2,4,32,512]{3,2,1,0:T(8,128)(2,1)S(1)} collective-permute-done((bf16[2,4,32,512]{3,2,1,0:T(8,128)(2,1)S(1)}, bf16[2,4,32,512]{3,2,1,0:T(8,128)(2,1)S(1)}, u32[]{:S(2)}, u32[]{:S(2)}) %collective-permute-start.5) | collective-permute-done | bytes 262176 | tf_op jit(solution)/shard_map/ppermute | solution.py:44
  28.5 12.5 %collective-permute-done.6.refs_2_.refs_4_ = bf16[2,4,32,512]{3,2,1,0:T(8,128)(2,1)S(1)} collective-permute-done((bf16[2,4,32,512]{3,2,1,0:T(8,128)(2,1)S(1)}, bf16[2,4,32,512]{3,2,1,0:T(8,128)(2,1)S(1)}, u32[]{:S(2)}, u32[]{:S(2)}) %collective-permute-start.6) | collective-permute-done | bytes 262176 | tf_op jit(solution)/shard_map/ppermute | solution.py:44
  41.0 0.1 collective-permute-start.8
  41.1 1.1 slice_bitcast_fusion.1.refs_1_
  42.2 0.8 collective-permute-done.8.refs_6_
  43.0 0.7 back.1
  43.7 4.5 %collective-permute-done.3.refs_3_.refs_1_.refs_4_ = bf16[1408,512]{1,0:T(8,128)(2,1)S(1)} collective-permute-done((bf16[1408,512]{1,0:T(8,128)(2,1)S(1)}, bf16[1408,512]{1,0:T(8,128)(2,1)S(1)}, u32[]{:S(2)}, u32[]{:S(2)}) %collective-permute-start.3) | collective-permute-done | bytes 1441824 | tf_op jit(solution)/shard_map/ppermute | solution.py:38
  48.2 1.0 collective-permute-done.4.refs_4_.refs_0_.refs_5_.refs_6_
  49.2 0.1 pass.1
  49.3 0.8 collective-permute-start.9
  50.1 1.4 %collective-permute-start.10 = (bf16[640,512]{1,0:T(8,128)(2,1)S(1)}, bf16[640,512]{1,0:T(8,128)(2,1)S(1)}, u32[]{:S(2)}, u32[]{:S(2)}) collective-permute-start(bf16[640,512]{1,0:T(8,128)(2,1)S(1)} %get-tuple-element.43), channel_id=1, source_target_pairs={{0,2},{1,3},{2,0},{3,1},{4,6},{5,7},{6,4},{7,5},{8,10},{9,11},{10,... | collective-permute-start | bytes 1966088 | tf_op jit(solution)/shard_map/ppermute | solution.py:38
  51.5 0.4 collective-permute-start.11
  51.9 1.5 %collective-permute-start.12 = (bf16[256,512]{1,0:T(8,128)(2,1)S(1)}, bf16[256,512]{1,0:T(8,128)(2,1)S(1)}, u32[]{:S(2)}, u32[]{:S(2)}) collective-permute-start(bf16[256,512]{1,0:T(8,128)(2,1)S(1)} %get-tuple-element.45), channel_id=1, source_target_pairs={{0,2},{1,3},{2,0},{3,1},{4,6},{5,7},{6,4},{7,5},{8,10},{9,11},{10,... | collective-permute-start | bytes 786440 | tf_op jit(solution)/shard_map/ppermute | solution.py:38
  53.4 1.5 %collective-permute-start.13 = (bf16[256,512]{1,0:T(8,128)(2,1)S(1)}, bf16[256,512]{1,0:T(8,128)(2,1)S(1)}, u32[]{:S(2)}, u32[]{:S(2)}) collective-permute-start(bf16[256,512]{1,0:T(8,128)(2,1)S(1)} %get-tuple-element.46), channel_id=1, source_target_pairs={{0,3},{1,2},{2,1},{3,0},{4,7},{5,6},{6,5},{7,4},{8,11},{9,10},{10,... | collective-permute-start | bytes 786440 | tf_op jit(solution)/shard_map/ppermute | solution.py:38
  55.0 1.0 forward.1.refs_2_
  56.0 11.1 %collective-permute-done.9.refs_3_.refs_6_.refs_4_ = bf16[640,512]{1,0:T(8,128)(2,1)S(1)} collective-permute-done((bf16[640,512]{1,0:T(8,128)(2,1)S(1)}, bf16[640,512]{1,0:T(8,128)(2,1)S(1)}, u32[]{:S(2)}, u32[]{:S(2)}) %collective-permute-start.9) | collective-permute-done | bytes 655392 | tf_op jit(solution)/shard_map/ppermute | solution.py:38
  67.1 1.0 collective-permute-done.10.refs_4_.refs_7_.refs_5_
  68.0 0.4 rest.1.refs_0_
  68.5 3.7 %collective-permute-done.11.refs_2_ = bf16[256,512]{1,0:T(8,128)(2,1)S(1)} collective-permute-done((bf16[256,512]{1,0:T(8,128)(2,1)S(1)}, bf16[256,512]{1,0:T(8,128)(2,1)S(1)}, u32[]{:S(2)}, u32[]{:S(2)}) %collective-permute-start.11) | collective-permute-done | bytes 262176 | tf_op jit(solution)/shard_map/ppermute | solution.py:38
  72.2 3.2 %collective-permute-done.12.refs_3_ = bf16[256,512]{1,0:T(8,128)(2,1)S(1)} collective-permute-done((bf16[256,512]{1,0:T(8,128)(2,1)S(1)}, bf16[256,512]{1,0:T(8,128)(2,1)S(1)}, u32[]{:S(2)}, u32[]{:S(2)}) %collective-permute-start.12) | collective-permute-done | bytes 262176 | tf_op jit(solution)/shard_map/ppermute | solution.py:38
  75.4 0.0 collective-permute-done.13.refs_4_
  75.4 0.4 factors.1.refs_2_.refs_3_
  75.8 1.7 %collective-permute-start.17 = (bf16[2,384,512]{2,1,0:T(8,128)(2,1)S(1)}, bf16[2,384,512]{2,1,0:T(8,128)(2,1)S(1)}, u32[]{:S(2)}, u32[]{:S(2)}) collective-permute-start(bf16[2,384,512]{2,1,0:T(8,128)(2,1)S(1)} %factors.1.refs_2_.refs_3_), channel_id=1, source_target_pairs={{0,1},{1,0},{2,3},{3,2},{4,5},{5,4},{6,7},{7,6},{8,9},{9,8},{10,11... | collective-permute-start | bytes 2359304 | tf_op jit(solution)/shard_map/ppermute | solution.py:38
  77.5 0.2 collective-permute-start.18
  77.7 1.3 %slots.1 = (bf16[2,32,2048]{2,1,0:T(8,128)(2,1)S(1)}, bf16[2,32,2048]{2,1,0:T(8,128)(2,1)S(1)}, bf16[2,32,2048]{2,1,0:T(8,128)(2,1)S(1)}, bf16[2,32,2048]{2,1,0:T(8,128)(2,1)S(1)}) custom-call(s32[1]{0:T(128)} %bitcast.1.refs_0_, s32[1]{0:T(128)} %bitcast.refs_0_.refs_1_, bf16[2,384,512]{2,1,0:T(8,128)(2,1)S(1)} %factors.1.refs_2_.refs_3_, ...), custom_call_target="tpu_custom_call" | custom-call | tf_op jit(solution)/shard_map/slots/pallas_call | solution.py:186
  79.0 2.5 %collective-permute-start.14 = (bf16[2,32,2048]{2,1,0:T(8,128)(2,1)S(1)}, bf16[2,32,2048]{2,1,0:T(8,128)(2,1)S(1)}, u32[]{:S(2)}, u32[]{:S(2)}) collective-permute-start(bf16[2,32,2048]{2,1,0:T(8,128)(2,1)S(1)} %get-tuple-element.48), channel_id=1, source_target_pairs={{0,8},{4,12},{8,0},{12,4},{16,24},{20,28},{24,16},{28,20},{1,9},{5... | collective-permute-start | bytes 786440 | tf_op jit(solution)/shard_map/ppermute | solution.py:44
  81.5 2.8 %collective-permute-start.15 = (bf16[2,32,2048]{2,1,0:T(8,128)(2,1)S(1)}, bf16[2,32,2048]{2,1,0:T(8,128)(2,1)S(1)}, u32[]{:S(2)}, u32[]{:S(2)}) collective-permute-start(bf16[2,32,2048]{2,1,0:T(8,128)(2,1)S(1)} %get-tuple-element.49), channel_id=1, source_target_pairs={{0,16},{4,20},{8,24},{12,28},{16,0},{20,4},{24,8},{28,12},{1,17},{... | collective-permute-start | bytes 786440 | tf_op jit(solution)/shard_map/ppermute | solution.py:44
  84.4 9.1 %collective-permute-done.17.refs_5_.refs_1_ = bf16[2,384,512]{2,1,0:T(8,128)(2,1)S(1)} collective-permute-done((bf16[2,384,512]{2,1,0:T(8,128)(2,1)S(1)}, bf16[2,384,512]{2,1,0:T(8,128)(2,1)S(1)}, u32[]{:S(2)}, u32[]{:S(2)}) %collective-permute-start.17) | collective-permute-done | bytes 786464 | tf_op jit(solution)/shard_map/ppermute | solution.py:38
  93.5 0.0 collective-permute-done.18.refs_7_.refs_0_
  93.5 0.1 cut.1
  93.5 1.7 %collective-permute-start.21 = (bf16[384,512]{1,0:T(8,128)(2,1)S(1)}, bf16[384,512]{1,0:T(8,128)(2,1)S(1)}, u32[]{:S(2)}, u32[]{:S(2)}) collective-permute-start(bf16[384,512]{1,0:T(8,128)(2,1)S(1)} %get-tuple-element.56), channel_id=1, source_target_pairs={{0,1},{1,0},{2,3},{3,2},{4,5},{5,4},{6,7},{7,6},{8,9},{9,8},{10,11... | collective-permute-start | bytes 1179656 | tf_op jit(solution)/shard_map/ppermute | solution.py:38
  95.3 0.5 collective-permute-start.22
  95.8 2.1 %gram.1 = (f32[3,3,512,512]{3,2,1,0:T(8,128)S(1)}, f32[16,128]{1,0:T(8,128)S(1)}) custom-call(s32[1]{0:T(128)} %bitcast.1.refs_0_, bf16[4,8,32,512]{3,2,1,0:T(8,128)(2,1)S(1)} %get-tuple-element.51.refs_1_.refs_3_, bf16[256,2048]{1,0:T(8,128)(2,1)S(1)} %bitcast.12, bf16[2,384,512]{2,1,0:T(8,128)(2,1)S(1)} %factors.1.refs_2_.refs_3_, ...), custom_call_target="tpu_custom_call" | custom-call | tf_op jit(solution)/shard_map/gram/pallas_call | solution.py:186
  97.9 0.0 collective-permute-done.14.refs_1_.refs_3_
  97.9 1.5 %collective-permute-done.15.refs_2_.refs_4_ = bf16[2,32,2048]{2,1,0:T(8,128)(2,1)S(1)} collective-permute-done((bf16[2,32,2048]{2,1,0:T(8,128)(2,1)S(1)}, bf16[2,32,2048]{2,1,0:T(8,128)(2,1)S(1)}, u32[]{:S(2)}, u32[]{:S(2)}) %collective-permute-start.15) | collective-permute-done | bytes 262176 | tf_op jit(solution)/shard_map/ppermute | solution.py:44
  99.5 0.0 collective-permute-done.16.refs_3_.refs_5_
  99.5 0.1 collective-permute-start.19
  99.6 0.5 collective-permute-start.20
  100.1 1.3 %collective-permute-done.21.refs_6_ = bf16[384,512]{1,0:T(8,128)(2,1)S(1)} collective-permute-done((bf16[384,512]{1,0:T(8,128)(2,1)S(1)}, bf16[384,512]{1,0:T(8,128)(2,1)S(1)}, u32[]{:S(2)}, u32[]{:S(2)}) %collective-permute-start.21) | collective-permute-done | bytes 393248 | tf_op jit(solution)/shard_map/ppermute | solution.py:38
  101.4 1.7 %collective-permute-done.22.refs_7_ = bf16[384,512]{1,0:T(8,128)(2,1)S(1)} collective-permute-done((bf16[384,512]{1,0:T(8,128)(2,1)S(1)}, bf16[384,512]{1,0:T(8,128)(2,1)S(1)}, u32[]{:S(2)}, u32[]{:S(2)}) %collective-permute-start.22) | collective-permute-done | bytes 393248 | tf_op jit(solution)/shard_map/ppermute | solution.py:38
  103.0 1.2 %gram_late.1 = (f32[1,3,512,512]{3,2,1,0:T(8,128)S(1)}, f32[16,128]{1,0:T(8,128)S(1)}) custom-call(s32[1]{0:T(128)} %bitcast.1.refs_0_, f32[16,128]{1,0:T(8,128)S(1)} %get-tuple-element.52.refs_4_.refs_1_, f32[3,3,512,512]{3,2,1,0:T(8,128)S(1)} %get-tuple-element.55.refs_2_.refs_5_, bf16[4,8,32,512]{3,2,1,0:T(8,128)(2,1)S(1)} %get-tuple-element.51.refs_1_.refs_3_, ...), custom_call_target="tpu_custom_call" | custom-call | tf_op jit(solution)/shard_map/gram_late/pallas_call | solution.py:186
  104.3 1.5 %collective-permute-start.23 = (f32[16,128]{1,0:T(8,128)S(1)}, f32[16,128]{1,0:T(8,128)S(1)}, u32[]{:S(2)}, u32[]{:S(2)}) collective-permute-start(f32[16,128]{1,0:T(8,128)S(1)} %get-tuple-element.58.refs_8_.refs_1_), channel_id=1, source_target_pairs={{0,3},{1,2},{2,1},{3,0},{4,7},{5,6},{6,5},{7,4},{8,11},{9,10},{10,... | collective-permute-start | bytes 24584 | tf_op jit(solution)/shard_map/ppermute | solution.py:38
  105.8 0.4 collective-permute-start.24
  106.2 1.7 %collective-permute-start.25 = (f32[16,128]{1,0:T(8,128)S(1)}, f32[16,128]{1,0:T(8,128)S(1)}, u32[]{:S(2)}, u32[]{:S(2)}) collective-permute-start(f32[16,128]{1,0:T(8,128)S(1)} %get-tuple-element.58.refs_8_.refs_1_), channel_id=1, source_target_pairs={{0,1},{1,0},{2,3},{3,2},{4,5},{5,4},{6,7},{7,6},{8,9},{9,8},{10,11... | collective-permute-start | bytes 24584 | tf_op jit(solution)/shard_map/ppermute | solution.py:38
  107.8 1.2 %unplace.1 = bf16[1,128,2048]{2,1,0:T(8,128)(2,1)} custom-call(s32[1]{0:T(128)} %bitcast.refs_0_.refs_1_, bf16[144,512]{1,0:T(8,128)(2,1)S(1)} %copy-done.3, bf16[2,32,2048]{2,1,0:T(8,128)(2,1)S(1)} %get-tuple-element.47.refs_0_.refs_2_, bf16[2,32,2048]{2,1,0:T(8,128)(2,1)S(1)} %collective-permute-done.14.refs_1_.refs_3_, ...), custom_call_target="tpu_custom_call" | custom-call | tf_op jit(solution)/shard_map/unplace/pallas_call | solution.py:186
  109.0 0.4 collective-permute-done.24.refs_3_
  109.4 0.4 collective-permute-done.25.refs_4_
  109.8 4.2 %adam.1 = f32[1,3,512,512]{3,2,1,0:T(8,128)} custom-call(s32[1]{0:T(128)} %bitcast.1.refs_0_, f32[16,128]{1,0:T(8,128)S(1)} %get-tuple-element.58.refs_8_.refs_1_, f32[16,128]{1,0:T(8,128)S(1)} %collective-permute-done.23.refs_2_, f32[16,128]{1,0:T(8,128)S(1)} %collective-permute-done.24.refs_3_, f32[16,128]{1,0:T(8,128)S(1)} %collective-permute-done.25.refs_4_, ...), custom_call_target="tpu_custom_call" | custom-call | tf_op jit(solution)/shard_map/adam/pallas_call | solution.py:186
  (15 shorter events, 0.1 us)
Async XLA Ops:
  0.6 14.4 %copy-start = (bf16[1,1,256,2048]{3,2,1,0:T(8,128)(2,1)S(1)}, bf16[1,1,256,2048]{3,2,1,0:T(8,128)(2,1)}, u32[]{:S(2)}) copy-start(bf16[1,1,256,2048]{3,2,1,0:T(8,128)(2,1)} %param.15) | copy-start | bytes 3145732
  3.4 7.5 %collective-permute-start = (bf16[144,512]{1,0:T(8,128)(2,1)}, bf16[144,512]{1,0:T(8,128)(2,1)S(1)}, u32[]{:S(2)}, u32[]{:S(2)}) collective-permute-start(bf16[144,512]{1,0:T(8,128)(2,1)} %get-tuple-element.32), channel_id=1, source_target_pairs={{0,1},{1,0},{2,3},{3,2},{4,5},{5,4},{6,7},{7,6},{8,9},{9,8},{10,11... | collective-permute-start | bytes 442376 | tf_op jit(solution)/shard_map/ppermute | solution.py:38
  6.3 8.7 %collective-permute-start.1 = (bf16[144,512]{1,0:T(8,128)(2,1)}, bf16[144,512]{1,0:T(8,128)(2,1)S(1)}, u32[]{:S(2)}, u32[]{:S(2)}) collective-permute-start(bf16[144,512]{1,0:T(8,128)(2,1)} %get-tuple-element.33), channel_id=1, source_target_pairs={{0,2},{1,3},{2,0},{3,1},{4,6},{5,7},{6,4},{7,5},{8,10},{9,11},{10,... | collective-permute-start | bytes 442376 | tf_op jit(solution)/shard_map/ppermute | solution.py:38
  7.9 7.2 %collective-permute-start.2 = (bf16[144,512]{1,0:T(8,128)(2,1)}, bf16[144,512]{1,0:T(8,128)(2,1)S(1)}, u32[]{:S(2)}, u32[]{:S(2)}) collective-permute-start(bf16[144,512]{1,0:T(8,128)(2,1)} %get-tuple-element.34), channel_id=1, source_target_pairs={{0,3},{1,2},{2,1},{3,0},{4,7},{5,6},{6,5},{7,4},{8,11},{9,10},{10,... | collective-permute-start | bytes 442376 | tf_op jit(solution)/shard_map/ppermute | solution.py:38
  9.2 8.7 %copy-start.3 = (bf16[144,512]{1,0:T(8,128)(2,1)S(1)}, bf16[144,512]{1,0:T(8,128)(2,1)}, u32[]{:S(2)}) copy-start(bf16[144,512]{1,0:T(8,128)(2,1)} %get-tuple-element.31.refs_1_) | copy-start | bytes 442372
  15.8 32.5 %collective-permute-start.3 = (bf16[1408,512]{1,0:T(8,128)(2,1)S(1)}, bf16[1408,512]{1,0:T(8,128)(2,1)S(1)}, u32[]{:S(2)}, u32[]{:S(2)}) collective-permute-start(bf16[1408,512]{1,0:T(8,128)(2,1)S(1)} %get-tuple-element.35), channel_id=1, source_target_pairs={{0,1},{1,0},{2,3},{3,2},{4,5},{5,4},{6,7},{7,6},{8,9},{9,8},{10,11... | collective-permute-start | bytes 4325384 | tf_op jit(solution)/shard_map/ppermute | solution.py:38
  17.1 32.2 %collective-permute-start.4 = (bf16[1408,512]{1,0:T(8,128)(2,1)S(1)}, bf16[1408,512]{1,0:T(8,128)(2,1)S(1)}, u32[]{:S(2)}, u32[]{:S(2)}) collective-permute-start(bf16[1408,512]{1,0:T(8,128)(2,1)S(1)} %get-tuple-element.36), channel_id=1, source_target_pairs={{0,2},{1,3},{2,0},{3,1},{4,6},{5,7},{6,4},{7,5},{8,10},{9,11},{10,... | collective-permute-start | bytes 4325384 | tf_op jit(solution)/shard_map/ppermute | solution.py:38
  18.3 10.1 %collective-permute-start.5 = (bf16[2,4,32,512]{3,2,1,0:T(8,128)(2,1)S(1)}, bf16[2,4,32,512]{3,2,1,0:T(8,128)(2,1)S(1)}, u32[]{:S(2)}, u32[]{:S(2)}) collective-permute-start(bf16[2,4,32,512]{3,2,1,0:T(8,128)(2,1)S(1)} %get-tuple-element.38), channel_id=1, source_target_pairs={{0,8},{4,12},{8,0},{12,4},{16,24},{20,28},{24,16},{28,20},{1,9},{5... | collective-permute-start | bytes 786440 | tf_op jit(solution)/shard_map/ppermute | solution.py:44
  20.0 21.0 %collective-permute-start.6 = (bf16[2,4,32,512]{3,2,1,0:T(8,128)(2,1)S(1)}, bf16[2,4,32,512]{3,2,1,0:T(8,128)(2,1)S(1)}, u32[]{:S(2)}, u32[]{:S(2)}) collective-permute-start(bf16[2,4,32,512]{3,2,1,0:T(8,128)(2,1)S(1)} %get-tuple-element.39), channel_id=1, source_target_pairs={{0,16},{4,20},{8,24},{12,28},{16,0},{20,4},{24,8},{28,12},{1,17},{... | collective-permute-start | bytes 786440 | tf_op jit(solution)/shard_map/ppermute | solution.py:44
  22.6 18.4 %collective-permute-start.7 = (bf16[2,4,32,512]{3,2,1,0:T(8,128)(2,1)S(1)}, bf16[2,4,32,512]{3,2,1,0:T(8,128)(2,1)S(1)}, u32[]{:S(2)}, u32[]{:S(2)}) collective-permute-start(bf16[2,4,32,512]{3,2,1,0:T(8,128)(2,1)S(1)} %get-tuple-element.40), channel_id=1, source_target_pairs={{0,24},{4,28},{8,16},{12,20},{16,8},{20,12},{24,0},{28,4},{1,25},{... | collective-permute-start | bytes 786440 | tf_op jit(solution)/shard_map/ppermute | solution.py:44
  41.0 2.0 %collective-permute-start.8 = (bf16[4,4,32,512]{3,2,1,0:T(8,128)(2,1)S(1)}, bf16[4,4,32,512]{3,2,1,0:T(8,128)(2,1)S(1)}, u32[]{:S(2)}, u32[]{:S(2)}) collective-permute-start(bf16[4,4,32,512]{3,2,1,0:T(8,128)(2,1)S(1)} %pick.2), channel_id=1, source_target_pairs={{0,4},{4,0},{8,12},{12,8},{16,20},{20,16},{24,28},{28,24},{1,5},{5... | collective-permute-start | bytes 1572872 | tf_op jit(solution)/shard_map/ppermute | solution.py:68
  49.3 17.7 %collective-permute-start.9 = (bf16[640,512]{1,0:T(8,128)(2,1)S(1)}, bf16[640,512]{1,0:T(8,128)(2,1)S(1)}, u32[]{:S(2)}, u32[]{:S(2)}) collective-permute-start(bf16[640,512]{1,0:T(8,128)(2,1)S(1)} %get-tuple-element.42), channel_id=1, source_target_pairs={{0,1},{1,0},{2,3},{3,2},{4,5},{5,4},{6,7},{7,6},{8,9},{9,8},{10,11... | collective-permute-start | bytes 1966088 | tf_op jit(solution)/shard_map/ppermute | solution.py:38
  50.1 17.9 %collective-permute-start.10 = (bf16[640,512]{1,0:T(8,128)(2,1)S(1)}, bf16[640,512]{1,0:T(8,128)(2,1)S(1)}, u32[]{:S(2)}, u32[]{:S(2)}) collective-permute-start(bf16[640,512]{1,0:T(8,128)(2,1)S(1)} %get-tuple-element.43), channel_id=1, source_target_pairs={{0,2},{1,3},{2,0},{3,1},{4,6},{5,7},{6,4},{7,5},{8,10},{9,11},{10,... | collective-permute-start | bytes 1966088 | tf_op jit(solution)/shard_map/ppermute | solution.py:38
  51.5 20.7 %collective-permute-start.11 = (bf16[256,512]{1,0:T(8,128)(2,1)S(1)}, bf16[256,512]{1,0:T(8,128)(2,1)S(1)}, u32[]{:S(2)}, u32[]{:S(2)}) collective-permute-start(bf16[256,512]{1,0:T(8,128)(2,1)S(1)} %get-tuple-element.44), channel_id=1, source_target_pairs={{0,1},{1,0},{2,3},{3,2},{4,5},{5,4},{6,7},{7,6},{8,9},{9,8},{10,11... | collective-permute-start | bytes 786440 | tf_op jit(solution)/shard_map/ppermute | solution.py:38
  51.9 23.5 %collective-permute-start.12 = (bf16[256,512]{1,0:T(8,128)(2,1)S(1)}, bf16[256,512]{1,0:T(8,128)(2,1)S(1)}, u32[]{:S(2)}, u32[]{:S(2)}) collective-permute-start(bf16[256,512]{1,0:T(8,128)(2,1)S(1)} %get-tuple-element.45), channel_id=1, source_target_pairs={{0,2},{1,3},{2,0},{3,1},{4,6},{5,7},{6,4},{7,5},{8,10},{9,11},{10,... | collective-permute-start | bytes 786440 | tf_op jit(solution)/shard_map/ppermute | solution.py:38
  53.4 22.0 %collective-permute-start.13 = (bf16[256,512]{1,0:T(8,128)(2,1)S(1)}, bf16[256,512]{1,0:T(8,128)(2,1)S(1)}, u32[]{:S(2)}, u32[]{:S(2)}) collective-permute-start(bf16[256,512]{1,0:T(8,128)(2,1)S(1)} %get-tuple-element.46), channel_id=1, source_target_pairs={{0,3},{1,2},{2,1},{3,0},{4,7},{5,6},{6,5},{7,4},{8,11},{9,10},{10,... | collective-permute-start | bytes 786440 | tf_op jit(solution)/shard_map/ppermute | solution.py:38
  75.8 17.6 %collective-permute-start.17 = (bf16[2,384,512]{2,1,0:T(8,128)(2,1)S(1)}, bf16[2,384,512]{2,1,0:T(8,128)(2,1)S(1)}, u32[]{:S(2)}, u32[]{:S(2)}) collective-permute-start(bf16[2,384,512]{2,1,0:T(8,128)(2,1)S(1)} %factors.1.refs_2_.refs_3_), channel_id=1, source_target_pairs={{0,1},{1,0},{2,3},{3,2},{4,5},{5,4},{6,7},{7,6},{8,9},{9,8},{10,11... | collective-permute-start | bytes 2359304 | tf_op jit(solution)/shard_map/ppermute | solution.py:38
  77.5 16.0 %collective-permute-start.18 = (bf16[2,384,512]{2,1,0:T(8,128)(2,1)S(1)}, bf16[2,384,512]{2,1,0:T(8,128)(2,1)S(1)}, u32[]{:S(2)}, u32[]{:S(2)}) collective-permute-start(bf16[2,384,512]{2,1,0:T(8,128)(2,1)S(1)} %factors.1.refs_2_.refs_3_), channel_id=1, source_target_pairs={{0,2},{1,3},{2,0},{3,1},{4,6},{5,7},{6,4},{7,5},{8,10},{9,11},{10,... | collective-permute-start | bytes 2359304 | tf_op jit(solution)/shard_map/ppermute | solution.py:38
  79.0 18.9 %collective-permute-start.14 = (bf16[2,32,2048]{2,1,0:T(8,128)(2,1)S(1)}, bf16[2,32,2048]{2,1,0:T(8,128)(2,1)S(1)}, u32[]{:S(2)}, u32[]{:S(2)}) collective-permute-start(bf16[2,32,2048]{2,1,0:T(8,128)(2,1)S(1)} %get-tuple-element.48), channel_id=1, source_target_pairs={{0,8},{4,12},{8,0},{12,4},{16,24},{20,28},{24,16},{28,20},{1,9},{5... | collective-permute-start | bytes 786440 | tf_op jit(solution)/shard_map/ppermute | solution.py:44
  81.5 17.9 %collective-permute-start.15 = (bf16[2,32,2048]{2,1,0:T(8,128)(2,1)S(1)}, bf16[2,32,2048]{2,1,0:T(8,128)(2,1)S(1)}, u32[]{:S(2)}, u32[]{:S(2)}) collective-permute-start(bf16[2,32,2048]{2,1,0:T(8,128)(2,1)S(1)} %get-tuple-element.49), channel_id=1, source_target_pairs={{0,16},{4,20},{8,24},{12,28},{16,0},{20,4},{24,8},{28,12},{1,17},{... | collective-permute-start | bytes 786440 | tf_op jit(solution)/shard_map/ppermute | solution.py:44
  84.4 15.1 %collective-permute-start.16 = (bf16[2,32,2048]{2,1,0:T(8,128)(2,1)S(1)}, bf16[2,32,2048]{2,1,0:T(8,128)(2,1)S(1)}, u32[]{:S(2)}, u32[]{:S(2)}) collective-permute-start(bf16[2,32,2048]{2,1,0:T(8,128)(2,1)S(1)} %get-tuple-element.50), channel_id=1, source_target_pairs={{0,24},{4,28},{8,16},{12,20},{16,8},{20,12},{24,0},{28,4},{1,25},{... | collective-permute-start | bytes 786440 | tf_op jit(solution)/shard_map/ppermute | solution.py:44
  93.5 7.8 %collective-permute-start.21 = (bf16[384,512]{1,0:T(8,128)(2,1)S(1)}, bf16[384,512]{1,0:T(8,128)(2,1)S(1)}, u32[]{:S(2)}, u32[]{:S(2)}) collective-permute-start(bf16[384,512]{1,0:T(8,128)(2,1)S(1)} %get-tuple-element.56), channel_id=1, source_target_pairs={{0,1},{1,0},{2,3},{3,2},{4,5},{5,4},{6,7},{7,6},{8,9},{9,8},{10,11... | collective-permute-start | bytes 1179656 | tf_op jit(solution)/shard_map/ppermute | solution.py:38
  95.3 7.8 %collective-permute-start.22 = (bf16[384,512]{1,0:T(8,128)(2,1)S(1)}, bf16[384,512]{1,0:T(8,128)(2,1)S(1)}, u32[]{:S(2)}, u32[]{:S(2)}) collective-permute-start(bf16[384,512]{1,0:T(8,128)(2,1)S(1)} %get-tuple-element.57), channel_id=1, source_target_pairs={{0,2},{1,3},{2,0},{3,1},{4,6},{5,7},{6,4},{7,5},{8,10},{9,11},{10,... | collective-permute-start | bytes 1179656 | tf_op jit(solution)/shard_map/ppermute | solution.py:38
  99.5 8.3 %collective-permute-start.19 = (bf16[2,32,2048]{2,1,0:T(8,128)(2,1)S(1)}, bf16[2,32,2048]{2,1,0:T(8,128)(2,1)S(1)}, u32[]{:S(2)}, u32[]{:S(2)}) collective-permute-start(bf16[2,32,2048]{2,1,0:T(8,128)(2,1)S(1)} %get-tuple-element.53), channel_id=1, source_target_pairs={{0,4},{4,0},{8,12},{12,8},{16,20},{20,16},{24,28},{28,24},{1,5},{5... | collective-permute-start | bytes 786440 | tf_op jit(solution)/shard_map/ppermute | solution.py:68
  99.6 8.2 %collective-permute-start.20 = (bf16[2,32,2048]{2,1,0:T(8,128)(2,1)S(1)}, bf16[2,32,2048]{2,1,0:T(8,128)(2,1)S(1)}, u32[]{:S(2)}, u32[]{:S(2)}) collective-permute-start(bf16[2,32,2048]{2,1,0:T(8,128)(2,1)S(1)} %get-tuple-element.54), channel_id=1, source_target_pairs={{0,4},{4,0},{8,12},{12,8},{16,20},{20,16},{24,28},{28,24},{1,5},{5... | collective-permute-start | bytes 786440 | tf_op jit(solution)/shard_map/ppermute | solution.py:68
  103.0 6.8 %copy-start.1 = (f32[1,3,512,512]{3,2,1,0:T(8,128)S(1)}, f32[1,3,512,512]{3,2,1,0:T(8,128)}, u32[]{:S(2)}) copy-start(f32[1,3,512,512]{3,2,1,0:T(8,128)} %refs_7_.1) | copy-start | bytes 9437188
  103.0 6.8 %copy-start.2 = (f32[1,3,512,512]{3,2,1,0:T(8,128)S(1)}, f32[1,3,512,512]{3,2,1,0:T(8,128)}, u32[]{:S(2)}) copy-start(f32[1,3,512,512]{3,2,1,0:T(8,128)} %refs_8_.1) | copy-start | bytes 9437188
  104.3 4.7 %collective-permute-start.23 = (f32[16,128]{1,0:T(8,128)S(1)}, f32[16,128]{1,0:T(8,128)S(1)}, u32[]{:S(2)}, u32[]{:S(2)}) collective-permute-start(f32[16,128]{1,0:T(8,128)S(1)} %get-tuple-element.58.refs_8_.refs_1_), channel_id=1, source_target_pairs={{0,3},{1,2},{2,1},{3,0},{4,7},{5,6},{6,5},{7,4},{8,11},{9,10},{10,... | collective-permute-start | bytes 24584 | tf_op jit(solution)/shard_map/ppermute | solution.py:38
  105.8 3.7 %collective-permute-start.24 = (f32[16,128]{1,0:T(8,128)S(1)}, f32[16,128]{1,0:T(8,128)S(1)}, u32[]{:S(2)}, u32[]{:S(2)}) collective-permute-start(f32[16,128]{1,0:T(8,128)S(1)} %get-tuple-element.58.refs_8_.refs_1_), channel_id=1, source_target_pairs={{0,2},{1,3},{2,0},{3,1},{4,6},{5,7},{6,4},{7,5},{8,10},{9,11},{10,... | collective-permute-start | bytes 24584 | tf_op jit(solution)/shard_map/ppermute | solution.py:38
  106.2 3.7 %collective-permute-start.25 = (f32[16,128]{1,0:T(8,128)S(1)}, f32[16,128]{1,0:T(8,128)S(1)}, u32[]{:S(2)}, u32[]{:S(2)}) collective-permute-start(f32[16,128]{1,0:T(8,128)S(1)} %get-tuple-element.58.refs_8_.refs_1_), channel_id=1, source_target_pairs={{0,1},{1,0},{2,3},{3,2},{4,5},{5,4},{6,7},{7,6},{8,9},{9,8},{10,11... | collective-permute-start | bytes 24584 | tf_op jit(solution)/shard_map/ppermute | solution.py:38

commit v11 on v10

--- a/solution.py
+++ b/solution.py
@@ -100,26 +100,37 @@
         ]
 
 
-def pass_kernel(from_two_ref, from_one_ref, *out_refs):
-    for part, (near_ref, out_ref) in enumerate(zip((from_two_ref, from_one_ref), out_refs)):
-        seg_rows = near_ref.shape[1]
-        half = out_ref.shape[0] - seg_rows
-        out_ref[pl.ds(0, seg_rows), :] = near_ref[pl.ds(part * seg_rows, seg_rows), :]
-        out_ref[pl.ds(seg_rows, half), :] = near_ref[pl.ds(near_ref.shape[0] - half, half), :]
+def pass_kernel(from_two_ref, from_one_ref, first_ref, second_ref):
+    seg_rows = first_ref.shape[1]
+    half = (first_ref.shape[0] + second_ref.shape[0]) // 2 - seg_rows
+    split = first_ref.shape[0] - half
+    tail = pl.ds(from_one_ref.shape[0] - half, half)
+    first_ref[pl.ds(0, split), :] = from_two_ref[pl.ds(0, split), :]
+    first_ref[pl.ds(split, half), :] = from_two_ref[tail, :]
+    rest = 2 * seg_rows - split
+    second_ref[pl.ds(0, rest), :] = from_one_ref[pl.ds(split, rest), :]
+    second_ref[pl.ds(rest, half), :] = from_one_ref[tail, :]
 
 
 def projection_rows(refs):
+    seg_rows = refs[0].shape[-1]
     if len(refs) == 1 and len(refs[0].shape) == 3:
-        return refs[0].at[0], refs[0].at[1]
-    seg_rows = refs[0].shape[1]
-    start = 0 if len(refs) == 2 else seg_rows
-    return refs[0].at[pl.ds(0, seg_rows)], refs[-1].at[pl.ds(start, seg_rows)]
+        return refs[0][0], refs[0][1]
+    if len(refs) == 1:
+        return refs[0][pl.ds(0, seg_rows), :], refs[0][pl.ds(seg_rows, seg_rows), :]
+    first_ref, second_ref = refs
+    half = (first_ref.shape[0] + second_ref.shape[0]) // 2 - seg_rows
+    split = first_ref.shape[0] - half
+    rest = seg_rows - split
+    gate = jnp.concatenate([first_ref[pl.ds(0, split), :], second_ref[pl.ds(0, rest), :]], axis=0)
+    return gate, second_ref[pl.ds(rest, seg_rows), :]
 
 
 def input_rows(rep_ref, refs, slot_count, seg_rows):
     if len(refs) == 2:
-        rows = pl.ds(seg_rows, slot_count // 2)
-        return jnp.concatenate([refs[1][rows], refs[0][rows]], axis=0)
+        half = slot_count // 2
+        tails = [ref[pl.ds(ref.shape[0] - half, half), :] for ref in (refs[1], refs[0])]
+        return jnp.concatenate(tails, axis=0)
     (ref,) = refs
     if ref.shape[0] > slot_count:
         return ref[pl.ds(2 * seg_rows, slot_count), :]
@@ -127,8 +138,9 @@
 
 
 def cut_kernel(from_two_ref, from_one_ref, first_ref, second_ref):
-    first_ref[...] = from_two_ref[0]
-    second_ref[...] = from_one_ref[1]
+    rows = first_ref.shape[0]
+    first_ref[...] = from_two_ref[pl.ds(0, rows), :]
+    second_ref[...] = from_one_ref[pl.ds(rows, second_ref.shape[0]), :]
 
 
 def gather_near(payload):
@@ -143,15 +155,22 @@
     whole = [(part,) for part in near]
     if lax.axis_size("replica") != 4:
         return whole
-    half = jax.ShapeDtypeStruct(near[0].shape[1:], near[0].dtype)
+    rows, width = near[0].shape
+    split = rows * 5 // 12 // 16 * 16
+    parts = [
+        jax.ShapeDtypeStruct((count, width), near[0].dtype) for count in (split, rows - split)
+    ]
     first, second = call(
-        cut_kernel, "cut", [near[2], near[1]], [VMEM, VMEM], [half, half], after=after
+        cut_kernel, "cut", [near[2], near[1]], [VMEM, VMEM], parts, after=after
     )
     return whole + [(from_peer(first, 1), from_peer(second, 2))]
 
 
-def halves(refs):
-    return refs if len(refs) == 2 else (refs[0].at[0], refs[0].at[1])
+def factor_rows(refs, slot_count):
+    if len(refs) == 1:
+        return [refs[0].at[pl.ds(place * slot_count, slot_count)] for place in range(3)]
+    payload = jnp.concatenate([ref[...] for ref in refs], axis=0)
+    return [payload[place * slot_count : (place + 1) * slot_count] for place in range(3)]
 
 
 def regroup(refs, lengths):
@@ -294,9 +313,9 @@
         gate, up = weight_refs[0][0], weight_refs[0][1]
         weight_refs = weight_refs[1:]
     for offset, group in zip(offsets, regroup(weight_refs, lengths)):
-        gate_ref, up_ref = projection_rows(group)
-        rows = inputs_ref[:, segment(rep_ref, offset, gate_ref.shape[0])]
-        gate_part, up_part = multiply(rows, gate_ref[...]), multiply(rows, up_ref[...])
+        gate_rows, up_rows = projection_rows(group)
+        rows = inputs_ref[:, segment(rep_ref, offset, gate_rows.shape[0])]
+        gate_part, up_part = multiply(rows, gate_rows), multiply(rows, up_rows)
         gate = gate_part if gate is None else gate + gate_part
         up = up_part if up is None else up + up_part
     out_ref[0] = gate
@@ -306,30 +325,28 @@
 def factor_kernel(forward_ref, *refs):
     back_refs, out_ref = refs[:-1], refs[-1]
     slot_count = forward_ref.shape[1]
-    half = slot_count // 2
     hidden_grad = back_refs[0][...]
     for back_ref in back_refs[1:]:
         hidden_grad = hidden_grad + back_ref[...].astype(jnp.float32)
     gate_pre, up_pre = forward_ref[0], forward_ref[1]
     sigmoid_gate = jax.nn.sigmoid(gate_pre)
     gate_act = gate_pre * sigmoid_gate
-    hidden = (gate_act * up_pre).astype(jnp.bfloat16)
     gate_grad = hidden_grad * up_pre * sigmoid_gate * (1.0 + gate_pre * (1.0 - sigmoid_gate))
-    out_ref[0, pl.ds(0, slot_count)] = gate_grad.astype(jnp.bfloat16)
-    out_ref[1, pl.ds(0, slot_count)] = (hidden_grad * gate_act).astype(jnp.bfloat16)
-    for part in range(2):
-        out_ref[part, pl.ds(slot_count, half)] = hidden[part * half : (part + 1) * half]
+    parts = (gate_grad, hidden_grad * gate_act, gate_act * up_pre)
+    for place, part in enumerate(parts):
+        out_ref[pl.ds(place * slot_count, slot_count), :] = part.astype(jnp.bfloat16)
 
 
 def slot_kernel(lengths, rep_ref, spot_ref, factor_ref, *refs):
     chips = refs[-1].shape[1] // 2
     weight_refs, out_refs, slots_ref = refs[: -chips - 1], refs[-chips - 1 : -1], refs[-1]
     _, expert_count, capacity, seg_rows = slots_ref.shape
-    rows = pl.ds(0, expert_count * capacity)
-    gate_grad, up_grad = factor_ref[0, rows], factor_ref[1, rows]
+    slot_count = expert_count * capacity
+    gate_grad = factor_ref[pl.ds(0, slot_count), :]
+    up_grad = factor_ref[pl.ds(slot_count, slot_count), :]
     for offset, group in enumerate(regroup(weight_refs, lengths)):
-        gate_ref, up_ref = projection_rows(group)
-        total = contract_last(gate_grad, gate_ref[...]) + contract_last(up_grad, up_ref[...])
+        gate_rows, up_rows = projection_rows(group)
+        total = contract_last(gate_grad, gate_rows) + contract_last(up_grad, up_rows)
         total = total.reshape(expert_count, capacity, seg_rows)
         slots_ref[offset] = total.astype(jnp.bfloat16)
         columns = segment(rep_ref, offset, seg_rows)
@@ -342,7 +359,6 @@
     if place:
         before_ref, earlier_ref, refs = refs[0], refs[1], refs[2:]
     incoming_ref, operand_refs, grads_ref, gram_ref = refs[0], refs[1:-2], refs[-2], refs[-1]
-    middle = incoming_ref.shape[1] // 2
     seg_rows, hidden_width = grads_ref.shape[2:]
     slot_count = incoming_ref.shape[1] * incoming_ref.shape[2]
     groups = regroup(operand_refs, lengths)
@@ -354,28 +370,17 @@
     operands = []
     for at, offset in enumerate(offsets):
         input_refs, factor_refs = groups[2 * at : 2 * at + 2]
-        rest = pl.ds(slot_count, slot_count // 2)
         columns = input_rows(rep_ref, input_refs, slot_count, seg_rows)
-        gate_ref, up_ref = (ref.at[pl.ds(0, slot_count)] for ref in halves(factor_refs))
-        first_ref, second_ref = (ref.at[rest] for ref in halves(factor_refs))
-        upper = flat_rows(incoming_ref[offset, :middle])
-        lower = flat_rows(incoming_ref[offset, middle:])
-        operands.append(
-            [
-                [(columns, gate_ref)],
-                [(columns, up_ref)],
-                [(upper, first_ref), (lower, second_ref)],
-            ]
-        )
+        gate_ref, up_ref, hidden_ref = factor_rows(factor_refs, slot_count)
+        received = flat_rows(incoming_ref[offset])
+        operands.append([(columns, gate_ref), (columns, up_ref), (received, hidden_ref)])
     for matrix in range(3):
         for start in range(0, seg_rows, tile):
             rows = pl.ds(start, tile)
             blocks = [earlier_ref[at, matrix, rows] for at in range(place)]
             for at in range(len(offsets)):
-                block = None
-                for left, right_ref in operands[at][matrix]:
-                    part = contract_first(left[:, start : start + tile], right_ref[...])
-                    block = part if block is None else block + part
+                left, right_ref = operands[at][matrix]
+                block = contract_first(left[:, start : start + tile], right_ref[...])
                 grads_ref[at, matrix, rows] = block
                 blocks.append(block)
             for place_of, (i, j) in enumerate(pairs):
@@ -471,8 +476,7 @@
     grads = []
     for offset in range(count):
         (payload,) = factors[offset]
-        gate_grad, up_grad = payload[:, : 2 * half]
-        hidden = payload[:, 2 * half :].reshape(2 * half, -1)
+        gate_grad, up_grad, hidden = payload.reshape(3, 2 * half, -1)
         received = incoming[offset].reshape(2 * half, incoming.shape[3])
         grads.append(
             jnp.stack(
@@ -508,7 +512,7 @@
 
 def adasum(rep, inputs, incoming, factors):
     count = len(inputs)
-    seg_rows, hidden_width = incoming.shape[3], factors[0][0].shape[2]
+    seg_rows, hidden_width = incoming.shape[3], factors[0][0].shape[-1]
     shape = jax.ShapeDtypeStruct
     groups = [[k for k in range(count) if k < 3], [k for k in range(count) if k == 3]]
     groups = [group for group in groups if group]
@@ -637,13 +641,16 @@
     own_back = back[:1]
     back = exchange(back)
     if packed:
-        passed = shape((seg_rows + half, seg_rows), jnp.bfloat16)
+        split = seg_rows * 3 // 4
+        passed = [
+            shape((count + half, seg_rows), jnp.bfloat16) for count in (split, 2 * seg_rows - split)
+        ]
         first, second = call(
             pass_kernel,
             "pass",
             [from_two, from_one],
             [VMEM, VMEM],
-            [passed, passed],
+            passed,
             after=own_back,
         )
         last = (from_peer(first, 1), from_peer(second, 2))
@@ -672,7 +679,7 @@
         "factors",
         [forward, *back],
         [VMEM] * (1 + len(back)),
-        [shape((2, slot_count + half, hidden_width), jnp.bfloat16)],
+        [shape((3 * slot_count, hidden_width), jnp.bfloat16)],
     )
     near_factors = gather_near(own_factors)
 

time: 114 us -> 117 us (1.026)
  waiting for transfers between devices: 63.7 us -> 68.4 us
    ppermute x17, waiting for transfers between devices: 43.2 us -> 48.2 us  [from_peer(): lax.ppermute(array, 'replica', [(i, i ^ offset) for i in range(count)])]
where the time goes in v11:
time: 117 us
  waiting for transfers between devices  68.4 us (58%)
  starting transfers between devices  29.2 us (25%)
  Pallas kernels  15.6 us (13%)
  local copies, waits for them, and re-layouts  2.39 us (2%)
  between operations  1.54 us (1%)
    ppermute x17, waiting for transfers between devices, from_peer(): lax.ppermute(array, 'replica', [(i, i ^ offset) for i in range(count)])  48.2 us
    ppermute x17, starting transfers between devices, from_peer(): lax.ppermute(array, 'replica', [(i, i ^ offset) for i in range(count)])  19.6 us
    ppermute x6, waiting for transfers between devices, across_chips(): lax.ppermute(part, 'expert', [(i, i ^ 2 * k) for i in range(count)])  19.3 us
    pallas_call x16, Pallas kernels, call(): pl.pallas_call(body, grid=grid, in_specs=list(specs) + [VMEM] * len(after...  15.6 us
    ppermute x6, starting transfers between devices, across_chips(): lax.ppermute(part, 'expert', [(i, i ^ 2 * k) for i in range(count)])  8.9 us
  transfers between devices with their start and end apart: 26, of which 17 were waited for; matrix products, arithmetic and copies ran while one was open for 2% of the time, Pallas kernels for 7%

profile of v11, /device:TPU:0, one launch (start us, length us, event | category | flops | bytes accessed | tf_op | source)
XLA Modules:
  0.0 117.1 jit_solution(6289301870920906612)
XLA Ops:
  1.4 2.0 %rows.1 = (bf16[144,512]{1,0:T(8,128)(2,1)}, bf16[144,512]{1,0:T(8,128)(2,1)}, bf16[144,512]{1,0:T(8,128)(2,1)}, bf16[144,512]{1,0:T(8,128)(2,1)}) custom-call(s32[1]{0:T(128)} %bitcast.1.refs_0_, s32[1,1]{1,0:T(1,128)S(6)} %copy.10.refs_1_, f32[8]{0:T(128)} %refs_2_.1, s32[1,128]{1,0:T(1,128)} %bitcast.14, bf16[128,2048]{1,0:T(8,128)(2,1)} %bitcast.13), custom_call_target="tpu_custom_call" | custom-call | tf_op jit(solution)/shard_map/rows/pallas_call | solution.py:205
  3.4 2.9 %collective-permute-start = (bf16[144,512]{1,0:T(8,128)(2,1)}, bf16[144,512]{1,0:T(8,128)(2,1)S(1)}, u32[]{:S(2)}, u32[]{:S(2)}) collective-permute-start(bf16[144,512]{1,0:T(8,128)(2,1)} %get-tuple-element.32), channel_id=1, source_target_pairs={{0,1},{1,0},{2,3},{3,2},{4,5},{5,4},{6,7},{7,6},{8,9},{9,8},{10,11... | collective-permute-start | bytes 442376 | tf_op jit(solution)/shard_map/ppermute | solution.py:38
  6.3 1.5 %collective-permute-start.1 = (bf16[144,512]{1,0:T(8,128)(2,1)}, bf16[144,512]{1,0:T(8,128)(2,1)S(1)}, u32[]{:S(2)}, u32[]{:S(2)}) collective-permute-start(bf16[144,512]{1,0:T(8,128)(2,1)} %get-tuple-element.33), channel_id=1, source_target_pairs={{0,2},{1,3},{2,0},{3,1},{4,6},{5,7},{6,4},{7,5},{8,10},{9,11},{10,... | collective-permute-start | bytes 442376 | tf_op jit(solution)/shard_map/ppermute | solution.py:38
  7.9 1.3 %slice_bitcast_fusion.refs_1_.refs_2_.refs_3_ = bf16[2,512,512]{2,1,0:T(8,128)(2,1)S(1)} fusion(bf16[1,3,512,512]{3,2,1,0:T(8,128)(2,1)} %param.8), kind=kLoop, calls=%fused_computation | loop fusion | bytes 2097152 | tf_op jit(solution)/shard_map/squeeze | solution.py:593
  9.2 0.0 copy-start.3
  9.2 0.1 pad_add_fusion.refs_0_
  9.3 1.7 %collective-permute-done.refs_3_.refs_2_ = bf16[144,512]{1,0:T(8,128)(2,1)S(1)} collective-permute-done((bf16[144,512]{1,0:T(8,128)(2,1)}, bf16[144,512]{1,0:T(8,128)(2,1)S(1)}, u32[]{:S(2)}, u32[]{:S(2)}) %collective-permute-start) | collective-permute-done | bytes 147488 | tf_op jit(solution)/shard_map/ppermute | solution.py:38
  10.9 4.1 %collective-permute-done.1.refs_4_.refs_3_ = bf16[144,512]{1,0:T(8,128)(2,1)S(1)} collective-permute-done((bf16[144,512]{1,0:T(8,128)(2,1)}, bf16[144,512]{1,0:T(8,128)(2,1)S(1)}, u32[]{:S(2)}, u32[]{:S(2)}) %collective-permute-start.1) | collective-permute-done | bytes 147488 | tf_op jit(solution)/shard_map/ppermute | solution.py:38
  15.0 0.0 collective-permute-done.2.refs_5_.refs_4_
  15.0 0.7 payload.1
  15.8 1.3 %collective-permute-start.3 = (bf16[1408,512]{1,0:T(8,128)(2,1)S(1)}, bf16[1408,512]{1,0:T(8,128)(2,1)S(1)}, u32[]{:S(2)}, u32[]{:S(2)}) collective-permute-start(bf16[1408,512]{1,0:T(8,128)(2,1)S(1)} %get-tuple-element.35), channel_id=1, source_target_pairs={{0,1},{1,0},{2,3},{3,2},{4,5},{5,4},{6,7},{7,6},{8,9},{9,8},{10,11... | collective-permute-start | bytes 4325384 | tf_op jit(solution)/shard_map/ppermute | solution.py:38
  17.1 0.8 collective-permute-start.4
  17.9 0.4 place.1
  18.3 1.6 %collective-permute-start.5 = (bf16[2,4,32,512]{3,2,1,0:T(8,128)(2,1)S(1)}, bf16[2,4,32,512]{3,2,1,0:T(8,128)(2,1)S(1)}, u32[]{:S(2)}, u32[]{:S(2)}) collective-permute-start(bf16[2,4,32,512]{3,2,1,0:T(8,128)(2,1)S(1)} %get-tuple-element.38), channel_id=1, source_target_pairs={{0,8},{4,12},{8,0},{12,4},{16,24},{20,28},{24,16},{28,20},{1,9},{5... | collective-permute-start | bytes 786440 | tf_op jit(solution)/shard_map/ppermute | solution.py:44
  20.0 2.6 %collective-permute-start.6 = (bf16[2,4,32,512]{3,2,1,0:T(8,128)(2,1)S(1)}, bf16[2,4,32,512]{3,2,1,0:T(8,128)(2,1)S(1)}, u32[]{:S(2)}, u32[]{:S(2)}) collective-permute-start(bf16[2,4,32,512]{3,2,1,0:T(8,128)(2,1)S(1)} %get-tuple-element.39), channel_id=1, source_target_pairs={{0,16},{4,20},{8,24},{12,28},{16,0},{20,4},{24,8},{28,12},{1,17},{... | collective-permute-start | bytes 786440 | tf_op jit(solution)/shard_map/ppermute | solution.py:44
  22.6 0.2 collective-permute-start.7
  22.8 5.7 %collective-permute-done.5.refs_1_.refs_3_ = bf16[2,4,32,512]{3,2,1,0:T(8,128)(2,1)S(1)} collective-permute-done((bf16[2,4,32,512]{3,2,1,0:T(8,128)(2,1)S(1)}, bf16[2,4,32,512]{3,2,1,0:T(8,128)(2,1)S(1)}, u32[]{:S(2)}, u32[]{:S(2)}) %collective-permute-start.5) | collective-permute-done | bytes 262176 | tf_op jit(solution)/shard_map/ppermute | solution.py:44
  28.5 12.5 %collective-permute-done.6.refs_2_.refs_4_ = bf16[2,4,32,512]{3,2,1,0:T(8,128)(2,1)S(1)} collective-permute-done((bf16[2,4,32,512]{3,2,1,0:T(8,128)(2,1)S(1)}, bf16[2,4,32,512]{3,2,1,0:T(8,128)(2,1)S(1)}, u32[]{:S(2)}, u32[]{:S(2)}) %collective-permute-start.6) | collective-permute-done | bytes 262176 | tf_op jit(solution)/shard_map/ppermute | solution.py:44
  41.0 0.0 collective-permute-done.7.refs_3_.refs_5_
  41.0 0.1 collective-permute-start.8
  41.1 1.1 slice_bitcast_fusion.1.refs_1_
  42.2 0.8 collective-permute-done.8.refs_6_
  43.0 0.7 back.1
  43.7 4.5 %collective-permute-done.3.refs_3_.refs_1_.refs_4_ = bf16[1408,512]{1,0:T(8,128)(2,1)S(1)} collective-permute-done((bf16[1408,512]{1,0:T(8,128)(2,1)S(1)}, bf16[1408,512]{1,0:T(8,128)(2,1)S(1)}, u32[]{:S(2)}, u32[]{:S(2)}) %collective-permute-start.3) | collective-permute-done | bytes 1441824 | tf_op jit(solution)/shard_map/ppermute | solution.py:38
  48.2 1.0 collective-permute-done.4.refs_4_.refs_0_.refs_5_.refs_6_
  49.2 0.1 pass.1
  49.3 0.6 collective-permute-start.10
  49.9 1.6 %collective-permute-start.9 = (bf16[512,512]{1,0:T(8,128)(2,1)S(1)}, bf16[512,512]{1,0:T(8,128)(2,1)S(1)}, u32[]{:S(2)}, u32[]{:S(2)}) collective-permute-start(bf16[512,512]{1,0:T(8,128)(2,1)S(1)} %get-tuple-element.42), channel_id=1, source_target_pairs={{0,1},{1,0},{2,3},{3,2},{4,5},{5,4},{6,7},{7,6},{8,9},{9,8},{10,11... | collective-permute-start | bytes 1572872 | tf_op jit(solution)/shard_map/ppermute | solution.py:38
  51.5 0.4 collective-permute-start.11
  51.9 1.5 %collective-permute-start.12 = (bf16[256,512]{1,0:T(8,128)(2,1)S(1)}, bf16[256,512]{1,0:T(8,128)(2,1)S(1)}, u32[]{:S(2)}, u32[]{:S(2)}) collective-permute-start(bf16[256,512]{1,0:T(8,128)(2,1)S(1)} %get-tuple-element.45), channel_id=1, source_target_pairs={{0,2},{1,3},{2,0},{3,1},{4,6},{5,7},{6,4},{7,5},{8,10},{9,11},{10,... | collective-permute-start | bytes 786440 | tf_op jit(solution)/shard_map/ppermute | solution.py:38
  53.4 1.5 %collective-permute-start.13 = (bf16[256,512]{1,0:T(8,128)(2,1)S(1)}, bf16[256,512]{1,0:T(8,128)(2,1)S(1)}, u32[]{:S(2)}, u32[]{:S(2)}) collective-permute-start(bf16[256,512]{1,0:T(8,128)(2,1)S(1)} %get-tuple-element.46), channel_id=1, source_target_pairs={{0,3},{1,2},{2,1},{3,0},{4,7},{5,6},{6,5},{7,4},{8,11},{9,10},{10,... | collective-permute-start | bytes 786440 | tf_op jit(solution)/shard_map/ppermute | solution.py:38
  55.0 1.0 forward.1.refs_2_
  56.0 8.8 %collective-permute-done.9.refs_3_.refs_6_.refs_4_ = bf16[512,512]{1,0:T(8,128)(2,1)S(1)} collective-permute-done((bf16[512,512]{1,0:T(8,128)(2,1)S(1)}, bf16[512,512]{1,0:T(8,128)(2,1)S(1)}, u32[]{:S(2)}, u32[]{:S(2)}) %collective-permute-start.9) | collective-permute-done | bytes 524320 | tf_op jit(solution)/shard_map/ppermute | solution.py:38
  64.8 10.3 %collective-permute-done.10.refs_4_.refs_7_.refs_5_ = bf16[768,512]{1,0:T(8,128)(2,1)S(1)} collective-permute-done((bf16[768,512]{1,0:T(8,128)(2,1)S(1)}, bf16[768,512]{1,0:T(8,128)(2,1)S(1)}, u32[]{:S(2)}, u32[]{:S(2)}) %collective-permute-start.10) | collective-permute-done | bytes 786464 | tf_op jit(solution)/shard_map/ppermute | solution.py:38
  75.0 0.4 rest.1.refs_0_
  75.5 2.3 %collective-permute-done.12.refs_3_ = bf16[256,512]{1,0:T(8,128)(2,1)S(1)} collective-permute-done((bf16[256,512]{1,0:T(8,128)(2,1)S(1)}, bf16[256,512]{1,0:T(8,128)(2,1)S(1)}, u32[]{:S(2)}, u32[]{:S(2)}) %collective-permute-start.12) | collective-permute-done | bytes 262176 | tf_op jit(solution)/shard_map/ppermute | solution.py:38
  77.8 0.0 collective-permute-done.13.refs_4_
  77.8 0.4 factors.1.refs_2_.refs_3_
  78.2 0.7 collective-permute-start.17
  79.0 1.2 %collective-permute-start.18 = (bf16[768,512]{1,0:T(8,128)(2,1)S(1)}, bf16[768,512]{1,0:T(8,128)(2,1)S(1)}, u32[]{:S(2)}, u32[]{:S(2)}) collective-permute-start(bf16[768,512]{1,0:T(8,128)(2,1)S(1)} %factors.1.refs_2_.refs_3_), channel_id=1, source_target_pairs={{0,2},{1,3},{2,0},{3,1},{4,6},{5,7},{6,4},{7,5},{8,10},{9,11},{10,... | collective-permute-start | bytes 2359304 | tf_op jit(solution)/shard_map/ppermute | solution.py:38
  80.2 1.3 %slots.1 = (bf16[2,32,2048]{2,1,0:T(8,128)(2,1)S(1)}, bf16[2,32,2048]{2,1,0:T(8,128)(2,1)S(1)}, bf16[2,32,2048]{2,1,0:T(8,128)(2,1)S(1)}, bf16[2,32,2048]{2,1,0:T(8,128)(2,1)S(1)}) custom-call(s32[1]{0:T(128)} %bitcast.1.refs_0_, s32[1]{0:T(128)} %bitcast.refs_0_.refs_1_, bf16[768,512]{1,0:T(8,128)(2,1)S(1)} %factors.1.refs_2_.refs_3_, ...), custom_call_target="tpu_custom_call" | custom-call | tf_op jit(solution)/shard_map/slots/pallas_call | solution.py:205
  81.5 0.7 collective-permute-start.14
  82.2 2.6 %collective-permute-start.15 = (bf16[2,32,2048]{2,1,0:T(8,128)(2,1)S(1)}, bf16[2,32,2048]{2,1,0:T(8,128)(2,1)S(1)}, u32[]{:S(2)}, u32[]{:S(2)}) collective-permute-start(bf16[2,32,2048]{2,1,0:T(8,128)(2,1)S(1)} %get-tuple-element.49), channel_id=1, source_target_pairs={{0,16},{4,20},{8,24},{12,28},{16,0},{20,4},{24,8},{28,12},{1,17},{... | collective-permute-start | bytes 786440 | tf_op jit(solution)/shard_map/ppermute | solution.py:44
  84.8 1.2 collective-permute-start.16
  86.0 9.3 %collective-permute-done.17.refs_5_.refs_1_ = bf16[768,512]{1,0:T(8,128)(2,1)S(1)} collective-permute-done((bf16[768,512]{1,0:T(8,128)(2,1)S(1)}, bf16[768,512]{1,0:T(8,128)(2,1)S(1)}, u32[]{:S(2)}, u32[]{:S(2)}) %collective-permute-start.17) | collective-permute-done | bytes 786464 | tf_op jit(solution)/shard_map/ppermute | solution.py:38
  95.3 1.3 %collective-permute-done.18.refs_7_.refs_0_ = bf16[768,512]{1,0:T(8,128)(2,1)S(1)} collective-permute-done((bf16[768,512]{1,0:T(8,128)(2,1)S(1)}, bf16[768,512]{1,0:T(8,128)(2,1)S(1)}, u32[]{:S(2)}, u32[]{:S(2)}) %collective-permute-start.18) | collective-permute-done | bytes 786464 | tf_op jit(solution)/shard_map/ppermute | solution.py:38
  96.6 0.1 cut.1
  96.6 1.3 %collective-permute-start.22 = (bf16[448,512]{1,0:T(8,128)(2,1)S(1)}, bf16[448,512]{1,0:T(8,128)(2,1)S(1)}, u32[]{:S(2)}, u32[]{:S(2)}) collective-permute-start(bf16[448,512]{1,0:T(8,128)(2,1)S(1)} %get-tuple-element.57), channel_id=1, source_target_pairs={{0,2},{1,3},{2,0},{3,1},{4,6},{5,7},{6,4},{7,5},{8,10},{9,11},{10,... | collective-permute-start | bytes 1376264 | tf_op jit(solution)/shard_map/ppermute | solution.py:38
  97.9 0.6 collective-permute-start.21
  98.5 1.8 %gram.1 = (f32[3,3,512,512]{3,2,1,0:T(8,128)S(1)}, f32[16,128]{1,0:T(8,128)S(1)}) custom-call(s32[1]{0:T(128)} %bitcast.1.refs_0_, bf16[4,8,32,512]{3,2,1,0:T(8,128)(2,1)S(1)} %get-tuple-element.51.refs_1_.refs_3_, bf16[256,2048]{1,0:T(8,128)(2,1)S(1)} %bitcast.12, bf16[768,512]{1,0:T(8,128)(2,1)S(1)} %factors.1.refs_2_.refs_3_, ...), custom_call_target="tpu_custom_call" | custom-call | tf_op jit(solution)/shard_map/gram/pallas_call | solution.py:205
  100.2 0.0 collective-permute-done.14.refs_1_.refs_3_
  100.3 1.1 collective-permute-done.15.refs_2_.refs_4_
  101.4 0.1 collective-permute-start.19
  101.5 0.5 collective-permute-start.20
  102.0 3.0 %collective-permute-done.21.refs_6_ = bf16[320,512]{1,0:T(8,128)(2,1)S(1)} collective-permute-done((bf16[320,512]{1,0:T(8,128)(2,1)S(1)}, bf16[320,512]{1,0:T(8,128)(2,1)S(1)}, u32[]{:S(2)}, u32[]{:S(2)}) %collective-permute-start.21) | collective-permute-done | bytes 327712 | tf_op jit(solution)/shard_map/ppermute | solution.py:38
  105.0 0.2 collective-permute-done.22.refs_7_
  105.2 1.2 gram_late.1
  106.3 1.5 %collective-permute-start.23 = (f32[16,128]{1,0:T(8,128)S(1)}, f32[16,128]{1,0:T(8,128)S(1)}, u32[]{:S(2)}, u32[]{:S(2)}) collective-permute-start(f32[16,128]{1,0:T(8,128)S(1)} %get-tuple-element.58.refs_8_.refs_1_), channel_id=1, source_target_pairs={{0,3},{1,2},{2,1},{3,0},{4,7},{5,6},{6,5},{7,4},{8,11},{9,10},{10,... | collective-permute-start | bytes 24584 | tf_op jit(solution)/shard_map/ppermute | solution.py:38
  107.8 1.4 %collective-permute-start.24 = (f32[16,128]{1,0:T(8,128)S(1)}, f32[16,128]{1,0:T(8,128)S(1)}, u32[]{:S(2)}, u32[]{:S(2)}) collective-permute-start(f32[16,128]{1,0:T(8,128)S(1)} %get-tuple-element.58.refs_8_.refs_1_), channel_id=1, source_target_pairs={{0,2},{1,3},{2,0},{3,1},{4,6},{5,7},{6,4},{7,5},{8,10},{9,11},{10,... | collective-permute-start | bytes 24584 | tf_op jit(solution)/shard_map/ppermute | solution.py:38
  109.2 0.7 collective-permute-start.25
  109.9 1.2 %unplace.1 = bf16[1,128,2048]{2,1,0:T(8,128)(2,1)} custom-call(s32[1]{0:T(128)} %bitcast.refs_0_.refs_1_, bf16[144,512]{1,0:T(8,128)(2,1)S(1)} %copy-done.3, bf16[2,32,2048]{2,1,0:T(8,128)(2,1)S(1)} %get-tuple-element.47.refs_0_.refs_2_, bf16[2,32,2048]{2,1,0:T(8,128)(2,1)S(1)} %collective-permute-done.14.refs_1_.refs_3_, ...), custom_call_target="tpu_custom_call" | custom-call | tf_op jit(solution)/shard_map/unplace/pallas_call | solution.py:205
  111.1 0.4 collective-permute-done.24.refs_3_
  111.5 1.4 %collective-permute-done.25.refs_4_ = f32[16,128]{1,0:T(8,128)S(1)} collective-permute-done((f32[16,128]{1,0:T(8,128)S(1)}, f32[16,128]{1,0:T(8,128)S(1)}, u32[]{:S(2)}, u32[]{:S(2)}) %collective-permute-start.25) | collective-permute-done | bytes 8224 | tf_op jit(solution)/shard_map/ppermute | solution.py:38
  112.9 4.2 %adam.1 = f32[1,3,512,512]{3,2,1,0:T(8,128)} custom-call(s32[1]{0:T(128)} %bitcast.1.refs_0_, f32[16,128]{1,0:T(8,128)S(1)} %get-tuple-element.58.refs_8_.refs_1_, f32[16,128]{1,0:T(8,128)S(1)} %collective-permute-done.23.refs_2_, f32[16,128]{1,0:T(8,128)S(1)} %collective-permute-done.24.refs_3_, f32[16,128]{1,0:T(8,128)S(1)} %collective-permute-done.25.refs_4_, ...), custom_call_target="tpu_custom_call" | custom-call | tf_op jit(solution)/shard_map/adam/pallas_call | solution.py:205
  (15 shorter events, 0.1 us)
Async XLA Ops:
  0.6 14.4 %copy-start = (bf16[1,1,256,2048]{3,2,1,0:T(8,128)(2,1)S(1)}, bf16[1,1,256,2048]{3,2,1,0:T(8,128)(2,1)}, u32[]{:S(2)}) copy-start(bf16[1,1,256,2048]{3,2,1,0:T(8,128)(2,1)} %param.15) | copy-start | bytes 3145732
  3.4 7.5 %collective-permute-start = (bf16[144,512]{1,0:T(8,128)(2,1)}, bf16[144,512]{1,0:T(8,128)(2,1)S(1)}, u32[]{:S(2)}, u32[]{:S(2)}) collective-permute-start(bf16[144,512]{1,0:T(8,128)(2,1)} %get-tuple-element.32), channel_id=1, source_target_pairs={{0,1},{1,0},{2,3},{3,2},{4,5},{5,4},{6,7},{7,6},{8,9},{9,8},{10,11... | collective-permute-start | bytes 442376 | tf_op jit(solution)/shard_map/ppermute | solution.py:38
  6.3 8.7 %collective-permute-start.1 = (bf16[144,512]{1,0:T(8,128)(2,1)}, bf16[144,512]{1,0:T(8,128)(2,1)S(1)}, u32[]{:S(2)}, u32[]{:S(2)}) collective-permute-start(bf16[144,512]{1,0:T(8,128)(2,1)} %get-tuple-element.33), channel_id=1, source_target_pairs={{0,2},{1,3},{2,0},{3,1},{4,6},{5,7},{6,4},{7,5},{8,10},{9,11},{10,... | collective-permute-start | bytes 442376 | tf_op jit(solution)/shard_map/ppermute | solution.py:38
  7.9 7.2 %collective-permute-start.2 = (bf16[144,512]{1,0:T(8,128)(2,1)}, bf16[144,512]{1,0:T(8,128)(2,1)S(1)}, u32[]{:S(2)}, u32[]{:S(2)}) collective-permute-start(bf16[144,512]{1,0:T(8,128)(2,1)} %get-tuple-element.34), channel_id=1, source_target_pairs={{0,3},{1,2},{2,1},{3,0},{4,7},{5,6},{6,5},{7,4},{8,11},{9,10},{10,... | collective-permute-start | bytes 442376 | tf_op jit(solution)/shard_map/ppermute | solution.py:38
  9.2 8.7 %copy-start.3 = (bf16[144,512]{1,0:T(8,128)(2,1)S(1)}, bf16[144,512]{1,0:T(8,128)(2,1)}, u32[]{:S(2)}) copy-start(bf16[144,512]{1,0:T(8,128)(2,1)} %get-tuple-element.31.refs_1_) | copy-start | bytes 442372
  15.8 32.5 %collective-permute-start.3 = (bf16[1408,512]{1,0:T(8,128)(2,1)S(1)}, bf16[1408,512]{1,0:T(8,128)(2,1)S(1)}, u32[]{:S(2)}, u32[]{:S(2)}) collective-permute-start(bf16[1408,512]{1,0:T(8,128)(2,1)S(1)} %get-tuple-element.35), channel_id=1, source_target_pairs={{0,1},{1,0},{2,3},{3,2},{4,5},{5,4},{6,7},{7,6},{8,9},{9,8},{10,11... | collective-permute-start | bytes 4325384 | tf_op jit(solution)/shard_map/ppermute | solution.py:38
  17.1 32.2 %collective-permute-start.4 = (bf16[1408,512]{1,0:T(8,128)(2,1)S(1)}, bf16[1408,512]{1,0:T(8,128)(2,1)S(1)}, u32[]{:S(2)}, u32[]{:S(2)}) collective-permute-start(bf16[1408,512]{1,0:T(8,128)(2,1)S(1)} %get-tuple-element.36), channel_id=1, source_target_pairs={{0,2},{1,3},{2,0},{3,1},{4,6},{5,7},{6,4},{7,5},{8,10},{9,11},{10,... | collective-permute-start | bytes 4325384 | tf_op jit(solution)/shard_map/ppermute | solution.py:38
  18.3 10.1 %collective-permute-start.5 = (bf16[2,4,32,512]{3,2,1,0:T(8,128)(2,1)S(1)}, bf16[2,4,32,512]{3,2,1,0:T(8,128)(2,1)S(1)}, u32[]{:S(2)}, u32[]{:S(2)}) collective-permute-start(bf16[2,4,32,512]{3,2,1,0:T(8,128)(2,1)S(1)} %get-tuple-element.38), channel_id=1, source_target_pairs={{0,8},{4,12},{8,0},{12,4},{16,24},{20,28},{24,16},{28,20},{1,9},{5... | collective-permute-start | bytes 786440 | tf_op jit(solution)/shard_map/ppermute | solution.py:44
  20.0 21.0 %collective-permute-start.6 = (bf16[2,4,32,512]{3,2,1,0:T(8,128)(2,1)S(1)}, bf16[2,4,32,512]{3,2,1,0:T(8,128)(2,1)S(1)}, u32[]{:S(2)}, u32[]{:S(2)}) collective-permute-start(bf16[2,4,32,512]{3,2,1,0:T(8,128)(2,1)S(1)} %get-tuple-element.39), channel_id=1, source_target_pairs={{0,16},{4,20},{8,24},{12,28},{16,0},{20,4},{24,8},{28,12},{1,17},{... | collective-permute-start | bytes 786440 | tf_op jit(solution)/shard_map/ppermute | solution.py:44
  22.6 18.4 %collective-permute-start.7 = (bf16[2,4,32,512]{3,2,1,0:T(8,128)(2,1)S(1)}, bf16[2,4,32,512]{3,2,1,0:T(8,128)(2,1)S(1)}, u32[]{:S(2)}, u32[]{:S(2)}) collective-permute-start(bf16[2,4,32,512]{3,2,1,0:T(8,128)(2,1)S(1)} %get-tuple-element.40), channel_id=1, source_target_pairs={{0,24},{4,28},{8,16},{12,20},{16,8},{20,12},{24,0},{28,4},{1,25},{... | collective-permute-start | bytes 786440 | tf_op jit(solution)/shard_map/ppermute | solution.py:44
  41.0 2.0 %collective-permute-start.8 = (bf16[4,4,32,512]{3,2,1,0:T(8,128)(2,1)S(1)}, bf16[4,4,32,512]{3,2,1,0:T(8,128)(2,1)S(1)}, u32[]{:S(2)}, u32[]{:S(2)}) collective-permute-start(bf16[4,4,32,512]{3,2,1,0:T(8,128)(2,1)S(1)} %pick.2), channel_id=1, source_target_pairs={{0,4},{4,0},{8,12},{12,8},{16,20},{20,16},{24,28},{28,24},{1,5},{5... | collective-permute-start | bytes 1572872 | tf_op jit(solution)/shard_map/ppermute | solution.py:68
  49.3 25.7 %collective-permute-start.10 = (bf16[768,512]{1,0:T(8,128)(2,1)S(1)}, bf16[768,512]{1,0:T(8,128)(2,1)S(1)}, u32[]{:S(2)}, u32[]{:S(2)}) collective-permute-start(bf16[768,512]{1,0:T(8,128)(2,1)S(1)} %get-tuple-element.43), channel_id=1, source_target_pairs={{0,2},{1,3},{2,0},{3,1},{4,6},{5,7},{6,4},{7,5},{8,10},{9,11},{10,... | collective-permute-start | bytes 2359304 | tf_op jit(solution)/shard_map/ppermute | solution.py:38
  49.9 14.9 %collective-permute-start.9 = (bf16[512,512]{1,0:T(8,128)(2,1)S(1)}, bf16[512,512]{1,0:T(8,128)(2,1)S(1)}, u32[]{:S(2)}, u32[]{:S(2)}) collective-permute-start(bf16[512,512]{1,0:T(8,128)(2,1)S(1)} %get-tuple-element.42), channel_id=1, source_target_pairs={{0,1},{1,0},{2,3},{3,2},{4,5},{5,4},{6,7},{7,6},{8,9},{9,8},{10,11... | collective-permute-start | bytes 1572872 | tf_op jit(solution)/shard_map/ppermute | solution.py:38
  51.5 24.0 %collective-permute-start.11 = (bf16[256,512]{1,0:T(8,128)(2,1)S(1)}, bf16[256,512]{1,0:T(8,128)(2,1)S(1)}, u32[]{:S(2)}, u32[]{:S(2)}) collective-permute-start(bf16[256,512]{1,0:T(8,128)(2,1)S(1)} %get-tuple-element.44), channel_id=1, source_target_pairs={{0,1},{1,0},{2,3},{3,2},{4,5},{5,4},{6,7},{7,6},{8,9},{9,8},{10,11... | collective-permute-start | bytes 786440 | tf_op jit(solution)/shard_map/ppermute | solution.py:38
  51.9 25.9 %collective-permute-start.12 = (bf16[256,512]{1,0:T(8,128)(2,1)S(1)}, bf16[256,512]{1,0:T(8,128)(2,1)S(1)}, u32[]{:S(2)}, u32[]{:S(2)}) collective-permute-start(bf16[256,512]{1,0:T(8,128)(2,1)S(1)} %get-tuple-element.45), channel_id=1, source_target_pairs={{0,2},{1,3},{2,0},{3,1},{4,6},{5,7},{6,4},{7,5},{8,10},{9,11},{10,... | collective-permute-start | bytes 786440 | tf_op jit(solution)/shard_map/ppermute | solution.py:38
  53.4 24.4 %collective-permute-start.13 = (bf16[256,512]{1,0:T(8,128)(2,1)S(1)}, bf16[256,512]{1,0:T(8,128)(2,1)S(1)}, u32[]{:S(2)}, u32[]{:S(2)}) collective-permute-start(bf16[256,512]{1,0:T(8,128)(2,1)S(1)} %get-tuple-element.46), channel_id=1, source_target_pairs={{0,3},{1,2},{2,1},{3,0},{4,7},{5,6},{6,5},{7,4},{8,11},{9,10},{10,... | collective-permute-start | bytes 786440 | tf_op jit(solution)/shard_map/ppermute | solution.py:38
  78.2 17.0 %collective-permute-start.17 = (bf16[768,512]{1,0:T(8,128)(2,1)S(1)}, bf16[768,512]{1,0:T(8,128)(2,1)S(1)}, u32[]{:S(2)}, u32[]{:S(2)}) collective-permute-start(bf16[768,512]{1,0:T(8,128)(2,1)S(1)} %factors.1.refs_2_.refs_3_), channel_id=1, source_target_pairs={{0,1},{1,0},{2,3},{3,2},{4,5},{5,4},{6,7},{7,6},{8,9},{9,8},{10,11... | collective-permute-start | bytes 2359304 | tf_op jit(solution)/shard_map/ppermute | solution.py:38
  79.0 17.6 %collective-permute-start.18 = (bf16[768,512]{1,0:T(8,128)(2,1)S(1)}, bf16[768,512]{1,0:T(8,128)(2,1)S(1)}, u32[]{:S(2)}, u32[]{:S(2)}) collective-permute-start(bf16[768,512]{1,0:T(8,128)(2,1)S(1)} %factors.1.refs_2_.refs_3_), channel_id=1, source_target_pairs={{0,2},{1,3},{2,0},{3,1},{4,6},{5,7},{6,4},{7,5},{8,10},{9,11},{10,... | collective-permute-start | bytes 2359304 | tf_op jit(solution)/shard_map/ppermute | solution.py:38
  81.5 18.7 %collective-permute-start.14 = (bf16[2,32,2048]{2,1,0:T(8,128)(2,1)S(1)}, bf16[2,32,2048]{2,1,0:T(8,128)(2,1)S(1)}, u32[]{:S(2)}, u32[]{:S(2)}) collective-permute-start(bf16[2,32,2048]{2,1,0:T(8,128)(2,1)S(1)} %get-tuple-element.48), channel_id=1, source_target_pairs={{0,8},{4,12},{8,0},{12,4},{16,24},{20,28},{24,16},{28,20},{1,9},{5... | collective-permute-start | bytes 786440 | tf_op jit(solution)/shard_map/ppermute | solution.py:44
  82.2 19.1 %collective-permute-start.15 = (bf16[2,32,2048]{2,1,0:T(8,128)(2,1)S(1)}, bf16[2,32,2048]{2,1,0:T(8,128)(2,1)S(1)}, u32[]{:S(2)}, u32[]{:S(2)}) collective-permute-start(bf16[2,32,2048]{2,1,0:T(8,128)(2,1)S(1)} %get-tuple-element.49), channel_id=1, source_target_pairs={{0,16},{4,20},{8,24},{12,28},{16,0},{20,4},{24,8},{28,12},{1,17},{... | collective-permute-start | bytes 786440 | tf_op jit(solution)/shard_map/ppermute | solution.py:44
  84.8 16.6 %collective-permute-start.16 = (bf16[2,32,2048]{2,1,0:T(8,128)(2,1)S(1)}, bf16[2,32,2048]{2,1,0:T(8,128)(2,1)S(1)}, u32[]{:S(2)}, u32[]{:S(2)}) collective-permute-start(bf16[2,32,2048]{2,1,0:T(8,128)(2,1)S(1)} %get-tuple-element.50), channel_id=1, source_target_pairs={{0,24},{4,28},{8,16},{12,20},{16,8},{20,12},{24,0},{28,4},{1,25},{... | collective-permute-start | bytes 786440 | tf_op jit(solution)/shard_map/ppermute | solution.py:44
  96.6 8.5 %collective-permute-start.22 = (bf16[448,512]{1,0:T(8,128)(2,1)S(1)}, bf16[448,512]{1,0:T(8,128)(2,1)S(1)}, u32[]{:S(2)}, u32[]{:S(2)}) collective-permute-start(bf16[448,512]{1,0:T(8,128)(2,1)S(1)} %get-tuple-element.57), channel_id=1, source_target_pairs={{0,2},{1,3},{2,0},{3,1},{4,6},{5,7},{6,4},{7,5},{8,10},{9,11},{10,... | collective-permute-start | bytes 1376264 | tf_op jit(solution)/shard_map/ppermute | solution.py:38
  97.9 7.1 %collective-permute-start.21 = (bf16[320,512]{1,0:T(8,128)(2,1)S(1)}, bf16[320,512]{1,0:T(8,128)(2,1)S(1)}, u32[]{:S(2)}, u32[]{:S(2)}) collective-permute-start(bf16[320,512]{1,0:T(8,128)(2,1)S(1)} %get-tuple-element.56), channel_id=1, source_target_pairs={{0,1},{1,0},{2,3},{3,2},{4,5},{5,4},{6,7},{7,6},{8,9},{9,8},{10,11... | collective-permute-start | bytes 983048 | tf_op jit(solution)/shard_map/ppermute | solution.py:38
  101.4 8.5 %collective-permute-start.19 = (bf16[2,32,2048]{2,1,0:T(8,128)(2,1)S(1)}, bf16[2,32,2048]{2,1,0:T(8,128)(2,1)S(1)}, u32[]{:S(2)}, u32[]{:S(2)}) collective-permute-start(bf16[2,32,2048]{2,1,0:T(8,128)(2,1)S(1)} %get-tuple-element.53), channel_id=1, source_target_pairs={{0,4},{4,0},{8,12},{12,8},{16,20},{20,16},{24,28},{28,24},{1,5},{5... | collective-permute-start | bytes 786440 | tf_op jit(solution)/shard_map/ppermute | solution.py:68
  101.5 8.4 %collective-permute-start.20 = (bf16[2,32,2048]{2,1,0:T(8,128)(2,1)S(1)}, bf16[2,32,2048]{2,1,0:T(8,128)(2,1)S(1)}, u32[]{:S(2)}, u32[]{:S(2)}) collective-permute-start(bf16[2,32,2048]{2,1,0:T(8,128)(2,1)S(1)} %get-tuple-element.54), channel_id=1, source_target_pairs={{0,4},{4,0},{8,12},{12,8},{16,20},{20,16},{24,28},{28,24},{1,5},{5... | collective-permute-start | bytes 786440 | tf_op jit(solution)/shard_map/ppermute | solution.py:68
  105.2 7.7 %copy-start.1 = (f32[1,3,512,512]{3,2,1,0:T(8,128)S(1)}, f32[1,3,512,512]{3,2,1,0:T(8,128)}, u32[]{:S(2)}) copy-start(f32[1,3,512,512]{3,2,1,0:T(8,128)} %refs_7_.1) | copy-start | bytes 9437188
  105.2 7.7 %copy-start.2 = (f32[1,3,512,512]{3,2,1,0:T(8,128)S(1)}, f32[1,3,512,512]{3,2,1,0:T(8,128)}, u32[]{:S(2)}) copy-start(f32[1,3,512,512]{3,2,1,0:T(8,128)} %refs_8_.1) | copy-start | bytes 9437188
  106.3 4.7 %collective-permute-start.23 = (f32[16,128]{1,0:T(8,128)S(1)}, f32[16,128]{1,0:T(8,128)S(1)}, u32[]{:S(2)}, u32[]{:S(2)}) collective-permute-start(f32[16,128]{1,0:T(8,128)S(1)} %get-tuple-element.58.refs_8_.refs_1_), channel_id=1, source_target_pairs={{0,3},{1,2},{2,1},{3,0},{4,7},{5,6},{6,5},{7,4},{8,11},{9,10},{10,... | collective-permute-start | bytes 24584 | tf_op jit(solution)/shard_map/ppermute | solution.py:38
  107.8 3.7 %collective-permute-start.24 = (f32[16,128]{1,0:T(8,128)S(1)}, f32[16,128]{1,0:T(8,128)S(1)}, u32[]{:S(2)}, u32[]{:S(2)}) collective-permute-start(f32[16,128]{1,0:T(8,128)S(1)} %get-tuple-element.58.refs_8_.refs_1_), channel_id=1, source_target_pairs={{0,2},{1,3},{2,0},{3,1},{4,6},{5,7},{6,4},{7,5},{8,10},{9,11},{10,... | collective-permute-start | bytes 24584 | tf_op jit(solution)/shard_map/ppermute | solution.py:38
  109.2 3.7 %collective-permute-start.25 = (f32[16,128]{1,0:T(8,128)S(1)}, f32[16,128]{1,0:T(8,128)S(1)}, u32[]{:S(2)}, u32[]{:S(2)}) collective-permute-start(f32[16,128]{1,0:T(8,128)S(1)} %get-tuple-element.58.refs_8_.refs_1_), channel_id=1, source_target_pairs={{0,1},{1,0},{2,3},{3,2},{4,5},{5,4},{6,7},{7,6},{8,9},{9,8},{10,11... | collective-permute-start | bytes 24584 | tf_op jit(solution)/shard_map/ppermute | solution.py:38

commit v12 on v10

--- a/solution.py
+++ b/solution.py
@@ -276,14 +276,40 @@
     return blocks.reshape(rows, blocks.shape[2])
 
 
-def back_kernel(chips, arrays, spot_ref, weight_ref, *refs):
+def back_kernel(chips, arrays, packed, spot_ref, weight_ref, *refs):
     came_refs, incoming_ref, out_refs = refs[:arrays], refs[arrays], refs[arrays + 1 :]
-    for offset, out_ref in enumerate(out_refs):
+    for offset in range(incoming_ref.shape[0]):
         for expert in range(2 * chips):
             block_ref = spread_block(chips, came_refs, expert)
             incoming_ref[offset, spot_ref[0] ^ expert] = block_ref[offset]
         rows = flat_rows(incoming_ref[offset])
-        out_ref[...] = multiply(rows, weight_ref[...]).astype(out_ref.dtype)
+        total = multiply(rows, weight_ref[...])
+        if not packed or offset == 0:
+            out_refs[offset][...] = total.astype(out_refs[offset].dtype)
+            continue
+        _, near_ref, one_ref, two_ref = out_refs
+        half = total.shape[0] // 2
+        upper, lower = pl.ds(0, half), pl.ds(half, half)
+        if offset == 1:
+            one_ref[upper, :] = total[:half].astype(jnp.bfloat16)
+            near_ref[lower, :] = total[half:]
+        elif offset == 2:
+            two_ref[upper, :] = total[half:].astype(jnp.bfloat16)
+            near_ref[upper, :] = total[:half]
+        else:
+            one_ref[lower, :] = total[:half].astype(jnp.bfloat16)
+            two_ref[lower, :] = total[half:].astype(jnp.bfloat16)
+
+
+def add_kernel(near_ref, from_one_ref, from_two_ref, to_one_ref, to_two_ref):
+    half = to_one_ref.shape[0]
+    upper, lower = pl.ds(0, half), pl.ds(half, half)
+    to_two_ref[...] = (near_ref[upper, :] + from_one_ref[lower, :].astype(jnp.float32)).astype(
+        jnp.bfloat16
+    )
+    to_one_ref[...] = (near_ref[lower, :] + from_two_ref[lower, :].astype(jnp.float32)).astype(
+        jnp.bfloat16
+    )
 
 
 def forward_kernel(offsets, lengths, has_start, rep_ref, inputs_ref, *refs):
@@ -303,11 +329,18 @@
     out_ref[1] = up
 
 
-def factor_kernel(forward_ref, *refs):
+def factor_kernel(packed, forward_ref, *refs):
     back_refs, out_ref = refs[:-1], refs[-1]
     slot_count = forward_ref.shape[1]
     half = slot_count // 2
     hidden_grad = back_refs[0][...]
+    if packed:
+        upper, lower = [
+            near_ref[pl.ds(0, half), :].astype(jnp.float32) + far_ref[...].astype(jnp.float32)
+            for near_ref, far_ref in zip(back_refs[1:3], back_refs[3:])
+        ]
+        hidden_grad = hidden_grad + jnp.concatenate([upper, lower], axis=0)
+        back_refs = back_refs[:1]
     for back_ref in back_refs[1:]:
         hidden_grad = hidden_grad + back_ref[...].astype(jnp.float32)
     gate_pre, up_pre = forward_ref[0], forward_ref[1]
@@ -627,16 +660,21 @@
 
     back_shape = (slot_count, hidden_width)
     incoming, *back = call(
-        functools.partial(back_kernel, chips, len(came)),
+        functools.partial(back_kernel, chips, len(came), packed),
         "back",
         [spot, weights[0, 2], *came],
         [SMEM] + [VMEM] * (1 + len(came)),
         [shape((rep_count, expert_count, capacity, seg_rows), jnp.bfloat16)]
-        + [shape(back_shape, jnp.bfloat16 if k else jnp.float32) for k in offsets],
-    )
-    own_back = back[:1]
-    back = exchange(back)
+        + [
+            shape(back_shape, jnp.float32 if k == 0 or packed and k == 1 else jnp.bfloat16)
+            for k in offsets
+        ],
+    )
+    if not packed:
+        back = exchange(back)
     if packed:
+        own_back, near_back, to_one, to_two = back
+        back_one, back_two = from_peer(to_one, 1), from_peer(to_two, 2)
         passed = shape((seg_rows + half, seg_rows), jnp.bfloat16)
         first, second = call(
             pass_kernel,
@@ -644,9 +682,17 @@
             [from_two, from_one],
             [VMEM, VMEM],
             [passed, passed],
-            after=own_back,
+            after=[back_one, back_two],
         )
         last = (from_peer(first, 1), from_peer(second, 2))
+        to_one, to_two = call(
+            add_kernel,
+            "add",
+            [near_back, back_one, back_two],
+            [VMEM] * 3,
+            [shape((half, hidden_width), jnp.bfloat16)] * 2,
+        )
+        back = [own_back, back_one, back_two, from_peer(to_two, 2), from_peer(to_one, 1)]
         projections.append(last)
         inputs.append(last)
 
@@ -668,7 +714,7 @@
         )
 
     (own_factors,) = call(
-        factor_kernel,
+        functools.partial(factor_kernel, packed),
         "factors",
         [forward, *back],
         [VMEM] * (1 + len(back)),

time: 114 us -> 113 us (level)
  waiting for transfers between devices: 63.7 us -> 61.1 us
    ppermute x17 -> x18, waiting for transfers between devices: 43.2 us -> 38.3 us  [from_peer(): lax.ppermute(array, 'replica', [(i, i ^ offset) for i in range(count)])]
    ppermute x6, waiting for transfers between devices: 19.7 us -> 22 us  [across_chips(): lax.ppermute(part, 'expert', [(i, i ^ 2 * k) for i in range(count)])]
    ppermute x17 -> x18, starting transfers between devices: 19.9 us -> 21.5 us  [from_peer(): lax.ppermute(array, 'replica', [(i, i ^ offset) for i in range(count)])]
    pallas_call x16 -> x17, Pallas kernels: 16 us -> 15.8 us  [call(): pl.pallas_call(body, grid=grid, in_specs=list(specs) + [VMEM] * len(after...]
  transfers between devices with their start and end apart: 26 -> 27, of which waited for: 17 -> 15; matrix products, arithmetic and copies ran while one was open for 2% -> 2% of each run, Pallas kernels for 7% -> 8%
where the time goes in v12:
time: 113 us; the launch traced here: 112 us
  waiting for transfers between devices  61.1 us (54%)
  starting transfers between devices  31.3 us (28%)
  Pallas kernels  15.8 us (14%)
  local copies, waits for them, and re-layouts  2.39 us (2%)
  between operations  1.55 us (1%)
    ppermute x18, waiting for transfers between devices, from_peer(): lax.ppermute(array, 'replica', [(i, i ^ offset) for i in range(count)])  38.3 us
    ppermute x6, waiting for transfers between devices, across_chips(): lax.ppermute(part, 'expert', [(i, i ^ 2 * k) for i in range(count)])  22 us
    ppermute x18, starting transfers between devices, from_peer(): lax.ppermute(array, 'replica', [(i, i ^ offset) for i in range(count)])  21.5 us
    pallas_call x17, Pallas kernels, call(): pl.pallas_call(body, grid=grid, in_specs=list(specs) + [VMEM] * len(after...  15.8 us
    ppermute x6, starting transfers between devices, across_chips(): lax.ppermute(part, 'expert', [(i, i ^ 2 * k) for i in range(count)])  9.18 us
  transfers between devices with their start and end apart: 27, of which 15 were waited for; matrix products, arithmetic and copies ran while one was open for 2% of the time, Pallas kernels for 8%

profile of v12, /device:TPU:0, one launch (start us, length us, event | category | flops | bytes accessed | tf_op | source)
XLA Modules:
  0.0 112.3 jit_solution(7496530716652358088)
XLA Ops:
  1.4 2.0 %rows.1 = (bf16[144,512]{1,0:T(8,128)(2,1)}, bf16[144,512]{1,0:T(8,128)(2,1)}, bf16[144,512]{1,0:T(8,128)(2,1)}, bf16[144,512]{1,0:T(8,128)(2,1)}) custom-call(s32[1]{0:T(128)} %bitcast.1.refs_0_, s32[1,1]{1,0:T(1,128)S(6)} %copy.10.refs_1_, f32[8]{0:T(128)} %refs_2_.1, s32[1,128]{1,0:T(1,128)} %bitcast.14, bf16[128,2048]{1,0:T(8,128)(2,1)} %bitcast.13), custom_call_target="tpu_custom_call" | custom-call | tf_op jit(solution)/shard_map/rows/pallas_call | solution.py:186
  3.4 2.9 %collective-permute-start = (bf16[144,512]{1,0:T(8,128)(2,1)}, bf16[144,512]{1,0:T(8,128)(2,1)S(1)}, u32[]{:S(2)}, u32[]{:S(2)}) collective-permute-start(bf16[144,512]{1,0:T(8,128)(2,1)} %get-tuple-element.34), channel_id=1, source_target_pairs={{0,1},{1,0},{2,3},{3,2},{4,5},{5,4},{6,7},{7,6},{8,9},{9,8},{10,11... | collective-permute-start | bytes 442376 | tf_op jit(solution)/shard_map/ppermute | solution.py:38
  6.3 1.5 %collective-permute-start.1 = (bf16[144,512]{1,0:T(8,128)(2,1)}, bf16[144,512]{1,0:T(8,128)(2,1)S(1)}, u32[]{:S(2)}, u32[]{:S(2)}) collective-permute-start(bf16[144,512]{1,0:T(8,128)(2,1)} %get-tuple-element.35), channel_id=1, source_target_pairs={{0,2},{1,3},{2,0},{3,1},{4,6},{5,7},{6,4},{7,5},{8,10},{9,11},{10,... | collective-permute-start | bytes 442376 | tf_op jit(solution)/shard_map/ppermute | solution.py:38
  7.9 1.3 %slice_bitcast_fusion.refs_1_.refs_2_.refs_3_ = bf16[2,512,512]{2,1,0:T(8,128)(2,1)S(1)} fusion(bf16[1,3,512,512]{3,2,1,0:T(8,128)(2,1)} %param.8), kind=kLoop, calls=%fused_computation | loop fusion | bytes 2097152 | tf_op jit(solution)/shard_map/squeeze | solution.py:622
  9.2 0.0 copy-start.3
  9.2 0.1 pad_add_fusion.refs_0_
  9.3 1.7 %collective-permute-done.refs_3_.refs_2_ = bf16[144,512]{1,0:T(8,128)(2,1)S(1)} collective-permute-done((bf16[144,512]{1,0:T(8,128)(2,1)}, bf16[144,512]{1,0:T(8,128)(2,1)S(1)}, u32[]{:S(2)}, u32[]{:S(2)}) %collective-permute-start) | collective-permute-done | bytes 147488 | tf_op jit(solution)/shard_map/ppermute | solution.py:38
  10.9 4.1 %collective-permute-done.1.refs_4_.refs_3_ = bf16[144,512]{1,0:T(8,128)(2,1)S(1)} collective-permute-done((bf16[144,512]{1,0:T(8,128)(2,1)}, bf16[144,512]{1,0:T(8,128)(2,1)S(1)}, u32[]{:S(2)}, u32[]{:S(2)}) %collective-permute-start.1) | collective-permute-done | bytes 147488 | tf_op jit(solution)/shard_map/ppermute | solution.py:38
  15.0 0.7 payload.1
  15.8 1.3 %collective-permute-start.3 = (bf16[1408,512]{1,0:T(8,128)(2,1)S(1)}, bf16[1408,512]{1,0:T(8,128)(2,1)S(1)}, u32[]{:S(2)}, u32[]{:S(2)}) collective-permute-start(bf16[1408,512]{1,0:T(8,128)(2,1)S(1)} %get-tuple-element.37), channel_id=1, source_target_pairs={{0,1},{1,0},{2,3},{3,2},{4,5},{5,4},{6,7},{7,6},{8,9},{9,8},{10,11... | collective-permute-start | bytes 4325384 | tf_op jit(solution)/shard_map/ppermute | solution.py:38
  17.1 0.8 collective-permute-start.4
  17.9 0.4 place.1
  18.3 1.6 %collective-permute-start.5 = (bf16[2,4,32,512]{3,2,1,0:T(8,128)(2,1)S(1)}, bf16[2,4,32,512]{3,2,1,0:T(8,128)(2,1)S(1)}, u32[]{:S(2)}, u32[]{:S(2)}) collective-permute-start(bf16[2,4,32,512]{3,2,1,0:T(8,128)(2,1)S(1)} %get-tuple-element.40), channel_id=1, source_target_pairs={{0,8},{4,12},{8,0},{12,4},{16,24},{20,28},{24,16},{28,20},{1,9},{5... | collective-permute-start | bytes 786440 | tf_op jit(solution)/shard_map/ppermute | solution.py:44
  20.0 2.6 %collective-permute-start.6 = (bf16[2,4,32,512]{3,2,1,0:T(8,128)(2,1)S(1)}, bf16[2,4,32,512]{3,2,1,0:T(8,128)(2,1)S(1)}, u32[]{:S(2)}, u32[]{:S(2)}) collective-permute-start(bf16[2,4,32,512]{3,2,1,0:T(8,128)(2,1)S(1)} %get-tuple-element.41), channel_id=1, source_target_pairs={{0,16},{4,20},{8,24},{12,28},{16,0},{20,4},{24,8},{28,12},{1,17},{... | collective-permute-start | bytes 786440 | tf_op jit(solution)/shard_map/ppermute | solution.py:44
  22.6 0.2 collective-permute-start.7
  22.8 5.7 %collective-permute-done.5.refs_1_.refs_3_ = bf16[2,4,32,512]{3,2,1,0:T(8,128)(2,1)S(1)} collective-permute-done((bf16[2,4,32,512]{3,2,1,0:T(8,128)(2,1)S(1)}, bf16[2,4,32,512]{3,2,1,0:T(8,128)(2,1)S(1)}, u32[]{:S(2)}, u32[]{:S(2)}) %collective-permute-start.5) | collective-permute-done | bytes 262176 | tf_op jit(solution)/shard_map/ppermute | solution.py:44
  28.5 12.5 %collective-permute-done.6.refs_2_.refs_4_ = bf16[2,4,32,512]{3,2,1,0:T(8,128)(2,1)S(1)} collective-permute-done((bf16[2,4,32,512]{3,2,1,0:T(8,128)(2,1)S(1)}, bf16[2,4,32,512]{3,2,1,0:T(8,128)(2,1)S(1)}, u32[]{:S(2)}, u32[]{:S(2)}) %collective-permute-start.6) | collective-permute-done | bytes 262176 | tf_op jit(solution)/shard_map/ppermute | solution.py:44
  41.0 0.0 collective-permute-done.7.refs_3_.refs_5_
  41.0 0.1 collective-permute-start.8
  41.1 1.1 slice_bitcast_fusion.1.refs_1_
  42.2 0.8 collective-permute-done.8.refs_6_
  43.0 0.7 back.1
  43.7 0.8 collective-permute-start.9
  44.5 1.5 %collective-permute-start.10 = (bf16[256,512]{1,0:T(8,128)(2,1)S(1)}, bf16[256,512]{1,0:T(8,128)(2,1)S(1)}, u32[]{:S(2)}, u32[]{:S(2)}) collective-permute-start(bf16[256,512]{1,0:T(8,128)(2,1)S(1)} %get-tuple-element.44), channel_id=1, source_target_pairs={{0,2},{1,3},{2,0},{3,1},{4,6},{5,7},{6,4},{7,5},{8,10},{9,11},{10,... | collective-permute-start | bytes 786440 | tf_op jit(solution)/shard_map/ppermute | solution.py:38
  46.0 7.8 %collective-permute-done.9.refs_2_.refs_1_ = bf16[256,512]{1,0:T(8,128)(2,1)S(1)} collective-permute-done((bf16[256,512]{1,0:T(8,128)(2,1)S(1)}, bf16[256,512]{1,0:T(8,128)(2,1)S(1)}, u32[]{:S(2)}, u32[]{:S(2)}) %collective-permute-start.9) | collective-permute-done | bytes 262176 | tf_op jit(solution)/shard_map/ppermute | solution.py:38
  53.8 1.0 collective-permute-done.10.refs_3_.refs_2_
  54.9 0.0 collective-permute-done.3.refs_3_.refs_1_.refs_4_
  54.9 0.0 collective-permute-done.4.refs_4_.refs_0_.refs_5_.refs_6_
  54.9 0.1 pass.1
  55.0 0.8 collective-permute-start.11
  55.8 1.4 %collective-permute-start.12 = (bf16[640,512]{1,0:T(8,128)(2,1)S(1)}, bf16[640,512]{1,0:T(8,128)(2,1)S(1)}, u32[]{:S(2)}, u32[]{:S(2)}) collective-permute-start(bf16[640,512]{1,0:T(8,128)(2,1)S(1)} %get-tuple-element.46), channel_id=1, source_target_pairs={{0,2},{1,3},{2,0},{3,1},{4,6},{5,7},{6,4},{7,5},{8,10},{9,11},{10,... | collective-permute-start | bytes 1966088 | tf_op jit(solution)/shard_map/ppermute | solution.py:38
  57.2 0.7 collective-permute-start.13
  57.9 1.3 %collective-permute-start.14 = (bf16[128,512]{1,0:T(8,128)(2,1)S(1)}, bf16[128,512]{1,0:T(8,128)(2,1)S(1)}, u32[]{:S(2)}, u32[]{:S(2)}) collective-permute-start(bf16[128,512]{1,0:T(8,128)(2,1)S(1)} %get-tuple-element.50), channel_id=1, source_target_pairs={{0,1},{1,0},{2,3},{3,2},{4,5},{5,4},{6,7},{7,6},{8,9},{9,8},{10,11... | collective-permute-start | bytes 393224 | tf_op jit(solution)/shard_map/ppermute | solution.py:38
  59.2 1.0 forward.1.refs_2_
  60.2 10.8 %collective-permute-done.11.refs_3_.refs_6_.refs_4_ = bf16[640,512]{1,0:T(8,128)(2,1)S(1)} collective-permute-done((bf16[640,512]{1,0:T(8,128)(2,1)S(1)}, bf16[640,512]{1,0:T(8,128)(2,1)S(1)}, u32[]{:S(2)}, u32[]{:S(2)}) %collective-permute-start.11) | collective-permute-done | bytes 655392 | tf_op jit(solution)/shard_map/ppermute | solution.py:38
  71.0 1.0 collective-permute-done.12.refs_4_.refs_7_.refs_5_
  72.0 0.4 rest.1.refs_0_
  72.4 1.0 collective-permute-done.13.refs_4_
  73.4 0.0 collective-permute-done.14.refs_5_
  73.4 0.4 factors.1.refs_2_.refs_3_
  73.8 0.8 collective-permute-start.18
  74.6 1.5 %collective-permute-start.19 = (bf16[2,384,512]{2,1,0:T(8,128)(2,1)S(1)}, bf16[2,384,512]{2,1,0:T(8,128)(2,1)S(1)}, u32[]{:S(2)}, u32[]{:S(2)}) collective-permute-start(bf16[2,384,512]{2,1,0:T(8,128)(2,1)S(1)} %factors.1.refs_2_.refs_3_), channel_id=1, source_target_pairs={{0,2},{1,3},{2,0},{3,1},{4,6},{5,7},{6,4},{7,5},{8,10},{9,11},{10,... | collective-permute-start | bytes 2359304 | tf_op jit(solution)/shard_map/ppermute | solution.py:38
  76.1 1.3 %slots.1 = (bf16[2,32,2048]{2,1,0:T(8,128)(2,1)S(1)}, bf16[2,32,2048]{2,1,0:T(8,128)(2,1)S(1)}, bf16[2,32,2048]{2,1,0:T(8,128)(2,1)S(1)}, bf16[2,32,2048]{2,1,0:T(8,128)(2,1)S(1)}) custom-call(s32[1]{0:T(128)} %bitcast.1.refs_0_, s32[1]{0:T(128)} %bitcast.refs_0_.refs_1_, bf16[2,384,512]{2,1,0:T(8,128)(2,1)S(1)} %factors.1.refs_2_.refs_3_, ...), custom_call_target="tpu_custom_call" | custom-call | tf_op jit(solution)/shard_map/slots/pallas_call | solution.py:186
  77.4 2.2 %collective-permute-start.15 = (bf16[2,32,2048]{2,1,0:T(8,128)(2,1)S(1)}, bf16[2,32,2048]{2,1,0:T(8,128)(2,1)S(1)}, u32[]{:S(2)}, u32[]{:S(2)}) collective-permute-start(bf16[2,32,2048]{2,1,0:T(8,128)(2,1)S(1)} %get-tuple-element.52), channel_id=1, source_target_pairs={{0,8},{4,12},{8,0},{12,4},{16,24},{20,28},{24,16},{28,20},{1,9},{5... | collective-permute-start | bytes 786440 | tf_op jit(solution)/shard_map/ppermute | solution.py:44
  79.6 1.1 collective-permute-start.16
  80.7 1.4 %collective-permute-start.17 = (bf16[2,32,2048]{2,1,0:T(8,128)(2,1)S(1)}, bf16[2,32,2048]{2,1,0:T(8,128)(2,1)S(1)}, u32[]{:S(2)}, u32[]{:S(2)}) collective-permute-start(bf16[2,32,2048]{2,1,0:T(8,128)(2,1)S(1)} %get-tuple-element.54), channel_id=1, source_target_pairs={{0,24},{4,28},{8,16},{12,20},{16,8},{20,12},{24,0},{28,4},{1,25},{... | collective-permute-start | bytes 786440 | tf_op jit(solution)/shard_map/ppermute | solution.py:44
  82.1 8.7 %collective-permute-done.18.refs_5_.refs_1_ = bf16[2,384,512]{2,1,0:T(8,128)(2,1)S(1)} collective-permute-done((bf16[2,384,512]{2,1,0:T(8,128)(2,1)S(1)}, bf16[2,384,512]{2,1,0:T(8,128)(2,1)S(1)}, u32[]{:S(2)}, u32[]{:S(2)}) %collective-permute-start.18) | collective-permute-done | bytes 786464 | tf_op jit(solution)/shard_map/ppermute | solution.py:38
  90.8 0.7 collective-permute-done.19.refs_7_.refs_0_
  91.5 0.1 cut.1
  91.5 0.9 collective-permute-start.22
  92.4 1.7 %collective-permute-start.23 = (bf16[384,512]{1,0:T(8,128)(2,1)S(1)}, bf16[384,512]{1,0:T(8,128)(2,1)S(1)}, u32[]{:S(2)}, u32[]{:S(2)}) collective-permute-start(bf16[384,512]{1,0:T(8,128)(2,1)S(1)} %get-tuple-element.61), channel_id=1, source_target_pairs={{0,2},{1,3},{2,0},{3,1},{4,6},{5,7},{6,4},{7,5},{8,10},{9,11},{10,... | collective-permute-start | bytes 1179656 | tf_op jit(solution)/shard_map/ppermute | solution.py:38
  94.1 2.1 %gram.1 = (f32[3,3,512,512]{3,2,1,0:T(8,128)S(1)}, f32[16,128]{1,0:T(8,128)S(1)}) custom-call(s32[1]{0:T(128)} %bitcast.1.refs_0_, bf16[4,8,32,512]{3,2,1,0:T(8,128)(2,1)S(1)} %get-tuple-element.55.refs_1_.refs_3_, bf16[256,2048]{1,0:T(8,128)(2,1)S(1)} %bitcast.12, bf16[2,384,512]{2,1,0:T(8,128)(2,1)S(1)} %factors.1.refs_2_.refs_3_, ...), custom_call_target="tpu_custom_call" | custom-call | tf_op jit(solution)/shard_map/gram/pallas_call | solution.py:186
  96.2 3.8 %collective-permute-done.16.refs_2_.refs_4_ = bf16[2,32,2048]{2,1,0:T(8,128)(2,1)S(1)} collective-permute-done((bf16[2,32,2048]{2,1,0:T(8,128)(2,1)S(1)}, bf16[2,32,2048]{2,1,0:T(8,128)(2,1)S(1)}, u32[]{:S(2)}, u32[]{:S(2)}) %collective-permute-start.16) | collective-permute-done | bytes 262176 | tf_op jit(solution)/shard_map/ppermute | solution.py:44
  100.0 0.1 collective-permute-start.20
  100.1 0.5 collective-permute-start.21
  100.6 0.0 copy-start.2
  100.6 1.2 %gram_late.1 = (f32[1,3,512,512]{3,2,1,0:T(8,128)S(1)}, f32[16,128]{1,0:T(8,128)S(1)}) custom-call(s32[1]{0:T(128)} %bitcast.1.refs_0_, f32[16,128]{1,0:T(8,128)S(1)} %get-tuple-element.56.refs_4_.refs_1_, f32[3,3,512,512]{3,2,1,0:T(8,128)S(1)} %get-tuple-element.59.refs_2_.refs_5_, bf16[4,8,32,512]{3,2,1,0:T(8,128)(2,1)S(1)} %get-tuple-element.55.refs_1_.refs_3_, ...), custom_call_target="tpu_custom_call" | custom-call | tf_op jit(solution)/shard_map/gram_late/pallas_call | solution.py:186
  101.8 2.1 %collective-permute-start.24 = (f32[16,128]{1,0:T(8,128)S(1)}, f32[16,128]{1,0:T(8,128)S(1)}, u32[]{:S(2)}, u32[]{:S(2)}) collective-permute-start(f32[16,128]{1,0:T(8,128)S(1)} %get-tuple-element.62.refs_8_.refs_1_), channel_id=1, source_target_pairs={{0,3},{1,2},{2,1},{3,0},{4,7},{5,6},{6,5},{7,4},{8,11},{9,10},{10,... | collective-permute-start | bytes 24584 | tf_op jit(solution)/shard_map/ppermute | solution.py:38
  103.9 0.6 collective-permute-start.25
  104.4 0.9 collective-permute-start.26
  105.4 1.2 %unplace.1 = bf16[1,128,2048]{2,1,0:T(8,128)(2,1)} custom-call(s32[1]{0:T(128)} %bitcast.refs_0_.refs_1_, bf16[144,512]{1,0:T(8,128)(2,1)S(1)} %copy-done.3, bf16[2,32,2048]{2,1,0:T(8,128)(2,1)S(1)} %get-tuple-element.51.refs_0_.refs_2_, bf16[2,32,2048]{2,1,0:T(8,128)(2,1)S(1)} %collective-permute-done.15.refs_1_.refs_3_, ...), custom_call_target="tpu_custom_call" | custom-call | tf_op jit(solution)/shard_map/unplace/pallas_call | solution.py:186
  106.6 1.0 collective-permute-done.25.refs_3_
  107.5 0.6 collective-permute-done.26.refs_4_
  108.1 4.2 %adam.1 = f32[1,3,512,512]{3,2,1,0:T(8,128)} custom-call(s32[1]{0:T(128)} %bitcast.1.refs_0_, f32[16,128]{1,0:T(8,128)S(1)} %get-tuple-element.62.refs_8_.refs_1_, f32[16,128]{1,0:T(8,128)S(1)} %collective-permute-done.24.refs_2_, f32[16,128]{1,0:T(8,128)S(1)} %collective-permute-done.25.refs_3_, f32[16,128]{1,0:T(8,128)S(1)} %collective-permute-done.26.refs_4_, ...), custom_call_target="tpu_custom_call" | custom-call | tf_op jit(solution)/shard_map/adam/pallas_call | solution.py:186
  (18 shorter events, 0.2 us)
Async XLA Ops:
  0.6 14.4 %copy-start = (bf16[1,1,256,2048]{3,2,1,0:T(8,128)(2,1)S(1)}, bf16[1,1,256,2048]{3,2,1,0:T(8,128)(2,1)}, u32[]{:S(2)}) copy-start(bf16[1,1,256,2048]{3,2,1,0:T(8,128)(2,1)} %param.15) | copy-start | bytes 3145732
  3.4 7.5 %collective-permute-start = (bf16[144,512]{1,0:T(8,128)(2,1)}, bf16[144,512]{1,0:T(8,128)(2,1)S(1)}, u32[]{:S(2)}, u32[]{:S(2)}) collective-permute-start(bf16[144,512]{1,0:T(8,128)(2,1)} %get-tuple-element.34), channel_id=1, source_target_pairs={{0,1},{1,0},{2,3},{3,2},{4,5},{5,4},{6,7},{7,6},{8,9},{9,8},{10,11... | collective-permute-start | bytes 442376 | tf_op jit(solution)/shard_map/ppermute | solution.py:38
  6.3 8.7 %collective-permute-start.1 = (bf16[144,512]{1,0:T(8,128)(2,1)}, bf16[144,512]{1,0:T(8,128)(2,1)S(1)}, u32[]{:S(2)}, u32[]{:S(2)}) collective-permute-start(bf16[144,512]{1,0:T(8,128)(2,1)} %get-tuple-element.35), channel_id=1, source_target_pairs={{0,2},{1,3},{2,0},{3,1},{4,6},{5,7},{6,4},{7,5},{8,10},{9,11},{10,... | collective-permute-start | bytes 442376 | tf_op jit(solution)/shard_map/ppermute | solution.py:38
  7.9 7.2 %collective-permute-start.2 = (bf16[144,512]{1,0:T(8,128)(2,1)}, bf16[144,512]{1,0:T(8,128)(2,1)S(1)}, u32[]{:S(2)}, u32[]{:S(2)}) collective-permute-start(bf16[144,512]{1,0:T(8,128)(2,1)} %get-tuple-element.36), channel_id=1, source_target_pairs={{0,3},{1,2},{2,1},{3,0},{4,7},{5,6},{6,5},{7,4},{8,11},{9,10},{10,... | collective-permute-start | bytes 442376 | tf_op jit(solution)/shard_map/ppermute | solution.py:38
  9.2 8.7 %copy-start.3 = (bf16[144,512]{1,0:T(8,128)(2,1)S(1)}, bf16[144,512]{1,0:T(8,128)(2,1)}, u32[]{:S(2)}) copy-start(bf16[144,512]{1,0:T(8,128)(2,1)} %get-tuple-element.33.refs_1_) | copy-start | bytes 442372
  15.8 39.1 %collective-permute-start.3 = (bf16[1408,512]{1,0:T(8,128)(2,1)S(1)}, bf16[1408,512]{1,0:T(8,128)(2,1)S(1)}, u32[]{:S(2)}, u32[]{:S(2)}) collective-permute-start(bf16[1408,512]{1,0:T(8,128)(2,1)S(1)} %get-tuple-element.37), channel_id=1, source_target_pairs={{0,1},{1,0},{2,3},{3,2},{4,5},{5,4},{6,7},{7,6},{8,9},{9,8},{10,11... | collective-permute-start | bytes 4325384 | tf_op jit(solution)/shard_map/ppermute | solution.py:38
  17.1 37.8 %collective-permute-start.4 = (bf16[1408,512]{1,0:T(8,128)(2,1)S(1)}, bf16[1408,512]{1,0:T(8,128)(2,1)S(1)}, u32[]{:S(2)}, u32[]{:S(2)}) collective-permute-start(bf16[1408,512]{1,0:T(8,128)(2,1)S(1)} %get-tuple-element.38), channel_id=1, source_target_pairs={{0,2},{1,3},{2,0},{3,1},{4,6},{5,7},{6,4},{7,5},{8,10},{9,11},{10,... | collective-permute-start | bytes 4325384 | tf_op jit(solution)/shard_map/ppermute | solution.py:38
  18.3 10.1 %collective-permute-start.5 = (bf16[2,4,32,512]{3,2,1,0:T(8,128)(2,1)S(1)}, bf16[2,4,32,512]{3,2,1,0:T(8,128)(2,1)S(1)}, u32[]{:S(2)}, u32[]{:S(2)}) collective-permute-start(bf16[2,4,32,512]{3,2,1,0:T(8,128)(2,1)S(1)} %get-tuple-element.40), channel_id=1, source_target_pairs={{0,8},{4,12},{8,0},{12,4},{16,24},{20,28},{24,16},{28,20},{1,9},{5... | collective-permute-start | bytes 786440 | tf_op jit(solution)/shard_map/ppermute | solution.py:44
  20.0 21.0 %collective-permute-start.6 = (bf16[2,4,32,512]{3,2,1,0:T(8,128)(2,1)S(1)}, bf16[2,4,32,512]{3,2,1,0:T(8,128)(2,1)S(1)}, u32[]{:S(2)}, u32[]{:S(2)}) collective-permute-start(bf16[2,4,32,512]{3,2,1,0:T(8,128)(2,1)S(1)} %get-tuple-element.41), channel_id=1, source_target_pairs={{0,16},{4,20},{8,24},{12,28},{16,0},{20,4},{24,8},{28,12},{1,17},{... | collective-permute-start | bytes 786440 | tf_op jit(solution)/shard_map/ppermute | solution.py:44
  22.6 18.4 %collective-permute-start.7 = (bf16[2,4,32,512]{3,2,1,0:T(8,128)(2,1)S(1)}, bf16[2,4,32,512]{3,2,1,0:T(8,128)(2,1)S(1)}, u32[]{:S(2)}, u32[]{:S(2)}) collective-permute-start(bf16[2,4,32,512]{3,2,1,0:T(8,128)(2,1)S(1)} %get-tuple-element.42), channel_id=1, source_target_pairs={{0,24},{4,28},{8,16},{12,20},{16,8},{20,12},{24,0},{28,4},{1,25},{... | collective-permute-start | bytes 786440 | tf_op jit(solution)/shard_map/ppermute | solution.py:44
  41.0 2.0 %collective-permute-start.8 = (bf16[4,4,32,512]{3,2,1,0:T(8,128)(2,1)S(1)}, bf16[4,4,32,512]{3,2,1,0:T(8,128)(2,1)S(1)}, u32[]{:S(2)}, u32[]{:S(2)}) collective-permute-start(bf16[4,4,32,512]{3,2,1,0:T(8,128)(2,1)S(1)} %pick.2), channel_id=1, source_target_pairs={{0,4},{4,0},{8,12},{12,8},{16,20},{20,16},{24,28},{28,24},{1,5},{5... | collective-permute-start | bytes 1572872 | tf_op jit(solution)/shard_map/ppermute | solution.py:68
  43.7 10.1 %collective-permute-start.9 = (bf16[256,512]{1,0:T(8,128)(2,1)S(1)}, bf16[256,512]{1,0:T(8,128)(2,1)S(1)}, u32[]{:S(2)}, u32[]{:S(2)}) collective-permute-start(bf16[256,512]{1,0:T(8,128)(2,1)S(1)} %get-tuple-element.43), channel_id=1, source_target_pairs={{0,1},{1,0},{2,3},{3,2},{4,5},{5,4},{6,7},{7,6},{8,9},{9,8},{10,11... | collective-permute-start | bytes 786440 | tf_op jit(solution)/shard_map/ppermute | solution.py:38
  44.5 10.3 %collective-permute-start.10 = (bf16[256,512]{1,0:T(8,128)(2,1)S(1)}, bf16[256,512]{1,0:T(8,128)(2,1)S(1)}, u32[]{:S(2)}, u32[]{:S(2)}) collective-permute-start(bf16[256,512]{1,0:T(8,128)(2,1)S(1)} %get-tuple-element.44), channel_id=1, source_target_pairs={{0,2},{1,3},{2,0},{3,1},{4,6},{5,7},{6,4},{7,5},{8,10},{9,11},{10,... | collective-permute-start | bytes 786440 | tf_op jit(solution)/shard_map/ppermute | solution.py:38
  55.0 16.0 %collective-permute-start.11 = (bf16[640,512]{1,0:T(8,128)(2,1)S(1)}, bf16[640,512]{1,0:T(8,128)(2,1)S(1)}, u32[]{:S(2)}, u32[]{:S(2)}) collective-permute-start(bf16[640,512]{1,0:T(8,128)(2,1)S(1)} %get-tuple-element.45), channel_id=1, source_target_pairs={{0,1},{1,0},{2,3},{3,2},{4,5},{5,4},{6,7},{7,6},{8,9},{9,8},{10,11... | collective-permute-start | bytes 1966088 | tf_op jit(solution)/shard_map/ppermute | solution.py:38
  55.8 16.2 %collective-permute-start.12 = (bf16[640,512]{1,0:T(8,128)(2,1)S(1)}, bf16[640,512]{1,0:T(8,128)(2,1)S(1)}, u32[]{:S(2)}, u32[]{:S(2)}) collective-permute-start(bf16[640,512]{1,0:T(8,128)(2,1)S(1)} %get-tuple-element.46), channel_id=1, source_target_pairs={{0,2},{1,3},{2,0},{3,1},{4,6},{5,7},{6,4},{7,5},{8,10},{9,11},{10,... | collective-permute-start | bytes 1966088 | tf_op jit(solution)/shard_map/ppermute | solution.py:38
  57.2 16.2 %collective-permute-start.13 = (bf16[128,512]{1,0:T(8,128)(2,1)S(1)}, bf16[128,512]{1,0:T(8,128)(2,1)S(1)}, u32[]{:S(2)}, u32[]{:S(2)}) collective-permute-start(bf16[128,512]{1,0:T(8,128)(2,1)S(1)} %get-tuple-element.49), channel_id=1, source_target_pairs={{0,2},{1,3},{2,0},{3,1},{4,6},{5,7},{6,4},{7,5},{8,10},{9,11},{10,... | collective-permute-start | bytes 393224 | tf_op jit(solution)/shard_map/ppermute | solution.py:38
  57.9 15.5 %collective-permute-start.14 = (bf16[128,512]{1,0:T(8,128)(2,1)S(1)}, bf16[128,512]{1,0:T(8,128)(2,1)S(1)}, u32[]{:S(2)}, u32[]{:S(2)}) collective-permute-start(bf16[128,512]{1,0:T(8,128)(2,1)S(1)} %get-tuple-element.50), channel_id=1, source_target_pairs={{0,1},{1,0},{2,3},{3,2},{4,5},{5,4},{6,7},{7,6},{8,9},{9,8},{10,11... | collective-permute-start | bytes 393224 | tf_op jit(solution)/shard_map/ppermute | solution.py:38
  73.8 17.0 %collective-permute-start.18 = (bf16[2,384,512]{2,1,0:T(8,128)(2,1)S(1)}, bf16[2,384,512]{2,1,0:T(8,128)(2,1)S(1)}, u32[]{:S(2)}, u32[]{:S(2)}) collective-permute-start(bf16[2,384,512]{2,1,0:T(8,128)(2,1)S(1)} %factors.1.refs_2_.refs_3_), channel_id=1, source_target_pairs={{0,1},{1,0},{2,3},{3,2},{4,5},{5,4},{6,7},{7,6},{8,9},{9,8},{10,11... | collective-permute-start | bytes 2359304 | tf_op jit(solution)/shard_map/ppermute | solution.py:38
  74.6 16.9 %collective-permute-start.19 = (bf16[2,384,512]{2,1,0:T(8,128)(2,1)S(1)}, bf16[2,384,512]{2,1,0:T(8,128)(2,1)S(1)}, u32[]{:S(2)}, u32[]{:S(2)}) collective-permute-start(bf16[2,384,512]{2,1,0:T(8,128)(2,1)S(1)} %factors.1.refs_2_.refs_3_), channel_id=1, source_target_pairs={{0,2},{1,3},{2,0},{3,1},{4,6},{5,7},{6,4},{7,5},{8,10},{9,11},{10,... | collective-permute-start | bytes 2359304 | tf_op jit(solution)/shard_map/ppermute | solution.py:38
  77.4 18.8 %collective-permute-start.15 = (bf16[2,32,2048]{2,1,0:T(8,128)(2,1)S(1)}, bf16[2,32,2048]{2,1,0:T(8,128)(2,1)S(1)}, u32[]{:S(2)}, u32[]{:S(2)}) collective-permute-start(bf16[2,32,2048]{2,1,0:T(8,128)(2,1)S(1)} %get-tuple-element.52), channel_id=1, source_target_pairs={{0,8},{4,12},{8,0},{12,4},{16,24},{20,28},{24,16},{28,20},{1,9},{5... | collective-permute-start | bytes 786440 | tf_op jit(solution)/shard_map/ppermute | solution.py:44
  79.6 20.3 %collective-permute-start.16 = (bf16[2,32,2048]{2,1,0:T(8,128)(2,1)S(1)}, bf16[2,32,2048]{2,1,0:T(8,128)(2,1)S(1)}, u32[]{:S(2)}, u32[]{:S(2)}) collective-permute-start(bf16[2,32,2048]{2,1,0:T(8,128)(2,1)S(1)} %get-tuple-element.53), channel_id=1, source_target_pairs={{0,16},{4,20},{8,24},{12,28},{16,0},{20,4},{24,8},{28,12},{1,17},{... | collective-permute-start | bytes 786440 | tf_op jit(solution)/shard_map/ppermute | solution.py:44
  80.7 19.2 %collective-permute-start.17 = (bf16[2,32,2048]{2,1,0:T(8,128)(2,1)S(1)}, bf16[2,32,2048]{2,1,0:T(8,128)(2,1)S(1)}, u32[]{:S(2)}, u32[]{:S(2)}) collective-permute-start(bf16[2,32,2048]{2,1,0:T(8,128)(2,1)S(1)} %get-tuple-element.54), channel_id=1, source_target_pairs={{0,24},{4,28},{8,16},{12,20},{16,8},{20,12},{24,0},{28,4},{1,25},{... | collective-permute-start | bytes 786440 | tf_op jit(solution)/shard_map/ppermute | solution.py:44
  91.5 9.0 %collective-permute-start.22 = (bf16[384,512]{1,0:T(8,128)(2,1)S(1)}, bf16[384,512]{1,0:T(8,128)(2,1)S(1)}, u32[]{:S(2)}, u32[]{:S(2)}) collective-permute-start(bf16[384,512]{1,0:T(8,128)(2,1)S(1)} %get-tuple-element.60), channel_id=1, source_target_pairs={{0,1},{1,0},{2,3},{3,2},{4,5},{5,4},{6,7},{7,6},{8,9},{9,8},{10,11... | collective-permute-start | bytes 1179656 | tf_op jit(solution)/shard_map/ppermute | solution.py:38
  92.4 8.2 %collective-permute-start.23 = (bf16[384,512]{1,0:T(8,128)(2,1)S(1)}, bf16[384,512]{1,0:T(8,128)(2,1)S(1)}, u32[]{:S(2)}, u32[]{:S(2)}) collective-permute-start(bf16[384,512]{1,0:T(8,128)(2,1)S(1)} %get-tuple-element.61), channel_id=1, source_target_pairs={{0,2},{1,3},{2,0},{3,1},{4,6},{5,7},{6,4},{7,5},{8,10},{9,11},{10,... | collective-permute-start | bytes 1179656 | tf_op jit(solution)/shard_map/ppermute | solution.py:38
  100.0 5.4 %collective-permute-start.20 = (bf16[2,32,2048]{2,1,0:T(8,128)(2,1)S(1)}, bf16[2,32,2048]{2,1,0:T(8,128)(2,1)S(1)}, u32[]{:S(2)}, u32[]{:S(2)}) collective-permute-start(bf16[2,32,2048]{2,1,0:T(8,128)(2,1)S(1)} %get-tuple-element.57), channel_id=1, source_target_pairs={{0,4},{4,0},{8,12},{12,8},{16,20},{20,16},{24,28},{28,24},{1,5},{5... | collective-permute-start | bytes 786440 | tf_op jit(solution)/shard_map/ppermute | solution.py:68
  100.1 5.3 %collective-permute-start.21 = (bf16[2,32,2048]{2,1,0:T(8,128)(2,1)S(1)}, bf16[2,32,2048]{2,1,0:T(8,128)(2,1)S(1)}, u32[]{:S(2)}, u32[]{:S(2)}) collective-permute-start(bf16[2,32,2048]{2,1,0:T(8,128)(2,1)S(1)} %get-tuple-element.58), channel_id=1, source_target_pairs={{0,4},{4,0},{8,12},{12,8},{16,20},{20,16},{24,28},{28,24},{1,5},{5... | collective-permute-start | bytes 786440 | tf_op jit(solution)/shard_map/ppermute | solution.py:68
  100.6 7.5 %copy-start.1 = (f32[1,3,512,512]{3,2,1,0:T(8,128)S(1)}, f32[1,3,512,512]{3,2,1,0:T(8,128)}, u32[]{:S(2)}) copy-start(f32[1,3,512,512]{3,2,1,0:T(8,128)} %refs_7_.1) | copy-start | bytes 9437188
  100.6 7.5 %copy-start.2 = (f32[1,3,512,512]{3,2,1,0:T(8,128)S(1)}, f32[1,3,512,512]{3,2,1,0:T(8,128)}, u32[]{:S(2)}) copy-start(f32[1,3,512,512]{3,2,1,0:T(8,128)} %refs_8_.1) | copy-start | bytes 9437188
  101.8 4.7 %collective-permute-start.24 = (f32[16,128]{1,0:T(8,128)S(1)}, f32[16,128]{1,0:T(8,128)S(1)}, u32[]{:S(2)}, u32[]{:S(2)}) collective-permute-start(f32[16,128]{1,0:T(8,128)S(1)} %get-tuple-element.62.refs_8_.refs_1_), channel_id=1, source_target_pairs={{0,3},{1,2},{2,1},{3,0},{4,7},{5,6},{6,5},{7,4},{8,11},{9,10},{10,... | collective-permute-start | bytes 24584 | tf_op jit(solution)/shard_map/ppermute | solution.py:38
  103.9 3.7 %collective-permute-start.25 = (f32[16,128]{1,0:T(8,128)S(1)}, f32[16,128]{1,0:T(8,128)S(1)}, u32[]{:S(2)}, u32[]{:S(2)}) collective-permute-start(f32[16,128]{1,0:T(8,128)S(1)} %get-tuple-element.62.refs_8_.refs_1_), channel_id=1, source_target_pairs={{0,2},{1,3},{2,0},{3,1},{4,6},{5,7},{6,4},{7,5},{8,10},{9,11},{10,... | collective-permute-start | bytes 24584 | tf_op jit(solution)/shard_map/ppermute | solution.py:38
  104.4 3.7 %collective-permute-start.26 = (f32[16,128]{1,0:T(8,128)S(1)}, f32[16,128]{1,0:T(8,128)S(1)}, u32[]{:S(2)}, u32[]{:S(2)}) collective-permute-start(f32[16,128]{1,0:T(8,128)S(1)} %get-tuple-element.62.refs_8_.refs_1_), channel_id=1, source_target_pairs={{0,1},{1,0},{2,3},{3,2},{4,5},{5,4},{6,7},{7,6},{8,9},{9,8},{10,11... | collective-permute-start | bytes 24584 | tf_op jit(solution)/shard_map/ppermute | solution.py:38

commit v13 on v12

--- a/solution.py
+++ b/solution.py
@@ -571,7 +571,7 @@
     count = sum(len(group) for group in groups)
     seg_rows, hidden_width = first_moment.shape[2:]
     grams = [gram] + [from_peer(gram, k) for k in reversed(range(1, count))]
-    tile = min(seg_rows, 256)
+    tile = min(seg_rows, 512)
     moment_spec = pl.BlockSpec((1, 1, tile, hidden_width), lambda m, d: (0, m, d, 0))
     (adam_step,) = call(
         functools.partial(adam_kernel, count, groups),

time: 113 us -> 112 us (level)
  no operation moved by 1% of the time
where the time goes in v13:
time: 112 us
  waiting for transfers between devices  61.1 us (55%)
  starting transfers between devices  31.3 us (28%)
  Pallas kernels  15.4 us (14%)
  local copies, waits for them, and re-layouts  2.39 us (2%)
  between operations  1.55 us (1%)
    ppermute x18, waiting for transfers between devices, from_peer(): lax.ppermute(array, 'replica', [(i, i ^ offset) for i in range(count)])  38.3 us
    ppermute x6, waiting for transfers between devices, across_chips(): lax.ppermute(part, 'expert', [(i, i ^ 2 * k) for i in range(count)])  22 us
    ppermute x18, starting transfers between devices, from_peer(): lax.ppermute(array, 'replica', [(i, i ^ offset) for i in range(count)])  21.5 us
    pallas_call x17, Pallas kernels, call(): pl.pallas_call(body, grid=grid, in_specs=list(specs) + [VMEM] * len(after...  15.4 us
    ppermute x6, starting transfers between devices, across_chips(): lax.ppermute(part, 'expert', [(i, i ^ 2 * k) for i in range(count)])  9.18 us
  transfers between devices with their start and end apart: 27, of which 15 were waited for; matrix products, arithmetic and copies ran while one was open for 2% of the time, Pallas kernels for 8%

profile of v13, /device:TPU:0, one launch (start us, length us, event | category | flops | bytes accessed | tf_op | source)
XLA Modules:
  0.0 111.8 jit_solution(5660004350347278093)
XLA Ops:
  1.4 2.0 %rows.1 = (bf16[144,512]{1,0:T(8,128)(2,1)}, bf16[144,512]{1,0:T(8,128)(2,1)}, bf16[144,512]{1,0:T(8,128)(2,1)}, bf16[144,512]{1,0:T(8,128)(2,1)}) custom-call(s32[1]{0:T(128)} %bitcast.1.refs_0_, s32[1,1]{1,0:T(1,128)S(6)} %copy.10.refs_1_, f32[8]{0:T(128)} %refs_2_.1, s32[1,128]{1,0:T(1,128)} %bitcast.14, bf16[128,2048]{1,0:T(8,128)(2,1)} %bitcast.13), custom_call_target="tpu_custom_call" | custom-call | tf_op jit(solution)/shard_map/rows/pallas_call | solution.py:186
  3.4 2.9 %collective-permute-start = (bf16[144,512]{1,0:T(8,128)(2,1)}, bf16[144,512]{1,0:T(8,128)(2,1)S(1)}, u32[]{:S(2)}, u32[]{:S(2)}) collective-permute-start(bf16[144,512]{1,0:T(8,128)(2,1)} %get-tuple-element.34), channel_id=1, source_target_pairs={{0,1},{1,0},{2,3},{3,2},{4,5},{5,4},{6,7},{7,6},{8,9},{9,8},{10,11... | collective-permute-start | bytes 442376 | tf_op jit(solution)/shard_map/ppermute | solution.py:38
  6.3 1.5 %collective-permute-start.1 = (bf16[144,512]{1,0:T(8,128)(2,1)}, bf16[144,512]{1,0:T(8,128)(2,1)S(1)}, u32[]{:S(2)}, u32[]{:S(2)}) collective-permute-start(bf16[144,512]{1,0:T(8,128)(2,1)} %get-tuple-element.35), channel_id=1, source_target_pairs={{0,2},{1,3},{2,0},{3,1},{4,6},{5,7},{6,4},{7,5},{8,10},{9,11},{10,... | collective-permute-start | bytes 442376 | tf_op jit(solution)/shard_map/ppermute | solution.py:38
  7.9 1.3 %slice_bitcast_fusion.refs_1_.refs_2_.refs_3_ = bf16[2,512,512]{2,1,0:T(8,128)(2,1)S(1)} fusion(bf16[1,3,512,512]{3,2,1,0:T(8,128)(2,1)} %param.8), kind=kLoop, calls=%fused_computation | loop fusion | bytes 2097152 | tf_op jit(solution)/shard_map/squeeze | solution.py:622
  9.2 0.0 copy-start.3
  9.2 0.1 pad_add_fusion.refs_0_
  9.3 1.7 %collective-permute-done.refs_3_.refs_2_ = bf16[144,512]{1,0:T(8,128)(2,1)S(1)} collective-permute-done((bf16[144,512]{1,0:T(8,128)(2,1)}, bf16[144,512]{1,0:T(8,128)(2,1)S(1)}, u32[]{:S(2)}, u32[]{:S(2)}) %collective-permute-start) | collective-permute-done | bytes 147488 | tf_op jit(solution)/shard_map/ppermute | solution.py:38
  10.9 4.1 %collective-permute-done.1.refs_4_.refs_3_ = bf16[144,512]{1,0:T(8,128)(2,1)S(1)} collective-permute-done((bf16[144,512]{1,0:T(8,128)(2,1)}, bf16[144,512]{1,0:T(8,128)(2,1)S(1)}, u32[]{:S(2)}, u32[]{:S(2)}) %collective-permute-start.1) | collective-permute-done | bytes 147488 | tf_op jit(solution)/shard_map/ppermute | solution.py:38
  15.0 0.0 collective-permute-done.2.refs_5_.refs_4_
  15.0 0.7 payload.1
  15.8 1.3 %collective-permute-start.3 = (bf16[1408,512]{1,0:T(8,128)(2,1)S(1)}, bf16[1408,512]{1,0:T(8,128)(2,1)S(1)}, u32[]{:S(2)}, u32[]{:S(2)}) collective-permute-start(bf16[1408,512]{1,0:T(8,128)(2,1)S(1)} %get-tuple-element.37), channel_id=1, source_target_pairs={{0,1},{1,0},{2,3},{3,2},{4,5},{5,4},{6,7},{7,6},{8,9},{9,8},{10,11... | collective-permute-start | bytes 4325384 | tf_op jit(solution)/shard_map/ppermute | solution.py:38
  17.1 0.8 collective-permute-start.4
  17.9 0.4 place.1
  18.3 1.6 %collective-permute-start.5 = (bf16[2,4,32,512]{3,2,1,0:T(8,128)(2,1)S(1)}, bf16[2,4,32,512]{3,2,1,0:T(8,128)(2,1)S(1)}, u32[]{:S(2)}, u32[]{:S(2)}) collective-permute-start(bf16[2,4,32,512]{3,2,1,0:T(8,128)(2,1)S(1)} %get-tuple-element.40), channel_id=1, source_target_pairs={{0,8},{4,12},{8,0},{12,4},{16,24},{20,28},{24,16},{28,20},{1,9},{5... | collective-permute-start | bytes 786440 | tf_op jit(solution)/shard_map/ppermute | solution.py:44
  20.0 2.6 %collective-permute-start.6 = (bf16[2,4,32,512]{3,2,1,0:T(8,128)(2,1)S(1)}, bf16[2,4,32,512]{3,2,1,0:T(8,128)(2,1)S(1)}, u32[]{:S(2)}, u32[]{:S(2)}) collective-permute-start(bf16[2,4,32,512]{3,2,1,0:T(8,128)(2,1)S(1)} %get-tuple-element.41), channel_id=1, source_target_pairs={{0,16},{4,20},{8,24},{12,28},{16,0},{20,4},{24,8},{28,12},{1,17},{... | collective-permute-start | bytes 786440 | tf_op jit(solution)/shard_map/ppermute | solution.py:44
  22.6 0.2 collective-permute-start.7
  22.8 5.7 %collective-permute-done.5.refs_1_.refs_3_ = bf16[2,4,32,512]{3,2,1,0:T(8,128)(2,1)S(1)} collective-permute-done((bf16[2,4,32,512]{3,2,1,0:T(8,128)(2,1)S(1)}, bf16[2,4,32,512]{3,2,1,0:T(8,128)(2,1)S(1)}, u32[]{:S(2)}, u32[]{:S(2)}) %collective-permute-start.5) | collective-permute-done | bytes 262176 | tf_op jit(solution)/shard_map/ppermute | solution.py:44
  28.5 12.5 %collective-permute-done.6.refs_2_.refs_4_ = bf16[2,4,32,512]{3,2,1,0:T(8,128)(2,1)S(1)} collective-permute-done((bf16[2,4,32,512]{3,2,1,0:T(8,128)(2,1)S(1)}, bf16[2,4,32,512]{3,2,1,0:T(8,128)(2,1)S(1)}, u32[]{:S(2)}, u32[]{:S(2)}) %collective-permute-start.6) | collective-permute-done | bytes 262176 | tf_op jit(solution)/shard_map/ppermute | solution.py:44
  41.0 0.1 collective-permute-start.8
  41.1 1.1 slice_bitcast_fusion.1.refs_1_
  42.2 0.8 collective-permute-done.8.refs_6_
  43.0 0.7 back.1
  43.7 0.8 collective-permute-start.9
  44.5 1.5 %collective-permute-start.10 = (bf16[256,512]{1,0:T(8,128)(2,1)S(1)}, bf16[256,512]{1,0:T(8,128)(2,1)S(1)}, u32[]{:S(2)}, u32[]{:S(2)}) collective-permute-start(bf16[256,512]{1,0:T(8,128)(2,1)S(1)} %get-tuple-element.44), channel_id=1, source_target_pairs={{0,2},{1,3},{2,0},{3,1},{4,6},{5,7},{6,4},{7,5},{8,10},{9,11},{10,... | collective-permute-start | bytes 786440 | tf_op jit(solution)/shard_map/ppermute | solution.py:38
  46.0 7.8 %collective-permute-done.9.refs_2_.refs_1_ = bf16[256,512]{1,0:T(8,128)(2,1)S(1)} collective-permute-done((bf16[256,512]{1,0:T(8,128)(2,1)S(1)}, bf16[256,512]{1,0:T(8,128)(2,1)S(1)}, u32[]{:S(2)}, u32[]{:S(2)}) %collective-permute-start.9) | collective-permute-done | bytes 262176 | tf_op jit(solution)/shard_map/ppermute | solution.py:38
  53.8 1.0 collective-permute-done.10.refs_3_.refs_2_
  54.9 0.1 pass.1
  55.0 0.8 collective-permute-start.11
  55.8 1.4 %collective-permute-start.12 = (bf16[640,512]{1,0:T(8,128)(2,1)S(1)}, bf16[640,512]{1,0:T(8,128)(2,1)S(1)}, u32[]{:S(2)}, u32[]{:S(2)}) collective-permute-start(bf16[640,512]{1,0:T(8,128)(2,1)S(1)} %get-tuple-element.46), channel_id=1, source_target_pairs={{0,2},{1,3},{2,0},{3,1},{4,6},{5,7},{6,4},{7,5},{8,10},{9,11},{10,... | collective-permute-start | bytes 1966088 | tf_op jit(solution)/shard_map/ppermute | solution.py:38
  57.2 0.7 collective-permute-start.13
  57.9 1.3 %collective-permute-start.14 = (bf16[128,512]{1,0:T(8,128)(2,1)S(1)}, bf16[128,512]{1,0:T(8,128)(2,1)S(1)}, u32[]{:S(2)}, u32[]{:S(2)}) collective-permute-start(bf16[128,512]{1,0:T(8,128)(2,1)S(1)} %get-tuple-element.50), channel_id=1, source_target_pairs={{0,1},{1,0},{2,3},{3,2},{4,5},{5,4},{6,7},{7,6},{8,9},{9,8},{10,11... | collective-permute-start | bytes 393224 | tf_op jit(solution)/shard_map/ppermute | solution.py:38
  59.2 1.0 forward.1.refs_2_
  60.2 10.8 %collective-permute-done.11.refs_3_.refs_6_.refs_4_ = bf16[640,512]{1,0:T(8,128)(2,1)S(1)} collective-permute-done((bf16[640,512]{1,0:T(8,128)(2,1)S(1)}, bf16[640,512]{1,0:T(8,128)(2,1)S(1)}, u32[]{:S(2)}, u32[]{:S(2)}) %collective-permute-start.11) | collective-permute-done | bytes 655392 | tf_op jit(solution)/shard_map/ppermute | solution.py:38
  71.0 1.0 collective-permute-done.12.refs_4_.refs_7_.refs_5_
  72.0 0.4 rest.1.refs_0_
  72.4 1.0 collective-permute-done.13.refs_4_
  73.4 0.4 factors.1.refs_2_.refs_3_
  73.8 0.8 collective-permute-start.18
  74.6 1.5 %collective-permute-start.19 = (bf16[2,384,512]{2,1,0:T(8,128)(2,1)S(1)}, bf16[2,384,512]{2,1,0:T(8,128)(2,1)S(1)}, u32[]{:S(2)}, u32[]{:S(2)}) collective-permute-start(bf16[2,384,512]{2,1,0:T(8,128)(2,1)S(1)} %factors.1.refs_2_.refs_3_), channel_id=1, source_target_pairs={{0,2},{1,3},{2,0},{3,1},{4,6},{5,7},{6,4},{7,5},{8,10},{9,11},{10,... | collective-permute-start | bytes 2359304 | tf_op jit(solution)/shard_map/ppermute | solution.py:38
  76.1 1.3 %slots.1 = (bf16[2,32,2048]{2,1,0:T(8,128)(2,1)S(1)}, bf16[2,32,2048]{2,1,0:T(8,128)(2,1)S(1)}, bf16[2,32,2048]{2,1,0:T(8,128)(2,1)S(1)}, bf16[2,32,2048]{2,1,0:T(8,128)(2,1)S(1)}) custom-call(s32[1]{0:T(128)} %bitcast.1.refs_0_, s32[1]{0:T(128)} %bitcast.refs_0_.refs_1_, bf16[2,384,512]{2,1,0:T(8,128)(2,1)S(1)} %factors.1.refs_2_.refs_3_, ...), custom_call_target="tpu_custom_call" | custom-call | tf_op jit(solution)/shard_map/slots/pallas_call | solution.py:186
  77.4 2.2 %collective-permute-start.15 = (bf16[2,32,2048]{2,1,0:T(8,128)(2,1)S(1)}, bf16[2,32,2048]{2,1,0:T(8,128)(2,1)S(1)}, u32[]{:S(2)}, u32[]{:S(2)}) collective-permute-start(bf16[2,32,2048]{2,1,0:T(8,128)(2,1)S(1)} %get-tuple-element.52), channel_id=1, source_target_pairs={{0,8},{4,12},{8,0},{12,4},{16,24},{20,28},{24,16},{28,20},{1,9},{5... | collective-permute-start | bytes 786440 | tf_op jit(solution)/shard_map/ppermute | solution.py:44
  79.6 1.1 collective-permute-start.16
  80.7 1.4 %collective-permute-start.17 = (bf16[2,32,2048]{2,1,0:T(8,128)(2,1)S(1)}, bf16[2,32,2048]{2,1,0:T(8,128)(2,1)S(1)}, u32[]{:S(2)}, u32[]{:S(2)}) collective-permute-start(bf16[2,32,2048]{2,1,0:T(8,128)(2,1)S(1)} %get-tuple-element.54), channel_id=1, source_target_pairs={{0,24},{4,28},{8,16},{12,20},{16,8},{20,12},{24,0},{28,4},{1,25},{... | collective-permute-start | bytes 786440 | tf_op jit(solution)/shard_map/ppermute | solution.py:44
  82.1 8.7 %collective-permute-done.18.refs_5_.refs_1_ = bf16[2,384,512]{2,1,0:T(8,128)(2,1)S(1)} collective-permute-done((bf16[2,384,512]{2,1,0:T(8,128)(2,1)S(1)}, bf16[2,384,512]{2,1,0:T(8,128)(2,1)S(1)}, u32[]{:S(2)}, u32[]{:S(2)}) %collective-permute-start.18) | collective-permute-done | bytes 786464 | tf_op jit(solution)/shard_map/ppermute | solution.py:38
  90.8 0.7 collective-permute-done.19.refs_7_.refs_0_
  91.5 0.1 cut.1
  91.5 0.9 collective-permute-start.22
  92.4 1.7 %collective-permute-start.23 = (bf16[384,512]{1,0:T(8,128)(2,1)S(1)}, bf16[384,512]{1,0:T(8,128)(2,1)S(1)}, u32[]{:S(2)}, u32[]{:S(2)}) collective-permute-start(bf16[384,512]{1,0:T(8,128)(2,1)S(1)} %get-tuple-element.61), channel_id=1, source_target_pairs={{0,2},{1,3},{2,0},{3,1},{4,6},{5,7},{6,4},{7,5},{8,10},{9,11},{10,... | collective-permute-start | bytes 1179656 | tf_op jit(solution)/shard_map/ppermute | solution.py:38
  94.1 2.0 %gram.1 = (f32[3,3,512,512]{3,2,1,0:T(8,128)S(1)}, f32[16,128]{1,0:T(8,128)S(1)}) custom-call(s32[1]{0:T(128)} %bitcast.1.refs_0_, bf16[4,8,32,512]{3,2,1,0:T(8,128)(2,1)S(1)} %get-tuple-element.55.refs_1_.refs_3_, bf16[256,2048]{1,0:T(8,128)(2,1)S(1)} %bitcast.12, bf16[2,384,512]{2,1,0:T(8,128)(2,1)S(1)} %factors.1.refs_2_.refs_3_, ...), custom_call_target="tpu_custom_call" | custom-call | tf_op jit(solution)/shard_map/gram/pallas_call | solution.py:186
  96.1 0.0 collective-permute-done.15.refs_1_.refs_3_
  96.2 3.8 %collective-permute-done.16.refs_2_.refs_4_ = bf16[2,32,2048]{2,1,0:T(8,128)(2,1)S(1)} collective-permute-done((bf16[2,32,2048]{2,1,0:T(8,128)(2,1)S(1)}, bf16[2,32,2048]{2,1,0:T(8,128)(2,1)S(1)}, u32[]{:S(2)}, u32[]{:S(2)}) %collective-permute-start.16) | collective-permute-done | bytes 262176 | tf_op jit(solution)/shard_map/ppermute | solution.py:44
  100.0 0.1 collective-permute-start.20
  100.1 0.5 collective-permute-start.21
  100.6 0.0 copy-start.2
  100.6 1.2 %gram_late.1 = (f32[1,3,512,512]{3,2,1,0:T(8,128)S(1)}, f32[16,128]{1,0:T(8,128)S(1)}) custom-call(s32[1]{0:T(128)} %bitcast.1.refs_0_, f32[16,128]{1,0:T(8,128)S(1)} %get-tuple-element.56.refs_4_.refs_1_, f32[3,3,512,512]{3,2,1,0:T(8,128)S(1)} %get-tuple-element.59.refs_2_.refs_5_, bf16[4,8,32,512]{3,2,1,0:T(8,128)(2,1)S(1)} %get-tuple-element.55.refs_1_.refs_3_, ...), custom_call_target="tpu_custom_call" | custom-call | tf_op jit(solution)/shard_map/gram_late/pallas_call | solution.py:186
  101.8 2.1 %collective-permute-start.24 = (f32[16,128]{1,0:T(8,128)S(1)}, f32[16,128]{1,0:T(8,128)S(1)}, u32[]{:S(2)}, u32[]{:S(2)}) collective-permute-start(f32[16,128]{1,0:T(8,128)S(1)} %get-tuple-element.62.refs_8_.refs_1_), channel_id=1, source_target_pairs={{0,3},{1,2},{2,1},{3,0},{4,7},{5,6},{6,5},{7,4},{8,11},{9,10},{10,... | collective-permute-start | bytes 24584 | tf_op jit(solution)/shard_map/ppermute | solution.py:38
  103.9 0.6 collective-permute-start.25
  104.4 0.9 collective-permute-start.26
  105.4 0.0 collective-permute-done.20.refs_6_
  105.4 0.0 collective-permute-done.21.refs_7_
  105.4 1.2 %unplace.1 = bf16[1,128,2048]{2,1,0:T(8,128)(2,1)} custom-call(s32[1]{0:T(128)} %bitcast.refs_0_.refs_1_, bf16[144,512]{1,0:T(8,128)(2,1)S(1)} %copy-done.3, bf16[2,32,2048]{2,1,0:T(8,128)(2,1)S(1)} %get-tuple-element.51.refs_0_.refs_2_, bf16[2,32,2048]{2,1,0:T(8,128)(2,1)S(1)} %collective-permute-done.15.refs_1_.refs_3_, ...), custom_call_target="tpu_custom_call" | custom-call | tf_op jit(solution)/shard_map/unplace/pallas_call | solution.py:186
  106.6 1.0 collective-permute-done.25.refs_3_
  107.5 0.6 collective-permute-done.26.refs_4_
  108.1 3.7 %adam.1 = f32[1,3,512,512]{3,2,1,0:T(8,128)} custom-call(s32[1]{0:T(128)} %bitcast.1.refs_0_, f32[16,128]{1,0:T(8,128)S(1)} %get-tuple-element.62.refs_8_.refs_1_, f32[16,128]{1,0:T(8,128)S(1)} %collective-permute-done.24.refs_2_, f32[16,128]{1,0:T(8,128)S(1)} %collective-permute-done.25.refs_3_, f32[16,128]{1,0:T(8,128)S(1)} %collective-permute-done.26.refs_4_, ...), custom_call_target="tpu_custom_call" | custom-call | tf_op jit(solution)/shard_map/adam/pallas_call | solution.py:186
  (18 shorter events, 0.2 us)
Async XLA Ops:
  0.6 14.4 %copy-start = (bf16[1,1,256,2048]{3,2,1,0:T(8,128)(2,1)S(1)}, bf16[1,1,256,2048]{3,2,1,0:T(8,128)(2,1)}, u32[]{:S(2)}) copy-start(bf16[1,1,256,2048]{3,2,1,0:T(8,128)(2,1)} %param.15) | copy-start | bytes 3145732
  3.4 7.5 %collective-permute-start = (bf16[144,512]{1,0:T(8,128)(2,1)}, bf16[144,512]{1,0:T(8,128)(2,1)S(1)}, u32[]{:S(2)}, u32[]{:S(2)}) collective-permute-start(bf16[144,512]{1,0:T(8,128)(2,1)} %get-tuple-element.34), channel_id=1, source_target_pairs={{0,1},{1,0},{2,3},{3,2},{4,5},{5,4},{6,7},{7,6},{8,9},{9,8},{10,11... | collective-permute-start | bytes 442376 | tf_op jit(solution)/shard_map/ppermute | solution.py:38
  6.3 8.7 %collective-permute-start.1 = (bf16[144,512]{1,0:T(8,128)(2,1)}, bf16[144,512]{1,0:T(8,128)(2,1)S(1)}, u32[]{:S(2)}, u32[]{:S(2)}) collective-permute-start(bf16[144,512]{1,0:T(8,128)(2,1)} %get-tuple-element.35), channel_id=1, source_target_pairs={{0,2},{1,3},{2,0},{3,1},{4,6},{5,7},{6,4},{7,5},{8,10},{9,11},{10,... | collective-permute-start | bytes 442376 | tf_op jit(solution)/shard_map/ppermute | solution.py:38
  7.9 7.2 %collective-permute-start.2 = (bf16[144,512]{1,0:T(8,128)(2,1)}, bf16[144,512]{1,0:T(8,128)(2,1)S(1)}, u32[]{:S(2)}, u32[]{:S(2)}) collective-permute-start(bf16[144,512]{1,0:T(8,128)(2,1)} %get-tuple-element.36), channel_id=1, source_target_pairs={{0,3},{1,2},{2,1},{3,0},{4,7},{5,6},{6,5},{7,4},{8,11},{9,10},{10,... | collective-permute-start | bytes 442376 | tf_op jit(solution)/shard_map/ppermute | solution.py:38
  9.2 8.7 %copy-start.3 = (bf16[144,512]{1,0:T(8,128)(2,1)S(1)}, bf16[144,512]{1,0:T(8,128)(2,1)}, u32[]{:S(2)}) copy-start(bf16[144,512]{1,0:T(8,128)(2,1)} %get-tuple-element.33.refs_1_) | copy-start | bytes 442372
  15.8 39.1 %collective-permute-start.3 = (bf16[1408,512]{1,0:T(8,128)(2,1)S(1)}, bf16[1408,512]{1,0:T(8,128)(2,1)S(1)}, u32[]{:S(2)}, u32[]{:S(2)}) collective-permute-start(bf16[1408,512]{1,0:T(8,128)(2,1)S(1)} %get-tuple-element.37), channel_id=1, source_target_pairs={{0,1},{1,0},{2,3},{3,2},{4,5},{5,4},{6,7},{7,6},{8,9},{9,8},{10,11... | collective-permute-start | bytes 4325384 | tf_op jit(solution)/shard_map/ppermute | solution.py:38
  17.1 37.8 %collective-permute-start.4 = (bf16[1408,512]{1,0:T(8,128)(2,1)S(1)}, bf16[1408,512]{1,0:T(8,128)(2,1)S(1)}, u32[]{:S(2)}, u32[]{:S(2)}) collective-permute-start(bf16[1408,512]{1,0:T(8,128)(2,1)S(1)} %get-tuple-element.38), channel_id=1, source_target_pairs={{0,2},{1,3},{2,0},{3,1},{4,6},{5,7},{6,4},{7,5},{8,10},{9,11},{10,... | collective-permute-start | bytes 4325384 | tf_op jit(solution)/shard_map/ppermute | solution.py:38
  18.3 10.1 %collective-permute-start.5 = (bf16[2,4,32,512]{3,2,1,0:T(8,128)(2,1)S(1)}, bf16[2,4,32,512]{3,2,1,0:T(8,128)(2,1)S(1)}, u32[]{:S(2)}, u32[]{:S(2)}) collective-permute-start(bf16[2,4,32,512]{3,2,1,0:T(8,128)(2,1)S(1)} %get-tuple-element.40), channel_id=1, source_target_pairs={{0,8},{4,12},{8,0},{12,4},{16,24},{20,28},{24,16},{28,20},{1,9},{5... | collective-permute-start | bytes 786440 | tf_op jit(solution)/shard_map/ppermute | solution.py:44
  20.0 21.0 %collective-permute-start.6 = (bf16[2,4,32,512]{3,2,1,0:T(8,128)(2,1)S(1)}, bf16[2,4,32,512]{3,2,1,0:T(8,128)(2,1)S(1)}, u32[]{:S(2)}, u32[]{:S(2)}) collective-permute-start(bf16[2,4,32,512]{3,2,1,0:T(8,128)(2,1)S(1)} %get-tuple-element.41), channel_id=1, source_target_pairs={{0,16},{4,20},{8,24},{12,28},{16,0},{20,4},{24,8},{28,12},{1,17},{... | collective-permute-start | bytes 786440 | tf_op jit(solution)/shard_map/ppermute | solution.py:44
  22.6 18.4 %collective-permute-start.7 = (bf16[2,4,32,512]{3,2,1,0:T(8,128)(2,1)S(1)}, bf16[2,4,32,512]{3,2,1,0:T(8,128)(2,1)S(1)}, u32[]{:S(2)}, u32[]{:S(2)}) collective-permute-start(bf16[2,4,32,512]{3,2,1,0:T(8,128)(2,1)S(1)} %get-tuple-element.42), channel_id=1, source_target_pairs={{0,24},{4,28},{8,16},{12,20},{16,8},{20,12},{24,0},{28,4},{1,25},{... | collective-permute-start | bytes 786440 | tf_op jit(solution)/shard_map/ppermute | solution.py:44
  41.0 2.0 %collective-permute-start.8 = (bf16[4,4,32,512]{3,2,1,0:T(8,128)(2,1)S(1)}, bf16[4,4,32,512]{3,2,1,0:T(8,128)(2,1)S(1)}, u32[]{:S(2)}, u32[]{:S(2)}) collective-permute-start(bf16[4,4,32,512]{3,2,1,0:T(8,128)(2,1)S(1)} %pick.2), channel_id=1, source_target_pairs={{0,4},{4,0},{8,12},{12,8},{16,20},{20,16},{24,28},{28,24},{1,5},{5... | collective-permute-start | bytes 1572872 | tf_op jit(solution)/shard_map/ppermute | solution.py:68
  43.7 10.1 %collective-permute-start.9 = (bf16[256,512]{1,0:T(8,128)(2,1)S(1)}, bf16[256,512]{1,0:T(8,128)(2,1)S(1)}, u32[]{:S(2)}, u32[]{:S(2)}) collective-permute-start(bf16[256,512]{1,0:T(8,128)(2,1)S(1)} %get-tuple-element.43), channel_id=1, source_target_pairs={{0,1},{1,0},{2,3},{3,2},{4,5},{5,4},{6,7},{7,6},{8,9},{9,8},{10,11... | collective-permute-start | bytes 786440 | tf_op jit(solution)/shard_map/ppermute | solution.py:38
  44.5 10.3 %collective-permute-start.10 = (bf16[256,512]{1,0:T(8,128)(2,1)S(1)}, bf16[256,512]{1,0:T(8,128)(2,1)S(1)}, u32[]{:S(2)}, u32[]{:S(2)}) collective-permute-start(bf16[256,512]{1,0:T(8,128)(2,1)S(1)} %get-tuple-element.44), channel_id=1, source_target_pairs={{0,2},{1,3},{2,0},{3,1},{4,6},{5,7},{6,4},{7,5},{8,10},{9,11},{10,... | collective-permute-start | bytes 786440 | tf_op jit(solution)/shard_map/ppermute | solution.py:38
  55.0 16.0 %collective-permute-start.11 = (bf16[640,512]{1,0:T(8,128)(2,1)S(1)}, bf16[640,512]{1,0:T(8,128)(2,1)S(1)}, u32[]{:S(2)}, u32[]{:S(2)}) collective-permute-start(bf16[640,512]{1,0:T(8,128)(2,1)S(1)} %get-tuple-element.45), channel_id=1, source_target_pairs={{0,1},{1,0},{2,3},{3,2},{4,5},{5,4},{6,7},{7,6},{8,9},{9,8},{10,11... | collective-permute-start | bytes 1966088 | tf_op jit(solution)/shard_map/ppermute | solution.py:38
  55.8 16.2 %collective-permute-start.12 = (bf16[640,512]{1,0:T(8,128)(2,1)S(1)}, bf16[640,512]{1,0:T(8,128)(2,1)S(1)}, u32[]{:S(2)}, u32[]{:S(2)}) collective-permute-start(bf16[640,512]{1,0:T(8,128)(2,1)S(1)} %get-tuple-element.46), channel_id=1, source_target_pairs={{0,2},{1,3},{2,0},{3,1},{4,6},{5,7},{6,4},{7,5},{8,10},{9,11},{10,... | collective-permute-start | bytes 1966088 | tf_op jit(solution)/shard_map/ppermute | solution.py:38
  57.2 16.2 %collective-permute-start.13 = (bf16[128,512]{1,0:T(8,128)(2,1)S(1)}, bf16[128,512]{1,0:T(8,128)(2,1)S(1)}, u32[]{:S(2)}, u32[]{:S(2)}) collective-permute-start(bf16[128,512]{1,0:T(8,128)(2,1)S(1)} %get-tuple-element.49), channel_id=1, source_target_pairs={{0,2},{1,3},{2,0},{3,1},{4,6},{5,7},{6,4},{7,5},{8,10},{9,11},{10,... | collective-permute-start | bytes 393224 | tf_op jit(solution)/shard_map/ppermute | solution.py:38
  57.9 15.5 %collective-permute-start.14 = (bf16[128,512]{1,0:T(8,128)(2,1)S(1)}, bf16[128,512]{1,0:T(8,128)(2,1)S(1)}, u32[]{:S(2)}, u32[]{:S(2)}) collective-permute-start(bf16[128,512]{1,0:T(8,128)(2,1)S(1)} %get-tuple-element.50), channel_id=1, source_target_pairs={{0,1},{1,0},{2,3},{3,2},{4,5},{5,4},{6,7},{7,6},{8,9},{9,8},{10,11... | collective-permute-start | bytes 393224 | tf_op jit(solution)/shard_map/ppermute | solution.py:38
  73.8 17.0 %collective-permute-start.18 = (bf16[2,384,512]{2,1,0:T(8,128)(2,1)S(1)}, bf16[2,384,512]{2,1,0:T(8,128)(2,1)S(1)}, u32[]{:S(2)}, u32[]{:S(2)}) collective-permute-start(bf16[2,384,512]{2,1,0:T(8,128)(2,1)S(1)} %factors.1.refs_2_.refs_3_), channel_id=1, source_target_pairs={{0,1},{1,0},{2,3},{3,2},{4,5},{5,4},{6,7},{7,6},{8,9},{9,8},{10,11... | collective-permute-start | bytes 2359304 | tf_op jit(solution)/shard_map/ppermute | solution.py:38
  74.6 16.9 %collective-permute-start.19 = (bf16[2,384,512]{2,1,0:T(8,128)(2,1)S(1)}, bf16[2,384,512]{2,1,0:T(8,128)(2,1)S(1)}, u32[]{:S(2)}, u32[]{:S(2)}) collective-permute-start(bf16[2,384,512]{2,1,0:T(8,128)(2,1)S(1)} %factors.1.refs_2_.refs_3_), channel_id=1, source_target_pairs={{0,2},{1,3},{2,0},{3,1},{4,6},{5,7},{6,4},{7,5},{8,10},{9,11},{10,... | collective-permute-start | bytes 2359304 | tf_op jit(solution)/shard_map/ppermute | solution.py:38
  77.4 18.8 %collective-permute-start.15 = (bf16[2,32,2048]{2,1,0:T(8,128)(2,1)S(1)}, bf16[2,32,2048]{2,1,0:T(8,128)(2,1)S(1)}, u32[]{:S(2)}, u32[]{:S(2)}) collective-permute-start(bf16[2,32,2048]{2,1,0:T(8,128)(2,1)S(1)} %get-tuple-element.52), channel_id=1, source_target_pairs={{0,8},{4,12},{8,0},{12,4},{16,24},{20,28},{24,16},{28,20},{1,9},{5... | collective-permute-start | bytes 786440 | tf_op jit(solution)/shard_map/ppermute | solution.py:44
  79.6 20.3 %collective-permute-start.16 = (bf16[2,32,2048]{2,1,0:T(8,128)(2,1)S(1)}, bf16[2,32,2048]{2,1,0:T(8,128)(2,1)S(1)}, u32[]{:S(2)}, u32[]{:S(2)}) collective-permute-start(bf16[2,32,2048]{2,1,0:T(8,128)(2,1)S(1)} %get-tuple-element.53), channel_id=1, source_target_pairs={{0,16},{4,20},{8,24},{12,28},{16,0},{20,4},{24,8},{28,12},{1,17},{... | collective-permute-start | bytes 786440 | tf_op jit(solution)/shard_map/ppermute | solution.py:44
  80.7 19.2 %collective-permute-start.17 = (bf16[2,32,2048]{2,1,0:T(8,128)(2,1)S(1)}, bf16[2,32,2048]{2,1,0:T(8,128)(2,1)S(1)}, u32[]{:S(2)}, u32[]{:S(2)}) collective-permute-start(bf16[2,32,2048]{2,1,0:T(8,128)(2,1)S(1)} %get-tuple-element.54), channel_id=1, source_target_pairs={{0,24},{4,28},{8,16},{12,20},{16,8},{20,12},{24,0},{28,4},{1,25},{... | collective-permute-start | bytes 786440 | tf_op jit(solution)/shard_map/ppermute | solution.py:44
  91.5 9.0 %collective-permute-start.22 = (bf16[384,512]{1,0:T(8,128)(2,1)S(1)}, bf16[384,512]{1,0:T(8,128)(2,1)S(1)}, u32[]{:S(2)}, u32[]{:S(2)}) collective-permute-start(bf16[384,512]{1,0:T(8,128)(2,1)S(1)} %get-tuple-element.60), channel_id=1, source_target_pairs={{0,1},{1,0},{2,3},{3,2},{4,5},{5,4},{6,7},{7,6},{8,9},{9,8},{10,11... | collective-permute-start | bytes 1179656 | tf_op jit(solution)/shard_map/ppermute | solution.py:38
  92.4 8.2 %collective-permute-start.23 = (bf16[384,512]{1,0:T(8,128)(2,1)S(1)}, bf16[384,512]{1,0:T(8,128)(2,1)S(1)}, u32[]{:S(2)}, u32[]{:S(2)}) collective-permute-start(bf16[384,512]{1,0:T(8,128)(2,1)S(1)} %get-tuple-element.61), channel_id=1, source_target_pairs={{0,2},{1,3},{2,0},{3,1},{4,6},{5,7},{6,4},{7,5},{8,10},{9,11},{10,... | collective-permute-start | bytes 1179656 | tf_op jit(solution)/shard_map/ppermute | solution.py:38
  100.0 5.4 %collective-permute-start.20 = (bf16[2,32,2048]{2,1,0:T(8,128)(2,1)S(1)}, bf16[2,32,2048]{2,1,0:T(8,128)(2,1)S(1)}, u32[]{:S(2)}, u32[]{:S(2)}) collective-permute-start(bf16[2,32,2048]{2,1,0:T(8,128)(2,1)S(1)} %get-tuple-element.57), channel_id=1, source_target_pairs={{0,4},{4,0},{8,12},{12,8},{16,20},{20,16},{24,28},{28,24},{1,5},{5... | collective-permute-start | bytes 786440 | tf_op jit(solution)/shard_map/ppermute | solution.py:68
  100.1 5.3 %collective-permute-start.21 = (bf16[2,32,2048]{2,1,0:T(8,128)(2,1)S(1)}, bf16[2,32,2048]{2,1,0:T(8,128)(2,1)S(1)}, u32[]{:S(2)}, u32[]{:S(2)}) collective-permute-start(bf16[2,32,2048]{2,1,0:T(8,128)(2,1)S(1)} %get-tuple-element.58), channel_id=1, source_target_pairs={{0,4},{4,0},{8,12},{12,8},{16,20},{20,16},{24,28},{28,24},{1,5},{5... | collective-permute-start | bytes 786440 | tf_op jit(solution)/shard_map/ppermute | solution.py:68
  100.6 7.5 %copy-start.1 = (f32[1,3,512,512]{3,2,1,0:T(8,128)S(1)}, f32[1,3,512,512]{3,2,1,0:T(8,128)}, u32[]{:S(2)}) copy-start(f32[1,3,512,512]{3,2,1,0:T(8,128)} %refs_7_.1) | copy-start | bytes 9437188
  100.6 7.5 %copy-start.2 = (f32[1,3,512,512]{3,2,1,0:T(8,128)S(1)}, f32[1,3,512,512]{3,2,1,0:T(8,128)}, u32[]{:S(2)}) copy-start(f32[1,3,512,512]{3,2,1,0:T(8,128)} %refs_8_.1) | copy-start | bytes 9437188
  101.8 4.7 %collective-permute-start.24 = (f32[16,128]{1,0:T(8,128)S(1)}, f32[16,128]{1,0:T(8,128)S(1)}, u32[]{:S(2)}, u32[]{:S(2)}) collective-permute-start(f32[16,128]{1,0:T(8,128)S(1)} %get-tuple-element.62.refs_8_.refs_1_), channel_id=1, source_target_pairs={{0,3},{1,2},{2,1},{3,0},{4,7},{5,6},{6,5},{7,4},{8,11},{9,10},{10,... | collective-permute-start | bytes 24584 | tf_op jit(solution)/shard_map/ppermute | solution.py:38
  103.9 3.7 %collective-permute-start.25 = (f32[16,128]{1,0:T(8,128)S(1)}, f32[16,128]{1,0:T(8,128)S(1)}, u32[]{:S(2)}, u32[]{:S(2)}) collective-permute-start(f32[16,128]{1,0:T(8,128)S(1)} %get-tuple-element.62.refs_8_.refs_1_), channel_id=1, source_target_pairs={{0,2},{1,3},{2,0},{3,1},{4,6},{5,7},{6,4},{7,5},{8,10},{9,11},{10,... | collective-permute-start | bytes 24584 | tf_op jit(solution)/shard_map/ppermute | solution.py:38
  104.4 3.7 %collective-permute-start.26 = (f32[16,128]{1,0:T(8,128)S(1)}, f32[16,128]{1,0:T(8,128)S(1)}, u32[]{:S(2)}, u32[]{:S(2)}) collective-permute-start(f32[16,128]{1,0:T(8,128)S(1)} %get-tuple-element.62.refs_8_.refs_1_), channel_id=1, source_target_pairs={{0,1},{1,0},{2,3},{3,2},{4,5},{5,4},{6,7},{7,6},{8,9},{9,8},{10,11... | collective-permute-start | bytes 24584 | tf_op jit(solution)/shard_map/ppermute | solution.py:38
